TPU v7x, 32 devices: a whole 2x2x4 slice. The times are simulated.
32 devices in a mesh: row: 8 (over y, x, core), col: 4 (over z).
Axes of the slice: x: 2, y: 2, z: 4, core: 2. Of those that a mesh axis runs over, the one named last changes fastest.
Arguments:
- forcing_right_hand: float32 [4, 128, 512], P(None, 'row', 'col'), may hold values from 0 to 2
- material: int32 [4, 128, 512], P(None, 'row', 'col'), may hold values from 0 to 7
- capacity: float32 [8], replicated, may hold values from 0.3 to 3
- conductivity: float32 [8], replicated, may hold values from 0.2 to 2
- vent_open: float32 [128, 512], P('row', 'col'), may hold values from 0.5 to 2
- partners: int32 [8, 4, 2], P('row', 'col'), may hold values from 0 to 7, as said below
- subspace_basis: bfloat16 [64, 4, 128, 512], P(None, None, 'row', 'col'), may hold values from -0.5 to 1.5
Outputs:
- thermal_iterate: float32 [4, 128, 512], P(None, 'row', 'col')
- defect_vector: float32 [4, 128, 512], P(None, 'row', 'col')
- restricted_operator_blocks: float32 [8, 4, 8, 64, 64], P('row', 'col')
Inputs may be any that keep to these rules, and one draw needn't show every extreme that they name: In each round the row indices of one col index pair up: partners[q, c, k] = r whenever partners[r, c, k] = q, and q never equals r.
All inputs are finite; a program needn't handle non-finite values.
Results may differ from a plain program's by a relative error of at most 0.01.
Values may be sent and summed in bfloat16 or wider, within the bound.
No kernel may reach another device: no remote copies, remote signals or barrier semaphores. Data moves between devices by JAX's collectives and lax.ppermute only.
A program may use at most 64 MiB of HBM per device.

v0:
```python
import jax
import jax.numpy as jnp
from jax import lax
from jax.sharding import PartitionSpec as P

ITERS = 2


highest = lax.Precision.HIGHEST
plenum_gain = 1.0


def padded_2(block, sides, width):
    for axis, dim in sides:
        count = lax.axis_size(axis)
        forward = [(i, i + 1) for i in range(count - 1)]
        backward = [(target, source) for source, target in forward]
        low = lax.ppermute(
            lax.slice_in_dim(block, block.shape[dim] - width, None, axis=dim), axis, forward
        )
        high = lax.ppermute(lax.slice_in_dim(block, 0, width, axis=dim), axis, backward)
        block = jnp.concatenate([low, block, high], axis=dim)
    return block


def harmonic(left_side, right_side):
    return 2.0 * left_side * right_side / (left_side + right_side)


def lookup(material, table):
    result = jnp.zeros(material.shape, jnp.float32)
    for class_id in range(table.shape[0]):
        result = result + jnp.where(material == class_id, table[class_id], 0.0)
    return result


def local_apply(basis_block, coef_parts):
    diagonal, upper_z, lower_z, upper_x, lower_x, upper_y, lower_y = coef_parts
    padded = jnp.pad(basis_block, ((0, 0), (1, 1), (1, 1), (1, 1)))
    beside_all = upper_z * padded[:, 2:, 1:-1, 1:-1] + lower_z * padded[:, :-2, 1:-1, 1:-1]
    beside_all = (
        beside_all + upper_x * padded[:, 1:-1, 2:, 1:-1] + lower_x * padded[:, 1:-1, :-2, 1:-1]
    )
    beside_all = (
        beside_all + upper_y * padded[:, 1:-1, 1:-1, 2:] + lower_y * padded[:, 1:-1, 1:-1, :-2]
    )
    return diagonal * basis_block - beside_all


def body(forcing_right_hand, material, capacity, conductivity, vent_open, partners, subspace_basis):
    layers = forcing_right_hand.shape[0]
    vectors = subspace_basis.shape[0]
    cells = forcing_right_hand.size
    row_count = lax.axis_size("row")
    row_at = lax.axis_index("row")
    row_numbers = jnp.arange(row_count, dtype=jnp.int32)
    conduct_field = lookup(material, conductivity)
    capacity_field = lookup(material, capacity)
    rim_conduct = padded_2(conduct_field, (("row", 1), ("col", 2)), 1)
    padded_z = jnp.pad(conduct_field, ((1, 1), (0, 0), (0, 0)))
    upper_z = harmonic(conduct_field, padded_z[2:])
    lower_z = harmonic(conduct_field, padded_z[:-2])
    upper_x = harmonic(conduct_field, rim_conduct[:, 2:, 1:-1])
    lower_x = harmonic(conduct_field, rim_conduct[:, :-2, 1:-1])
    upper_y = harmonic(conduct_field, rim_conduct[:, 1:-1, 2:])
    lower_y = harmonic(conduct_field, rim_conduct[:, 1:-1, :-2])
    own_partners = partners.reshape(-1)
    vent_rows = lax.all_gather(vent_open[None], "row", axis=0, tiled=True)
    vent_sum = jnp.zeros_like(vent_open)
    for pair_round in range(own_partners.shape[0]):
        vent_sum = vent_sum + vent_rows[own_partners[pair_round]]
    diagonal = capacity_field + upper_z + lower_z + upper_x + lower_x + upper_y + lower_y
    diagonal = diagonal.at[layers - 1].add(plenum_gain * vent_open * vent_sum)
    coef_parts = (diagonal, upper_z, lower_z, upper_x, lower_x, upper_y, lower_y)

    def operator_apply(values):
        padded = padded_2(values, (("row", 1), ("col", 2)), 1)
        stacked_z = jnp.pad(values, ((1, 1), (0, 0), (0, 0)))
        beside_all = upper_z * stacked_z[2:] + lower_z * stacked_z[:-2]
        beside_all = beside_all + upper_x * padded[:, 2:, 1:-1] + lower_x * padded[:, :-2, 1:-1]
        beside_all = beside_all + upper_y * padded[:, 1:-1, 2:] + lower_y * padded[:, 1:-1, :-2]
        result = diagonal * values - beside_all
        top_rows = lax.all_gather((vent_open * values[layers - 1])[None], "row", axis=0, tiled=True)
        coupled = jnp.zeros_like(vent_open)
        for pair_round in range(own_partners.shape[0]):
            coupled = coupled + top_rows[own_partners[pair_round]]
        return result.at[layers - 1].add(-plenum_gain * vent_open * coupled)

    basis_full = subspace_basis.astype(jnp.float32)
    basis_flat = basis_full.reshape(vectors, -1)
    own_applied = local_apply(basis_full, coef_parts)
    own_block = jnp.dot(basis_flat, own_applied.reshape(vectors, -1).T, precision=highest)
    basis_rim = padded_2(subspace_basis, (("row", 2), ("col", 3)), 1).astype(jnp.float32)
    ahead_x = -jnp.einsum(
        "azy,bzy->ab",
        basis_full[:, :, -1, :] * upper_x[:, -1, :],
        basis_rim[:, :, -1, 1:-1],
        precision=highest,
    )
    behind_x = -jnp.einsum(
        "azy,bzy->ab",
        basis_full[:, :, 0, :] * lower_x[:, 0, :],
        basis_rim[:, :, 0, 1:-1],
        precision=highest,
    )
    upper_col = -jnp.einsum(
        "azx,bzx->ab",
        basis_full[:, :, :, -1] * upper_y[:, :, -1],
        basis_rim[:, :, 1:-1, -1],
        precision=highest,
    )
    lower_col = -jnp.einsum(
        "azx,bzx->ab",
        basis_full[:, :, :, 0] * lower_y[:, :, 0],
        basis_rim[:, :, 1:-1, 0],
        precision=highest,
    )
    own_top = basis_full[:, layers - 1].reshape(vectors, -1) * vent_open.reshape(-1)
    multiplicity = jnp.zeros((row_count,), jnp.float32)
    for pair_round in range(own_partners.shape[0]):
        multiplicity = multiplicity + (row_numbers == own_partners[pair_round]).astype(jnp.float32)
    vent_flat = vent_rows.reshape(row_count, -1)
    panel = subspace_basis[:, layers - 1].reshape(1, vectors, -1)
    partner_top = (
        lax.all_gather(panel, "row", axis=0, tiled=True).astype(jnp.float32) * vent_flat[:, None, :]
    )
    blocks = -plenum_gain * jnp.einsum("as,nbs->nab", own_top, partner_top, precision=highest)
    plenum_blocks = blocks * multiplicity[:, None, None]
    own_hot = (row_numbers == row_at).astype(jnp.float32)[:, None, None]
    next_hot = (row_numbers == row_at + 1).astype(jnp.float32)[:, None, None]
    prev_hot = (row_numbers == row_at - 1).astype(jnp.float32)[:, None, None]
    galerkin_rows = own_block * own_hot + ahead_x * next_hot + behind_x * prev_hot + plenum_blocks
    factor = jnp.linalg.cholesky(own_block)

    def coarse_apply(values):
        all_rows = lax.all_gather(values[None], "row", axis=0, tiled=True)
        beside = padded_2(values[None], (("col", 0),), 1)
        along = jnp.einsum("qab,qb->a", galerkin_rows, all_rows, precision=highest)
        along = along + jnp.dot(lower_col, beside[0], precision=highest)
        return along + jnp.dot(upper_col, beside[2], precision=highest)

    def invert_galerkin_operator(right_side):
        values = jax.scipy.linalg.cho_solve((factor, True), right_side)
        values = values + jax.scipy.linalg.cho_solve(
            (factor, True), right_side - coarse_apply(values)
        )
        return values

    def remove_subspace_part(values):
        return jnp.dot(basis_flat, values.reshape(-1), precision=highest)

    def spread_subspace_values(coarse_vector):
        return jnp.dot(coarse_vector, basis_flat, precision=highest).reshape(
            forcing_right_hand.shape
        )

    thermal_iterate = spread_subspace_values(
        invert_galerkin_operator(remove_subspace_part(forcing_right_hand))
    )
    defect_vector = forcing_right_hand - operator_apply(thermal_iterate)
    conjugate_update = defect_vector - spread_subspace_values(
        invert_galerkin_operator(remove_subspace_part(operator_apply(defect_vector)))
    )
    norm_now = lax.psum(jnp.sum(defect_vector * defect_vector), ("row", "col"))
    for iteration in range(ITERS):
        applied = operator_apply(conjugate_update)
        curvature = lax.psum(jnp.sum(conjugate_update * applied), ("row", "col"))
        update_factor = norm_now / curvature
        thermal_iterate = thermal_iterate + update_factor * conjugate_update
        defect_vector = defect_vector - update_factor * applied
        if iteration + 1 < ITERS:
            norm_next = lax.psum(jnp.sum(defect_vector * defect_vector), ("row", "col"))
        if iteration + 1 < ITERS:
            correction = spread_subspace_values(
                invert_galerkin_operator(remove_subspace_part(operator_apply(defect_vector)))
            )
            conjugate_update = norm_next / norm_now * conjugate_update + defect_vector - correction
            norm_now = norm_next
    restricted_operator_blocks = (galerkin_rows / cells)[None, None]
    return (thermal_iterate, defect_vector, restricted_operator_blocks)


def solution(mesh):
    return jax.shard_map(
        body,
        mesh=mesh,
        in_specs=(
            P(None, "row", "col"),
            P(None, "row", "col"),
            P(),
            P(),
            P("row", "col"),
            P("row", "col", None),
            P(None, None, "row", "col"),
        ),
        out_specs=(P(None, "row", "col"), P(None, "row", "col"), P("row", "col", None, None, None)),
        check_vma=False,
    )
```

profile of v0, /device:TPU:0, one launch (start us, length us, event | category | flops | bytes accessed | tf_op | source)
XLA Modules:
  0.0 454.7 jit_solution(7491494327586576353)
XLA Ops:
  8.9 6.4 %select_add_fusion = (f32[4,16,128]{2,1,0:T(8,128)S(1)}, pred[4,16,128]{2,1,0:T(8,128)(4,1)S(1)}, pred[4,16,128]{2,1,0:T(8,128)(4,1)}, pred[4,16,128]{2,1,0:T(8,...) fusion(f32[]{:T(128)} %bitcast.15, f32[]{:T(128)} %bitcast.14, ...), kind=kLoop, calls=%fused_computation.269 | loop fusion | flops 188416 | bytes 131104 | tf_op jit(solution)/shard_map/add | solution.py:33
  23.6 5.7 %collective-permute-start.5 = (bf16[64,4,1,128]{3,0,1,2:T(8,128)(2,1)}, bf16[64,4,1,128]{3,0,1,2:T(8,128)(2,1)}, u32[]{:S(2)}, u32[]{:S(2)}) collective-permute-start(bf16[64,4,1,128]{3,0,1,2:T(8,128)(2,1)} %copy.138), channel_id=1, source_target_pairs={{0,4},{4,8},{8,12},{12,16},{16,20},{20,24},{24,28},{1,5},{5,9},{9,... | collective-permute-start | bytes 196616 | tf_op jit(solution)/shard_map/ppermute | solution.py:18
  41.9 10.5 %all-gather = f32[128,128]{1,0:T(8,128)S(1)} all-gather(f32[16,128]{1,0:T(8,128)S(1)} %copy-done.1), channel_id=2, replica_groups=mesh['row'=8,'col'=4] {'row'}, dimensions={0}, use_global_device_ids=true | all-gather | bytes 73728 | tf_op jit(solution)/shard_map/all_gather | solution.py:68
  70.6 4.7 %collective-permute-start.3 = (f32[4,18,1]{2,1,0:T(8,128)S(1)}, f32[4,18,1]{2,1,0:T(8,128)S(1)}, u32[]{:S(2)}, u32[]{:S(2)}) collective-permute-start(f32[4,18,1]{2,1,0:T(8,128)S(1)} %get-tuple-element.129), channel_id=1, source_target_pairs={{0,1},{1,2},{2,3},{4,5},{5,6},{6,7},{8,9},{9,10},{10,11},{12,13},{... | collective-permute-start | bytes 872 | tf_op jit(solution)/shard_map/ppermute | solution.py:18
  77.0 5.9 %add_add_fusion = (f32[4,16,128]{2,1,0:T(8,128)S(1)}, f32[4,16,128]{2,1,0:T(8,128)S(1)}, f32[4,16,128]{2,1,0:T(8,128)S(1)}, f32[4,16,128]{2,1,0:T(8,128)S(1)}, f...) fusion(pred[4,16,128]{2,1,0:T(8,128)(4,1)S(1)} %copy-done.11, ...), kind=kLoop, calls=%fused_computation.265 | loop fusion | flops 393216 | bytes 332384 | tf_op jit(solution)/shard_map/add | solution.py:72
  86.6 12.4 %fusion.6 = f32[64,4,16,128]{0,2,3,1:T(8,128)S(1)} fusion(f32[64,4,16,128]{0,2,3,1:T(8,128)} %convert_element_type.51, f32[4,16,128]{1,2,0:T(8,128)} %copy.103, f32[4,16,128]{1,2,0:T(8,128)S(1)} %copy.102, f32[4,16,128]{1,2,0:T(8,128)S(1)} %copy.101, f32[4,16,128]{1,2,0:T(8,128)S(1)} %copy.100, f32[4,16,128]{1,2,0:T(8,128)} %copy.99, ...), kind=kLoop, calls=%fused_computation.12 | loop fusion | flops 6815744 | bytes 4423680 | tf_op jit(solution)/shard_map/sub | solution.py:47
  103.5 5.8 %cholesky.18 = f32[64,64]{1,0:T(8,128)S(1)} custom-call(f32[64,64]{1,0:T(8,128)S(1)} %fusion.159), custom_call_target="Cholesky" | custom-call | tf_op jit(solution)/shard_map/jit(cholesky)/cholesky | solution.py:133
  110.7 4.9 %custom-call.13 = f32[1,64,64]{1,2,0:T(8,128)S(1)} custom-call(f32[1,64,64]{2,1,0:T(8,128)S(1)} %fusion.73), custom_call_target="InvertDiagBlocksLowerTriangular" | custom-call | tf_op jit(solution)/shard_map/jit(_cho_solve)/triangular_solve | solution.py:143
  116.4 4.8 %collective-permute-start.7 = (f32[1,64]{1,0:T(1,128)}, f32[1,64]{1,0:T(1,128)}, u32[]{:S(2)}, u32[]{:S(2)}) collective-permute-start(f32[1,64]{1,0:T(1,128)} %fusion.156), channel_id=1, source_target_pairs={{0,1},{1,2},{2,3},{4,5},{5,6},{6,7},{8,9},{9,10},{10,11},{12,13},{... | collective-permute-start | bytes 776 | tf_op jit(solution)/shard_map/ppermute | solution.py:18
  123.2 11.8 %all-reduce.7 = f32[512]{0:T(512)S(1)} all-reduce(f32[512]{0:T(512)S(1)} %bitcast_dynamic-update-slice_fusion.2), channel_id=3, replica_groups=mesh['row'=8,'col'=4] {'row'}, use_global_device_ids=true, to_apply=%add.7 | all-reduce | flops 512 | bytes 4096
  139.1 4.6 %collective-permute-start.6 = (bf16[64,4,18,1]{0,2,1,3:T(8,128)(2,1)}, bf16[64,4,18,1]{0,2,1,3:T(8,128)(2,1)S(1)}, u32[]{:S(2)}, u32[]{:S(2)}) collective-permute-start(bf16[64,4,18,1]{0,2,1,3:T(8,128)(2,1)} %get-tuple-element.114), channel_id=1, source_target_pairs={{0,1},{1,2},{2,3},{4,5},{5,6},{6,7},{8,9},{9,10},{10,11},{12,13},{... | collective-permute-start | bytes 27656 | tf_op jit(solution)/shard_map/ppermute | solution.py:18
  153.3 5.2 %fusion.24 = f32[8,64,64]{1,2,0:T(8,128)S(1)} fusion(bf16[8,64,2048]{2,1,0:T(8,128)(2,1)} %all-gather.11.cloned.1.call-done, f32[8,2048]{1,0:T(8,128)} %mul.418, f32[8,8,16,128]{3,2,1,0:T(8,128)} %bitcast.414, f32[2048]{0:T(1024)S(1)} %bitcast.406, f32[8]{0:T(128)} %fusion.174, f32[8]{0:T(128)} %get-tuple-element.161, f32[64,64]{0,1:T(8,128)S(1)} %copy.113, ...), kind=kOutput, calls=%fused_computation.26 | convolution fusion | flops 807763968 | bytes 2875520 | tf_op jit(solution)/shard_map/as,nbs->nab/dot_general | solution.py:127
  173.4 11.9 %all-gather.2 = f32[128,128]{1,0:T(8,128)S(1)} all-gather(f32[16,128]{1,0:T(8,128)S(1)} %fusion.170), channel_id=4, replica_groups=mesh['row'=8,'col'=4] {'row'}, dimensions={0}, use_global_device_ids=true | all-gather | bytes 73728 | tf_op jit(solution)/shard_map/all_gather | solution.py:83
  197.1 11.8 %all-gather.3 = f32[128,128]{1,0:T(8,128)S(1)} all-gather(f32[16,128]{1,0:T(8,128)S(1)} %fusion.168), channel_id=5, replica_groups=mesh['row'=8,'col'=4] {'row'}, dimensions={0}, use_global_device_ids=true | all-gather | bytes 73728 | tf_op jit(solution)/shard_map/all_gather | solution.py:83
  215.0 12.9 %all-reduce.8 = f32[512]{0:T(512)S(1)} all-reduce(f32[512]{0:T(512)S(1)} %bitcast_dynamic-update-slice_fusion.1), channel_id=6, replica_groups=mesh['row'=8,'col'=4] {'row'}, use_global_device_ids=true, to_apply=%add.8 | all-reduce | flops 512 | bytes 4096
  236.4 5.2 %collective-permute-start.23 = (f32[4,18,1]{2,1,0:T(8,128)S(1)}, f32[4,18,1]{2,1,0:T(8,128)S(1)}, u32[]{:S(2)}, u32[]{:S(2)}) collective-permute-start(f32[4,18,1]{2,1,0:T(8,128)S(1)} %get-tuple-element.124), channel_id=1, source_target_pairs={{0,1},{1,2},{2,3},{4,5},{5,6},{6,7},{8,9},{9,10},{10,11},{12,13},{... | collective-permute-start | bytes 872 | tf_op jit(solution)/shard_map/ppermute | solution.py:18
  241.6 10.4 %all-gather.5 = f32[128,128]{1,0:T(8,128)S(1)} all-gather(f32[16,128]{1,0:T(8,128)S(1)} %fusion.166), channel_id=7, replica_groups=mesh['row'=8,'col'=4] {'row'}, dimensions={0}, use_global_device_ids=true | all-gather | bytes 73728 | tf_op jit(solution)/shard_map/all_gather | solution.py:83
  252.7 40.3 %all-reduce.10 = (f32[]{:T(128)}, f32[]{:T(128)}) all-reduce(f32[]{:T(128)} %get-tuple-element.95, f32[]{:T(128)} %multiply_reduce_fusion.2), channel_id=1, replica_groups=mesh['row'=8,'col'=4] {'row','col'}, use_global_device_ids=true, to_apply=%region_3.5 | all-reduce | flops 2 | bytes 16 | tf_op jit(solution)/shard_map/psum | solution.py:164
  306.3 12.8 %all-gather.6 = f32[128,128]{1,0:T(8,128)S(1)} all-gather(f32[16,128]{1,0:T(8,128)S(1)} %fusion.164), channel_id=8, replica_groups=mesh['row'=8,'col'=4] {'row'}, dimensions={0}, use_global_device_ids=true | all-gather | bytes 73728 | tf_op jit(solution)/shard_map/all_gather | solution.py:83
  319.1 37.9 %psum.30 = f32[]{:T(128)} all-reduce(f32[]{:T(128)} %get-tuple-element.93), channel_id=1, replica_groups=mesh['row'=8,'col'=4] {'row','col'}, use_global_device_ids=true, to_apply=%region_7.9 | all-reduce | flops 1 | bytes 8 | tf_op jit(solution)/shard_map/psum | solution.py:172
  365.4 12.6 %all-reduce.9 = f32[512]{0:T(512)S(1)} all-reduce(f32[512]{0:T(512)S(1)} %bitcast_dynamic-update-slice_fusion), channel_id=9, replica_groups=mesh['row'=8,'col'=4] {'row'}, use_global_device_ids=true, to_apply=%add.9 | all-reduce | flops 512 | bytes 4096
  386.6 4.9 %collective-permute-start.33 = (f32[4,18,1]{2,1,0:T(8,128)S(1)}, f32[4,18,1]{2,1,0:T(8,128)S(1)}, u32[]{:S(2)}, u32[]{:S(2)}) collective-permute-start(f32[4,18,1]{2,1,0:T(8,128)S(1)} %get-tuple-element.120), channel_id=1, source_target_pairs={{0,1},{1,2},{2,3},{4,5},{5,6},{6,7},{8,9},{9,10},{10,11},{12,13},{... | collective-permute-start | bytes 872 | tf_op jit(solution)/shard_map/ppermute | solution.py:18
  391.5 12.3 %all-gather.8 = f32[128,128]{1,0:T(8,128)S(1)} all-gather(f32[16,128]{1,0:T(8,128)S(1)} %fusion.162), channel_id=10, replica_groups=mesh['row'=8,'col'=4] {'row'}, dimensions={0}, use_global_device_ids=true | all-gather | bytes 73728 | tf_op jit(solution)/shard_map/all_gather | solution.py:83
  405.3 39.9 %psum.31 = f32[]{:T(128)} all-reduce(f32[]{:T(128)} %multiply_reduce_fusion), channel_id=1, replica_groups=mesh['row'=8,'col'=4] {'row','col'}, use_global_device_ids=true, to_apply=%region_9.11 | all-reduce | flops 1 | bytes 8 | tf_op jit(solution)/shard_map/psum | solution.py:167
  (228 shorter events, 136.1 us)
Async XLA Ops:
  7.2 146.1 %all-gather.11.cloned.1.call-start = ((), (), s32[]{:S(2)}) async-start(), calls=%async_computation | async-start | bytes 2359296 | tf_op jit(solution)/shard_map/all_gather | solution.py:125
  15.3 52.8 %collective-permute-start = (f32[4,1,128]{2,1,0:T(1,128)S(1)}, f32[4,1,128]{2,1,0:T(1,128)S(1)}, u32[]{:S(2)}, u32[]{:S(2)}) collective-permute-start(f32[4,1,128]{2,1,0:T(1,128)S(1)} %get-tuple-element.142), channel_id=1, source_target_pairs={{4,0},{8,4},{12,8},{16,12},{20,16},{24,20},{28,24},{5,1},{9,5},{13... | collective-permute-start | bytes 6152 | tf_op jit(solution)/shard_map/ppermute | solution.py:21
  16.6 51.5 %collective-permute-start.1 = (f32[4,1,128]{2,1,0:T(1,128)S(1)}, f32[4,1,128]{2,1,0:T(1,128)S(1)}, u32[]{:S(2)}, u32[]{:S(2)}) collective-permute-start(f32[4,1,128]{2,1,0:T(1,128)S(1)} %get-tuple-element.141), channel_id=1, source_target_pairs={{0,4},{4,8},{8,12},{12,16},{16,20},{20,24},{24,28},{1,5},{5,9},{9,... | collective-permute-start | bytes 6152 | tf_op jit(solution)/shard_map/ppermute | solution.py:18
  21.6 115.9 %collective-permute-start.4 = (bf16[64,4,1,128]{3,0,1,2:T(8,128)(2,1)}, bf16[64,4,1,128]{3,0,1,2:T(8,128)(2,1)S(1)}, u32[]{:S(2)}, u32[]{:S(2)}) collective-permute-start(bf16[64,4,1,128]{3,0,1,2:T(8,128)(2,1)} %copy.137), channel_id=1, source_target_pairs={{4,0},{8,4},{12,8},{16,12},{20,16},{24,20},{28,24},{5,1},{9,5},{13... | collective-permute-start | bytes 196616 | tf_op jit(solution)/shard_map/ppermute | solution.py:21
  23.6 112.9 %collective-permute-start.5 = (bf16[64,4,1,128]{3,0,1,2:T(8,128)(2,1)}, bf16[64,4,1,128]{3,0,1,2:T(8,128)(2,1)}, u32[]{:S(2)}, u32[]{:S(2)}) collective-permute-start(bf16[64,4,1,128]{3,0,1,2:T(8,128)(2,1)} %copy.138), channel_id=1, source_target_pairs={{0,4},{4,8},{8,12},{12,16},{16,20},{20,24},{24,28},{1,5},{5,9},{9,... | collective-permute-start | bytes 196616 | tf_op jit(solution)/shard_map/ppermute | solution.py:18
  69.3 7.4 %collective-permute-start.2 = (f32[4,18,1]{2,1,0:T(8,128)S(1)}, f32[4,18,1]{2,1,0:T(8,128)S(1)}, u32[]{:S(2)}, u32[]{:S(2)}) collective-permute-start(f32[4,18,1]{2,1,0:T(8,128)S(1)} %get-tuple-element.130), channel_id=1, source_target_pairs={{1,0},{2,1},{3,2},{5,4},{6,5},{7,6},{9,8},{10,9},{11,10},{13,12},{... | collective-permute-start | bytes 872 | tf_op jit(solution)/shard_map/ppermute | solution.py:21
  70.6 6.3 %collective-permute-start.3 = (f32[4,18,1]{2,1,0:T(8,128)S(1)}, f32[4,18,1]{2,1,0:T(8,128)S(1)}, u32[]{:S(2)}, u32[]{:S(2)}) collective-permute-start(f32[4,18,1]{2,1,0:T(8,128)S(1)} %get-tuple-element.129), channel_id=1, source_target_pairs={{0,1},{1,2},{2,3},{4,5},{5,6},{6,7},{8,9},{9,10},{10,11},{12,13},{... | collective-permute-start | bytes 872 | tf_op jit(solution)/shard_map/ppermute | solution.py:18
  116.4 42.3 %collective-permute-start.7 = (f32[1,64]{1,0:T(1,128)}, f32[1,64]{1,0:T(1,128)}, u32[]{:S(2)}, u32[]{:S(2)}) collective-permute-start(f32[1,64]{1,0:T(1,128)} %fusion.156), channel_id=1, source_target_pairs={{0,1},{1,2},{2,3},{4,5},{5,6},{6,7},{8,9},{9,10},{10,11},{12,13},{... | collective-permute-start | bytes 776 | tf_op jit(solution)/shard_map/ppermute | solution.py:18
  121.2 38.3 %collective-permute-start.9 = (f32[1,64]{1,0:T(1,128)}, f32[1,64]{1,0:T(1,128)}, u32[]{:S(2)}, u32[]{:S(2)}) collective-permute-start(f32[1,64]{1,0:T(1,128)} %fusion.156), channel_id=1, source_target_pairs={{1,0},{2,1},{3,2},{5,4},{6,5},{7,6},{9,8},{10,9},{11,10},{13,12},{... | collective-permute-start | bytes 776 | tf_op jit(solution)/shard_map/ppermute | solution.py:21
  139.1 8.7 %collective-permute-start.6 = (bf16[64,4,18,1]{0,2,1,3:T(8,128)(2,1)}, bf16[64,4,18,1]{0,2,1,3:T(8,128)(2,1)S(1)}, u32[]{:S(2)}, u32[]{:S(2)}) collective-permute-start(bf16[64,4,18,1]{0,2,1,3:T(8,128)(2,1)} %get-tuple-element.114), channel_id=1, source_target_pairs={{0,1},{1,2},{2,3},{4,5},{5,6},{6,7},{8,9},{9,10},{10,11},{12,13},{... | collective-permute-start | bytes 27656 | tf_op jit(solution)/shard_map/ppermute | solution.py:18
  167.6 17.7 %collective-permute-start.12 = (f32[4,18,1]{2,1,0:T(8,128)S(1)}, f32[4,18,1]{2,1,0:T(8,128)S(1)}, u32[]{:S(2)}, u32[]{:S(2)}) collective-permute-start(f32[4,18,1]{2,1,0:T(8,128)S(1)} %get-tuple-element.127), channel_id=1, source_target_pairs={{1,0},{2,1},{3,2},{5,4},{6,5},{7,6},{9,8},{10,9},{11,10},{13,12},{... | collective-permute-start | bytes 872 | tf_op jit(solution)/shard_map/ppermute | solution.py:21
  168.9 16.4 %collective-permute-start.13 = (f32[4,18,1]{2,1,0:T(8,128)S(1)}, f32[4,18,1]{2,1,0:T(8,128)S(1)}, u32[]{:S(2)}, u32[]{:S(2)}) collective-permute-start(f32[4,18,1]{2,1,0:T(8,128)S(1)} %get-tuple-element.128), channel_id=1, source_target_pairs={{0,1},{1,2},{2,3},{4,5},{5,6},{6,7},{8,9},{9,10},{10,11},{12,13},{... | collective-permute-start | bytes 872 | tf_op jit(solution)/shard_map/ppermute | solution.py:18
  191.2 17.6 %collective-permute-start.16 = (f32[4,18,1]{2,1,0:T(8,128)S(1)}, f32[4,18,1]{2,1,0:T(8,128)S(1)}, u32[]{:S(2)}, u32[]{:S(2)}) collective-permute-start(f32[4,18,1]{2,1,0:T(8,128)S(1)} %get-tuple-element.125), channel_id=1, source_target_pairs={{1,0},{2,1},{3,2},{5,4},{6,5},{7,6},{9,8},{10,9},{11,10},{13,12},{... | collective-permute-start | bytes 872 | tf_op jit(solution)/shard_map/ppermute | solution.py:21
  192.5 16.3 %collective-permute-start.17 = (f32[4,18,1]{2,1,0:T(8,128)S(1)}, f32[4,18,1]{2,1,0:T(8,128)S(1)}, u32[]{:S(2)}, u32[]{:S(2)}) collective-permute-start(f32[4,18,1]{2,1,0:T(8,128)S(1)} %get-tuple-element.126), channel_id=1, source_target_pairs={{0,1},{1,2},{2,3},{4,5},{5,6},{6,7},{8,9},{9,10},{10,11},{12,13},{... | collective-permute-start | bytes 872 | tf_op jit(solution)/shard_map/ppermute | solution.py:18
  210.6 17.6 %collective-permute-start.18 = (f32[1,64]{1,0:T(1,128)S(1)}, f32[1,64]{1,0:T(1,128)S(1)}, u32[]{:S(2)}, u32[]{:S(2)}) collective-permute-start(f32[1,64]{1,0:T(1,128)S(1)} %fusion.151), channel_id=1, source_target_pairs={{0,1},{1,2},{2,3},{4,5},{5,6},{6,7},{8,9},{9,10},{10,11},{12,13},{... | collective-permute-start | bytes 776 | tf_op jit(solution)/shard_map/ppermute | solution.py:18
  213.6 14.8 %collective-permute-start.19 = (f32[1,64]{1,0:T(1,128)S(1)}, f32[1,64]{1,0:T(1,128)S(1)}, u32[]{:S(2)}, u32[]{:S(2)}) collective-permute-start(f32[1,64]{1,0:T(1,128)S(1)} %fusion.151), channel_id=1, source_target_pairs={{1,0},{2,1},{3,2},{5,4},{6,5},{7,6},{9,8},{10,9},{11,10},{13,12},{... | collective-permute-start | bytes 776 | tf_op jit(solution)/shard_map/ppermute | solution.py:21
  235.1 16.8 %collective-permute-start.22 = (f32[4,18,1]{2,1,0:T(8,128)S(1)}, f32[4,18,1]{2,1,0:T(8,128)S(1)}, u32[]{:S(2)}, u32[]{:S(2)}) collective-permute-start(f32[4,18,1]{2,1,0:T(8,128)S(1)} %get-tuple-element.123), channel_id=1, source_target_pairs={{1,0},{2,1},{3,2},{5,4},{6,5},{7,6},{9,8},{10,9},{11,10},{13,12},{... | collective-permute-start | bytes 872 | tf_op jit(solution)/shard_map/ppermute | solution.py:21
  236.4 15.6 %collective-permute-start.23 = (f32[4,18,1]{2,1,0:T(8,128)S(1)}, f32[4,18,1]{2,1,0:T(8,128)S(1)}, u32[]{:S(2)}, u32[]{:S(2)}) collective-permute-start(f32[4,18,1]{2,1,0:T(8,128)S(1)} %get-tuple-element.124), channel_id=1, source_target_pairs={{0,1},{1,2},{2,3},{4,5},{5,6},{6,7},{8,9},{9,10},{10,11},{12,13},{... | collective-permute-start | bytes 872 | tf_op jit(solution)/shard_map/ppermute | solution.py:18
  300.5 57.9 %collective-permute-start.26 = (f32[4,18,1]{2,1,0:T(8,128)S(1)}, f32[4,18,1]{2,1,0:T(8,128)S(1)}, u32[]{:S(2)}, u32[]{:S(2)}) collective-permute-start(f32[4,18,1]{2,1,0:T(8,128)S(1)} %get-tuple-element.121), channel_id=1, source_target_pairs={{1,0},{2,1},{3,2},{5,4},{6,5},{7,6},{9,8},{10,9},{11,10},{13,12},{... | collective-permute-start | bytes 872 | tf_op jit(solution)/shard_map/ppermute | solution.py:21
  301.8 56.6 %collective-permute-start.27 = (f32[4,18,1]{2,1,0:T(8,128)S(1)}, f32[4,18,1]{2,1,0:T(8,128)S(1)}, u32[]{:S(2)}, u32[]{:S(2)}) collective-permute-start(f32[4,18,1]{2,1,0:T(8,128)S(1)} %get-tuple-element.122), channel_id=1, source_target_pairs={{0,1},{1,2},{2,3},{4,5},{5,6},{6,7},{8,9},{9,10},{10,11},{12,13},{... | collective-permute-start | bytes 872 | tf_op jit(solution)/shard_map/ppermute | solution.py:18
  360.1 18.3 %collective-permute-start.28 = (f32[1,64]{1,0:T(1,128)S(1)}, f32[1,64]{1,0:T(1,128)S(1)}, u32[]{:S(2)}, u32[]{:S(2)}) collective-permute-start(f32[1,64]{1,0:T(1,128)S(1)} %fusion.146), channel_id=1, source_target_pairs={{0,1},{1,2},{2,3},{4,5},{5,6},{6,7},{8,9},{9,10},{10,11},{12,13},{... | collective-permute-start | bytes 776 | tf_op jit(solution)/shard_map/ppermute | solution.py:18
  364.0 14.5 %collective-permute-start.29 = (f32[1,64]{1,0:T(1,128)S(1)}, f32[1,64]{1,0:T(1,128)S(1)}, u32[]{:S(2)}, u32[]{:S(2)}) collective-permute-start(f32[1,64]{1,0:T(1,128)S(1)} %fusion.146), channel_id=1, source_target_pairs={{1,0},{2,1},{3,2},{5,4},{6,5},{7,6},{9,8},{10,9},{11,10},{13,12},{... | collective-permute-start | bytes 776 | tf_op jit(solution)/shard_map/ppermute | solution.py:21
  385.3 18.4 %collective-permute-start.32 = (f32[4,18,1]{2,1,0:T(8,128)S(1)}, f32[4,18,1]{2,1,0:T(8,128)S(1)}, u32[]{:S(2)}, u32[]{:S(2)}) collective-permute-start(f32[4,18,1]{2,1,0:T(8,128)S(1)} %get-tuple-element.119), channel_id=1, source_target_pairs={{1,0},{2,1},{3,2},{5,4},{6,5},{7,6},{9,8},{10,9},{11,10},{13,12},{... | collective-permute-start | bytes 872 | tf_op jit(solution)/shard_map/ppermute | solution.py:21
  386.6 17.1 %collective-permute-start.33 = (f32[4,18,1]{2,1,0:T(8,128)S(1)}, f32[4,18,1]{2,1,0:T(8,128)S(1)}, u32[]{:S(2)}, u32[]{:S(2)}) collective-permute-start(f32[4,18,1]{2,1,0:T(8,128)S(1)} %get-tuple-element.120), channel_id=1, source_target_pairs={{0,1},{1,2},{2,3},{4,5},{5,6},{6,7},{8,9},{9,10},{10,11},{12,13},{... | collective-permute-start | bytes 872 | tf_op jit(solution)/shard_map/ppermute | solution.py:18
  (29 other events, 451.9 us)
Sparse Core Ops, SparseCore 0:
  31.2 30.7 all-gather.10
where the time goes:
time: 457 us; the launch traced here: 455 us
  blocking collectives  225 us (49%)
  starting transfers between devices  91 us (20%)
  other arithmetic  47.8 us (10%)
  local copies, waits for them, and re-layouts  32.7 us (7%)
  matrix products  27.6 us (6%)
  between operations  23.2 us (5%)
  waiting for transfers between devices  7.52 us (2%)
    ppermute x17, starting transfers between devices, padded_2(): lax.ppermute(lax.slice_in_dim(block, block.shape[dim] - width, None, axis...  68.6 us
    all_gather x5, blocking collectives, operator_apply(): lax.all_gather((vent_open * values[layers - 1])[None], 'row', axis=0, til...  59 us
    psum x1, blocking collectives, body(): norm_now = lax.psum(jnp.sum(defect_vector * defect_vector), ('row', 'col'))  40.3 us
    psum x1, blocking collectives, body(): curvature = lax.psum(jnp.sum(conjugate_update * applied), ('row', 'col'))  39.9 us
    psum x1, blocking collectives, body(): norm_next = lax.psum(jnp.sum(defect_vector * defect_vector), ('row', 'col'))  37.9 us
    unnamed x3, blocking collectives  37.3 us
    ppermute x17, starting transfers between devices, padded_2(): lax.ppermute(lax.slice_in_dim(block, 0, width, axis=dim), axis, backward)  22.4 us
    unnamed x50, local copies, waits for them, and re-layouts  14.1 us
  transfers between devices with their start and end apart: 35, of which 7 were waited for; matrix products, arithmetic and copies ran while one was open for 19% of the time, Pallas kernels for 0%

commit v1 on v0

v1 whole, which is shorter than its diff:
```python
import functools

import jax
import jax.numpy as jnp
from jax import lax
from jax.experimental import pallas as pl
from jax.experimental.pallas import tpu as pltpu
from jax.sharding import PartitionSpec as P

F32 = jnp.float32
BF16 = jnp.bfloat16
VMEM = pl.BlockSpec(memory_space=pltpu.VMEM)
SMEM = pl.BlockSpec(memory_space=pltpu.SMEM)
VMEM_LIMIT = 40 * 1024 * 1024


def harmonic(a, b):
    return 2.0 * a * b / (a + b)


def lookup(material, table):
    result = jnp.zeros(material.shape, F32)
    for class_id in range(table.shape[0]):
        result = jnp.where(material == class_id, table[class_id], result)
    return result


class Grid:
    def __init__(self, layers, width, depth):
        self.layers, self.width, self.depth = layers, width, depth
        self.rows = layers * width

    def masks(self):
        shape = (self.rows, self.depth)
        row = lax.broadcasted_iota(jnp.int32, shape, 0)
        lane = lax.broadcasted_iota(jnp.int32, shape, 1)
        return lax.rem(row, self.width), lane, row

    def spread(self, face):
        parts = [
            jnp.broadcast_to(face[z : z + 1], (self.width, self.depth)) for z in range(self.layers)
        ]
        return jnp.concatenate(parts, axis=0)

    def faces(self, v):
        w = self.width
        last = [v[z * w + w - 1 : z * w + w] for z in range(self.layers)]
        first = [v[z * w : z * w + 1] for z in range(self.layers)]
        return last + first

    def payload(self, top, v):
        return jnp.concatenate([top] + self.faces(v), axis=0)

    def around(self, v, low_x, high_x, low_y, high_y):
        xi, lane, _ = self.masks()
        n, d = self.rows, self.depth
        zero = jnp.zeros((n, d), F32)
        own = zero if v is None else v
        plus = zero if v is None else pltpu.roll(v, n - 1, 0)
        minus = zero if v is None else pltpu.roll(v, 1, 0)
        up_x = jnp.where(xi == self.width - 1, self.spread(high_x), plus)
        down_x = jnp.where(xi == 0, self.spread(low_x), minus)
        up_y = pltpu.roll(jnp.where(lane == 0, high_y, own), d - 1, 1)
        down_y = pltpu.roll(jnp.where(lane == d - 1, low_y, own), 1, 1)
        return up_x, down_x, up_y, down_y

    def shifted_z(self, v):
        w = self.width
        return jnp.concatenate([v[w:], v[:w]], axis=0), jnp.concatenate([v[-w:], v[:-w]], axis=0)


def received(grid, ids, pairs, rec):
    count = rec.shape[0]
    w, layers = grid.width, grid.layers
    coupled = rec[ids[0], 0:w, :]
    for k in range(1, pairs):
        coupled = coupled + rec[ids[k], 0:w, :]
    row_at = ids[pairs]
    low = rec[jnp.maximum(row_at - 1, 0), w : w + layers, :]
    high = rec[jnp.minimum(row_at + 1, count - 1), w + layers : w + 2 * layers, :]
    return coupled, low, high


def operate(grid, coef, vent, v, rest):
    coupled, low_x, high_x, low_y, high_y = rest
    up_x, down_x, up_y, down_y = grid.around(v, low_x, high_x, low_y, high_y)
    beside = coef[3] * up_x + coef[4] * down_x + coef[5] * up_y + coef[6] * down_y
    if v is None:
        xi, lane, _ = grid.masks()
        result = -beside
    else:
        up_z, down_z = grid.shifted_z(v)
        result = coef[0] * v - (beside + coef[1] * up_z + coef[2] * down_z)
    w = grid.width
    return jnp.concatenate([result[:-w], result[-w:] - vent * coupled], axis=0)


def project(grid, zm, v):
    d = grid.depth
    parts = [None, None]
    for row in range(grid.rows):
        term = zm[:, row * d : (row + 1) * d].astype(F32) * v[row : row + 1, :]
        k = row % 2
        parts[k] = term if parts[k] is None else parts[k] + term
    return jnp.sum(parts[0] + parts[1], axis=1, keepdims=True)


def solve_own(inverse, column):
    size = inverse.shape[0]
    along = jnp.sum(inverse[...] * column, axis=0, keepdims=True)
    eye = lax.broadcasted_iota(jnp.int32, (size, size), 0) == lax.broadcasted_iota(
        jnp.int32, (size, size), 1
    )
    return jnp.sum(jnp.where(eye, along, 0.0), axis=1, keepdims=True)


def expand(grid, zm, column, out):
    d = grid.depth
    wide = jnp.broadcast_to(column, (column.shape[0], d))
    for row in range(grid.rows):
        out[row : row + 1, :] = jnp.sum(
            zm[:, row * d : (row + 1) * d].astype(F32) * wide, axis=0, keepdims=True
        )


def to_all(grid, pay, top, v):
    block = grid.payload(top, v)
    for slot in range(pay.shape[0]):
        pay[slot] = block


def split3(w):
    hi = w.astype(BF16)
    rest = w - hi.astype(F32)
    mid = rest.astype(BF16)
    lo = (rest - mid.astype(F32)).astype(BF16)
    return hi, mid, lo


def dot_nt(a, b):
    return lax.dot_general(a, b, (((1,), (1,)), ((), ())), preferred_element_type=F32)


def fold3(stacked):
    size = stacked.shape[0] // 3
    return stacked[:size] + (stacked[size : 2 * size] + stacked[2 * size :])


def gram(grid, zm, w3, weights, first_row=0):
    d = grid.depth
    size = zm.shape[0]
    total = None
    group = 8
    rows = weights.shape[0]
    for start in range(0, rows, group):
        stop = min(start + group, rows)
        for row in range(start, stop):
            at = slice(row * d, (row + 1) * d)
            src = slice((first_row + row) * d, (first_row + row + 1) * d)
            hi, mid, lo = split3(zm[:, src].astype(F32) * weights[row : row + 1, :])
            w3[0:size, at] = hi
            w3[size : 2 * size, at] = mid
            w3[2 * size : 3 * size, at] = lo
        part = dot_nt(
            w3[:, start * d : stop * d],
            zm[:, (first_row + start) * d : (first_row + stop) * d],
        )
        total = part if total is None else total + part
    return fold3(total)


def invert_spd(m):
    size = m.shape[0]
    row_id = lax.broadcasted_iota(jnp.int32, (size, size), 0)
    col_id = lax.broadcasted_iota(jnp.int32, (size, size), 1)
    for k in range(size):
        row = m[k : k + 1, :]
        col = m[:, k : k + 1]
        inv = 1.0 / m[k : k + 1, k : k + 1]
        scaled_row = row * inv
        new = m - col * scaled_row
        new = jnp.where(col_id == k, col * inv, new)
        new = jnp.where(row_id == k, scaled_row, new)
        m = jnp.where((row_id == k) & (col_id == k), -inv, new)
    return -m


def k_first(grid, material, conductivity, vent, cond_out, pay):
    cond = lookup(material[...], conductivity)
    cond_out[...] = cond
    to_all(grid, pay, vent[...], cond)


def conductances(grid, cond, low_x, high_x, low_y, high_y):
    _, _, row = grid.masks()
    up_z, down_z = grid.shifted_z(cond)
    uz = jnp.where(row < grid.rows - grid.width, harmonic(cond, up_z), 0.0)
    lz = jnp.where(row >= grid.width, harmonic(cond, down_z), 0.0)
    ux, lx, uy, ly = [harmonic(cond, c) for c in grid.around(cond, low_x, high_x, low_y, high_y)]
    return uz, lz, ux, lx, uy, ly


def k_basis(
    grid, basis, rhs, material, conductivity, capacity,
    zm, own, projected, panel, face_last, face_first, zs, zr, w3, coef,
):
    n, d, w = grid.rows, grid.depth, grid.width
    size = basis.shape[0]
    cond = lookup(material[...], conductivity)
    zero_face = jnp.zeros((grid.layers, d), F32)
    zero = jnp.zeros((n, d), F32)
    uz, lz, ux, lx, uy, ly = conductances(grid, cond, zero_face, zero_face, zero, zero)
    coef[0] = lookup(material[...], capacity) + uz + lz + ux + lx + uy + ly
    for i, c in enumerate((uz, lz, ux, lx, uy, ly)):
        coef[i + 1] = c

    def unpack(a, _):
        zs[pl.ds(a * n, n), :] = basis[a].astype(F32)
        return 0

    lax.fori_loop(0, size, unpack, 0, unroll=4)
    parts = [None, None]
    for row in range(n):
        z = zs[pl.ds(row, size, stride=n), :]
        zr[row] = z
        packed = z.astype(BF16)
        zm[:, row * d : (row + 1) * d] = packed
        layer, x = divmod(row, w)
        if layer == grid.layers - 1:
            panel[:, x * d : (x + 1) * d] = packed
        if x == w - 1:
            face_last[:, layer * d : (layer + 1) * d] = packed
        if x == 0:
            face_first[:, layer * d : (layer + 1) * d] = packed
        term = z * rhs[row : row + 1, :]
        parts[row % 2] = term if parts[row % 2] is None else parts[row % 2] + term
    projected[...] = parts[0] + parts[1]
    total = None
    for start in range(0, n, 8):
        for row in range(start, start + 8):
            z = zr[row]

            def c(i):
                return coef[i, row : row + 1, :]

            acc = c(0) * z
            if row + w < n:
                acc = acc - c(1) * zr[row + w]
            if row >= w:
                acc = acc - c(2) * zr[row - w]
            if row % w < w - 1:
                acc = acc - c(3) * zr[row + 1]
            if row % w > 0:
                acc = acc - c(4) * zr[row - 1]
            acc = acc - c(5) * pltpu.roll(z, d - 1, 1) - c(6) * pltpu.roll(z, 1, 1)
            at = slice(row * d, (row + 1) * d)
            hi, mid, lo = split3(acc)
            w3[0:size, at] = hi
            w3[size : 2 * size, at] = mid
            w3[2 * size : 3 * size, at] = lo
        part = dot_nt(w3[:, start * d : (start + 8) * d], zm[:, start * d : (start + 8) * d])
        total = part if total is None else total + part
    own[...] = fold3(total)


def k_setup(
    grid, pairs, cols, ids, conductivity, capacity, material, vent, cond, cond_low, cond_high, rec,
    zm, own_inner, projected, coef, own, inverse, v0, pay, w3,
):
    n, d, w = grid.rows, grid.depth, grid.width
    count = rec.shape[0]
    vent_sum, low_x, high_x = received(grid, ids, pairs, rec)
    row_at, col_at = ids[pairs], ids[pairs + 1]
    low_x = jnp.where(row_at > 0, low_x, 0.0)
    high_x = jnp.where(row_at < count - 1, high_x, 0.0)
    low_y = jnp.where(col_at > 0, cond_low[...], 0.0)
    high_y = jnp.where(col_at < cols - 1, cond_high[...], 0.0)
    uz, lz, ux, lx, uy, ly = conductances(grid, cond[...], low_x, high_x, low_y, high_y)
    xi, lane, row = grid.masks()
    extra = (
        jnp.where(xi == w - 1, ux, 0.0)
        + jnp.where(xi == 0, lx, 0.0)
        + jnp.where(lane == d - 1, uy, 0.0)
        + jnp.where(lane == 0, ly, 0.0)
    )
    plenum = vent[...] * vent_sum
    extra = jnp.concatenate([extra[:-w], extra[-w:] + plenum], axis=0)
    diagonal = lookup(material[...], capacity) + uz + lz + ux + lx + uy + ly
    coef[0] = jnp.concatenate([diagonal[:-w], diagonal[-w:] + plenum], axis=0)
    for i, c in enumerate((uz, lz, ux, lx, uy, ly)):
        coef[i + 1] = c
    block = own_inner[...] + gram(grid, zm, w3, extra)
    own[...] = block
    inverse[...] = invert_spd(block)
    y0 = solve_own(inverse, jnp.sum(projected[...], axis=1, keepdims=True))
    expand(grid, zm, y0, v0)
    field = v0[...]
    to_all(grid, pay, vent[...] * field[-w:], field)


def incoming(grid, pairs, ids, rec, low, high):
    coupled, low_x, high_x = received(grid, ids, pairs, rec)
    return coupled, low_x, high_x, low[...], high[...]


def k_coarse(grid, pairs, base, ids, coef, vent, zm, inverse, field, rec, low, high, *outs):
    if base:
        base_ref, out, pay, scratch = outs
    else:
        out, pay, scratch = outs
    beside = operate(grid, coef, vent[...], None, incoming(grid, pairs, ids, rec, low, high))
    expand(grid, zm, solve_own(inverse, project(grid, zm, beside)), scratch)
    result = field[...] - scratch[...]
    if base:
        result = base_ref[...] - result
    out[...] = result
    to_all(grid, pay, vent[...] * result[-grid.width :], result)


def k_apply(grid, pairs, base, ids, coef, vent, field, rec, low, high, *outs):
    image = operate(grid, coef, vent[...], field[...], incoming(grid, pairs, ids, rec, low, high))
    if base:
        base_ref, out, pay = outs
        image = base_ref[...] - image
    else:
        out, pay = outs
    out[...] = image
    to_all(grid, pay, vent[...] * image[-grid.width :], image)


def k_apply_solve(grid, pairs, ids, coef, vent, zm, inverse, field, rec, low, high, out, pay):
    image = operate(grid, coef, vent[...], field[...], incoming(grid, pairs, ids, rec, low, high))
    expand(grid, zm, solve_own(inverse, project(grid, zm, image)), out)
    result = out[...]
    to_all(grid, pay, vent[...] * result[-grid.width :], result)


def k_dots(grid, pairs, ids, coef, vent, field, rec, low, high, r0, p0, i0, out, pay):
    image = operate(grid, coef, vent[...], field[...], incoming(grid, pairs, ids, rec, low, high))
    out[...] = image
    d, r, p, i = field[...], r0[...], p0[...], i0[...]
    products = (r * r, p * i, r * i, i * i, d * i, d * image)
    parts = [jnp.sum(q, axis=0, keepdims=True) for q in products]
    parts.append(jnp.zeros((8 - len(parts), grid.depth), F32))
    block = jnp.concatenate(parts, axis=0)
    for slot in range(pay.shape[0]):
        pay[slot] = block


def k_last(rec, x0, r0, p0, i0, d, image, x2, r2):
    total = rec[0]
    for slot in range(1, rec.shape[0]):
        total = total + rec[slot]
    sums = jnp.sum(total, axis=1, keepdims=True)
    rr, pi, ri, ii, di, dd = [sums[k : k + 1, :] for k in range(6)]
    a1 = rr / pi
    new = rr - 2.0 * a1 * ri + a1 * a1 * ii
    grow = 1.0 + new / rr
    a2 = new / (grow * grow * pi - 2.0 * grow * a1 * di + a1 * a1 * dd)
    x2[...] = x0[...] + (a1 + a2 * grow) * p0[...] - (a2 * a1) * d[...]
    r2[...] = r0[...] - (a1 + a2 * grow) * i0[...] + (a2 * a1) * image[...]


def k_blocks(
    grid, pairs, scale, ids, vent, coef, rec, panel, panels, own, face_last, face_first,
    next_first, prev_last, out, w3,
):
    n, d, w, layers = grid.rows, grid.depth, grid.width, grid.layers
    count, size = out.shape[0], out.shape[1]
    row_at = ids[pairs]
    for slot in range(count):
        out[slot] = jnp.zeros((size, size), F32)
    out[row_at] = own[...] * scale

    def weighted(src, weights, other):
        rows = weights.shape[0]
        for row in range(rows):
            at = slice(row * d, (row + 1) * d)
            hi, mid, lo = split3(src[:, at].astype(F32) * weights[row : row + 1, :])
            w3[0:size, at] = hi
            w3[size : 2 * size, at] = mid
            w3[2 * size : 3 * size, at] = lo
        return fold3(dot_nt(w3[:, : rows * d], other)) * (-scale)

    ux = coef[3]
    lx = coef[4]
    high = jnp.concatenate([ux[z * w + w - 1 : z * w + w] for z in range(layers)], axis=0)
    low = jnp.concatenate([lx[z * w : z * w + 1] for z in range(layers)], axis=0)
    ahead = weighted(face_last, high, next_first[...])
    up = jnp.minimum(row_at + 1, count - 1)
    out[up] = out[up] + jnp.where(row_at < count - 1, ahead, 0.0)
    behind = weighted(face_first, low, prev_last[...])
    down = jnp.maximum(row_at - 1, 0)
    out[down] = out[down] + jnp.where(row_at > 0, behind, 0.0)
    for k in range(pairs):
        at = ids[k]
        block = weighted(panel, vent[...] * rec[at, 0:w, :], panels[at])
        out[at] = out[at] + block


def call(kernel, outs, operands, scratch=(), smem=0, cost=None):
    specs = [SMEM] * smem + [VMEM] * (len(operands) - smem)
    return pl.pallas_call(
        kernel,
        out_shape=tuple(jax.ShapeDtypeStruct(s, t) for s, t in outs),
        in_specs=specs,
        out_specs=tuple([VMEM] * len(outs)),
        scratch_shapes=list(scratch),
        compiler_params=pltpu.CompilerParams(vmem_limit_bytes=VMEM_LIMIT),
        cost_estimate=cost,
    )(*operands)


def body(forcing_right_hand, material, capacity, conductivity, vent_open, partners, subspace_basis):
    layers, width, depth = forcing_right_hand.shape
    size = subspace_basis.shape[0]
    grid = Grid(layers, width, depth)
    n, cells = grid.rows, forcing_right_hand.size
    row_count, col_count = lax.axis_size("row"), lax.axis_size("col")
    pairs = partners.shape[-1]
    ids = jnp.concatenate(
        [
            partners.reshape(-1),
            jnp.stack([lax.axis_index("row"), lax.axis_index("col")]).astype(jnp.int32),
        ]
    )
    rhs = forcing_right_hand.reshape(n, depth)
    classes = material.reshape(n, depth)
    basis = subspace_basis.reshape(size, n, depth)
    field = ((n, depth), F32)
    pay = ((row_count, width + 2 * layers, depth), F32)
    small = ((size, size), F32)

    def cyclic(value, axis, step):
        count = lax.axis_size(axis)
        return lax.ppermute(value, axis, [(i, (i + step) % count) for i in range(count)])

    def exchange(value, payload):
        low = cyclic(value, "col", 1)
        high = cyclic(value, "col", -1)
        rec = lax.all_to_all(payload, "row", 0, 0)
        return rec, low, high

    cond, pay0 = call(
        lambda c, m, v, o, p: k_first(grid, m, c, v, o, p),
        (field, pay),
        (conductivity, classes, vent_open),
        smem=1,
    )
    rec0, cond_low, cond_high = exchange(cond, pay0)

    zm, own_inner, projected, panel, face_last, face_first = call(
        lambda c, k, b, f, m, *rest: k_basis(grid, b, f, m, c, k, *rest),
        (
            ((size, n * depth), BF16),
            small,
            ((size, depth), F32),
            ((size, width * depth), BF16),
            ((size, layers * depth), BF16),
            ((size, layers * depth), BF16),
        ),
        (conductivity, capacity, basis, rhs, classes),
        scratch=(
            pltpu.VMEM((size * n, depth), F32),
            pltpu.VMEM((n, size, depth), F32),
            pltpu.VMEM((3 * size, n * depth), BF16),
            pltpu.VMEM((7, n, depth), F32),
        ),
        smem=2,
        cost=pl.CostEstimate(flops=200_000_000, bytes_accessed=8_000_000, transcendentals=0),
    )
    panels = lax.all_gather(panel, "row", axis=0)
    prev_last = cyclic(face_last, "row", 1)
    next_first = cyclic(face_first, "row", -1)

    coef, own, inverse, v0, pay1 = call(
        functools.partial(k_setup, grid, pairs, col_count),
        (((7, n, depth), F32), small, small, field, pay),
        (
            ids, conductivity, capacity, classes, vent_open, cond, cond_low, cond_high, rec0,
            zm, own_inner, projected,
        ),
        scratch=(pltpu.VMEM((3 * size, n * depth), BF16),),
        smem=3,
    )
    rec, low, high = exchange(v0, pay1)
    x0, pay2 = call(
        functools.partial(k_coarse, grid, pairs, False),
        (field, pay),
        (ids, coef, vent_open, zm, inverse, v0, rec, low, high),
        scratch=(pltpu.VMEM((n, depth), F32),),
        smem=1,
    )
    rec, low, high = exchange(x0, pay2)
    r0, pay3 = call(
        functools.partial(k_apply, grid, pairs, True),
        (field, pay),
        (ids, coef, vent_open, x0, rec, low, high, rhs),
        smem=1,
    )
    rec, low, high = exchange(r0, pay3)
    u0, pay4 = call(
        functools.partial(k_apply_solve, grid, pairs),
        (field, pay),
        (ids, coef, vent_open, zm, inverse, r0, rec, low, high),
        smem=1,
    )
    rec, low, high = exchange(u0, pay4)
    p0, pay5 = call(
        functools.partial(k_coarse, grid, pairs, True),
        (field, pay),
        (ids, coef, vent_open, zm, inverse, u0, rec, low, high, r0),
        scratch=(pltpu.VMEM((n, depth), F32),),
        smem=1,
    )
    rec, low, high = exchange(p0, pay5)
    i0, pay6 = call(
        functools.partial(k_apply, grid, pairs, False),
        (field, pay),
        (ids, coef, vent_open, p0, rec, low, high),
        smem=1,
    )
    rec, low, high = exchange(i0, pay6)
    s0, pay7 = call(
        functools.partial(k_apply_solve, grid, pairs),
        (field, pay),
        (ids, coef, vent_open, zm, inverse, i0, rec, low, high),
        smem=1,
    )
    rec, low, high = exchange(s0, pay7)
    d0, pay8 = call(
        functools.partial(k_coarse, grid, pairs, True),
        (field, pay),
        (ids, coef, vent_open, zm, inverse, s0, rec, low, high, i0),
        scratch=(pltpu.VMEM((n, depth), F32),),
        smem=1,
    )
    rec, low, high = exchange(d0, pay8)
    image, pay9 = call(
        functools.partial(k_dots, grid, pairs),
        (field, ((row_count * col_count, 8, depth), F32)),
        (ids, coef, vent_open, d0, rec, low, high, r0, p0, i0),
        smem=1,
    )
    rec9 = lax.all_to_all(pay9, ("row", "col"), 0, 0)
    x2, r2 = call(k_last, (field, field), (rec9, x0, r0, p0, i0, d0, image))

    (blocks,) = call(
        functools.partial(k_blocks, grid, pairs, 1.0 / cells),
        (((row_count, size, size), F32),),
        (
            ids, vent_open, coef, rec0, panel, panels, own, face_last, face_first,
            next_first, prev_last,
        ),
        scratch=(pltpu.VMEM((3 * size, width * depth), BF16),),
        smem=1,
        cost=pl.CostEstimate(flops=100_000_000, bytes_accessed=4_000_000, transcendentals=0),
    )
    shape = forcing_right_hand.shape
    return x2.reshape(shape), r2.reshape(shape), blocks[None, None]


def solution(mesh):
    return jax.shard_map(
        body,
        mesh=mesh,
        in_specs=(
            P(None, "row", "col"),
            P(None, "row", "col"),
            P(),
            P(),
            P("row", "col"),
            P("row", "col", None),
            P(None, None, "row", "col"),
        ),
        out_specs=(P(None, "row", "col"), P(None, "row", "col"), P("row", "col", None, None, None)),
        check_vma=False,
    )
```

time: 457 us -> 169 us (0.37)
  blocking collectives: 225 us -> 0 us
  other arithmetic: 47.8 us -> 0.73 us
  Pallas kernels: 0 us -> 34.2 us
  matrix products: 27.6 us -> 0 us
  local copies, waits for them, and re-layouts: 32.7 us -> 10.5 us
  waiting for transfers between devices: 7.52 us -> 26.8 us
  starting transfers between devices: 91 us -> 80.9 us
  between operations: 23.2 us -> 14.1 us
    psum x3 -> x0, blocking collectives: 118 us -> none  [the longest x1 40.3 us: body(): norm_now = lax.psum(jnp.sum(defect_vector * defect_vector), ('row', 'col'))]
    all_gather x6 -> x0, blocking collectives: 69.5 us -> none  [the longest x5 59 us: operator_apply(): lax.all_gather((vent_open * values[layers - 1])[None], 'row', axis=0, til...]
    ppermute x34 -> x20, starting transfers between devices: 90.9 us -> 38.4 us  [cyclic(): lax.ppermute(value, axis, [(i, (i + step) % count) for i in range(count)])]
    all_to_all x0 -> x10, starting transfers between devices: none -> 42.4 us  [the longest x9 36 us: exchange(): rec = lax.all_to_all(payload, 'row', 0, 0)]
    unnamed x3 -> x0, blocking collectives: 37.3 us -> none
    pallas_call x0 -> x13, Pallas kernels: none -> 34.2 us  [call(): pl.pallas_call(kernel, out_shape=tuple((jax.ShapeDtypeStruct(s, t) for s,...]
    dot_general x21 -> x0, matrix products: 24.5 us -> none  [the longest x1 5.16 us: body(): jnp.einsum('as,nbs->nab', own_top, partner_top, precision=highest)]
    sub x9 -> x0, other arithmetic: 13.5 us -> none  [the longest x1 12.4 us: local_apply(): return diagonal * basis_block - beside_all]
  transfers between devices with their start and end apart: 35 -> 31, of which waited for: 7 -> 10; matrix products, arithmetic and copies ran while one was open for 19% -> 0% of each run, Pallas kernels for 0% -> 16%
where the time goes in v1:
time: 169 us; the launch traced here: 167 us
  starting transfers between devices  80.9 us (48%)
  Pallas kernels  34.2 us (20%)
  waiting for transfers between devices  26.8 us (16%)
  between operations  14.1 us (8%)
  local copies, waits for them, and re-layouts  10.5 us (6%)
    ppermute x20, starting transfers between devices, cyclic(): lax.ppermute(value, axis, [(i, (i + step) % count) for i in range(count)])  38.4 us
    all_to_all x9, starting transfers between devices, exchange(): rec = lax.all_to_all(payload, 'row', 0, 0)  36 us
    pallas_call x13, Pallas kernels, call(): pl.pallas_call(kernel, out_shape=tuple((jax.ShapeDtypeStruct(s, t) for s,...  34.2 us
    ppermute x20, waiting for transfers between devices, cyclic(): lax.ppermute(value, axis, [(i, (i + step) % count) for i in range(count)])  16.2 us
    unnamed x30, local copies, waits for them, and re-layouts  10.5 us
    all_to_all x1, starting transfers between devices, body(): rec9 = lax.all_to_all(pay9, ('row', 'col'), 0, 0)  6.38 us
    all_to_all x1, waiting for transfers between devices, body(): rec9 = lax.all_to_all(pay9, ('row', 'col'), 0, 0)  5.93 us
    all_to_all x9, waiting for transfers between devices, exchange(): rec = lax.all_to_all(payload, 'row', 0, 0)  4.66 us
  transfers between devices with their start and end apart: 31, of which 10 were waited for; matrix products, arithmetic and copies ran while one was open for 0% of the time, Pallas kernels for 16%

profile of v1, /device:TPU:0, one launch (start us, length us, event | category | flops | bytes accessed | tf_op | source)
XLA Modules:
  0.0 167.2 jit_solution(590912557423686779)
XLA Ops:
  11.3 4.6 %shard_map.95 = (bf16[64,8192]{1,0:T(8,128)(2,1)S(1)}, f32[64,64]{1,0:T(8,128)S(1)}, f32[64,128]{1,0:T(8,128)S(1)}, bf16[64,2048]{1,0:T(8,128)(2,1)}, bf16[64,51...) custom-call(f32[8]{0:T(128)S(1)} %copy-done.10, f32[8]{0:T(128)S(1)} %copy-done.13, bf16[64,64,128]{2,1,0:T(8,128)(2,1)S(1)} %bitcast.11, ...), custom_call_target="tpu_custom_call" | custom-call | flops 200000000 | bytes 8000000 | tf_op jit(solution)/shard_map/pallas_call | solution.py:403
  19.2 3.0 %collective-permute-start = (f32[64,128]{1,0:T(8,128)S(1)}, f32[64,128]{1,0:T(8,128)S(1)}, u32[]{:S(2)}, u32[]{:S(2)}) collective-permute-start(f32[64,128]{1,0:T(8,128)S(1)} %get-tuple-element.34.cond), channel_id=1, source_target_pairs={{0,1},{1,2},{2,3},{3,0},{4,5},{5,6},{6,7},{7,4},{8,9},{9,10},{10,1... | collective-permute-start | bytes 98312 | tf_op jit(solution)/shard_map/ppermute | solution.py:436
  24.3 3.9 %all-to-all-start = ((f32[8,24,128]{2,1,0:T(8,128)}), f32[8,24,128]{2,1,0:T(8,128)S(1)}, u32[]{:S(2)}, u32[]{:S(2)}) async-start(f32[8,24,128]{2,1,0:T(8,128)} %get-tuple-element.35), calls=%async_computation | async-start | bytes 196608 | tf_op jit(solution)/shard_map/all_to_all | solution.py:441
  29.0 4.6 %all-to-all-done.rec = f32[8,24,128]{2,1,0:T(8,128)S(1)} async-done(((f32[8,24,128]{2,1,0:T(8,128)}), f32[8,24,128]{2,1,0:T(8,128)S(1)}, u32[]{:S(2)}, u32[]{:S(2)}) %all-to-all-start) | async-done | bytes 98336 | tf_op jit(solution)/shard_map/all_to_all | solution.py:441
  36.4 11.5 %shard_map.96 = (f32[7,64,128]{2,1,0:T(8,128)S(1)}, f32[64,64]{1,0:T(8,128)S(1)}, f32[64,64]{1,0:T(8,128)S(1)}, f32[64,128]{1,0:T(8,128)S(1)}, f32[8,24,128]{2,1,0:T(8,128)}) custom-call(s32[4]{0:T(128)S(1)} %pad_add_fusion.ids, f32[8]{0:T(128)S(1)} %copy-done.12, f32[8]{0:T(128)S(1)} %copy-done.14, s32[64,128]{1,0:T(8,128)S(1)} %bitcast.14, ...), custom_call_target="tpu_custom_call" | custom-call | tf_op jit(solution)/shard_map/pallas_call | solution.py:403
  47.8 3.4 %all-to-all-start.1 = ((f32[8,24,128]{2,1,0:T(8,128)}), f32[8,24,128]{2,1,0:T(8,128)S(1)}, u32[]{:S(2)}, u32[]{:S(2)}) async-start(f32[8,24,128]{2,1,0:T(8,128)} %get-tuple-element.42), calls=%async_computation.1 | async-start | bytes 196608 | tf_op jit(solution)/shard_map/all_to_all | solution.py:441
  52.0 3.1 %collective-permute-start.3 = (f32[64,128]{1,0:T(8,128)S(1)}, f32[64,128]{1,0:T(8,128)S(1)}, u32[]{:S(2)}, u32[]{:S(2)}) collective-permute-start(f32[64,128]{1,0:T(8,128)S(1)} %get-tuple-element.41.field), channel_id=1, source_target_pairs={{0,3},{1,0},{2,1},{3,2},{4,7},{5,4},{6,5},{7,6},{8,11},{9,8},{10,9... | collective-permute-start | bytes 98312 | tf_op jit(solution)/shard_map/ppermute | solution.py:436
  59.2 4.1 %all-to-all-start.2 = ((f32[8,24,128]{2,1,0:T(8,128)}), f32[8,24,128]{2,1,0:T(8,128)S(1)}, u32[]{:S(2)}, u32[]{:S(2)}) async-start(f32[8,24,128]{2,1,0:T(8,128)} %get-tuple-element.44), calls=%async_computation.2 | async-start | bytes 196608 | tf_op jit(solution)/shard_map/all_to_all | solution.py:441
  63.7 3.4 %collective-permute-start.5 = (f32[64,128]{1,0:T(8,128)S(1)}, f32[64,128]{1,0:T(8,128)S(1)}, u32[]{:S(2)}, u32[]{:S(2)}) collective-permute-start(f32[64,128]{1,0:T(8,128)S(1)} %get-tuple-element.43.field.x0), channel_id=1, source_target_pairs={{0,3},{1,0},{2,1},{3,2},{4,7},{5,4},{6,5},{7,6},{8,11},{9,8},{10,9... | collective-permute-start | bytes 98312 | tf_op jit(solution)/shard_map/ppermute | solution.py:436
  70.3 4.2 %all-to-all-start.3 = ((f32[8,24,128]{2,1,0:T(8,128)}), f32[8,24,128]{2,1,0:T(8,128)S(1)}, u32[]{:S(2)}, u32[]{:S(2)}) async-start(f32[8,24,128]{2,1,0:T(8,128)} %get-tuple-element.46), calls=%async_computation.3 | async-start | bytes 196608 | tf_op jit(solution)/shard_map/all_to_all | solution.py:441
  75.4 3.0 %collective-permute-start.7 = (f32[64,128]{1,0:T(8,128)S(1)}, f32[64,128]{1,0:T(8,128)S(1)}, u32[]{:S(2)}, u32[]{:S(2)}) collective-permute-start(f32[64,128]{1,0:T(8,128)S(1)} %get-tuple-element.45.field.outs_0_.r0), channel_id=1, source_target_pairs={{0,3},{1,0},{2,1},{3,2},{4,7},{5,4},{6,5},{7,6},{8,11},{9,8},{10,9... | collective-permute-start | bytes 98312 | tf_op jit(solution)/shard_map/ppermute | solution.py:436
  82.3 4.0 %all-to-all-start.4 = ((f32[8,24,128]{2,1,0:T(8,128)}), f32[8,24,128]{2,1,0:T(8,128)S(1)}, u32[]{:S(2)}, u32[]{:S(2)}) async-start(f32[8,24,128]{2,1,0:T(8,128)} %get-tuple-element.48), calls=%async_computation.4 | async-start | bytes 196608 | tf_op jit(solution)/shard_map/all_to_all | solution.py:441
  87.4 2.8 %collective-permute-start.9 = (f32[64,128]{1,0:T(8,128)S(1)}, f32[64,128]{1,0:T(8,128)S(1)}, u32[]{:S(2)}, u32[]{:S(2)}) collective-permute-start(f32[64,128]{1,0:T(8,128)S(1)} %get-tuple-element.47.field), channel_id=1, source_target_pairs={{0,3},{1,0},{2,1},{3,2},{4,7},{5,4},{6,5},{7,6},{8,11},{9,8},{10,9... | collective-permute-start | bytes 98312 | tf_op jit(solution)/shard_map/ppermute | solution.py:436
  94.1 4.1 %all-to-all-start.5 = ((f32[8,24,128]{2,1,0:T(8,128)}), f32[8,24,128]{2,1,0:T(8,128)S(1)}, u32[]{:S(2)}, u32[]{:S(2)}) async-start(f32[8,24,128]{2,1,0:T(8,128)} %get-tuple-element.50), calls=%async_computation.5 | async-start | bytes 196608 | tf_op jit(solution)/shard_map/all_to_all | solution.py:441
  99.5 2.6 %collective-permute-start.11 = (f32[64,128]{1,0:T(8,128)S(1)}, f32[64,128]{1,0:T(8,128)S(1)}, u32[]{:S(2)}, u32[]{:S(2)}) collective-permute-start(f32[64,128]{1,0:T(8,128)S(1)} %get-tuple-element.49.field.p0), channel_id=1, source_target_pairs={{0,3},{1,0},{2,1},{3,2},{4,7},{5,4},{6,5},{7,6},{8,11},{9,8},{10,9... | collective-permute-start | bytes 98312 | tf_op jit(solution)/shard_map/ppermute | solution.py:436
  105.4 4.1 %all-to-all-start.6 = ((f32[8,24,128]{2,1,0:T(8,128)}), f32[8,24,128]{2,1,0:T(8,128)S(1)}, u32[]{:S(2)}, u32[]{:S(2)}) async-start(f32[8,24,128]{2,1,0:T(8,128)} %get-tuple-element.52), calls=%async_computation.6 | async-start | bytes 196608 | tf_op jit(solution)/shard_map/all_to_all | solution.py:441
  110.7 2.8 %collective-permute-start.13 = (f32[64,128]{1,0:T(8,128)S(1)}, f32[64,128]{1,0:T(8,128)S(1)}, u32[]{:S(2)}, u32[]{:S(2)}) collective-permute-start(f32[64,128]{1,0:T(8,128)S(1)} %get-tuple-element.51.field.outs_0_.i0), channel_id=1, source_target_pairs={{0,3},{1,0},{2,1},{3,2},{4,7},{5,4},{6,5},{7,6},{8,11},{9,8},{10,9... | collective-permute-start | bytes 98312 | tf_op jit(solution)/shard_map/ppermute | solution.py:436
  117.3 4.1 %all-to-all-start.7 = ((f32[8,24,128]{2,1,0:T(8,128)}), f32[8,24,128]{2,1,0:T(8,128)S(1)}, u32[]{:S(2)}, u32[]{:S(2)}) async-start(f32[8,24,128]{2,1,0:T(8,128)} %get-tuple-element.54), calls=%async_computation.7 | async-start | bytes 196608 | tf_op jit(solution)/shard_map/all_to_all | solution.py:441
  122.6 2.7 %collective-permute-start.15 = (f32[64,128]{1,0:T(8,128)S(1)}, f32[64,128]{1,0:T(8,128)S(1)}, u32[]{:S(2)}, u32[]{:S(2)}) collective-permute-start(f32[64,128]{1,0:T(8,128)S(1)} %get-tuple-element.53.field), channel_id=1, source_target_pairs={{0,3},{1,0},{2,1},{3,2},{4,7},{5,4},{6,5},{7,6},{8,11},{9,8},{10,9... | collective-permute-start | bytes 98312 | tf_op jit(solution)/shard_map/ppermute | solution.py:436
  129.2 4.1 %all-to-all-start.8 = ((f32[8,24,128]{2,1,0:T(8,128)}), f32[8,24,128]{2,1,0:T(8,128)S(1)}, u32[]{:S(2)}, u32[]{:S(2)}) async-start(f32[8,24,128]{2,1,0:T(8,128)} %get-tuple-element.56), calls=%async_computation.8 | async-start | bytes 196608 | tf_op jit(solution)/shard_map/all_to_all | solution.py:441
  134.4 2.7 %collective-permute-start.17 = (f32[64,128]{1,0:T(8,128)S(1)}, f32[64,128]{1,0:T(8,128)S(1)}, u32[]{:S(2)}, u32[]{:S(2)}) collective-permute-start(f32[64,128]{1,0:T(8,128)S(1)} %get-tuple-element.55.field.d), channel_id=1, source_target_pairs={{0,3},{1,0},{2,1},{3,2},{4,7},{5,4},{6,5},{7,6},{8,11},{9,8},{10,9... | collective-permute-start | bytes 98312 | tf_op jit(solution)/shard_map/ppermute | solution.py:436
  140.5 6.4 %all-to-all-start.9 = ((f32[32,8,128]{2,1,0:T(8,128)}), f32[32,8,128]{2,1,0:T(8,128)S(1)}, u32[]{:S(2)}, u32[]{:S(2)}) async-start(f32[32,8,128]{2,1,0:T(8,128)} %get-tuple-element.57), calls=%async_computation.9 | async-start | bytes 262144 | tf_op jit(solution)/shard_map/all_to_all | solution.py:545
  149.3 5.9 %all-to-all-done.9.rec = f32[32,8,128]{2,1,0:T(8,128)S(1)} async-done(((f32[32,8,128]{2,1,0:T(8,128)}), f32[32,8,128]{2,1,0:T(8,128)S(1)}, u32[]{:S(2)}, u32[]{:S(2)}) %all-to-all-start.9) | async-done | bytes 131104 | tf_op jit(solution)/shard_map/all_to_all | solution.py:545
  157.7 2.6 %shard_map.106 = f32[8,64,64]{2,1,0:T(8,128)} custom-call(s32[4]{0:T(128)S(1)} %pad_add_fusion.ids, f32[16,128]{1,0:T(8,128)S(1)} %copy-done.4, f32[7,64,128]{2,1,0:T(8,128)S(1)} %get-tuple-element.39.coef, f32[8,24,128]{2,1,0:T(8,128)S(1)} %all-to-all-done.rec, bf16[64,2048]{1,0:T(8,128)(2,1)} %get-tuple-element.61.panel, ...), custom_call_target="tpu_custom_call" | custom-call | flops 100000000 | bytes 4000000 | tf_op jit(solution)/shard_map/pallas_call | solution.py:403
  (83 shorter events, 55.3 us)
Async XLA Ops:
  7.2 148.9 %all-gather.3.cloned.1.call-start = ((), (), s32[]{:S(2)}) async-start(), calls=%async_computation.10 | async-start | bytes 2359296 | tf_op jit(solution)/shard_map/all_gather | solution.py:472
  19.2 9.7 %collective-permute-start = (f32[64,128]{1,0:T(8,128)S(1)}, f32[64,128]{1,0:T(8,128)S(1)}, u32[]{:S(2)}, u32[]{:S(2)}) collective-permute-start(f32[64,128]{1,0:T(8,128)S(1)} %get-tuple-element.34.cond), channel_id=1, source_target_pairs={{0,1},{1,2},{2,3},{3,0},{4,5},{5,6},{6,7},{7,4},{8,9},{9,10},{10,1... | collective-permute-start | bytes 98312 | tf_op jit(solution)/shard_map/ppermute | solution.py:436
  22.2 6.7 %collective-permute-start.1 = (f32[64,128]{1,0:T(8,128)S(1)}, f32[64,128]{1,0:T(8,128)S(1)}, u32[]{:S(2)}, u32[]{:S(2)}) collective-permute-start(f32[64,128]{1,0:T(8,128)S(1)} %get-tuple-element.34.cond), channel_id=1, source_target_pairs={{0,3},{1,0},{2,1},{3,2},{4,7},{5,4},{6,5},{7,6},{8,11},{9,8},{10,9... | collective-permute-start | bytes 98312 | tf_op jit(solution)/shard_map/ppermute | solution.py:436
  24.3 9.3 %all-to-all-start = ((f32[8,24,128]{2,1,0:T(8,128)}), f32[8,24,128]{2,1,0:T(8,128)S(1)}, u32[]{:S(2)}, u32[]{:S(2)}) async-start(f32[8,24,128]{2,1,0:T(8,128)} %get-tuple-element.35), calls=%async_computation | async-start | bytes 196608 | tf_op jit(solution)/shard_map/all_to_all | solution.py:441
  47.8 9.4 %all-to-all-start.1 = ((f32[8,24,128]{2,1,0:T(8,128)}), f32[8,24,128]{2,1,0:T(8,128)S(1)}, u32[]{:S(2)}, u32[]{:S(2)}) async-start(f32[8,24,128]{2,1,0:T(8,128)} %get-tuple-element.42), calls=%async_computation.1 | async-start | bytes 196608 | tf_op jit(solution)/shard_map/all_to_all | solution.py:441
  51.2 6.0 %collective-permute-start.2 = (f32[64,128]{1,0:T(8,128)S(1)}, f32[64,128]{1,0:T(8,128)S(1)}, u32[]{:S(2)}, u32[]{:S(2)}) collective-permute-start(f32[64,128]{1,0:T(8,128)S(1)} %get-tuple-element.41.field), channel_id=1, source_target_pairs={{0,1},{1,2},{2,3},{3,0},{4,5},{5,6},{6,7},{7,4},{8,9},{9,10},{10,1... | collective-permute-start | bytes 98312 | tf_op jit(solution)/shard_map/ppermute | solution.py:436
  59.2 9.9 %all-to-all-start.2 = ((f32[8,24,128]{2,1,0:T(8,128)}), f32[8,24,128]{2,1,0:T(8,128)S(1)}, u32[]{:S(2)}, u32[]{:S(2)}) async-start(f32[8,24,128]{2,1,0:T(8,128)} %get-tuple-element.44), calls=%async_computation.2 | async-start | bytes 196608 | tf_op jit(solution)/shard_map/all_to_all | solution.py:441
  63.3 5.8 %collective-permute-start.4 = (f32[64,128]{1,0:T(8,128)S(1)}, f32[64,128]{1,0:T(8,128)S(1)}, u32[]{:S(2)}, u32[]{:S(2)}) collective-permute-start(f32[64,128]{1,0:T(8,128)S(1)} %get-tuple-element.43.field.x0), channel_id=1, source_target_pairs={{0,1},{1,2},{2,3},{3,0},{4,5},{5,6},{6,7},{7,4},{8,9},{9,10},{10,1... | collective-permute-start | bytes 98312 | tf_op jit(solution)/shard_map/ppermute | solution.py:436
  63.7 5.3 %collective-permute-start.5 = (f32[64,128]{1,0:T(8,128)S(1)}, f32[64,128]{1,0:T(8,128)S(1)}, u32[]{:S(2)}, u32[]{:S(2)}) collective-permute-start(f32[64,128]{1,0:T(8,128)S(1)} %get-tuple-element.43.field.x0), channel_id=1, source_target_pairs={{0,3},{1,0},{2,1},{3,2},{4,7},{5,4},{6,5},{7,6},{8,11},{9,8},{10,9... | collective-permute-start | bytes 98312 | tf_op jit(solution)/shard_map/ppermute | solution.py:436
  70.3 10.1 %all-to-all-start.3 = ((f32[8,24,128]{2,1,0:T(8,128)}), f32[8,24,128]{2,1,0:T(8,128)S(1)}, u32[]{:S(2)}, u32[]{:S(2)}) async-start(f32[8,24,128]{2,1,0:T(8,128)} %get-tuple-element.46), calls=%async_computation.3 | async-start | bytes 196608 | tf_op jit(solution)/shard_map/all_to_all | solution.py:441
  74.5 5.9 %collective-permute-start.6 = (f32[64,128]{1,0:T(8,128)S(1)}, f32[64,128]{1,0:T(8,128)S(1)}, u32[]{:S(2)}, u32[]{:S(2)}) collective-permute-start(f32[64,128]{1,0:T(8,128)S(1)} %get-tuple-element.45.field.outs_0_.r0), channel_id=1, source_target_pairs={{0,1},{1,2},{2,3},{3,0},{4,5},{5,6},{6,7},{7,4},{8,9},{9,10},{10,1... | collective-permute-start | bytes 98312 | tf_op jit(solution)/shard_map/ppermute | solution.py:436
  82.3 9.9 %all-to-all-start.4 = ((f32[8,24,128]{2,1,0:T(8,128)}), f32[8,24,128]{2,1,0:T(8,128)S(1)}, u32[]{:S(2)}, u32[]{:S(2)}) async-start(f32[8,24,128]{2,1,0:T(8,128)} %get-tuple-element.48), calls=%async_computation.4 | async-start | bytes 196608 | tf_op jit(solution)/shard_map/all_to_all | solution.py:441
  86.3 5.9 %collective-permute-start.8 = (f32[64,128]{1,0:T(8,128)S(1)}, f32[64,128]{1,0:T(8,128)S(1)}, u32[]{:S(2)}, u32[]{:S(2)}) collective-permute-start(f32[64,128]{1,0:T(8,128)S(1)} %get-tuple-element.47.field), channel_id=1, source_target_pairs={{0,1},{1,2},{2,3},{3,0},{4,5},{5,6},{6,7},{7,4},{8,9},{9,10},{10,1... | collective-permute-start | bytes 98312 | tf_op jit(solution)/shard_map/ppermute | solution.py:436
  94.1 10.0 %all-to-all-start.5 = ((f32[8,24,128]{2,1,0:T(8,128)}), f32[8,24,128]{2,1,0:T(8,128)S(1)}, u32[]{:S(2)}, u32[]{:S(2)}) async-start(f32[8,24,128]{2,1,0:T(8,128)} %get-tuple-element.50), calls=%async_computation.5 | async-start | bytes 196608 | tf_op jit(solution)/shard_map/all_to_all | solution.py:441
  98.2 5.9 %collective-permute-start.10 = (f32[64,128]{1,0:T(8,128)S(1)}, f32[64,128]{1,0:T(8,128)S(1)}, u32[]{:S(2)}, u32[]{:S(2)}) collective-permute-start(f32[64,128]{1,0:T(8,128)S(1)} %get-tuple-element.49.field.p0), channel_id=1, source_target_pairs={{0,1},{1,2},{2,3},{3,0},{4,5},{5,6},{6,7},{7,4},{8,9},{9,10},{10,1... | collective-permute-start | bytes 98312 | tf_op jit(solution)/shard_map/ppermute | solution.py:436
  105.4 10.0 %all-to-all-start.6 = ((f32[8,24,128]{2,1,0:T(8,128)}), f32[8,24,128]{2,1,0:T(8,128)S(1)}, u32[]{:S(2)}, u32[]{:S(2)}) async-start(f32[8,24,128]{2,1,0:T(8,128)} %get-tuple-element.52), calls=%async_computation.6 | async-start | bytes 196608 | tf_op jit(solution)/shard_map/all_to_all | solution.py:441
  109.5 5.8 %collective-permute-start.12 = (f32[64,128]{1,0:T(8,128)S(1)}, f32[64,128]{1,0:T(8,128)S(1)}, u32[]{:S(2)}, u32[]{:S(2)}) collective-permute-start(f32[64,128]{1,0:T(8,128)S(1)} %get-tuple-element.51.field.outs_0_.i0), channel_id=1, source_target_pairs={{0,1},{1,2},{2,3},{3,0},{4,5},{5,6},{6,7},{7,4},{8,9},{9,10},{10,1... | collective-permute-start | bytes 98312 | tf_op jit(solution)/shard_map/ppermute | solution.py:436
  117.3 10.0 %all-to-all-start.7 = ((f32[8,24,128]{2,1,0:T(8,128)}), f32[8,24,128]{2,1,0:T(8,128)S(1)}, u32[]{:S(2)}, u32[]{:S(2)}) async-start(f32[8,24,128]{2,1,0:T(8,128)} %get-tuple-element.54), calls=%async_computation.7 | async-start | bytes 196608 | tf_op jit(solution)/shard_map/all_to_all | solution.py:441
  121.4 5.9 %collective-permute-start.14 = (f32[64,128]{1,0:T(8,128)S(1)}, f32[64,128]{1,0:T(8,128)S(1)}, u32[]{:S(2)}, u32[]{:S(2)}) collective-permute-start(f32[64,128]{1,0:T(8,128)S(1)} %get-tuple-element.53.field), channel_id=1, source_target_pairs={{0,1},{1,2},{2,3},{3,0},{4,5},{5,6},{6,7},{7,4},{8,9},{9,10},{10,1... | collective-permute-start | bytes 98312 | tf_op jit(solution)/shard_map/ppermute | solution.py:436
  129.2 10.0 %all-to-all-start.8 = ((f32[8,24,128]{2,1,0:T(8,128)}), f32[8,24,128]{2,1,0:T(8,128)S(1)}, u32[]{:S(2)}, u32[]{:S(2)}) async-start(f32[8,24,128]{2,1,0:T(8,128)} %get-tuple-element.56), calls=%async_computation.8 | async-start | bytes 196608 | tf_op jit(solution)/shard_map/all_to_all | solution.py:441
  133.3 5.9 %collective-permute-start.16 = (f32[64,128]{1,0:T(8,128)S(1)}, f32[64,128]{1,0:T(8,128)S(1)}, u32[]{:S(2)}, u32[]{:S(2)}) collective-permute-start(f32[64,128]{1,0:T(8,128)S(1)} %get-tuple-element.55.field.d), channel_id=1, source_target_pairs={{0,1},{1,2},{2,3},{3,0},{4,5},{5,6},{6,7},{7,4},{8,9},{9,10},{10,1... | collective-permute-start | bytes 98312 | tf_op jit(solution)/shard_map/ppermute | solution.py:436
  140.5 14.8 %all-to-all-start.9 = ((f32[32,8,128]{2,1,0:T(8,128)}), f32[32,8,128]{2,1,0:T(8,128)S(1)}, u32[]{:S(2)}, u32[]{:S(2)}) async-start(f32[32,8,128]{2,1,0:T(8,128)} %get-tuple-element.57), calls=%async_computation.9 | async-start | bytes 262144 | tf_op jit(solution)/shard_map/all_to_all | solution.py:545
  146.9 9.2 %collective-permute-start.18 = (bf16[64,512]{1,0:T(8,128)(2,1)S(1)}, bf16[64,512]{1,0:T(8,128)(2,1)S(1)}, u32[]{:S(2)}, u32[]{:S(2)}) collective-permute-start(bf16[64,512]{1,0:T(8,128)(2,1)S(1)} %get-tuple-element.64.face_first), channel_id=1, source_target_pairs={{0,28},{4,0},{8,4},{12,8},{16,12},{20,16},{24,20},{28,24},{1,29},{... | collective-permute-start | bytes 196616 | tf_op jit(solution)/shard_map/ppermute | solution.py:436
  149.3 6.7 %collective-permute-start.19 = (bf16[64,512]{1,0:T(8,128)(2,1)S(1)}, bf16[64,512]{1,0:T(8,128)(2,1)S(1)}, u32[]{:S(2)}, u32[]{:S(2)}) collective-permute-start(bf16[64,512]{1,0:T(8,128)(2,1)S(1)} %get-tuple-element.63.face_last), channel_id=1, source_target_pairs={{0,4},{4,8},{8,12},{12,16},{16,20},{20,24},{24,28},{28,0},{1,5},{5... | collective-permute-start | bytes 196616 | tf_op jit(solution)/shard_map/ppermute | solution.py:436
  (22 other events, 143.5 us)
Sparse Core Ops, SparseCore 0:
  16.0 31.6 all-gather.2

commit v2 on v1

--- a/solution.py
+++ b/solution.py
@@ -11,6 +11,8 @@
 BF16 = jnp.bfloat16
 VMEM = pl.BlockSpec(memory_space=pltpu.VMEM)
 SMEM = pl.BlockSpec(memory_space=pltpu.SMEM)
+HBM = pl.BlockSpec(memory_space=pltpu.HBM)
+ANY = pl.BlockSpec(memory_space=pl.ANY)
 VMEM_LIMIT = 40 * 1024 * 1024
 
 
@@ -123,8 +125,8 @@
         )
 
 
-def to_all(grid, pay, top, v):
-    block = grid.payload(top, v)
+def to_all(grid, pay, top, v, *more):
+    block = jnp.concatenate([grid.payload(top, v), *more], axis=0)
     for slot in range(pay.shape[0]):
         pay[slot] = block
 
@@ -169,26 +171,61 @@
     return fold3(total)
 
 
-def invert_spd(m):
+def invert_spd(m, ahead=5):
     size = m.shape[0]
     row_id = lax.broadcasted_iota(jnp.int32, (size, size), 0)
     col_id = lax.broadcasted_iota(jnp.int32, (size, size), 1)
+
+    def column(k):
+        return jnp.broadcast_to(m[:, k : k + 1], (size, size))
+
+    waiting = {k: column(k) for k in range(min(ahead + 1, size))}
     for k in range(size):
-        row = m[k : k + 1, :]
-        col = m[:, k : k + 1]
-        inv = 1.0 / m[k : k + 1, k : k + 1]
-        scaled_row = row * inv
-        new = m - col * scaled_row
-        new = jnp.where(col_id == k, col * inv, new)
-        new = jnp.where(row_id == k, scaled_row, new)
-        m = jnp.where((row_id == k) & (col_id == k), -inv, new)
+        col = waiting.pop(k)
+        inv = 1.0 / col[k : k + 1, :]
+        for j in list(waiting):
+            at_row = col[j : j + 1, :] * inv
+            waiting[j] = jnp.where(row_id == k, at_row, waiting[j] - col * at_row)
+        scaled_row = jnp.where(col_id[:1] == k, -inv, m[k : k + 1, :] * inv)
+        m = jnp.where(row_id == k, scaled_row, jnp.where(col_id == k, 0.0, m) - col * scaled_row)
+        if k + ahead + 1 < size:
+            waiting[k + ahead + 1] = column(k + ahead + 1)
     return -m
 
 
-def k_first(grid, material, conductivity, vent, cond_out, pay):
-    cond = lookup(material[...], conductivity)
-    cond_out[...] = cond
-    to_all(grid, pay, vent[...], cond)
+def opposite(place):
+    return {1: 2, 2: 1, 3: 4, 4: 3}.get(place, place)
+
+
+def k_first(
+    grid, material, conductivity, capacity, vent, partners, cond_out, cap_out, vent_out, pay,
+    classes, cond_table, cap_table, pair_table, sems,
+):
+    copies = [
+        pltpu.make_async_copy(src, dst, sems.at[i])
+        for i, (src, dst) in enumerate(
+            (
+                (material, classes),
+                (conductivity, cond_table),
+                (capacity, cap_table),
+                (vent, vent_out),
+                (partners, pair_table),
+            )
+        )
+    ]
+    for copy in copies:
+        copy.start()
+    for copy in copies:
+        copy.wait()
+    cond = lookup(classes[...], cond_table)
+    lane = lax.broadcasted_iota(jnp.int32, (8, grid.depth), 1)
+    names = jnp.zeros((8, grid.depth), F32)
+    for k in range(pair_table.shape[0]):
+        names = jnp.where(lane == k, pair_table[k].astype(F32), names)
+    cond_out[0 : grid.rows, :] = cond
+    cond_out[grid.rows :, :] = names
+    cap_out[...] = lookup(classes[...], cap_table)
+    to_all(grid, pay, vent_out[...], cond, names)
 
 
 def conductances(grid, cond, low_x, high_x, low_y, high_y):
@@ -200,41 +237,74 @@
     return uz, lz, ux, lx, uy, ly
 
 
+def k_panel(grid, basis, _, panel, top, wide, sem):
+    w, d = grid.width, grid.depth
+    size = basis.shape[0]
+    copy = pltpu.make_async_copy(basis.at[:, pl.ds(grid.rows - w, w), :], top, sem)
+    copy.start()
+    copy.wait()
+
+    def unpack(a, _):
+        wide[pl.ds(a * w, w), :] = top[a].astype(F32)
+        return 0
+
+    lax.fori_loop(0, size, unpack, 0, unroll=8)
+    for x in range(w):
+        panel[:, x * d : (x + 1) * d] = wide[pl.ds(x, size, stride=w), :].astype(BF16)
+
+
 def k_basis(
-    grid, basis, rhs, material, conductivity, capacity,
-    zm, own, projected, panel, face_last, face_first, zs, zr, w3, coef,
+    grid, basis, rhs_in, cond_ref, cap_ref,
+    zm, own, projected, face_last, face_first, face_y, rhs, zs, zr, w3, coef, packed_basis, sems,
 ):
     n, d, w = grid.rows, grid.depth, grid.width
     size = basis.shape[0]
-    cond = lookup(material[...], conductivity)
+    pieces = sems.shape[0] - 1
+    step = size // pieces
+    copies = [
+        pltpu.make_async_copy(
+            basis.at[pl.ds(i * step, step)], packed_basis.at[pl.ds(i * step, step)], sems.at[i]
+        )
+        for i in range(pieces)
+    ]
+    copies.append(pltpu.make_async_copy(rhs_in, rhs, sems.at[pieces]))
+    for copy in copies:
+        copy.start()
+    cond = cond_ref[0:n, :]
     zero_face = jnp.zeros((grid.layers, d), F32)
     zero = jnp.zeros((n, d), F32)
     uz, lz, ux, lx, uy, ly = conductances(grid, cond, zero_face, zero_face, zero, zero)
-    coef[0] = lookup(material[...], capacity) + uz + lz + ux + lx + uy + ly
+    coef[0] = cap_ref[...] + uz + lz + ux + lx + uy + ly
     for i, c in enumerate((uz, lz, ux, lx, uy, ly)):
         coef[i + 1] = c
 
     def unpack(a, _):
-        zs[pl.ds(a * n, n), :] = basis[a].astype(F32)
+        zs[pl.ds(a * n, n), :] = packed_basis[a].astype(F32)
         return 0
 
-    lax.fori_loop(0, size, unpack, 0, unroll=4)
+    for i in range(pieces):
+        copies[i].wait()
+        lax.fori_loop(i * step, (i + 1) * step, unpack, 0, unroll=4)
+    copies[pieces].wait()
     parts = [None, None]
+    lane = lax.broadcasted_iota(jnp.int32, (size, d), 1)
+    sides = jnp.zeros((size, d), F32)
     for row in range(n):
         z = zs[pl.ds(row, size, stride=n), :]
         zr[row] = z
         packed = z.astype(BF16)
         zm[:, row * d : (row + 1) * d] = packed
         layer, x = divmod(row, w)
-        if layer == grid.layers - 1:
-            panel[:, x * d : (x + 1) * d] = packed
         if x == w - 1:
             face_last[:, layer * d : (layer + 1) * d] = packed
         if x == 0:
             face_first[:, layer * d : (layer + 1) * d] = packed
+        sides = jnp.where(lane == row, z[:, 0:1], sides)
+        sides = jnp.where(lane == n + row, z[:, d - 1 : d], sides)
         term = z * rhs[row : row + 1, :]
         parts[row % 2] = term if parts[row % 2] is None else parts[row % 2] + term
     projected[...] = parts[0] + parts[1]
+    face_y[...] = sides.astype(BF16)
     total = None
     for start in range(0, n, 8):
         for row in range(start, start + 8):
@@ -264,8 +334,8 @@
 
 
 def k_setup(
-    grid, pairs, cols, ids, conductivity, capacity, material, vent, cond, cond_low, cond_high, rec,
-    zm, own_inner, projected, coef, own, inverse, v0, pay, w3,
+    grid, pairs, cols, ids, cap, vent, cond, cond_low, cond_high, rec,
+    zm, own_inner, projected, coef, own, inverse, sent, pay, w3, v0,
 ):
     n, d, w = grid.rows, grid.depth, grid.width
     count = rec.shape[0]
@@ -273,9 +343,9 @@
     row_at, col_at = ids[pairs], ids[pairs + 1]
     low_x = jnp.where(row_at > 0, low_x, 0.0)
     high_x = jnp.where(row_at < count - 1, high_x, 0.0)
-    low_y = jnp.where(col_at > 0, cond_low[...], 0.0)
-    high_y = jnp.where(col_at < cols - 1, cond_high[...], 0.0)
-    uz, lz, ux, lx, uy, ly = conductances(grid, cond[...], low_x, high_x, low_y, high_y)
+    low_y = jnp.where(col_at > 0, cond_low[0:n, :], 0.0)
+    high_y = jnp.where(col_at < cols - 1, cond_high[0:n, :], 0.0)
+    uz, lz, ux, lx, uy, ly = conductances(grid, cond[0:n, :], low_x, high_x, low_y, high_y)
     xi, lane, row = grid.masks()
     extra = (
         jnp.where(xi == w - 1, ux, 0.0)
@@ -285,7 +355,7 @@
     )
     plenum = vent[...] * vent_sum
     extra = jnp.concatenate([extra[:-w], extra[-w:] + plenum], axis=0)
-    diagonal = lookup(material[...], capacity) + uz + lz + ux + lx + uy + ly
+    diagonal = cap[...] + uz + lz + ux + lx + uy + ly
     coef[0] = jnp.concatenate([diagonal[:-w], diagonal[-w:] + plenum], axis=0)
     for i, c in enumerate((uz, lz, ux, lx, uy, ly)):
         coef[i + 1] = c
@@ -295,12 +365,17 @@
     y0 = solve_own(inverse, jnp.sum(projected[...], axis=1, keepdims=True))
     expand(grid, zm, y0, v0)
     field = v0[...]
-    to_all(grid, pay, vent[...] * field[-w:], field)
+    half = zm.shape[0] // 2
+    folded = jnp.concatenate([inverse[0:half, :], inverse[half:, :]], axis=1)
+    sent[0:n, :] = field
+    sent[n:, :] = folded
+    to_all(grid, pay, vent[...] * field[-w:], field, folded)
 
 
 def incoming(grid, pairs, ids, rec, low, high):
     coupled, low_x, high_x = received(grid, ids, pairs, rec)
-    return coupled, low_x, high_x, low[...], high[...]
+    n = grid.rows
+    return coupled, low_x, high_x, low[0:n, :], high[0:n, :]
 
 
 def k_coarse(grid, pairs, base, ids, coef, vent, zm, inverse, field, rec, low, high, *outs):
@@ -310,7 +385,7 @@
         out, pay, scratch = outs
     beside = operate(grid, coef, vent[...], None, incoming(grid, pairs, ids, rec, low, high))
     expand(grid, zm, solve_own(inverse, project(grid, zm, beside)), scratch)
-    result = field[...] - scratch[...]
+    result = field[0 : grid.rows, :] - scratch[...]
     if base:
         result = base_ref[...] - result
     out[...] = result
@@ -328,10 +403,90 @@
     to_all(grid, pay, vent[...] * image[-grid.width :], image)
 
 
-def k_apply_solve(grid, pairs, ids, coef, vent, zm, inverse, field, rec, low, high, out, pay):
-    image = operate(grid, coef, vent[...], field[...], incoming(grid, pairs, ids, rec, low, high))
-    expand(grid, zm, solve_own(inverse, project(grid, zm, image)), out)
-    result = out[...]
+def k_partials(
+    grid, pairs, base, pick, ids, coef, vent, field, rec, low, high, rec0, zm,
+    next_first, prev_last, y_low, y_high, panels, *rest,
+):
+    rest = list(rest)
+    base_ref = rest.pop(0) if base else None
+    out, pay = rest[:2]
+    n, d, w, layers = grid.rows, grid.depth, grid.width, grid.layers
+    size = zm.shape[0]
+    if pick:
+        chosen, sems = rest[2:]
+        copies = [
+            pltpu.make_async_copy(panels.at[ids[k]], chosen.at[k], sems.at[k])
+            for k in range(pairs)
+        ]
+        for copy in copies:
+            copy.start()
+    else:
+        chosen = panels
+    v = operate(grid, coef, vent[...], field[...], incoming(grid, pairs, ids, rec, low, high))
+    if base:
+        v = base_ref[...] - v
+    out[...] = v
+    face, zero = jnp.zeros((layers, d), F32), jnp.zeros((n, d), F32)
+    own = operate(grid, coef, vent[...], v, (jnp.zeros((w, d), F32), face, face, zero, zero))
+
+    def along(basis, weights):
+        total = None
+        for i, weight in enumerate(weights):
+            term = basis[:, i * d : (i + 1) * d].astype(F32) * weight
+            total = term if total is None else total + term
+        return total
+
+    even = along(zm, [own[i : i + 1] for i in range(n)])
+    ux, lx, uy, ly = [coef[i] * v for i in (3, 4, 5, 6)]
+    sums = [
+        even,
+        -along(next_first, [ux[z * w + w - 1 : z * w + w] for z in range(layers)]),
+        -along(prev_last, [lx[z * w : z * w + 1] for z in range(layers)]),
+    ]
+    row = lax.broadcasted_iota(jnp.int32, (n, d), 0)
+    lane = lax.broadcasted_iota(jnp.int32, (n, d), 1)
+    up = jnp.sum(jnp.where(lane == row, uy[:, d - 1 : d], 0.0), axis=0, keepdims=True)
+    down = jnp.sum(jnp.where(lane == n + row, ly[:, 0:1], 0.0), axis=0, keepdims=True)
+    sums.append(-(y_high[...].astype(F32) * up))
+    sums.append(-(y_low[...].astype(F32) * down))
+    if pick:
+        for copy in copies:
+            copy.wait()
+    top = vent[...] * v[-w:]
+    for k in range(pairs):
+        weight = rec0[ids[k], 0:w, :] * top
+        sums.append(-along(chosen.at[k], [weight[i : i + 1] for i in range(w)]))
+    ones = jnp.ones((8, d), F32)
+    rows = [
+        lax.dot_general(
+            ones, q, (((1,), (1,)), ((), ())),
+            precision=lax.Precision.HIGHEST, preferred_element_type=F32,
+        )[0:1]
+        for q in sums
+    ]
+    block = jnp.concatenate(rows + [jnp.zeros((8 - len(rows), size), F32)], axis=0)
+    block = jnp.concatenate([block, jnp.zeros((8, d - size), F32)], axis=1)
+    for slot in range(pay.shape[0]):
+        pay[slot] = block
+
+
+def k_combine(grid, table, rec, weights, zm, base, vent, out, pay, scratch):
+    size = zm.shape[0]
+    count = weights.shape[0]
+    total = None
+    for j in range(count):
+        g = None
+        for i in range(count):
+            at = table[j * count + i]
+            back = opposite(i)
+            term = rec[jnp.maximum(at, 0), back : back + 1, :]
+            term = jnp.where(at >= 0, term, 0.0)
+            g = term if g is None else g + term
+        term = weights[j] * g[:, 0:size]
+        total = term if total is None else total + term
+    expand(grid, zm, jnp.sum(total, axis=1, keepdims=True), scratch)
+    result = base[...] - scratch[...]
+    out[...] = result
     to_all(grid, pay, vent[...] * result[-grid.width :], result)
 
 
@@ -362,49 +517,116 @@
 
 
 def k_blocks(
-    grid, pairs, scale, ids, vent, coef, rec, panel, panels, own, face_last, face_first,
-    next_first, prev_last, out, w3,
+    grid, pairs, rows, cols, scale, ids, vent, coef, rec0, cond_low, cond_high, rec, low, high,
+    panel, chosen, own, inverse, face_last, face_first, next_first, prev_last,
+    face_y, y_low, y_high, _, out, weights, table, w3,
 ):
     n, d, w, layers = grid.rows, grid.depth, grid.width, grid.layers
-    count, size = out.shape[0], out.shape[1]
-    row_at = ids[pairs]
-    for slot in range(count):
-        out[slot] = jnp.zeros((size, size), F32)
-    out[row_at] = own[...] * scale
-
-    def weighted(src, weights, other):
-        rows = weights.shape[0]
-        for row in range(rows):
-            at = slice(row * d, (row + 1) * d)
-            hi, mid, lo = split3(src[:, at].astype(F32) * weights[row : row + 1, :])
+    size = out.shape[1]
+    row_at, col_at = ids[pairs], ids[pairs + 1]
+    up, down = jnp.minimum(row_at + 1, rows - 1), jnp.maximum(row_at - 1, 0)
+
+    lane = lax.broadcasted_iota(jnp.int32, (1, d), 1)
+
+    def names(line):
+        return [
+            jnp.sum(jnp.where(lane == k, line, 0.0)).astype(jnp.int32) for k in range(pairs)
+        ]
+
+    line = w + 2 * layers
+
+    def at_row(r):
+        return names(rec0[r, line : line + 1, :])
+
+    near = [
+        (row_at, col_at, [ids[k] for k in range(pairs)]),
+        (row_at + 1, col_at, at_row(up)),
+        (row_at - 1, col_at, at_row(down)),
+        (row_at, col_at + 1, names(cond_high[n : n + 1, :])),
+        (row_at, col_at - 1, names(cond_low[n : n + 1, :])),
+    ]
+    near += [(ids[k], col_at, at_row(ids[k])) for k in range(pairs)]
+    count = len(near)
+    for j, (r, c, others) in enumerate(near):
+        places = [(r, c), (r + 1, c), (r - 1, c), (r, c + 1), (r, c - 1)]
+        places += [(q, c) for q in others]
+        there = (r >= 0) & (r < rows) & (c >= 0) & (c < cols)
+        for i, (pr, pc) in enumerate(places):
+            good = there & (pr >= 0) & (pr < rows) & (pc >= 0) & (pc < cols)
+            table[j * count + i] = jnp.where(good, pr * cols + pc, -1)
+
+    def weighted(src, row_weights, other):
+        m = len(row_weights)
+        k = other.shape[1] // m
+        for i, weight in enumerate(row_weights):
+            at = slice(i * k, (i + 1) * k)
+            hi, mid, lo = split3(src[:, at].astype(F32) * weight)
             w3[0:size, at] = hi
             w3[size : 2 * size, at] = mid
             w3[2 * size : 3 * size, at] = lo
-        return fold3(dot_nt(w3[:, : rows * d], other)) * (-scale)
-
-    ux = coef[3]
-    lx = coef[4]
-    high = jnp.concatenate([ux[z * w + w - 1 : z * w + w] for z in range(layers)], axis=0)
-    low = jnp.concatenate([lx[z * w : z * w + 1] for z in range(layers)], axis=0)
-    ahead = weighted(face_last, high, next_first[...])
-    up = jnp.minimum(row_at + 1, count - 1)
-    out[up] = out[up] + jnp.where(row_at < count - 1, ahead, 0.0)
-    behind = weighted(face_first, low, prev_last[...])
-    down = jnp.maximum(row_at - 1, 0)
-    out[down] = out[down] + jnp.where(row_at > 0, behind, 0.0)
+        return -fold3(dot_nt(w3[:, : m * k], other))
+
+    def dot(a, b):
+        return lax.dot_general(
+            a, b, (((1,), (0,)), ((), ())),
+            precision=lax.Precision.HIGHEST, preferred_element_type=F32,
+        )
+
+    ux, lx, uy, ly = coef[3], coef[4], coef[5], coef[6]
+    found = [
+        weighted(
+            face_last, [ux[z * w + w - 1 : z * w + w] for z in range(layers)], next_first[...]
+        ),
+        weighted(face_first, [lx[z * w : z * w + 1] for z in range(layers)], prev_last[...]),
+    ]
+    row = lax.broadcasted_iota(jnp.int32, (n, d), 0)
+    wide = lax.broadcasted_iota(jnp.int32, (n, d), 1)
+    high_weight = jnp.sum(jnp.where(wide == row, uy[:, d - 1 : d], 0.0), axis=0, keepdims=True)
+    low_weight = jnp.sum(jnp.where(wide == n + row, ly[:, 0:1], 0.0), axis=0, keepdims=True)
+    sides = face_y[...].astype(F32)
+    swapped = pltpu.roll(sides, n, 1)
+    found.append(weighted(swapped, [high_weight], y_high[...]))
+    found.append(weighted(swapped, [low_weight], y_low[...]))
+    top = vent[...]
     for k in range(pairs):
-        at = ids[k]
-        block = weighted(panel, vent[...] * rec[at, 0:w, :], panels[at])
-        out[at] = out[at] + block
-
-
-def call(kernel, outs, operands, scratch=(), smem=0, cost=None):
-    specs = [SMEM] * smem + [VMEM] * (len(operands) - smem)
+        weight = top * rec0[ids[k], 0:w, :]
+        found.append(weighted(panel, [weight[i : i + 1] for i in range(w)], chosen[k]))
+
+    for slot in range(rows):
+        out[slot] = jnp.zeros((size, size), F32)
+    out[row_at] = own[...] * scale
+    out[up] = out[up] + jnp.where(row_at < rows - 1, found[0] * scale, 0.0)
+    out[down] = out[down] + jnp.where(row_at > 0, found[1] * scale, 0.0)
+    for k in range(pairs):
+        out[ids[k]] = out[ids[k]] + found[4 + k] * scale
+
+    half = size // 2
+    first = w + 2 * layers
+
+    def unfold(folded):
+        return jnp.concatenate([folded[:, 0:size], folded[:, size:]], axis=0)
+
+    theirs = [
+        unfold(rec[up, first : first + half, :]),
+        unfold(rec[down, first : first + half, :]),
+        unfold(high[n : n + half, :]),
+        unfold(low[n : n + half, :]),
+    ]
+    theirs += [unfold(rec[ids[k], first : first + half, :]) for k in range(pairs)]
+    weights[0] = inverse[...]
+    for j, (block, solve) in enumerate(zip(found, theirs)):
+        weights[j + 1] = -dot(inverse[...], dot(block, solve))
+
+
+def call(kernel, outs, operands, scratch=(), smem=0, hbm=(), smem_outs=(), cost=None):
+    specs = [
+        SMEM if i < smem else HBM if i in hbm else VMEM for i in range(len(operands))
+    ]
     return pl.pallas_call(
         kernel,
         out_shape=tuple(jax.ShapeDtypeStruct(s, t) for s, t in outs),
         in_specs=specs,
-        out_specs=tuple([VMEM] * len(outs)),
+        out_specs=tuple(SMEM if i in smem_outs else VMEM for i in range(len(outs))),
         scratch_shapes=list(scratch),
         compiler_params=pltpu.CompilerParams(vmem_limit_bytes=VMEM_LIMIT),
         cost_estimate=cost,
@@ -441,121 +663,151 @@
         rec = lax.all_to_all(payload, "row", 0, 0)
         return rec, low, high
 
-    cond, pay0 = call(
-        lambda c, m, v, o, p: k_first(grid, m, c, v, o, p),
-        (field, pay),
-        (conductivity, classes, vent_open),
-        smem=1,
+    def rows_of(count):
+        return ((row_count, width + 2 * layers + count, depth), F32)
+
+    cond, cap, vent, pay0 = call(
+        functools.partial(k_first, grid),
+        (((n + 8, depth), F32), field, ((width, depth), F32), rows_of(8)),
+        (classes, conductivity, capacity, vent_open, partners.reshape(-1)),
+        scratch=(
+            pltpu.VMEM((n, depth), jnp.int32),
+            pltpu.SMEM(conductivity.shape, F32),
+            pltpu.SMEM(capacity.shape, F32),
+            pltpu.SMEM((pairs,), jnp.int32),
+            pltpu.SemaphoreType.DMA((5,)),
+        ),
+        hbm=(0, 1, 2, 3, 4),
     )
     rec0, cond_low, cond_high = exchange(cond, pay0)
-
-    zm, own_inner, projected, panel, face_last, face_first = call(
-        lambda c, k, b, f, m, *rest: k_basis(grid, b, f, m, c, k, *rest),
+    (panel,) = call(
+        functools.partial(k_panel, grid),
+        (((size, width * depth), BF16),),
+        (basis, cond),
+        scratch=(
+            pltpu.VMEM((size, width, depth), BF16),
+            pltpu.VMEM((size * width, depth), F32),
+            pltpu.SemaphoreType.DMA,
+        ),
+        hbm=(0, 1),
+    )
+    panels = lax.all_gather(panel, "row", axis=0)
+
+    zm, own_inner, projected, face_last, face_first, face_y, rhs = call(
+        functools.partial(k_basis, grid),
         (
             ((size, n * depth), BF16),
             small,
             ((size, depth), F32),
-            ((size, width * depth), BF16),
             ((size, layers * depth), BF16),
             ((size, layers * depth), BF16),
-        ),
-        (conductivity, capacity, basis, rhs, classes),
+            ((size, depth), BF16),
+            field,
+        ),
+        (basis, rhs, cond, cap),
         scratch=(
             pltpu.VMEM((size * n, depth), F32),
             pltpu.VMEM((n, size, depth), F32),
             pltpu.VMEM((3 * size, n * depth), BF16),
             pltpu.VMEM((7, n, depth), F32),
-        ),
-        smem=2,
+            pltpu.VMEM((size, n, depth), BF16),
+            pltpu.SemaphoreType.DMA((5,)),
+        ),
+        hbm=(0, 1),
         cost=pl.CostEstimate(flops=200_000_000, bytes_accessed=8_000_000, transcendentals=0),
     )
-    panels = lax.all_gather(panel, "row", axis=0)
-    prev_last = cyclic(face_last, "row", 1)
-    next_first = cyclic(face_first, "row", -1)
-
-    coef, own, inverse, v0, pay1 = call(
+
+    coef, own, inverse, sent, pay1 = call(
         functools.partial(k_setup, grid, pairs, col_count),
-        (((7, n, depth), F32), small, small, field, pay),
-        (
-            ids, conductivity, capacity, classes, vent_open, cond, cond_low, cond_high, rec0,
-            zm, own_inner, projected,
-        ),
-        scratch=(pltpu.VMEM((3 * size, n * depth), BF16),),
-        smem=3,
-    )
-    rec, low, high = exchange(v0, pay1)
+        (((7, n, depth), F32), small, small, ((n + size // 2, depth), F32), rows_of(size // 2)),
+        (ids, cap, vent, cond, cond_low, cond_high, rec0, zm, own_inner, projected),
+        scratch=(
+            pltpu.VMEM((3 * size, n * depth), BF16),
+            pltpu.VMEM((n, depth), F32),
+        ),
+        smem=1,
+    )
+    rec1, low1, high1 = exchange(sent, pay1)
+    face_last_, face_first_, face_y_, _ = lax.optimization_barrier(
+        (face_last, face_first, face_y, pay1)
+    )
+    prev_last = cyclic(face_last_, "row", 1)
+    next_first = cyclic(face_first_, "row", -1)
+    y_low = cyclic(face_y_, "col", 1)
+    y_high = cyclic(face_y_, "col", -1)
     x0, pay2 = call(
         functools.partial(k_coarse, grid, pairs, False),
         (field, pay),
-        (ids, coef, vent_open, zm, inverse, v0, rec, low, high),
+        (ids, coef, vent, zm, inverse, sent, rec1, low1, high1),
         scratch=(pltpu.VMEM((n, depth), F32),),
         smem=1,
     )
     rec, low, high = exchange(x0, pay2)
-    r0, pay3 = call(
-        functools.partial(k_apply, grid, pairs, True),
+    everyone = ((row_count * col_count, 8, depth), F32)
+    r0, pay3, chosen = call(
+        functools.partial(k_partials, grid, pairs, True, True),
+        (field, everyone, ((pairs, size, width * depth), BF16)),
+        (
+            ids, coef, vent, x0, rec, low, high, rec0, zm, next_first, prev_last, y_low, y_high,
+            panels, rhs,
+        ),
+        scratch=(pltpu.SemaphoreType.DMA((pairs,)),),
+        smem=1,
+        hbm=(13,),
+    )
+    places = 5 + pairs
+    blocks, weights, table = call(
+        functools.partial(k_blocks, grid, pairs, row_count, col_count, 1.0 / cells),
+        (
+            ((row_count, size, size), F32),
+            ((places, size, size), F32),
+            ((places * places,), jnp.int32),
+        ),
+        (
+            ids, vent, coef, rec0, cond_low, cond_high, rec1, low1, high1, panel, chosen, own,
+            inverse, face_last, face_first, next_first, prev_last, face_y, y_low, y_high, pay3,
+        ),
+        scratch=(pltpu.VMEM((3 * size, width * depth), BF16),),
+        smem=1,
+        hbm=(20,),
+        smem_outs=(2,),
+        cost=pl.CostEstimate(flops=100_000_000, bytes_accessed=4_000_000, transcendentals=0),
+    )
+    sums = lax.all_to_all(pay3, ("row", "col"), 0, 0)
+    p0, pay4 = call(
+        functools.partial(k_combine, grid),
         (field, pay),
-        (ids, coef, vent_open, x0, rec, low, high, rhs),
-        smem=1,
-    )
-    rec, low, high = exchange(r0, pay3)
-    u0, pay4 = call(
-        functools.partial(k_apply_solve, grid, pairs),
-        (field, pay),
-        (ids, coef, vent_open, zm, inverse, r0, rec, low, high),
-        smem=1,
-    )
-    rec, low, high = exchange(u0, pay4)
-    p0, pay5 = call(
-        functools.partial(k_coarse, grid, pairs, True),
-        (field, pay),
-        (ids, coef, vent_open, zm, inverse, u0, rec, low, high, r0),
+        (table, sums, weights, zm, r0, vent),
         scratch=(pltpu.VMEM((n, depth), F32),),
         smem=1,
     )
-    rec, low, high = exchange(p0, pay5)
-    i0, pay6 = call(
-        functools.partial(k_apply, grid, pairs, False),
+    rec, low, high = exchange(p0, pay4)
+    i0, pay5 = call(
+        functools.partial(k_partials, grid, pairs, False, False),
+        (field, everyone),
+        (
+            ids, coef, vent, p0, rec, low, high, rec0, zm, next_first, prev_last, y_low, y_high,
+            chosen,
+        ),
+        smem=1,
+    )
+    sums = lax.all_to_all(pay5, ("row", "col"), 0, 0)
+    d0, pay6 = call(
+        functools.partial(k_combine, grid),
         (field, pay),
-        (ids, coef, vent_open, p0, rec, low, high),
-        smem=1,
-    )
-    rec, low, high = exchange(i0, pay6)
-    s0, pay7 = call(
-        functools.partial(k_apply_solve, grid, pairs),
-        (field, pay),
-        (ids, coef, vent_open, zm, inverse, i0, rec, low, high),
-        smem=1,
-    )
-    rec, low, high = exchange(s0, pay7)
-    d0, pay8 = call(
-        functools.partial(k_coarse, grid, pairs, True),
-        (field, pay),
-        (ids, coef, vent_open, zm, inverse, s0, rec, low, high, i0),
+        (table, sums, weights, zm, i0, vent),
         scratch=(pltpu.VMEM((n, depth), F32),),
         smem=1,
     )
-    rec, low, high = exchange(d0, pay8)
-    image, pay9 = call(
+    rec, low, high = exchange(d0, pay6)
+    image, pay7 = call(
         functools.partial(k_dots, grid, pairs),
-        (field, ((row_count * col_count, 8, depth), F32)),
-        (ids, coef, vent_open, d0, rec, low, high, r0, p0, i0),
+        (field, everyone),
+        (ids, coef, vent, d0, rec, low, high, r0, p0, i0),
         smem=1,
     )
-    rec9 = lax.all_to_all(pay9, ("row", "col"), 0, 0)
-    x2, r2 = call(k_last, (field, field), (rec9, x0, r0, p0, i0, d0, image))
-
-    (blocks,) = call(
-        functools.partial(k_blocks, grid, pairs, 1.0 / cells),
-        (((row_count, size, size), F32),),
-        (
-            ids, vent_open, coef, rec0, panel, panels, own, face_last, face_first,
-            next_first, prev_last,
-        ),
-        scratch=(pltpu.VMEM((3 * size, width * depth), BF16),),
-        smem=1,
-        cost=pl.CostEstimate(flops=100_000_000, bytes_accessed=4_000_000, transcendentals=0),
-    )
+    total = lax.all_to_all(pay7, ("row", "col"), 0, 0)
+    x2, r2 = call(k_last, (field, field), (total, x0, r0, p0, i0, d0, image))
     shape = forcing_right_hand.shape
     return x2.reshape(shape), r2.reshape(shape), blocks[None, None]
 

time: 169 us -> 139 us (0.82)
  starting transfers between devices: 80.9 us -> 41.5 us
  blocking collectives: 0 us -> 22.8 us
  Pallas kernels: 34.2 us -> 24.7 us
  local copies, waits for them, and re-layouts: 10.5 us -> 6.98 us
    all_to_all x0 -> x2, blocking collectives: none -> 22.8 us  [the longest x1 11.4 us: body(): sums = lax.all_to_all(pay5, ('row', 'col'), 0, 0)]
    all_to_all x9 -> x5, starting transfers between devices: 36 us -> 17.9 us  [exchange(): rec = lax.all_to_all(payload, 'row', 0, 0)]
    ppermute x20 -> x14, starting transfers between devices: 38.4 us -> 20.7 us  [cyclic(): lax.ppermute(value, axis, [(i, (i + step) % count) for i in range(count)])]
    pallas_call x13 -> x12, Pallas kernels: 34.2 us -> 24.7 us  [call(): pl.pallas_call(kernel, out_shape=tuple((jax.ShapeDtypeStruct(s, t) for s,...]
    ppermute x20 -> x14, waiting for transfers between devices: 16.2 us -> 21.1 us  [cyclic(): lax.ppermute(value, axis, [(i, (i + step) % count) for i in range(count)])]
    all_to_all x1, starting transfers between devices: 6.38 us -> 2.76 us  [body(): sums = lax.all_to_all(pay3, ('row', 'col'), 0, 0)]
    unnamed x30 -> x18, local copies, waits for them, and re-layouts: 10.5 us -> 6.98 us
    all_to_all x9 -> x5, waiting for transfers between devices: 4.66 us -> 1.42 us  [exchange(): rec = lax.all_to_all(payload, 'row', 0, 0)]
  transfers between devices with their start and end apart: 31 -> 21, of which waited for: 10 -> 9; matrix products, arithmetic and copies ran while one was open for 0% -> 0% of each run, Pallas kernels for 16% -> 10%
where the time goes in v2:
time: 139 us; the launch traced here: 138 us
  starting transfers between devices  41.5 us (30%)
  waiting for transfers between devices  27.5 us (20%)
  Pallas kernels  24.7 us (18%)
  blocking collectives  22.8 us (16%)
  between operations  14.2 us (10%)
  local copies, waits for them, and re-layouts  6.98 us (5%)
    pallas_call x12, Pallas kernels, call(): pl.pallas_call(kernel, out_shape=tuple((jax.ShapeDtypeStruct(s, t) for s,...  24.7 us
    ppermute x14, waiting for transfers between devices, cyclic(): lax.ppermute(value, axis, [(i, (i + step) % count) for i in range(count)])  21.1 us
    ppermute x14, starting transfers between devices, cyclic(): lax.ppermute(value, axis, [(i, (i + step) % count) for i in range(count)])  20.7 us
    all_to_all x5, starting transfers between devices, exchange(): rec = lax.all_to_all(payload, 'row', 0, 0)  17.9 us
    all_to_all x1, blocking collectives, body(): sums = lax.all_to_all(pay5, ('row', 'col'), 0, 0)  11.4 us
    all_to_all x1, blocking collectives, body(): total = lax.all_to_all(pay7, ('row', 'col'), 0, 0)  11.4 us
    unnamed x18, local copies, waits for them, and re-layouts  6.98 us
    all_to_all x1, waiting for transfers between devices, body(): sums = lax.all_to_all(pay3, ('row', 'col'), 0, 0)  4.87 us
  transfers between devices with their start and end apart: 21, of which 9 were waited for; matrix products, arithmetic and copies ran while one was open for 0% of the time, Pallas kernels for 10%

profile of v2, /device:TPU:0, one launch (start us, length us, event | category | flops | bytes accessed | tf_op | source)
XLA Modules:
  0.0 137.6 jit_solution(4010179758765664285)
XLA Ops:
  14.2 5.1 %collective-permute-start.1 = (f32[72,128]{1,0:T(8,128)S(1)}, f32[72,128]{1,0:T(8,128)S(1)}, u32[]{:S(2)}, u32[]{:S(2)}) collective-permute-start(f32[72,128]{1,0:T(8,128)S(1)} %get-tuple-element.42.cond_ref.cond._), channel_id=1, source_target_pairs={{0,3},{1,0},{2,1},{3,2},{4,7},{5,4},{6,5},{7,6},{8,11},{9,8},{10,9... | collective-permute-start | bytes 110600 | tf_op jit(solution)/shard_map/ppermute | solution.py:658
  19.3 3.7 %all-to-all-start = ((f32[8,32,128]{2,1,0:T(8,128)}), f32[8,32,128]{2,1,0:T(8,128)S(1)}, u32[]{:S(2)}, u32[]{:S(2)}) async-start(f32[8,32,128]{2,1,0:T(8,128)} %get-tuple-element.43), calls=%async_computation | async-start | bytes 262144 | tf_op jit(solution)/shard_map/all_to_all | solution.py:663
  23.9 4.3 %shard_map.95 = (bf16[64,8192]{1,0:T(8,128)(2,1)S(1)}, f32[64,64]{1,0:T(8,128)S(1)}, f32[64,128]{1,0:T(8,128)S(1)}, bf16[64,512]{1,0:T(8,128)(2,1)S(1)}, bf16[64...) custom-call(bf16[64,64,128]{2,1,0:T(8,128)(2,1)S(1)} %bitcast.11, ...), custom_call_target="tpu_custom_call" | custom-call | flops 200000000 | bytes 8000000 | tf_op jit(solution)/shard_map/pallas_call | solution.py:625
  29.6 4.4 %shard_map.96 = (f32[7,64,128]{2,1,0:T(8,128)S(1)}, f32[64,64]{1,0:T(8,128)S(1)}, f32[64,64]{1,0:T(8,128)S(1)}, f32[96,128]{1,0:T(8,128)S(1)}, f32[8,56,128]{2,1,0:T(8,128)}) custom-call(s32[4]{0:T(128)S(1)} %pad_add_fusion.ids, f32[64,128]{1,0:T(8,128)S(1)} %get-tuple-element.40.cap_ref.cap, f32[16,128]{1,0:T(8,128)S(1)} %get-tuple-element.41.vent, ...), custom_call_target="tpu_custom_call" | custom-call | tf_op jit(solution)/shard_map/pallas_call | solution.py:625
  34.0 3.4 %all-to-all-start.1 = ((f32[8,56,128]{2,1,0:T(8,128)}), f32[8,56,128]{2,1,0:T(8,128)S(1)}, u32[]{:S(2)}, u32[]{:S(2)}) async-start(f32[8,56,128]{2,1,0:T(8,128)} %get-tuple-element.48), calls=%async_computation.1 | async-start | bytes 458752 | tf_op jit(solution)/shard_map/all_to_all | solution.py:663
  37.4 4.2 %collective-permute-start.3 = (f32[96,128]{1,0:T(8,128)S(1)}, f32[96,128]{1,0:T(8,128)S(1)}, u32[]{:S(2)}, u32[]{:S(2)}) collective-permute-start(f32[96,128]{1,0:T(8,128)S(1)} %get-tuple-element.49.field), channel_id=1, source_target_pairs={{0,3},{1,0},{2,1},{3,2},{4,7},{5,4},{6,5},{7,6},{8,11},{9,8},{10,9... | collective-permute-start | bytes 147464 | tf_op jit(solution)/shard_map/ppermute | solution.py:658
  41.7 2.1 %collective-permute-done.3.high = f32[96,128]{1,0:T(8,128)S(1)} collective-permute-done((f32[96,128]{1,0:T(8,128)S(1)}, f32[96,128]{1,0:T(8,128)S(1)}, u32[]{:S(2)}, u32[]{:S(2)}) %collective-permute-start.3) | collective-permute-done | bytes 49184 | tf_op jit(solution)/shard_map/ppermute | solution.py:658
  43.7 3.8 %collective-permute-done.2.low = f32[96,128]{1,0:T(8,128)S(1)} collective-permute-done((f32[96,128]{1,0:T(8,128)S(1)}, f32[96,128]{1,0:T(8,128)S(1)}, u32[]{:S(2)}, u32[]{:S(2)}) %collective-permute-start.2) | collective-permute-done | bytes 49184 | tf_op jit(solution)/shard_map/ppermute | solution.py:658
  47.6 1.9 %shard_map.98 = (f32[64,128]{1,0:T(8,128)S(1)}, f32[8,24,128]{2,1,0:T(8,128)}) custom-call(s32[4]{0:T(128)S(1)} %pad_add_fusion.ids, f32[7,64,128]{2,1,0:T(8,128)S(1)} %get-tuple-element.47.coef, f32[16,128]{1,0:T(8,128)S(1)} %get-tuple-element.41.vent, bf16[64,8192]{1,0:T(8,128)(2,1)S(1)} %get-tuple-element.44.zm, f32[64,64]{1,0:T(8,128)S(1)} %get-tuple-element.50.inverse, ...), custom_call_target="tpu_custom_call" | custom-call | tf_op jit(solution)/shard_map/pallas_call | solution.py:625
  49.5 4.1 %all-to-all-start.2 = ((f32[8,24,128]{2,1,0:T(8,128)}), f32[8,24,128]{2,1,0:T(8,128)S(1)}, u32[]{:S(2)}, u32[]{:S(2)}) async-start(f32[8,24,128]{2,1,0:T(8,128)} %get-tuple-element.52), calls=%async_computation.2 | async-start | bytes 196608 | tf_op jit(solution)/shard_map/all_to_all | solution.py:663
  53.6 2.7 %collective-permute-start.6 = (bf16[64,512]{1,0:T(8,128)(2,1)S(1)}, bf16[64,512]{1,0:T(8,128)(2,1)S(1)}, u32[]{:S(2)}, u32[]{:S(2)}) collective-permute-start(bf16[64,512]{1,0:T(8,128)(2,1)S(1)} %get-tuple-element.56.face_first), channel_id=1, source_target_pairs={{0,28},{4,0},{8,4},{12,8},{16,12},{20,16},{24,20},{28,24},{1,29},{... | collective-permute-start | bytes 196616 | tf_op jit(solution)/shard_map/ppermute | solution.py:658
  56.3 2.5 %collective-permute-start.9 = (bf16[64,128]{1,0:T(8,128)(2,1)S(1)}, bf16[64,128]{1,0:T(8,128)(2,1)S(1)}, u32[]{:S(2)}, u32[]{:S(2)}) collective-permute-start(bf16[64,128]{1,0:T(8,128)(2,1)S(1)} %get-tuple-element.58.face_y), channel_id=1, source_target_pairs={{0,3},{1,0},{2,1},{3,2},{4,7},{5,4},{6,5},{7,6},{8,11},{9,8},{10,9... | collective-permute-start | bytes 49160 | tf_op jit(solution)/shard_map/ppermute | solution.py:658
  58.8 2.0 %collective-permute-start.4 = (f32[64,128]{1,0:T(8,128)S(1)}, f32[64,128]{1,0:T(8,128)S(1)}, u32[]{:S(2)}, u32[]{:S(2)}) collective-permute-start(f32[64,128]{1,0:T(8,128)S(1)} %get-tuple-element.51.field.x0), channel_id=1, source_target_pairs={{0,1},{1,2},{2,3},{3,0},{4,5},{5,6},{6,7},{7,4},{8,9},{9,10},{10,1... | collective-permute-start | bytes 98312 | tf_op jit(solution)/shard_map/ppermute | solution.py:658
  60.8 5.5 %collective-permute-done.8.y_low = bf16[64,128]{1,0:T(8,128)(2,1)S(1)} collective-permute-done((bf16[64,128]{1,0:T(8,128)(2,1)S(1)}, bf16[64,128]{1,0:T(8,128)(2,1)S(1)}, u32[]{:S(2)}, u32[]{:S(2)}) %collective-permute-start.8) | collective-permute-done | bytes 16416 | tf_op jit(solution)/shard_map/ppermute | solution.py:658
  68.0 2.2 %shard_map.99 = (f32[64,128]{1,0:T(8,128)S(1)}, f32[32,8,128]{2,1,0:T(8,128)}, bf16[2,64,2048]{2,1,0:T(8,128)(2,1)S(1)}) custom-call(s32[4]{0:T(128)S(1)} %pad_add_fusion.ids, f32[7,64,128]{2,1,0:T(8,128)S(1)} %get-tuple-element.47.coef, f32[16,128]{1,0:T(8,128)S(1)} %get-tuple-element.41.vent, f32[64,128]{1,0:T(8,128)S(1)} %get-tuple-element.51.field.x0, ...), custom_call_target="tpu_custom_call" | custom-call | tf_op jit(solution)/shard_map/pallas_call | solution.py:625
  70.2 2.8 %all-to-all-start.3 = ((f32[32,8,128]{2,1,0:T(8,128)}), f32[32,8,128]{2,1,0:T(8,128)S(1)}, u32[]{:S(2)}, u32[]{:S(2)}) async-start(f32[32,8,128]{2,1,0:T(8,128)} %get-tuple-element.62._), calls=%async_computation.3 | async-start | bytes 262144 | tf_op jit(solution)/shard_map/all_to_all | solution.py:776
  72.9 3.3 %shard_map.100 = (f32[8,64,64]{2,1,0:T(8,128)}, f32[7,64,64]{2,1,0:T(8,128)S(1)}, s32[49]{0:T(128)S(1)}) custom-call(s32[4]{0:T(128)S(1)} %pad_add_fusion.ids, f32[16,128]{1,0:T(8,128)S(1)} %get-tuple-element.41.vent, f32[7,64,128]{2,1,0:T(8,128)S(1)} %get-tuple-element.47.coef, f32[8,32,128]{2,1,0:T(8,128)S(1)} %all-to-all-done.rec.rec0, ...), custom_call_target="tpu_custom_call" | custom-call | flops 100000000 | bytes 4000000 | tf_op jit(solution)/shard_map/pallas_call | solution.py:625
  76.3 4.9 %all-to-all-done.3.rec = f32[32,8,128]{2,1,0:T(8,128)S(1)} async-done(((f32[32,8,128]{2,1,0:T(8,128)}), f32[32,8,128]{2,1,0:T(8,128)S(1)}, u32[]{:S(2)}, u32[]{:S(2)}) %all-to-all-start.3) | async-done | bytes 131104 | tf_op jit(solution)/shard_map/all_to_all | solution.py:776
  82.8 3.4 %all-to-all-start.4 = ((f32[8,24,128]{2,1,0:T(8,128)}), f32[8,24,128]{2,1,0:T(8,128)S(1)}, u32[]{:S(2)}, u32[]{:S(2)}) async-start(f32[8,24,128]{2,1,0:T(8,128)} %get-tuple-element.67), calls=%async_computation.4 | async-start | bytes 196608 | tf_op jit(solution)/shard_map/all_to_all | solution.py:663
  90.2 2.9 %collective-permute-done.10.low = f32[64,128]{1,0:T(8,128)S(1)} collective-permute-done((f32[64,128]{1,0:T(8,128)S(1)}, f32[64,128]{1,0:T(8,128)S(1)}, u32[]{:S(2)}, u32[]{:S(2)}) %collective-permute-start.10) | collective-permute-done | bytes 32800 | tf_op jit(solution)/shard_map/ppermute | solution.py:658
  94.5 11.4 %all_to_all.40.rec = f32[32,8,128]{2,1,0:T(8,128)S(1)} all-to-all(f32[32,8,128]{2,1,0:T(8,128)S(1)} %get-tuple-element.68), channel_id=1, replica_groups=mesh['row'=8,'col'=4] {'row','col'}, dimensions={0} | all-to-all | bytes 262144 | tf_op jit(solution)/shard_map/all_to_all | solution.py:794
  107.6 3.4 %all-to-all-start.6 = ((f32[8,24,128]{2,1,0:T(8,128)}), f32[8,24,128]{2,1,0:T(8,128)S(1)}, u32[]{:S(2)}, u32[]{:S(2)}) async-start(f32[8,24,128]{2,1,0:T(8,128)} %get-tuple-element.71), calls=%async_computation.6 | async-start | bytes 196608 | tf_op jit(solution)/shard_map/all_to_all | solution.py:663
  114.9 3.0 %collective-permute-done.12.low = f32[64,128]{1,0:T(8,128)S(1)} collective-permute-done((f32[64,128]{1,0:T(8,128)S(1)}, f32[64,128]{1,0:T(8,128)S(1)}, u32[]{:S(2)}, u32[]{:S(2)}) %collective-permute-start.12) | collective-permute-done | bytes 32800 | tf_op jit(solution)/shard_map/ppermute | solution.py:658
  118.6 11.4 %all_to_all.41.rec = f32[32,8,128]{2,1,0:T(8,128)S(1)} all-to-all(f32[32,8,128]{2,1,0:T(8,128)S(1)} %get-tuple-element.72), channel_id=1, replica_groups=mesh['row'=8,'col'=4] {'row','col'}, dimensions={0} | all-to-all | bytes 262144 | tf_op jit(solution)/shard_map/all_to_all | solution.py:809
  (52 shorter events, 25.1 us)
Async XLA Ops:
  7.2 59.2 %all-gather.3.cloned.1.call-start = ((), (), s32[]{:S(2)}) async-start(), calls=%async_computation.8 | async-start | bytes 2359296 | tf_op jit(solution)/shard_map/all_gather | solution.py:694
  12.0 1.2 copy-start
  13.2 9.9 %copy-start.1 = (bf16[64,4,16,128]{3,2,1,0:T(8,128)(2,1)S(1)}, bf16[64,4,16,128]{3,2,1,0:T(8,128)(2,1)}, u32[]{:S(2)}) copy-start(bf16[64,4,16,128]{3,2,1,0:T(8,128)(2,1)} %param.13) | copy-start | bytes 3145732
  14.2 14.0 %collective-permute-start.1 = (f32[72,128]{1,0:T(8,128)S(1)}, f32[72,128]{1,0:T(8,128)S(1)}, u32[]{:S(2)}, u32[]{:S(2)}) collective-permute-start(f32[72,128]{1,0:T(8,128)S(1)} %get-tuple-element.42.cond_ref.cond._), channel_id=1, source_target_pairs={{0,3},{1,0},{2,1},{3,2},{4,7},{5,4},{6,5},{7,6},{8,11},{9,8},{10,9... | collective-permute-start | bytes 110600 | tf_op jit(solution)/shard_map/ppermute | solution.py:658
  19.3 8.9 %collective-permute-start = (f32[72,128]{1,0:T(8,128)S(1)}, f32[72,128]{1,0:T(8,128)S(1)}, u32[]{:S(2)}, u32[]{:S(2)}) collective-permute-start(f32[72,128]{1,0:T(8,128)S(1)} %get-tuple-element.42.cond_ref.cond._), channel_id=1, source_target_pairs={{0,1},{1,2},{2,3},{3,0},{4,5},{5,6},{6,7},{7,4},{8,9},{9,10},{10,1... | collective-permute-start | bytes 110600 | tf_op jit(solution)/shard_map/ppermute | solution.py:658
  19.3 10.3 %all-to-all-start = ((f32[8,32,128]{2,1,0:T(8,128)}), f32[8,32,128]{2,1,0:T(8,128)S(1)}, u32[]{:S(2)}, u32[]{:S(2)}) async-start(f32[8,32,128]{2,1,0:T(8,128)} %get-tuple-element.43), calls=%async_computation | async-start | bytes 262144 | tf_op jit(solution)/shard_map/all_to_all | solution.py:663
  34.0 13.5 %all-to-all-start.1 = ((f32[8,56,128]{2,1,0:T(8,128)}), f32[8,56,128]{2,1,0:T(8,128)S(1)}, u32[]{:S(2)}, u32[]{:S(2)}) async-start(f32[8,56,128]{2,1,0:T(8,128)} %get-tuple-element.48), calls=%async_computation.1 | async-start | bytes 458752 | tf_op jit(solution)/shard_map/all_to_all | solution.py:663
  37.4 6.3 %collective-permute-start.3 = (f32[96,128]{1,0:T(8,128)S(1)}, f32[96,128]{1,0:T(8,128)S(1)}, u32[]{:S(2)}, u32[]{:S(2)}) collective-permute-start(f32[96,128]{1,0:T(8,128)S(1)} %get-tuple-element.49.field), channel_id=1, source_target_pairs={{0,3},{1,0},{2,1},{3,2},{4,7},{5,4},{6,5},{7,6},{8,11},{9,8},{10,9... | collective-permute-start | bytes 147464 | tf_op jit(solution)/shard_map/ppermute | solution.py:658
  41.7 5.9 %collective-permute-start.2 = (f32[96,128]{1,0:T(8,128)S(1)}, f32[96,128]{1,0:T(8,128)S(1)}, u32[]{:S(2)}, u32[]{:S(2)}) collective-permute-start(f32[96,128]{1,0:T(8,128)S(1)} %get-tuple-element.49.field), channel_id=1, source_target_pairs={{0,1},{1,2},{2,3},{3,0},{4,5},{5,6},{6,7},{7,4},{8,9},{9,10},{10,1... | collective-permute-start | bytes 147464 | tf_op jit(solution)/shard_map/ppermute | solution.py:658
  49.5 16.9 %all-to-all-start.2 = ((f32[8,24,128]{2,1,0:T(8,128)}), f32[8,24,128]{2,1,0:T(8,128)S(1)}, u32[]{:S(2)}, u32[]{:S(2)}) async-start(f32[8,24,128]{2,1,0:T(8,128)} %get-tuple-element.52), calls=%async_computation.2 | async-start | bytes 196608 | tf_op jit(solution)/shard_map/all_to_all | solution.py:663
  53.6 12.7 %collective-permute-start.6 = (bf16[64,512]{1,0:T(8,128)(2,1)S(1)}, bf16[64,512]{1,0:T(8,128)(2,1)S(1)}, u32[]{:S(2)}, u32[]{:S(2)}) collective-permute-start(bf16[64,512]{1,0:T(8,128)(2,1)S(1)} %get-tuple-element.56.face_first), channel_id=1, source_target_pairs={{0,28},{4,0},{8,4},{12,8},{16,12},{20,16},{24,20},{28,24},{1,29},{... | collective-permute-start | bytes 196616 | tf_op jit(solution)/shard_map/ppermute | solution.py:658
  56.3 10.1 %collective-permute-start.7 = (bf16[64,512]{1,0:T(8,128)(2,1)S(1)}, bf16[64,512]{1,0:T(8,128)(2,1)S(1)}, u32[]{:S(2)}, u32[]{:S(2)}) collective-permute-start(bf16[64,512]{1,0:T(8,128)(2,1)S(1)} %get-tuple-element.57.face_last), channel_id=1, source_target_pairs={{0,4},{4,8},{8,12},{12,16},{16,20},{20,24},{24,28},{28,0},{1,5},{5... | collective-permute-start | bytes 196616 | tf_op jit(solution)/shard_map/ppermute | solution.py:658
  56.3 4.5 %collective-permute-start.9 = (bf16[64,128]{1,0:T(8,128)(2,1)S(1)}, bf16[64,128]{1,0:T(8,128)(2,1)S(1)}, u32[]{:S(2)}, u32[]{:S(2)}) collective-permute-start(bf16[64,128]{1,0:T(8,128)(2,1)S(1)} %get-tuple-element.58.face_y), channel_id=1, source_target_pairs={{0,3},{1,0},{2,1},{3,2},{4,7},{5,4},{6,5},{7,6},{8,11},{9,8},{10,9... | collective-permute-start | bytes 49160 | tf_op jit(solution)/shard_map/ppermute | solution.py:658
  58.8 7.6 %collective-permute-start.5 = (f32[64,128]{1,0:T(8,128)S(1)}, f32[64,128]{1,0:T(8,128)S(1)}, u32[]{:S(2)}, u32[]{:S(2)}) collective-permute-start(f32[64,128]{1,0:T(8,128)S(1)} %get-tuple-element.51.field.x0), channel_id=1, source_target_pairs={{0,3},{1,0},{2,1},{3,2},{4,7},{5,4},{6,5},{7,6},{8,11},{9,8},{10,9... | collective-permute-start | bytes 98312 | tf_op jit(solution)/shard_map/ppermute | solution.py:658
  58.8 7.5 %collective-permute-start.4 = (f32[64,128]{1,0:T(8,128)S(1)}, f32[64,128]{1,0:T(8,128)S(1)}, u32[]{:S(2)}, u32[]{:S(2)}) collective-permute-start(f32[64,128]{1,0:T(8,128)S(1)} %get-tuple-element.51.field.x0), channel_id=1, source_target_pairs={{0,1},{1,2},{2,3},{3,0},{4,5},{5,6},{6,7},{7,4},{8,9},{9,10},{10,1... | collective-permute-start | bytes 98312 | tf_op jit(solution)/shard_map/ppermute | solution.py:658
  60.8 5.5 %collective-permute-start.8 = (bf16[64,128]{1,0:T(8,128)(2,1)S(1)}, bf16[64,128]{1,0:T(8,128)(2,1)S(1)}, u32[]{:S(2)}, u32[]{:S(2)}) collective-permute-start(bf16[64,128]{1,0:T(8,128)(2,1)S(1)} %get-tuple-element.58.face_y), channel_id=1, source_target_pairs={{0,1},{1,2},{2,3},{3,0},{4,5},{5,6},{6,7},{7,4},{8,9},{9,10},{10,1... | collective-permute-start | bytes 49160 | tf_op jit(solution)/shard_map/ppermute | solution.py:658
  66.4 1.6 %copy-start.2 = (bf16[512,2048]{1,0:T(8,128)(2,1)S(1)}, bf16[512,2048]{1,0:T(8,128)(2,1)}, u32[]{:S(2)}) copy-start(bf16[512,2048]{1,0:T(8,128)(2,1)} %all-gather.3.cloned.1.call-done) | copy-start | bytes 6291460
  70.2 11.0 %all-to-all-start.3 = ((f32[32,8,128]{2,1,0:T(8,128)}), f32[32,8,128]{2,1,0:T(8,128)S(1)}, u32[]{:S(2)}, u32[]{:S(2)}) async-start(f32[32,8,128]{2,1,0:T(8,128)} %get-tuple-element.62._), calls=%async_computation.3 | async-start | bytes 262144 | tf_op jit(solution)/shard_map/all_to_all | solution.py:776
  82.8 10.3 %all-to-all-start.4 = ((f32[8,24,128]{2,1,0:T(8,128)}), f32[8,24,128]{2,1,0:T(8,128)S(1)}, u32[]{:S(2)}, u32[]{:S(2)}) async-start(f32[8,24,128]{2,1,0:T(8,128)} %get-tuple-element.67), calls=%async_computation.4 | async-start | bytes 196608 | tf_op jit(solution)/shard_map/all_to_all | solution.py:663
  86.2 4.0 %collective-permute-start.11 = (f32[64,128]{1,0:T(8,128)S(1)}, f32[64,128]{1,0:T(8,128)S(1)}, u32[]{:S(2)}, u32[]{:S(2)}) collective-permute-start(f32[64,128]{1,0:T(8,128)S(1)} %get-tuple-element.66.field.p0), channel_id=1, source_target_pairs={{0,3},{1,0},{2,1},{3,2},{4,7},{5,4},{6,5},{7,6},{8,11},{9,8},{10,9... | collective-permute-start | bytes 98312 | tf_op jit(solution)/shard_map/ppermute | solution.py:658
  87.4 5.7 %collective-permute-start.10 = (f32[64,128]{1,0:T(8,128)S(1)}, f32[64,128]{1,0:T(8,128)S(1)}, u32[]{:S(2)}, u32[]{:S(2)}) collective-permute-start(f32[64,128]{1,0:T(8,128)S(1)} %get-tuple-element.66.field.p0), channel_id=1, source_target_pairs={{0,1},{1,2},{2,3},{3,0},{4,5},{5,6},{6,7},{7,4},{8,9},{9,10},{10,1... | collective-permute-start | bytes 98312 | tf_op jit(solution)/shard_map/ppermute | solution.py:658
  107.6 10.3 %all-to-all-start.6 = ((f32[8,24,128]{2,1,0:T(8,128)}), f32[8,24,128]{2,1,0:T(8,128)S(1)}, u32[]{:S(2)}, u32[]{:S(2)}) async-start(f32[8,24,128]{2,1,0:T(8,128)} %get-tuple-element.71), calls=%async_computation.6 | async-start | bytes 196608 | tf_op jit(solution)/shard_map/all_to_all | solution.py:663
  110.9 4.0 %collective-permute-start.13 = (f32[64,128]{1,0:T(8,128)S(1)}, f32[64,128]{1,0:T(8,128)S(1)}, u32[]{:S(2)}, u32[]{:S(2)}) collective-permute-start(f32[64,128]{1,0:T(8,128)S(1)} %get-tuple-element.70.field.d), channel_id=1, source_target_pairs={{0,3},{1,0},{2,1},{3,2},{4,7},{5,4},{6,5},{7,6},{8,11},{9,8},{10,9... | collective-permute-start | bytes 98312 | tf_op jit(solution)/shard_map/ppermute | solution.py:658
  112.2 5.7 %collective-permute-start.12 = (f32[64,128]{1,0:T(8,128)S(1)}, f32[64,128]{1,0:T(8,128)S(1)}, u32[]{:S(2)}, u32[]{:S(2)}) collective-permute-start(f32[64,128]{1,0:T(8,128)S(1)} %get-tuple-element.70.field.d), channel_id=1, source_target_pairs={{0,1},{1,2},{2,3},{3,0},{4,5},{5,6},{6,7},{7,4},{8,9},{9,10},{10,1... | collective-permute-start | bytes 98312 | tf_op jit(solution)/shard_map/ppermute | solution.py:658
  (6 other events, 4.2 us)
Sparse Core Ops, SparseCore 0:
  14.3 33.9 all-gather.2

commit v3 on v2

--- a/solution.py
+++ b/solution.py
@@ -11,9 +11,8 @@
 BF16 = jnp.bfloat16
 VMEM = pl.BlockSpec(memory_space=pltpu.VMEM)
 SMEM = pl.BlockSpec(memory_space=pltpu.SMEM)
-HBM = pl.BlockSpec(memory_space=pltpu.HBM)
 ANY = pl.BlockSpec(memory_space=pl.ANY)
-VMEM_LIMIT = 40 * 1024 * 1024
+VMEM_LIMIT = 16 * 1024 * 1024
 
 
 def harmonic(a, b):
@@ -237,39 +236,30 @@
     return uz, lz, ux, lx, uy, ly
 
 
-def k_panel(grid, basis, _, panel, top, wide, sem):
-    w, d = grid.width, grid.depth
+def k_order(grid, basis, zm, panel, faces, wide):
+    n, d, w, layers = grid.rows, grid.depth, grid.width, grid.layers
     size = basis.shape[0]
-    copy = pltpu.make_async_copy(basis.at[:, pl.ds(grid.rows - w, w), :], top, sem)
-    copy.start()
-    copy.wait()
 
     def unpack(a, _):
-        wide[pl.ds(a * w, w), :] = top[a].astype(F32)
+        wide[pl.ds(a * n, n), :] = basis[a].astype(F32)
         return 0
 
-    lax.fori_loop(0, size, unpack, 0, unroll=8)
-    for x in range(w):
-        panel[:, x * d : (x + 1) * d] = wide[pl.ds(x, size, stride=w), :].astype(BF16)
-
-
-def k_basis(
-    grid, basis, rhs_in, cond_ref, cap_ref,
-    zm, own, projected, face_last, face_first, face_y, rhs, zs, zr, w3, coef, packed_basis, sems,
-):
+    lax.fori_loop(0, size, unpack, 0, unroll=4)
+    for row in range(n):
+        packed = wide[pl.ds(row, size, stride=n), :].astype(BF16)
+        zm[:, row * d : (row + 1) * d] = packed
+        layer, x = divmod(row, w)
+        if layer == layers - 1:
+            panel[:, x * d : (x + 1) * d] = packed
+        if x == 0:
+            faces[:, layer * d : (layer + 1) * d] = packed
+        if x == w - 1:
+            faces[:, (layers + layer) * d : (layers + layer + 1) * d] = packed
+
+
+def k_basis(grid, zm, rhs, cond_ref, cap_ref, own, projected, face_y, zr, w3, coef):
     n, d, w = grid.rows, grid.depth, grid.width
-    size = basis.shape[0]
-    pieces = sems.shape[0] - 1
-    step = size // pieces
-    copies = [
-        pltpu.make_async_copy(
-            basis.at[pl.ds(i * step, step)], packed_basis.at[pl.ds(i * step, step)], sems.at[i]
-        )
-        for i in range(pieces)
-    ]
-    copies.append(pltpu.make_async_copy(rhs_in, rhs, sems.at[pieces]))
-    for copy in copies:
-        copy.start()
+    size = zm.shape[0]
     cond = cond_ref[0:n, :]
     zero_face = jnp.zeros((grid.layers, d), F32)
     zero = jnp.zeros((n, d), F32)
@@ -278,33 +268,18 @@
     for i, c in enumerate((uz, lz, ux, lx, uy, ly)):
         coef[i + 1] = c
 
-    def unpack(a, _):
-        zs[pl.ds(a * n, n), :] = packed_basis[a].astype(F32)
-        return 0
-
-    for i in range(pieces):
-        copies[i].wait()
-        lax.fori_loop(i * step, (i + 1) * step, unpack, 0, unroll=4)
-    copies[pieces].wait()
     parts = [None, None]
     lane = lax.broadcasted_iota(jnp.int32, (size, d), 1)
     sides = jnp.zeros((size, d), F32)
     for row in range(n):
-        z = zs[pl.ds(row, size, stride=n), :]
+        z = zm[:, row * d : (row + 1) * d].astype(F32)
         zr[row] = z
-        packed = z.astype(BF16)
-        zm[:, row * d : (row + 1) * d] = packed
-        layer, x = divmod(row, w)
-        if x == w - 1:
-            face_last[:, layer * d : (layer + 1) * d] = packed
-        if x == 0:
-            face_first[:, layer * d : (layer + 1) * d] = packed
         sides = jnp.where(lane == row, z[:, 0:1], sides)
         sides = jnp.where(lane == n + row, z[:, d - 1 : d], sides)
         term = z * rhs[row : row + 1, :]
         parts[row % 2] = term if parts[row % 2] is None else parts[row % 2] + term
     projected[...] = parts[0] + parts[1]
-    face_y[...] = sides.astype(BF16)
+    face_y[...] = sides
     total = None
     for start in range(0, n, 8):
         for row in range(start, start + 8):
@@ -335,10 +310,41 @@
 
 def k_setup(
     grid, pairs, cols, ids, cap, vent, cond, cond_low, cond_high, rec,
-    zm, own_inner, projected, coef, own, inverse, sent, pay, w3, v0,
+    zm, own_inner, projected, face_y, faces, *rest,
 ):
-    n, d, w = grid.rows, grid.depth, grid.width
+    held = rest[:-12]
+    coef, own, inverse, sent, pay, mine, wanted, vents, names, w3, v0, sems = rest[-12:]
+    n, d, w, layers = grid.rows, grid.depth, grid.width, grid.layers
     count = rec.shape[0]
+    panel = w * d
+    line = w + 2 * layers
+    sibling = lax.bitwise_xor(ids[pairs], 1)
+    names_lane = lax.broadcasted_iota(jnp.int32, (1, d), 1)
+    targets = []
+    for k in range(pairs):
+        theirs = jnp.where(names_lane == k, rec[sibling, line : line + 1, :], 0.0)
+        targets += [
+            (ids[k], mine.at[k]),
+            (jnp.sum(theirs).astype(jnp.int32), wanted.at[:, pl.ds(k * panel, panel)]),
+        ]
+    for i, (partner, target) in enumerate(targets):
+        index = lax.shift_right_logical(lax.bitwise_xor(partner, ids[pairs]), 1)
+        for j, source in enumerate(held):
+
+            @pl.when(index == j)
+            def _(source=source, target=target, i=i):
+                pltpu.make_async_copy(source, target, sems.at[i]).start()
+
+    half = layers * d
+    upward = lax.bitwise_and(ids[pairs], 1) == 0
+    wanted[:, pairs * panel :] = jnp.where(upward, faces[:, half:], faces[:, :half])
+    for k in range(pairs):
+        vents[k] = vent[...] * rec[ids[k], 0:w, :]
+    up, down = jnp.minimum(ids[pairs] + 1, count - 1), jnp.maximum(ids[pairs] - 1, 0)
+    lines = [rec[r, line : line + 1, :] for r in (up, down)]
+    lines += [cond_high[n : n + 1, :], cond_low[n : n + 1, :]]
+    lines += [rec[ids[k], line : line + 1, :] for k in range(pairs)]
+    names[...] = jnp.concatenate(lines, axis=0)
     vent_sum, low_x, high_x = received(grid, ids, pairs, rec)
     row_at, col_at = ids[pairs], ids[pairs + 1]
     low_x = jnp.where(row_at > 0, low_x, 0.0)
@@ -368,8 +374,11 @@
     half = zm.shape[0] // 2
     folded = jnp.concatenate([inverse[0:half, :], inverse[half:, :]], axis=1)
     sent[0:n, :] = field
-    sent[n:, :] = folded
+    sent[n : n + half, :] = folded
+    sent[n + half :, :] = face_y[...]
     to_all(grid, pay, vent[...] * field[-w:], field, folded)
+    for i, (_, target) in enumerate(targets):
+        pltpu.make_async_copy(held[0], target, sems.at[i]).wait()
 
 
 def incoming(grid, pairs, ids, rec, low, high):
@@ -378,50 +387,53 @@
     return coupled, low_x, high_x, low[0:n, :], high[0:n, :]
 
 
-def k_coarse(grid, pairs, base, ids, coef, vent, zm, inverse, field, rec, low, high, *outs):
-    if base:
-        base_ref, out, pay, scratch = outs
-    else:
-        out, pay, scratch = outs
+def k_coarse(
+    grid, pairs, ids, coef, vent, zm, inverse, field, rec, low, high, out, pay, solves, y_faces, scratch
+):
+    n, w = grid.rows, grid.width
     beside = operate(grid, coef, vent[...], None, incoming(grid, pairs, ids, rec, low, high))
     expand(grid, zm, solve_own(inverse, project(grid, zm, beside)), scratch)
-    result = field[0 : grid.rows, :] - scratch[...]
-    if base:
-        result = base_ref[...] - result
+    result = field[0:n, :] - scratch[...]
     out[...] = result
-    to_all(grid, pay, vent[...] * result[-grid.width :], result)
-
-
-def k_apply(grid, pairs, base, ids, coef, vent, field, rec, low, high, *outs):
-    image = operate(grid, coef, vent[...], field[...], incoming(grid, pairs, ids, rec, low, high))
-    if base:
-        base_ref, out, pay = outs
-        image = base_ref[...] - image
-    else:
-        out, pay = outs
-    out[...] = image
-    to_all(grid, pay, vent[...] * image[-grid.width :], image)
+    to_all(grid, pay, vent[...] * result[-w:], result)
+    half = solves.shape[1]
+    first = w + 2 * grid.layers
+    row_at = ids[pairs]
+    solves[0] = rec[jnp.minimum(row_at + 1, rec.shape[0] - 1), first : first + half, :]
+    solves[1] = rec[jnp.maximum(row_at - 1, 0), first : first + half, :]
+    solves[2] = high[n : n + half, :]
+    solves[3] = low[n : n + half, :]
+    for k in range(pairs):
+        solves[4 + k] = rec[ids[k], first : first + half, :]
+    y_faces[0] = high[n + half :, :]
+    y_faces[1] = low[n + half :, :]
+
+
+def chosen(grid, pairs, ids, mine, others, k, at):
+    panel = grid.width * grid.depth
+    same = lax.bitwise_and(lax.bitwise_xor(ids[k], ids[pairs]), 1) == 0
+    there = slice(k * panel + at.start, k * panel + at.stop)
+    return jnp.where(same, mine[k, :, at].astype(F32), others[:, there].astype(F32))
+
+
+def x_faces(grid, pairs, ids, others, far):
+    half = grid.layers * grid.depth
+    near = others[:, pairs * grid.width * grid.depth :].astype(F32)
+    upward = lax.bitwise_and(ids[pairs], 1) == 0
+    return (
+        jnp.where(upward, near, far[:, :half].astype(F32)),
+        jnp.where(upward, far[:, half:].astype(F32), near),
+    )
 
 
 def k_partials(
-    grid, pairs, base, pick, ids, coef, vent, field, rec, low, high, rec0, zm,
-    next_first, prev_last, y_low, y_high, panels, *rest,
+    grid, pairs, base, ids, coef, vent, field, rec, low, high, vents, zm,
+    far, y_faces, mine, others, *rest,
 ):
-    rest = list(rest)
-    base_ref = rest.pop(0) if base else None
-    out, pay = rest[:2]
+    base_ref = rest[0] if base else None
+    out, pay = rest[-2:]
     n, d, w, layers = grid.rows, grid.depth, grid.width, grid.layers
     size = zm.shape[0]
-    if pick:
-        chosen, sems = rest[2:]
-        copies = [
-            pltpu.make_async_copy(panels.at[ids[k]], chosen.at[k], sems.at[k])
-            for k in range(pairs)
-        ]
-        for copy in copies:
-            copy.start()
-    else:
-        chosen = panels
     v = operate(grid, coef, vent[...], field[...], incoming(grid, pairs, ids, rec, low, high))
     if base:
         v = base_ref[...] - v
@@ -438,6 +450,7 @@
 
     even = along(zm, [own[i : i + 1] for i in range(n)])
     ux, lx, uy, ly = [coef[i] * v for i in (3, 4, 5, 6)]
+    next_first, prev_last = x_faces(grid, pairs, ids, others, far)
     sums = [
         even,
         -along(next_first, [ux[z * w + w - 1 : z * w + w] for z in range(layers)]),
@@ -447,15 +460,17 @@
     lane = lax.broadcasted_iota(jnp.int32, (n, d), 1)
     up = jnp.sum(jnp.where(lane == row, uy[:, d - 1 : d], 0.0), axis=0, keepdims=True)
     down = jnp.sum(jnp.where(lane == n + row, ly[:, 0:1], 0.0), axis=0, keepdims=True)
-    sums.append(-(y_high[...].astype(F32) * up))
-    sums.append(-(y_low[...].astype(F32) * down))
-    if pick:
-        for copy in copies:
-            copy.wait()
-    top = vent[...] * v[-w:]
+    sums.append(-(y_faces[0] * up))
+    sums.append(-(y_faces[1] * down))
+    top = v[-w:]
     for k in range(pairs):
-        weight = rec0[ids[k], 0:w, :] * top
-        sums.append(-along(chosen.at[k], [weight[i : i + 1] for i in range(w)]))
+        weight = vents[k] * top
+        total = None
+        for x in range(w):
+            at = slice(x * d, (x + 1) * d)
+            term = chosen(grid, pairs, ids, mine, others, k, at) * weight[x : x + 1]
+            total = term if total is None else total + term
+        sums.append(-total)
     ones = jnp.ones((8, d), F32)
     rows = [
         lax.dot_general(
@@ -464,8 +479,11 @@
         )[0:1]
         for q in sums
     ]
-    block = jnp.concatenate(rows + [jnp.zeros((8 - len(rows), size), F32)], axis=0)
-    block = jnp.concatenate([block, jnp.zeros((8, d - size), F32)], axis=1)
+    if len(rows) % 2:
+        rows.append(jnp.zeros((1, size), F32))
+    block = jnp.concatenate(
+        [jnp.concatenate(rows[i : i + 2], axis=1) for i in range(0, len(rows), 2)], axis=0
+    )
     for slot in range(pay.shape[0]):
         pay[slot] = block
 
@@ -475,14 +493,14 @@
     count = weights.shape[0]
     total = None
     for j in range(count):
-        g = None
+        sides = [None, None]
         for i in range(count):
             at = table[j * count + i]
-            back = opposite(i)
-            term = rec[jnp.maximum(at, 0), back : back + 1, :]
+            line, side = divmod(opposite(i), 2)
+            term = rec[jnp.maximum(at, 0), line : line + 1, :]
             term = jnp.where(at >= 0, term, 0.0)
-            g = term if g is None else g + term
-        term = weights[j] * g[:, 0:size]
+            sides[side] = term if sides[side] is None else sides[side] + term
+        term = weights[j] * (sides[0][:, 0:size] + sides[1][:, size : 2 * size])
         total = term if total is None else total + term
     expand(grid, zm, jnp.sum(total, axis=1, keepdims=True), scratch)
     result = base[...] - scratch[...]
@@ -495,9 +513,11 @@
     out[...] = image
     d, r, p, i = field[...], r0[...], p0[...], i0[...]
     products = (r * r, p * i, r * i, i * i, d * i, d * image)
-    parts = [jnp.sum(q, axis=0, keepdims=True) for q in products]
-    parts.append(jnp.zeros((8 - len(parts), grid.depth), F32))
-    block = jnp.concatenate(parts, axis=0)
+    lane = lax.broadcasted_iota(jnp.int32, pay.shape[1:], 1)
+    block = jnp.zeros(pay.shape[1:], F32)
+    for k, q in enumerate(products):
+        total = jnp.sum(jnp.sum(q, axis=0, keepdims=True), axis=1, keepdims=True)
+        block = jnp.where(lane == k, total, block)
     for slot in range(pay.shape[0]):
         pay[slot] = block
 
@@ -506,8 +526,7 @@
     total = rec[0]
     for slot in range(1, rec.shape[0]):
         total = total + rec[slot]
-    sums = jnp.sum(total, axis=1, keepdims=True)
-    rr, pi, ri, ii, di, dd = [sums[k : k + 1, :] for k in range(6)]
+    rr, pi, ri, ii, di, dd = [total[0:1, k : k + 1] for k in range(6)]
     a1 = rr / pi
     new = rr - 2.0 * a1 * ri + a1 * a1 * ii
     grow = 1.0 + new / rr
@@ -517,50 +536,38 @@
 
 
 def k_blocks(
-    grid, pairs, rows, cols, scale, ids, vent, coef, rec0, cond_low, cond_high, rec, low, high,
-    panel, chosen, own, inverse, face_last, face_first, next_first, prev_last,
-    face_y, y_low, y_high, _, out, weights, table, w3,
+    grid, pairs, cols, scale, ids, coef, vents, names, zm, mine, others, own, inverse, far,
+    face_y, y_faces, solves, _, out, weights, table, w3,
 ):
     n, d, w, layers = grid.rows, grid.depth, grid.width, grid.layers
-    size = out.shape[1]
-    row_at, col_at = ids[pairs], ids[pairs + 1]
+    rows, size = out.shape[0], out.shape[1]
+    row_at = ids[pairs]
     up, down = jnp.minimum(row_at + 1, rows - 1), jnp.maximum(row_at - 1, 0)
 
+    col_at = ids[pairs + 1]
     lane = lax.broadcasted_iota(jnp.int32, (1, d), 1)
-
-    def names(line):
-        return [
-            jnp.sum(jnp.where(lane == k, line, 0.0)).astype(jnp.int32) for k in range(pairs)
-        ]
-
-    line = w + 2 * layers
-
-    def at_row(r):
-        return names(rec0[r, line : line + 1, :])
-
-    near = [
-        (row_at, col_at, [ids[k] for k in range(pairs)]),
-        (row_at + 1, col_at, at_row(up)),
-        (row_at - 1, col_at, at_row(down)),
-        (row_at, col_at + 1, names(cond_high[n : n + 1, :])),
-        (row_at, col_at - 1, names(cond_low[n : n + 1, :])),
-    ]
-    near += [(ids[k], col_at, at_row(ids[k])) for k in range(pairs)]
+    near = [(row_at, col_at), (row_at + 1, col_at), (row_at - 1, col_at)]
+    near += [(row_at, col_at + 1), (row_at, col_at - 1)]
+    near += [(ids[k], col_at) for k in range(pairs)]
     count = len(near)
-    for j, (r, c, others) in enumerate(near):
+    for j, (r, c) in enumerate(near):
         places = [(r, c), (r + 1, c), (r - 1, c), (r, c + 1), (r, c - 1)]
-        places += [(q, c) for q in others]
+        for k in range(pairs):
+            met = ids[k]
+            if j > 0:
+                met = jnp.sum(jnp.where(lane == k, names[j - 1 : j, :], 0.0)).astype(jnp.int32)
+            places.append((met, c))
         there = (r >= 0) & (r < rows) & (c >= 0) & (c < cols)
         for i, (pr, pc) in enumerate(places):
             good = there & (pr >= 0) & (pr < rows) & (pc >= 0) & (pc < cols)
             table[j * count + i] = jnp.where(good, pr * cols + pc, -1)
 
-    def weighted(src, row_weights, other):
+    def weighted(parts, row_weights, other):
         m = len(row_weights)
         k = other.shape[1] // m
-        for i, weight in enumerate(row_weights):
+        for i, (part, weight) in enumerate(zip(parts, row_weights)):
             at = slice(i * k, (i + 1) * k)
-            hi, mid, lo = split3(src[:, at].astype(F32) * weight)
+            hi, mid, lo = split3(part.astype(F32) * weight)
             w3[0:size, at] = hi
             w3[size : 2 * size, at] = mid
             w3[2 * size : 3 * size, at] = lo
@@ -573,24 +580,28 @@
         )
 
     ux, lx, uy, ly = coef[3], coef[4], coef[5], coef[6]
+    last = [z * w + w - 1 for z in range(layers)]
+    first = [z * w for z in range(layers)]
+
+    def basis_rows(at):
+        return [zm[:, i * d : (i + 1) * d] for i in at]
+
+    next_first, prev_last = x_faces(grid, pairs, ids, others, far)
     found = [
-        weighted(
-            face_last, [ux[z * w + w - 1 : z * w + w] for z in range(layers)], next_first[...]
-        ),
-        weighted(face_first, [lx[z * w : z * w + 1] for z in range(layers)], prev_last[...]),
+        weighted(basis_rows(last), [ux[i : i + 1] for i in last], next_first.astype(BF16)),
+        weighted(basis_rows(first), [lx[i : i + 1] for i in first], prev_last.astype(BF16)),
     ]
     row = lax.broadcasted_iota(jnp.int32, (n, d), 0)
     wide = lax.broadcasted_iota(jnp.int32, (n, d), 1)
     high_weight = jnp.sum(jnp.where(wide == row, uy[:, d - 1 : d], 0.0), axis=0, keepdims=True)
     low_weight = jnp.sum(jnp.where(wide == n + row, ly[:, 0:1], 0.0), axis=0, keepdims=True)
-    sides = face_y[...].astype(F32)
-    swapped = pltpu.roll(sides, n, 1)
-    found.append(weighted(swapped, [high_weight], y_high[...]))
-    found.append(weighted(swapped, [low_weight], y_low[...]))
-    top = vent[...]
+    swapped = pltpu.roll(face_y[...], n, 1)
+    found.append(weighted([swapped], [high_weight], y_faces[0].astype(BF16)))
+    found.append(weighted([swapped], [low_weight], y_faces[1].astype(BF16)))
+    top = basis_rows(range(n - w, n))
     for k in range(pairs):
-        weight = top * rec0[ids[k], 0:w, :]
-        found.append(weighted(panel, [weight[i : i + 1] for i in range(w)], chosen[k]))
+        panel = chosen(grid, pairs, ids, mine, others, k, slice(0, w * d)).astype(BF16)
+        found.append(weighted(top, [vents[k, i : i + 1, :] for i in range(w)], panel))
 
     for slot in range(rows):
         out[slot] = jnp.zeros((size, size), F32)
@@ -600,27 +611,15 @@
     for k in range(pairs):
         out[ids[k]] = out[ids[k]] + found[4 + k] * scale
 
-    half = size // 2
-    first = w + 2 * layers
-
-    def unfold(folded):
-        return jnp.concatenate([folded[:, 0:size], folded[:, size:]], axis=0)
-
-    theirs = [
-        unfold(rec[up, first : first + half, :]),
-        unfold(rec[down, first : first + half, :]),
-        unfold(high[n : n + half, :]),
-        unfold(low[n : n + half, :]),
-    ]
-    theirs += [unfold(rec[ids[k], first : first + half, :]) for k in range(pairs)]
     weights[0] = inverse[...]
-    for j, (block, solve) in enumerate(zip(found, theirs)):
-        weights[j + 1] = -dot(inverse[...], dot(block, solve))
-
-
-def call(kernel, outs, operands, scratch=(), smem=0, hbm=(), smem_outs=(), cost=None):
+    for j, block in enumerate(found):
+        theirs = jnp.concatenate([solves[j, :, 0:size], solves[j, :, size:]], axis=0)
+        weights[j + 1] = -dot(inverse[...], dot(block, theirs))
+
+
+def call(kernel, outs, operands, scratch=(), smem=0, free=(), smem_outs=(), cost=None):
     specs = [
-        SMEM if i < smem else HBM if i in hbm else VMEM for i in range(len(operands))
+        SMEM if i < smem else ANY if i in free else VMEM for i in range(len(operands))
     ]
     return pl.pallas_call(
         kernel,
@@ -657,6 +656,10 @@
         count = lax.axis_size(axis)
         return lax.ppermute(value, axis, [(i, (i + step) % count) for i in range(count)])
 
+    def xor_step(value, axis, k):
+        count = lax.axis_size(axis)
+        return lax.ppermute(value, axis, [(i, i ^ k) for i in range(count)])
+
     def exchange(value, payload):
         low = cyclic(value, "col", 1)
         high = cyclic(value, "col", -1)
@@ -666,6 +669,22 @@
     def rows_of(count):
         return ((row_count, width + 2 * layers + count, depth), F32)
 
+    zm, panel, faces = call(
+        functools.partial(k_order, grid),
+        (
+            ((size, n * depth), BF16),
+            ((size, width * depth), BF16),
+            ((size, 2 * layers * depth), BF16),
+        ),
+        (basis,),
+        scratch=(pltpu.VMEM((size * n, depth), F32),),
+    )
+    held = [panel] + [xor_step(panel, "row", k) for k in range(2, row_count, 2)]
+    far = lax.ppermute(
+        faces,
+        "row",
+        [(i, (i + 1 if i % 2 else i - 1) % row_count) for i in range(row_count)],
+    )
     cond, cap, vent, pay0 = call(
         functools.partial(k_first, grid),
         (((n + 8, depth), F32), field, ((width, depth), F32), rows_of(8)),
@@ -677,99 +696,86 @@
             pltpu.SMEM((pairs,), jnp.int32),
             pltpu.SemaphoreType.DMA((5,)),
         ),
-        hbm=(0, 1, 2, 3, 4),
+        free=(0, 1, 2, 3, 4),
     )
     rec0, cond_low, cond_high = exchange(cond, pay0)
-    (panel,) = call(
-        functools.partial(k_panel, grid),
-        (((size, width * depth), BF16),),
-        (basis, cond),
+
+    own_inner, projected, face_y = call(
+        functools.partial(k_basis, grid),
+        (small, ((size, depth), F32), ((size, depth), F32)),
+        (zm, rhs, cond, cap),
         scratch=(
-            pltpu.VMEM((size, width, depth), BF16),
-            pltpu.VMEM((size * width, depth), F32),
-            pltpu.SemaphoreType.DMA,
-        ),
-        hbm=(0, 1),
-    )
-    panels = lax.all_gather(panel, "row", axis=0)
-
-    zm, own_inner, projected, face_last, face_first, face_y, rhs = call(
-        functools.partial(k_basis, grid),
-        (
-            ((size, n * depth), BF16),
-            small,
-            ((size, depth), F32),
-            ((size, layers * depth), BF16),
-            ((size, layers * depth), BF16),
-            ((size, depth), BF16),
-            field,
-        ),
-        (basis, rhs, cond, cap),
-        scratch=(
-            pltpu.VMEM((size * n, depth), F32),
             pltpu.VMEM((n, size, depth), F32),
             pltpu.VMEM((3 * size, n * depth), BF16),
             pltpu.VMEM((7, n, depth), F32),
-            pltpu.VMEM((size, n, depth), BF16),
-            pltpu.SemaphoreType.DMA((5,)),
-        ),
-        hbm=(0, 1),
+        ),
         cost=pl.CostEstimate(flops=200_000_000, bytes_accessed=8_000_000, transcendentals=0),
     )
 
-    coef, own, inverse, sent, pay1 = call(
+    panels = ((pairs, size, width * depth), BF16)
+    coef, own, inverse, sent, pay1, mine, wanted, vents, names = call(
         functools.partial(k_setup, grid, pairs, col_count),
-        (((7, n, depth), F32), small, small, ((n + size // 2, depth), F32), rows_of(size // 2)),
-        (ids, cap, vent, cond, cond_low, cond_high, rec0, zm, own_inner, projected),
+        (
+            ((7, n, depth), F32),
+            small,
+            small,
+            ((n + size // 2 + size, depth), F32),
+            rows_of(size // 2),
+            panels,
+            ((size, (pairs * width + layers) * depth), BF16),
+            ((pairs, width, depth), F32),
+            ((4 + pairs, depth), F32),
+        ),
+        (
+            ids, cap, vent, cond, cond_low, cond_high, rec0, zm, own_inner, projected, face_y,
+            faces, *held,
+        ),
         scratch=(
             pltpu.VMEM((3 * size, n * depth), BF16),
             pltpu.VMEM((n, depth), F32),
+            pltpu.SemaphoreType.DMA((2 * pairs,)),
         ),
         smem=1,
-    )
+        free=range(12, 12 + len(held)),
+    )
+    others = xor_step(wanted, "row", 1)
     rec1, low1, high1 = exchange(sent, pay1)
-    face_last_, face_first_, face_y_, _ = lax.optimization_barrier(
-        (face_last, face_first, face_y, pay1)
-    )
-    prev_last = cyclic(face_last_, "row", 1)
-    next_first = cyclic(face_first_, "row", -1)
-    y_low = cyclic(face_y_, "col", 1)
-    y_high = cyclic(face_y_, "col", -1)
-    x0, pay2 = call(
-        functools.partial(k_coarse, grid, pairs, False),
-        (field, pay),
+    places = 5 + pairs
+    x0, pay2, solves, y_faces = call(
+        functools.partial(k_coarse, grid, pairs),
+        (field, pay, ((4 + pairs, size // 2, depth), F32), ((2, size, depth), F32)),
         (ids, coef, vent, zm, inverse, sent, rec1, low1, high1),
         scratch=(pltpu.VMEM((n, depth), F32),),
         smem=1,
     )
     rec, low, high = exchange(x0, pay2)
-    everyone = ((row_count * col_count, 8, depth), F32)
-    r0, pay3, chosen = call(
-        functools.partial(k_partials, grid, pairs, True, True),
-        (field, everyone, ((pairs, size, width * depth), BF16)),
+
+    def everyone(lines):
+        return ((row_count * col_count, lines, depth), F32)
+
+    r0, pay3 = call(
+        functools.partial(k_partials, grid, pairs, True),
+        (field, everyone((places + 1) // 2)),
         (
-            ids, coef, vent, x0, rec, low, high, rec0, zm, next_first, prev_last, y_low, y_high,
-            panels, rhs,
-        ),
-        scratch=(pltpu.SemaphoreType.DMA((pairs,)),),
+            ids, coef, vent, x0, rec, low, high, vents, zm, far, y_faces,
+            mine, others, rhs,
+        ),
         smem=1,
-        hbm=(13,),
-    )
-    places = 5 + pairs
+    )
     blocks, weights, table = call(
-        functools.partial(k_blocks, grid, pairs, row_count, col_count, 1.0 / cells),
+        functools.partial(k_blocks, grid, pairs, col_count, 1.0 / cells),
         (
             ((row_count, size, size), F32),
             ((places, size, size), F32),
             ((places * places,), jnp.int32),
         ),
         (
-            ids, vent, coef, rec0, cond_low, cond_high, rec1, low1, high1, panel, chosen, own,
-            inverse, face_last, face_first, next_first, prev_last, face_y, y_low, y_high, pay3,
+            ids, coef, vents, names, zm, mine, others, own, inverse, far, face_y, y_faces,
+            solves, pay3,
         ),
         scratch=(pltpu.VMEM((3 * size, width * depth), BF16),),
         smem=1,
-        hbm=(20,),
+        free=(13,),
         smem_outs=(2,),
         cost=pl.CostEstimate(flops=100_000_000, bytes_accessed=4_000_000, transcendentals=0),
     )
@@ -783,11 +789,11 @@
     )
     rec, low, high = exchange(p0, pay4)
     i0, pay5 = call(
-        functools.partial(k_partials, grid, pairs, False, False),
-        (field, everyone),
+        functools.partial(k_partials, grid, pairs, False),
+        (field, everyone((places + 1) // 2)),
         (
-            ids, coef, vent, p0, rec, low, high, rec0, zm, next_first, prev_last, y_low, y_high,
-            chosen,
+            ids, coef, vent, p0, rec, low, high, vents, zm, far, y_faces,
+            mine, others,
         ),
         smem=1,
     )
@@ -802,7 +808,7 @@
     rec, low, high = exchange(d0, pay6)
     image, pay7 = call(
         functools.partial(k_dots, grid, pairs),
-        (field, everyone),
+        (field, everyone(2)),
         (ids, coef, vent, d0, rec, low, high, r0, p0, i0),
         smem=1,
     )

time: 139 us -> 122 us (0.88)
  between operations: 14.2 us -> 0.82 us
  waiting for transfers between devices: 27.5 us -> 16.6 us
  starting transfers between devices: 41.5 us -> 47 us
  blocking collectives: 22.8 us -> 27.1 us
    ppermute x14 -> x10, waiting for transfers between devices: 21.1 us -> 10.9 us  [cyclic(): lax.ppermute(value, axis, [(i, (i + step) % count) for i in range(count)])]
    ppermute x0 -> x5, starting transfers between devices: none -> 6.61 us  [the longest x4 4.61 us: xor_step(): return lax.ppermute(value, axis, [(i, i ^ k) for i in range(count)])]
    all_to_all x1, blocking collectives: 11.4 us -> 13.6 us  [body(): sums = lax.all_to_all(pay5, ('row', 'col'), 0, 0)]
    all_to_all x1, blocking collectives: 11.4 us -> 13.4 us  [body(): total = lax.all_to_all(pay7, ('row', 'col'), 0, 0)]
    ppermute x14 -> x10, starting transfers between devices: 20.7 us -> 18.7 us  [cyclic(): lax.ppermute(value, axis, [(i, (i + step) % count) for i in range(count)])]
    unnamed x18 -> x26, local copies, waits for them, and re-layouts: 6.98 us -> 5.97 us
  transfers between devices with their start and end apart: 21 -> 21, of which waited for: 9 -> 7; matrix products, arithmetic and copies ran while one was open for 0% -> 0% of each run, Pallas kernels for 10% -> 7%
where the time goes in v3:
time: 122 us; the launch traced here: 121 us
  starting transfers between devices  47 us (39%)
  blocking collectives  27.1 us (22%)
  Pallas kernels  23.9 us (20%)
  waiting for transfers between devices  16.6 us (14%)
  local copies, waits for them, and re-layouts  5.97 us (5%)
    pallas_call x12, Pallas kernels, call(): pl.pallas_call(kernel, out_shape=tuple((jax.ShapeDtypeStruct(s, t) for s,...  23.9 us
    ppermute x10, starting transfers between devices, cyclic(): lax.ppermute(value, axis, [(i, (i + step) % count) for i in range(count)])  18.7 us
    all_to_all x5, starting transfers between devices, exchange(): rec = lax.all_to_all(payload, 'row', 0, 0)  18.2 us
    all_to_all x1, blocking collectives, body(): sums = lax.all_to_all(pay5, ('row', 'col'), 0, 0)  13.6 us
    all_to_all x1, blocking collectives, body(): total = lax.all_to_all(pay7, ('row', 'col'), 0, 0)  13.4 us
    ppermute x10, waiting for transfers between devices, cyclic(): lax.ppermute(value, axis, [(i, (i + step) % count) for i in range(count)])  10.9 us
    unnamed x26, local copies, waits for them, and re-layouts  5.97 us
    ppermute x4, starting transfers between devices, xor_step(): return lax.ppermute(value, axis, [(i, i ^ k) for i in range(count)])  4.61 us
  transfers between devices with their start and end apart: 21, of which 7 were waited for; matrix products, arithmetic and copies ran while one was open for 0% of the time, Pallas kernels for 7%

profile of v3, /device:TPU:0, one launch (start us, length us, event | category | flops | bytes accessed | tf_op | source)
XLA Modules:
  0.0 121.5 jit_solution(1118058562948550039)
XLA Ops:
  3.3 3.0 %collective-permute-start.2 = (bf16[64,2048]{1,0:T(8,128)(2,1)S(1)}, bf16[64,2048]{1,0:T(8,128)(2,1)S(1)}, u32[]{:S(2)}, u32[]{:S(2)}) collective-permute-start(bf16[64,2048]{1,0:T(8,128)(2,1)S(1)} %get-tuple-element.50.rest_0_), channel_id=1, source_target_pairs={{0,8},{4,12},{8,0},{12,4},{16,24},{20,28},{24,16},{28,20},{1,9},{5... | collective-permute-start | bytes 786440 | tf_op jit(solution)/shard_map/ppermute | solution.py:661
  9.9 2.1 %collective-permute-start = (f32[72,128]{1,0:T(8,128)S(1)}, f32[72,128]{1,0:T(8,128)S(1)}, u32[]{:S(2)}, u32[]{:S(2)}) collective-permute-start(f32[72,128]{1,0:T(8,128)S(1)} %get-tuple-element.43.cond_ref.cond), channel_id=1, source_target_pairs={{0,1},{1,2},{2,3},{3,0},{4,5},{5,6},{6,7},{7,4},{8,9},{9,10},{10,1... | collective-permute-start | bytes 110600 | tf_op jit(solution)/shard_map/ppermute | solution.py:657
  12.0 2.1 %collective-permute-start.1 = (f32[72,128]{1,0:T(8,128)S(1)}, f32[72,128]{1,0:T(8,128)S(1)}, u32[]{:S(2)}, u32[]{:S(2)}) collective-permute-start(f32[72,128]{1,0:T(8,128)S(1)} %get-tuple-element.43.cond_ref.cond), channel_id=1, source_target_pairs={{0,3},{1,0},{2,1},{3,2},{4,7},{5,4},{6,5},{7,6},{8,11},{9,8},{10,9... | collective-permute-start | bytes 110600 | tf_op jit(solution)/shard_map/ppermute | solution.py:657
  14.1 4.0 %all-to-all-start = ((f32[8,32,128]{2,1,0:T(8,128)}), f32[8,32,128]{2,1,0:T(8,128)S(1)}, u32[]{:S(2)}, u32[]{:S(2)}) async-start(f32[8,32,128]{2,1,0:T(8,128)} %get-tuple-element.44), calls=%async_computation | async-start | bytes 262144 | tf_op jit(solution)/shard_map/all_to_all | solution.py:666
  18.1 2.8 %shard_map.96 = (f32[64,64]{1,0:T(8,128)S(1)}, f32[64,128]{1,0:T(8,128)S(1)}, f32[64,128]{1,0:T(8,128)S(1)}) custom-call(bf16[64,8192]{1,0:T(8,128)(2,1)S(1)} %get-tuple-element.45.zm, f32[64,128]{1,0:T(8,128)S(1)} %bitcast.10, f32[72,128]{1,0:T(8,128)S(1)} %get-tuple-element.43.cond_ref.cond, f32[64,128]{1,0:T(8,128)S(1)} %get-tuple-element.41.cap_ref.cap), custom_call_target="tpu_custom_call" | custom-call | flops 200000000 | bytes 8000000 | tf_op jit(solution)/shard_map/pallas_call | solution.py:624
  21.6 2.0 %all-to-all-done.rec = f32[8,32,128]{2,1,0:T(8,128)S(1)} async-done(((f32[8,32,128]{2,1,0:T(8,128)}), f32[8,32,128]{2,1,0:T(8,128)S(1)}, u32[]{:S(2)}, u32[]{:S(2)}) %all-to-all-start) | async-done | bytes 131104 | tf_op jit(solution)/shard_map/all_to_all | solution.py:666
  24.4 5.0 %shard_map.97 = (f32[7,64,128]{2,1,0:T(8,128)S(1)}, f32[64,64]{1,0:T(8,128)S(1)}, f32[64,64]{1,0:T(8,128)S(1)}, f32[160,128]{1,0:T(8,128)S(1)}, f32[8,56,128]{2,...) custom-call(s32[4]{0:T(128)S(1)} %pad_add_fusion.ids, ...), custom_call_target="tpu_custom_call" | custom-call | tf_op jit(solution)/shard_map/pallas_call | solution.py:624
  30.0 3.4 %all-to-all-start.1 = ((f32[8,56,128]{2,1,0:T(8,128)}), f32[8,56,128]{2,1,0:T(8,128)S(1)}, u32[]{:S(2)}, u32[]{:S(2)}) async-start(f32[8,56,128]{2,1,0:T(8,128)} %get-tuple-element.59), calls=%async_computation.1 | async-start | bytes 458752 | tf_op jit(solution)/shard_map/all_to_all | solution.py:666
  33.5 3.8 %collective-permute-start.8 = (f32[160,128]{1,0:T(8,128)S(1)}, f32[160,128]{1,0:T(8,128)S(1)}, u32[]{:S(2)}, u32[]{:S(2)}) collective-permute-start(f32[160,128]{1,0:T(8,128)S(1)} %get-tuple-element.58.field), channel_id=1, source_target_pairs={{0,3},{1,0},{2,1},{3,2},{4,7},{5,4},{6,5},{7,6},{8,11},{9,8},{10,9... | collective-permute-start | bytes 245768 | tf_op jit(solution)/shard_map/ppermute | solution.py:657
  37.3 2.0 %collective-permute-start.6 = (bf16[64,1024]{1,0:T(8,128)(2,1)S(1)}, bf16[64,1024]{1,0:T(8,128)(2,1)S(1)}, u32[]{:S(2)}, u32[]{:S(2)}) collective-permute-start(bf16[64,1024]{1,0:T(8,128)(2,1)S(1)} %get-tuple-element.49.faces), channel_id=1, source_target_pairs={{0,28},{4,8},{8,4},{12,16},{16,12},{20,24},{24,20},{28,0},{1,29},{... | collective-permute-start | bytes 393224 | tf_op jit(solution)/shard_map/ppermute | solution.py:683
  44.0 4.1 %all-to-all-start.2 = ((f32[8,24,128]{2,1,0:T(8,128)}), f32[8,24,128]{2,1,0:T(8,128)S(1)}, u32[]{:S(2)}, u32[]{:S(2)}) async-start(f32[8,24,128]{2,1,0:T(8,128)} %get-tuple-element.63), calls=%async_computation.2 | async-start | bytes 196608 | tf_op jit(solution)/shard_map/all_to_all | solution.py:666
  48.1 2.9 %collective-permute-start.10 = (f32[64,128]{1,0:T(8,128)S(1)}, f32[64,128]{1,0:T(8,128)S(1)}, u32[]{:S(2)}, u32[]{:S(2)}) collective-permute-start(f32[64,128]{1,0:T(8,128)S(1)} %get-tuple-element.62.field.x0), channel_id=1, source_target_pairs={{0,3},{1,0},{2,1},{3,2},{4,7},{5,4},{6,5},{7,6},{8,11},{9,8},{10,9... | collective-permute-start | bytes 98312 | tf_op jit(solution)/shard_map/ppermute | solution.py:657
  52.7 4.0 %collective-permute-done.9.low = f32[64,128]{1,0:T(8,128)S(1)} collective-permute-done((f32[64,128]{1,0:T(8,128)S(1)}, f32[64,128]{1,0:T(8,128)S(1)}, u32[]{:S(2)}, u32[]{:S(2)}) %collective-permute-start.9) | collective-permute-done | bytes 32800 | tf_op jit(solution)/shard_map/ppermute | solution.py:657
  56.8 2.1 %shard_map.99 = (f32[64,128]{1,0:T(8,128)S(1)}, f32[32,4,128]{2,1,0:T(4,128)}) custom-call(s32[4]{0:T(128)S(1)} %pad_add_fusion.ids, f32[7,64,128]{2,1,0:T(8,128)S(1)} %get-tuple-element.51.coef, f32[16,128]{1,0:T(8,128)S(1)} %get-tuple-element.42.vent, f32[64,128]{1,0:T(8,128)S(1)} %get-tuple-element.62.field.x0, f32[8,24,128]{2,1,0:T(8,128)S(1)} %all-to-all-done.2.rec, ...), custom_call_target="tpu_custom_call" | custom-call | tf_op jit(solution)/shard_map/pallas_call | solution.py:624
  58.9 3.5 %all-to-all-start.3 = ((f32[32,4,128]{2,1,0:T(4,128)}), f32[32,4,128]{2,1,0:T(4,128)S(1)}, u32[]{:S(2)}, u32[]{:S(2)}) async-start(f32[32,4,128]{2,1,0:T(4,128)} %get-tuple-element.64._), calls=%async_computation.3 | async-start | bytes 131072 | tf_op jit(solution)/shard_map/all_to_all | solution.py:782
  63.0 3.0 %shard_map.100 = (f32[8,64,64]{2,1,0:T(8,128)}, f32[7,64,64]{2,1,0:T(8,128)S(1)}, s32[49]{0:T(128)S(1)}) custom-call(s32[4]{0:T(128)S(1)} %pad_add_fusion.ids, f32[7,64,128]{2,1,0:T(8,128)S(1)} %get-tuple-element.51.coef, f32[2,16,128]{2,1,0:T(8,128)S(1)} %get-tuple-element.52.vents, f32[6,128]{1,0:T(8,128)S(1)} %copy-done.9, ...), custom_call_target="tpu_custom_call" | custom-call | flops 100000000 | bytes 4000000 | tf_op jit(solution)/shard_map/pallas_call | solution.py:624
  66.1 3.6 %all-to-all-done.3.rec = f32[32,4,128]{2,1,0:T(4,128)S(1)} async-done(((f32[32,4,128]{2,1,0:T(4,128)}), f32[32,4,128]{2,1,0:T(4,128)S(1)}, u32[]{:S(2)}, u32[]{:S(2)}) %all-to-all-start.3) | async-done | bytes 65568 | tf_op jit(solution)/shard_map/all_to_all | solution.py:782
  71.3 3.4 %all-to-all-start.4 = ((f32[8,24,128]{2,1,0:T(8,128)}), f32[8,24,128]{2,1,0:T(8,128)S(1)}, u32[]{:S(2)}, u32[]{:S(2)}) async-start(f32[8,24,128]{2,1,0:T(8,128)} %get-tuple-element.69), calls=%async_computation.4 | async-start | bytes 196608 | tf_op jit(solution)/shard_map/all_to_all | solution.py:666
  74.9 3.6 %collective-permute-start.12 = (f32[64,128]{1,0:T(8,128)S(1)}, f32[64,128]{1,0:T(8,128)S(1)}, u32[]{:S(2)}, u32[]{:S(2)}) collective-permute-start(f32[64,128]{1,0:T(8,128)S(1)} %get-tuple-element.68.field.p0), channel_id=1, source_target_pairs={{0,3},{1,0},{2,1},{3,2},{4,7},{5,4},{6,5},{7,6},{8,11},{9,8},{10,9... | collective-permute-start | bytes 98312 | tf_op jit(solution)/shard_map/ppermute | solution.py:657
  78.5 2.0 %collective-permute-done.11.low = f32[64,128]{1,0:T(8,128)S(1)} collective-permute-done((f32[64,128]{1,0:T(8,128)S(1)}, f32[64,128]{1,0:T(8,128)S(1)}, u32[]{:S(2)}, u32[]{:S(2)}) %collective-permute-start.11) | collective-permute-done | bytes 32800 | tf_op jit(solution)/shard_map/ppermute | solution.py:657
  82.0 13.6 %all_to_all.40.rec = f32[32,4,128]{2,1,0:T(4,128)S(1)} all-to-all(f32[32,4,128]{2,1,0:T(4,128)S(1)} %get-tuple-element.70), channel_id=1, replica_groups=mesh['row'=8,'col'=4] {'row','col'}, dimensions={0} | all-to-all | bytes 131072 | tf_op jit(solution)/shard_map/all_to_all | solution.py:800
  97.3 3.4 %all-to-all-start.6 = ((f32[8,24,128]{2,1,0:T(8,128)}), f32[8,24,128]{2,1,0:T(8,128)S(1)}, u32[]{:S(2)}, u32[]{:S(2)}) async-start(f32[8,24,128]{2,1,0:T(8,128)} %get-tuple-element.73), calls=%async_computation.6 | async-start | bytes 196608 | tf_op jit(solution)/shard_map/all_to_all | solution.py:666
  100.9 3.6 %collective-permute-start.14 = (f32[64,128]{1,0:T(8,128)S(1)}, f32[64,128]{1,0:T(8,128)S(1)}, u32[]{:S(2)}, u32[]{:S(2)}) collective-permute-start(f32[64,128]{1,0:T(8,128)S(1)} %get-tuple-element.72.field.d), channel_id=1, source_target_pairs={{0,3},{1,0},{2,1},{3,2},{4,7},{5,4},{6,5},{7,6},{8,11},{9,8},{10,9... | collective-permute-start | bytes 98312 | tf_op jit(solution)/shard_map/ppermute | solution.py:657
  107.2 13.4 %all_to_all.41.rec = f32[32,2,128]{2,1,0:T(2,128)S(1)} all-to-all(f32[32,2,128]{2,1,0:T(2,128)S(1)} %get-tuple-element.74), channel_id=1, replica_groups=mesh['row'=8,'col'=4] {'row','col'}, dimensions={0} | all-to-all | bytes 65536 | tf_op jit(solution)/shard_map/all_to_all | solution.py:815
  (59 shorter events, 24.3 us)
Async XLA Ops:
  1.9 6.0 %copy-start.6 = (s32[4,16,128]{2,1,0:T(8,128)S(1)}, s32[4,16,128]{2,1,0:T(8,128)}, u32[]{:S(2)}) copy-start(s32[4,16,128]{2,1,0:T(8,128)} %param.8) | copy-start | bytes 98308
  1.9 6.0 %copy-start.7 = (f32[16,128]{1,0:T(8,128)S(1)}, f32[16,128]{1,0:T(8,128)}, u32[]{:S(2)}) copy-start(f32[16,128]{1,0:T(8,128)} %vent.1) | copy-start | bytes 24580
  3.3 20.3 %collective-permute-start.2 = (bf16[64,2048]{1,0:T(8,128)(2,1)S(1)}, bf16[64,2048]{1,0:T(8,128)(2,1)S(1)}, u32[]{:S(2)}, u32[]{:S(2)}) collective-permute-start(bf16[64,2048]{1,0:T(8,128)(2,1)S(1)} %get-tuple-element.50.rest_0_), channel_id=1, source_target_pairs={{0,8},{4,12},{8,0},{12,4},{16,24},{20,28},{24,16},{28,20},{1,9},{5... | collective-permute-start | bytes 786440 | tf_op jit(solution)/shard_map/ppermute | solution.py:661
  6.3 17.3 %collective-permute-start.3 = (bf16[64,2048]{1,0:T(8,128)(2,1)S(1)}, bf16[64,2048]{1,0:T(8,128)(2,1)S(1)}, u32[]{:S(2)}, u32[]{:S(2)}) collective-permute-start(bf16[64,2048]{1,0:T(8,128)(2,1)S(1)} %get-tuple-element.50.rest_0_), channel_id=1, source_target_pairs={{0,16},{4,20},{8,24},{12,28},{16,0},{20,4},{24,8},{28,12},{1,17},{... | collective-permute-start | bytes 786440 | tf_op jit(solution)/shard_map/ppermute | solution.py:661
  7.8 15.8 %collective-permute-start.4 = (bf16[64,2048]{1,0:T(8,128)(2,1)S(1)}, bf16[64,2048]{1,0:T(8,128)(2,1)S(1)}, u32[]{:S(2)}, u32[]{:S(2)}) collective-permute-start(bf16[64,2048]{1,0:T(8,128)(2,1)S(1)} %get-tuple-element.50.rest_0_), channel_id=1, source_target_pairs={{0,24},{4,28},{8,16},{12,20},{16,8},{20,12},{24,0},{28,4},{1,25},{... | collective-permute-start | bytes 786440 | tf_op jit(solution)/shard_map/ppermute | solution.py:661
  9.9 11.7 %collective-permute-start = (f32[72,128]{1,0:T(8,128)S(1)}, f32[72,128]{1,0:T(8,128)S(1)}, u32[]{:S(2)}, u32[]{:S(2)}) collective-permute-start(f32[72,128]{1,0:T(8,128)S(1)} %get-tuple-element.43.cond_ref.cond), channel_id=1, source_target_pairs={{0,1},{1,2},{2,3},{3,0},{4,5},{5,6},{6,7},{7,4},{8,9},{9,10},{10,1... | collective-permute-start | bytes 110600 | tf_op jit(solution)/shard_map/ppermute | solution.py:657
  12.0 9.6 %collective-permute-start.1 = (f32[72,128]{1,0:T(8,128)S(1)}, f32[72,128]{1,0:T(8,128)S(1)}, u32[]{:S(2)}, u32[]{:S(2)}) collective-permute-start(f32[72,128]{1,0:T(8,128)S(1)} %get-tuple-element.43.cond_ref.cond), channel_id=1, source_target_pairs={{0,3},{1,0},{2,1},{3,2},{4,7},{5,4},{6,5},{7,6},{8,11},{9,8},{10,9... | collective-permute-start | bytes 110600 | tf_op jit(solution)/shard_map/ppermute | solution.py:657
  14.1 4.1 %copy-start.1 = (f32[4,16,128]{2,1,0:T(8,128)S(1)}, f32[4,16,128]{2,1,0:T(8,128)}, u32[]{:S(2)}) copy-start(f32[4,16,128]{2,1,0:T(8,128)} %param.7) | copy-start | bytes 98308
  14.1 9.5 %all-to-all-start = ((f32[8,32,128]{2,1,0:T(8,128)}), f32[8,32,128]{2,1,0:T(8,128)S(1)}, u32[]{:S(2)}, u32[]{:S(2)}) async-start(f32[8,32,128]{2,1,0:T(8,128)} %get-tuple-element.44), calls=%async_computation | async-start | bytes 262144 | tf_op jit(solution)/shard_map/all_to_all | solution.py:666
  29.4 27.4 %collective-permute-start.5 = (bf16[64,4608]{1,0:T(8,128)(2,1)}, bf16[64,4608]{1,0:T(8,128)(2,1)S(1)}, u32[]{:S(2)}, u32[]{:S(2)}) collective-permute-start(bf16[64,4608]{1,0:T(8,128)(2,1)} %get-tuple-element.55), channel_id=1, source_target_pairs={{0,4},{4,0},{8,12},{12,8},{16,20},{20,16},{24,28},{28,24},{1,5},{5... | collective-permute-start | bytes 1769480 | tf_op jit(solution)/shard_map/ppermute | solution.py:661
  30.0 11.2 %all-to-all-start.1 = ((f32[8,56,128]{2,1,0:T(8,128)}), f32[8,56,128]{2,1,0:T(8,128)S(1)}, u32[]{:S(2)}, u32[]{:S(2)}) async-start(f32[8,56,128]{2,1,0:T(8,128)} %get-tuple-element.59), calls=%async_computation.1 | async-start | bytes 458752 | tf_op jit(solution)/shard_map/all_to_all | solution.py:666
  33.4 7.2 %collective-permute-start.7 = (f32[160,128]{1,0:T(8,128)S(1)}, f32[160,128]{1,0:T(8,128)S(1)}, u32[]{:S(2)}, u32[]{:S(2)}) collective-permute-start(f32[160,128]{1,0:T(8,128)S(1)} %get-tuple-element.58.field), channel_id=1, source_target_pairs={{0,1},{1,2},{2,3},{3,0},{4,5},{5,6},{6,7},{7,4},{8,9},{9,10},{10,1... | collective-permute-start | bytes 245768 | tf_op jit(solution)/shard_map/ppermute | solution.py:657
  33.5 7.1 %collective-permute-start.8 = (f32[160,128]{1,0:T(8,128)S(1)}, f32[160,128]{1,0:T(8,128)S(1)}, u32[]{:S(2)}, u32[]{:S(2)}) collective-permute-start(f32[160,128]{1,0:T(8,128)S(1)} %get-tuple-element.58.field), channel_id=1, source_target_pairs={{0,3},{1,0},{2,1},{3,2},{4,7},{5,4},{6,5},{7,6},{8,11},{9,8},{10,9... | collective-permute-start | bytes 245768 | tf_op jit(solution)/shard_map/ppermute | solution.py:657
  37.3 13.8 %collective-permute-start.6 = (bf16[64,1024]{1,0:T(8,128)(2,1)S(1)}, bf16[64,1024]{1,0:T(8,128)(2,1)S(1)}, u32[]{:S(2)}, u32[]{:S(2)}) collective-permute-start(bf16[64,1024]{1,0:T(8,128)(2,1)S(1)} %get-tuple-element.49.faces), channel_id=1, source_target_pairs={{0,28},{4,8},{8,4},{12,16},{16,12},{20,24},{24,20},{28,0},{1,29},{... | collective-permute-start | bytes 393224 | tf_op jit(solution)/shard_map/ppermute | solution.py:683
  44.0 12.7 %all-to-all-start.2 = ((f32[8,24,128]{2,1,0:T(8,128)}), f32[8,24,128]{2,1,0:T(8,128)S(1)}, u32[]{:S(2)}, u32[]{:S(2)}) async-start(f32[8,24,128]{2,1,0:T(8,128)} %get-tuple-element.63), calls=%async_computation.2 | async-start | bytes 196608 | tf_op jit(solution)/shard_map/all_to_all | solution.py:666
  48.1 4.6 %collective-permute-start.10 = (f32[64,128]{1,0:T(8,128)S(1)}, f32[64,128]{1,0:T(8,128)S(1)}, u32[]{:S(2)}, u32[]{:S(2)}) collective-permute-start(f32[64,128]{1,0:T(8,128)S(1)} %get-tuple-element.62.field.x0), channel_id=1, source_target_pairs={{0,3},{1,0},{2,1},{3,2},{4,7},{5,4},{6,5},{7,6},{8,11},{9,8},{10,9... | collective-permute-start | bytes 98312 | tf_op jit(solution)/shard_map/ppermute | solution.py:657
  51.0 5.7 %collective-permute-start.9 = (f32[64,128]{1,0:T(8,128)S(1)}, f32[64,128]{1,0:T(8,128)S(1)}, u32[]{:S(2)}, u32[]{:S(2)}) collective-permute-start(f32[64,128]{1,0:T(8,128)S(1)} %get-tuple-element.62.field.x0), channel_id=1, source_target_pairs={{0,1},{1,2},{2,3},{3,0},{4,5},{5,6},{6,7},{7,4},{8,9},{9,10},{10,1... | collective-permute-start | bytes 98312 | tf_op jit(solution)/shard_map/ppermute | solution.py:657
  58.9 10.8 %all-to-all-start.3 = ((f32[32,4,128]{2,1,0:T(4,128)}), f32[32,4,128]{2,1,0:T(4,128)S(1)}, u32[]{:S(2)}, u32[]{:S(2)}) async-start(f32[32,4,128]{2,1,0:T(4,128)} %get-tuple-element.64._), calls=%async_computation.3 | async-start | bytes 131072 | tf_op jit(solution)/shard_map/all_to_all | solution.py:782
  71.3 9.2 %all-to-all-start.4 = ((f32[8,24,128]{2,1,0:T(8,128)}), f32[8,24,128]{2,1,0:T(8,128)S(1)}, u32[]{:S(2)}, u32[]{:S(2)}) async-start(f32[8,24,128]{2,1,0:T(8,128)} %get-tuple-element.69), calls=%async_computation.4 | async-start | bytes 196608 | tf_op jit(solution)/shard_map/all_to_all | solution.py:666
  74.7 5.8 %collective-permute-start.11 = (f32[64,128]{1,0:T(8,128)S(1)}, f32[64,128]{1,0:T(8,128)S(1)}, u32[]{:S(2)}, u32[]{:S(2)}) collective-permute-start(f32[64,128]{1,0:T(8,128)S(1)} %get-tuple-element.68.field.p0), channel_id=1, source_target_pairs={{0,1},{1,2},{2,3},{3,0},{4,5},{5,6},{6,7},{7,4},{8,9},{9,10},{10,1... | collective-permute-start | bytes 98312 | tf_op jit(solution)/shard_map/ppermute | solution.py:657
  74.9 5.6 %collective-permute-start.12 = (f32[64,128]{1,0:T(8,128)S(1)}, f32[64,128]{1,0:T(8,128)S(1)}, u32[]{:S(2)}, u32[]{:S(2)}) collective-permute-start(f32[64,128]{1,0:T(8,128)S(1)} %get-tuple-element.68.field.p0), channel_id=1, source_target_pairs={{0,3},{1,0},{2,1},{3,2},{4,7},{5,4},{6,5},{7,6},{8,11},{9,8},{10,9... | collective-permute-start | bytes 98312 | tf_op jit(solution)/shard_map/ppermute | solution.py:657
  97.3 9.2 %all-to-all-start.6 = ((f32[8,24,128]{2,1,0:T(8,128)}), f32[8,24,128]{2,1,0:T(8,128)S(1)}, u32[]{:S(2)}, u32[]{:S(2)}) async-start(f32[8,24,128]{2,1,0:T(8,128)} %get-tuple-element.73), calls=%async_computation.6 | async-start | bytes 196608 | tf_op jit(solution)/shard_map/all_to_all | solution.py:666
  100.6 5.8 %collective-permute-start.13 = (f32[64,128]{1,0:T(8,128)S(1)}, f32[64,128]{1,0:T(8,128)S(1)}, u32[]{:S(2)}, u32[]{:S(2)}) collective-permute-start(f32[64,128]{1,0:T(8,128)S(1)} %get-tuple-element.72.field.d), channel_id=1, source_target_pairs={{0,1},{1,2},{2,3},{3,0},{4,5},{5,6},{6,7},{7,4},{8,9},{9,10},{10,1... | collective-permute-start | bytes 98312 | tf_op jit(solution)/shard_map/ppermute | solution.py:657
  100.9 5.6 %collective-permute-start.14 = (f32[64,128]{1,0:T(8,128)S(1)}, f32[64,128]{1,0:T(8,128)S(1)}, u32[]{:S(2)}, u32[]{:S(2)}) collective-permute-start(f32[64,128]{1,0:T(8,128)S(1)} %get-tuple-element.72.field.d), channel_id=1, source_target_pairs={{0,3},{1,0},{2,1},{3,2},{4,7},{5,4},{6,5},{7,6},{8,11},{9,8},{10,9... | collective-permute-start | bytes 98312 | tf_op jit(solution)/shard_map/ppermute | solution.py:657
  (10 other events, 7.4 us)

commit v4 on v3

--- a/solution.py
+++ b/solution.py
@@ -147,27 +147,25 @@
     return stacked[:size] + (stacked[size : 2 * size] + stacked[2 * size :])
 
 
-def gram(grid, zm, w3, weights, first_row=0):
-    d = grid.depth
-    size = zm.shape[0]
-    total = None
-    group = 8
-    rows = weights.shape[0]
-    for start in range(0, rows, group):
-        stop = min(start + group, rows)
-        for row in range(start, stop):
-            at = slice(row * d, (row + 1) * d)
-            src = slice((first_row + row) * d, (first_row + row + 1) * d)
-            hi, mid, lo = split3(zm[:, src].astype(F32) * weights[row : row + 1, :])
-            w3[0:size, at] = hi
-            w3[size : 2 * size, at] = mid
-            w3[2 * size : 3 * size, at] = lo
-        part = dot_nt(
-            w3[:, start * d : stop * d],
-            zm[:, (first_row + start) * d : (first_row + stop) * d],
-        )
-        total = part if total is None else total + part
-    return fold3(total)
+def weighted_gram(w3, parts, weights, other):
+    size = other.shape[0]
+    k = other.shape[1] // len(weights)
+    for i, (part, weight) in enumerate(zip(parts, weights)):
+        at = slice(i * k, (i + 1) * k)
+        hi, mid, lo = split3(part.astype(F32) * weight)
+        w3[0:size, at] = hi
+        w3[size : 2 * size, at] = mid
+        w3[2 * size : 3 * size, at] = lo
+    return fold3(dot_nt(w3[:, : len(weights) * k], other))
+
+
+def y_weights(grid, first, last):
+    n, d = grid.rows, grid.depth
+    row = lax.broadcasted_iota(jnp.int32, (n, d), 0)
+    lane = lax.broadcasted_iota(jnp.int32, (n, d), 1)
+    wide = jnp.where(lane == row, first[:, 0:1], 0.0)
+    wide = wide + jnp.where(lane == n + row, last[:, d - 1 : d], 0.0)
+    return jnp.sum(wide, axis=0, keepdims=True)
 
 
 def invert_spd(m, ahead=5):
@@ -308,13 +306,27 @@
     own[...] = fold3(total)
 
 
+def pick(sources, targets, sems):
+    for i, (index, target) in enumerate(targets):
+        for j, source in enumerate(sources):
+
+            @pl.when(index == j)
+            def _(source=source, target=target, i=i):
+                pltpu.make_async_copy(source, target, sems.at[i]).start()
+
+
+def await_picks(sources, targets, sems):
+    for i, (_, target) in enumerate(targets):
+        pltpu.make_async_copy(sources[0], target, sems.at[i]).wait()
+
+
 def k_setup(
     grid, pairs, cols, ids, cap, vent, cond, cond_low, cond_high, rec,
-    zm, own_inner, projected, face_y, faces, *rest,
+    zm, own_inner, projected, face_y, *rest,
 ):
-    held = rest[:-12]
+    n, d, w, layers = grid.rows, grid.depth, grid.width, grid.layers
+    held = [zm.at[:, pl.ds((n - w) * d, w * d)], *rest[:-12]]
     coef, own, inverse, sent, pay, mine, wanted, vents, names, w3, v0, sems = rest[-12:]
-    n, d, w, layers = grid.rows, grid.depth, grid.width, grid.layers
     count = rec.shape[0]
     panel = w * d
     line = w + 2 * layers
@@ -323,21 +335,20 @@
     targets = []
     for k in range(pairs):
         theirs = jnp.where(names_lane == k, rec[sibling, line : line + 1, :], 0.0)
-        targets += [
+        for partner, target in (
             (ids[k], mine.at[k]),
             (jnp.sum(theirs).astype(jnp.int32), wanted.at[:, pl.ds(k * panel, panel)]),
-        ]
-    for i, (partner, target) in enumerate(targets):
-        index = lax.shift_right_logical(lax.bitwise_xor(partner, ids[pairs]), 1)
-        for j, source in enumerate(held):
-
-            @pl.when(index == j)
-            def _(source=source, target=target, i=i):
-                pltpu.make_async_copy(source, target, sems.at[i]).start()
-
-    half = layers * d
+        ):
+            index = lax.shift_right_logical(lax.bitwise_xor(partner, ids[pairs]), 1)
+            targets.append((index, target))
+    pick(held, targets, sems)
+
     upward = lax.bitwise_and(ids[pairs], 1) == 0
-    wanted[:, pairs * panel :] = jnp.where(upward, faces[:, half:], faces[:, :half])
+    for z in range(layers):
+        low_face = zm[:, z * panel : z * panel + d]
+        high_face = zm[:, (z + 1) * panel - d : (z + 1) * panel]
+        at = slice(pairs * panel + z * d, pairs * panel + (z + 1) * d)
+        wanted[:, at] = jnp.where(upward, high_face.astype(F32), low_face.astype(F32)).astype(BF16)
     for k in range(pairs):
         vents[k] = vent[...] * rec[ids[k], 0:w, :]
     up, down = jnp.minimum(ids[pairs] + 1, count - 1), jnp.maximum(ids[pairs] - 1, 0)
@@ -352,20 +363,25 @@
     low_y = jnp.where(col_at > 0, cond_low[0:n, :], 0.0)
     high_y = jnp.where(col_at < cols - 1, cond_high[0:n, :], 0.0)
     uz, lz, ux, lx, uy, ly = conductances(grid, cond[0:n, :], low_x, high_x, low_y, high_y)
-    xi, lane, row = grid.masks()
-    extra = (
-        jnp.where(xi == w - 1, ux, 0.0)
-        + jnp.where(xi == 0, lx, 0.0)
-        + jnp.where(lane == d - 1, uy, 0.0)
-        + jnp.where(lane == 0, ly, 0.0)
-    )
     plenum = vent[...] * vent_sum
-    extra = jnp.concatenate([extra[:-w], extra[-w:] + plenum], axis=0)
     diagonal = cap[...] + uz + lz + ux + lx + uy + ly
     coef[0] = jnp.concatenate([diagonal[:-w], diagonal[-w:] + plenum], axis=0)
     for i, c in enumerate((uz, lz, ux, lx, uy, ly)):
         coef[i + 1] = c
-    block = own_inner[...] + gram(grid, zm, w3, extra)
+    last, first = [ux[z * w + w - 1 :][:1] for z in range(layers)], [lx[z * w :][:1] for z in range(layers)]
+    top = [plenum[x : x + 1] for x in range(w)]
+    top[0] = top[0] + first[-1]
+    top[-1] = top[-1] + last[-1]
+    row = n - w
+    tops = zm[:, row * d :]
+    block = own_inner[...] + weighted_gram(
+        w3, [tops[:, x * d : (x + 1) * d] for x in range(w)], top, tops
+    )
+    for at, weights in ((0, first[:-1]), (panel - d, last[:-1])):
+        parts = [zm[:, z * panel + at : z * panel + at + d] for z in range(layers - 1)]
+        block = block + weighted_gram(w3, parts, weights, jnp.concatenate(parts, axis=1))
+    sides = face_y[...].astype(BF16)
+    block = block + weighted_gram(w3, [sides], [y_weights(grid, ly, uy)], sides)
     own[...] = block
     inverse[...] = invert_spd(block)
     y0 = solve_own(inverse, jnp.sum(projected[...], axis=1, keepdims=True))
@@ -377,8 +393,7 @@
     sent[n : n + half, :] = folded
     sent[n + half :, :] = face_y[...]
     to_all(grid, pay, vent[...] * field[-w:], field, folded)
-    for i, (_, target) in enumerate(targets):
-        pltpu.make_async_copy(held[0], target, sems.at[i]).wait()
+    await_picks(held, targets, sems)
 
 
 def incoming(grid, pairs, ids, rec, low, high):
@@ -427,13 +442,14 @@
 
 
 def k_partials(
-    grid, pairs, base, ids, coef, vent, field, rec, low, high, vents, zm,
-    far, y_faces, mine, others, *rest,
+    grid, pairs, base, ids, coef, vent, field, rec, low, high, vents, zm, y_faces, mine, others,
+    far, *rest,
 ):
+    n, d, w, layers = grid.rows, grid.depth, grid.width, grid.layers
+    size = zm.shape[0]
     base_ref = rest[0] if base else None
     out, pay = rest[-2:]
-    n, d, w, layers = grid.rows, grid.depth, grid.width, grid.layers
-    size = zm.shape[0]
+    next_first, prev_last = x_faces(grid, pairs, ids, others, far)
     v = operate(grid, coef, vent[...], field[...], incoming(grid, pairs, ids, rec, low, high))
     if base:
         v = base_ref[...] - v
@@ -450,25 +466,22 @@
 
     even = along(zm, [own[i : i + 1] for i in range(n)])
     ux, lx, uy, ly = [coef[i] * v for i in (3, 4, 5, 6)]
-    next_first, prev_last = x_faces(grid, pairs, ids, others, far)
     sums = [
         even,
         -along(next_first, [ux[z * w + w - 1 : z * w + w] for z in range(layers)]),
         -along(prev_last, [lx[z * w : z * w + 1] for z in range(layers)]),
     ]
-    row = lax.broadcasted_iota(jnp.int32, (n, d), 0)
-    lane = lax.broadcasted_iota(jnp.int32, (n, d), 1)
-    up = jnp.sum(jnp.where(lane == row, uy[:, d - 1 : d], 0.0), axis=0, keepdims=True)
-    down = jnp.sum(jnp.where(lane == n + row, ly[:, 0:1], 0.0), axis=0, keepdims=True)
-    sums.append(-(y_faces[0] * up))
-    sums.append(-(y_faces[1] * down))
+    toward = pltpu.roll(y_weights(grid, ly, uy), n, 1)
+    lane = lax.broadcasted_iota(jnp.int32, (1, d), 1)
+    sums.append(-(y_faces[0] * jnp.where(lane < n, toward, 0.0)))
+    sums.append(-(y_faces[1] * jnp.where(lane < n, 0.0, toward)))
     top = v[-w:]
     for k in range(pairs):
         weight = vents[k] * top
         total = None
         for x in range(w):
-            at = slice(x * d, (x + 1) * d)
-            term = chosen(grid, pairs, ids, mine, others, k, at) * weight[x : x + 1]
+            part = chosen(grid, pairs, ids, mine, others, k, slice(x * d, (x + 1) * d))
+            term = part * weight[x : x + 1]
             total = term if total is None else total + term
         sums.append(-total)
     ones = jnp.ones((8, d), F32)
@@ -536,7 +549,7 @@
 
 
 def k_blocks(
-    grid, pairs, cols, scale, ids, coef, vents, names, zm, mine, others, own, inverse, far,
+    grid, pairs, cols, scale, ids, coef, vents, names, zm, mine, others, far, own, inverse,
     face_y, y_faces, solves, _, out, weights, table, w3,
 ):
     n, d, w, layers = grid.rows, grid.depth, grid.width, grid.layers
@@ -562,17 +575,6 @@
             good = there & (pr >= 0) & (pr < rows) & (pc >= 0) & (pc < cols)
             table[j * count + i] = jnp.where(good, pr * cols + pc, -1)
 
-    def weighted(parts, row_weights, other):
-        m = len(row_weights)
-        k = other.shape[1] // m
-        for i, (part, weight) in enumerate(zip(parts, row_weights)):
-            at = slice(i * k, (i + 1) * k)
-            hi, mid, lo = split3(part.astype(F32) * weight)
-            w3[0:size, at] = hi
-            w3[size : 2 * size, at] = mid
-            w3[2 * size : 3 * size, at] = lo
-        return -fold3(dot_nt(w3[:, : m * k], other))
-
     def dot(a, b):
         return lax.dot_general(
             a, b, (((1,), (0,)), ((), ())),
@@ -586,22 +588,20 @@
     def basis_rows(at):
         return [zm[:, i * d : (i + 1) * d] for i in at]
 
-    next_first, prev_last = x_faces(grid, pairs, ids, others, far)
+    next_first, prev_last = [f.astype(BF16) for f in x_faces(grid, pairs, ids, others, far)]
     found = [
-        weighted(basis_rows(last), [ux[i : i + 1] for i in last], next_first.astype(BF16)),
-        weighted(basis_rows(first), [lx[i : i + 1] for i in first], prev_last.astype(BF16)),
+        weighted_gram(w3, basis_rows(last), [-ux[i : i + 1] for i in last], next_first),
+        weighted_gram(w3, basis_rows(first), [-lx[i : i + 1] for i in first], prev_last),
     ]
-    row = lax.broadcasted_iota(jnp.int32, (n, d), 0)
-    wide = lax.broadcasted_iota(jnp.int32, (n, d), 1)
-    high_weight = jnp.sum(jnp.where(wide == row, uy[:, d - 1 : d], 0.0), axis=0, keepdims=True)
-    low_weight = jnp.sum(jnp.where(wide == n + row, ly[:, 0:1], 0.0), axis=0, keepdims=True)
+    toward = -pltpu.roll(y_weights(grid, ly, uy), n, 1)
     swapped = pltpu.roll(face_y[...], n, 1)
-    found.append(weighted([swapped], [high_weight], y_faces[0].astype(BF16)))
-    found.append(weighted([swapped], [low_weight], y_faces[1].astype(BF16)))
+    for k, there in ((0, lane < n), (1, lane >= n)):
+        weight = jnp.where(there, toward, 0.0)
+        found.append(weighted_gram(w3, [swapped], [weight], y_faces[k].astype(BF16)))
     top = basis_rows(range(n - w, n))
     for k in range(pairs):
         panel = chosen(grid, pairs, ids, mine, others, k, slice(0, w * d)).astype(BF16)
-        found.append(weighted(top, [vents[k, i : i + 1, :] for i in range(w)], panel))
+        found.append(weighted_gram(w3, top, [-vents[k, i : i + 1, :] for i in range(w)], panel))
 
     for slot in range(rows):
         out[slot] = jnp.zeros((size, size), F32)
@@ -678,8 +678,9 @@
         ),
         (basis,),
         scratch=(pltpu.VMEM((size * n, depth), F32),),
-    )
-    held = [panel] + [xor_step(panel, "row", k) for k in range(2, row_count, 2)]
+        cost=pl.CostEstimate(flops=1000, bytes_accessed=1000, transcendentals=0),
+    )
+    held = [xor_step(panel, "row", k) for k in range(2, row_count, 2)]
     far = lax.ppermute(
         faces,
         "row",
@@ -709,7 +710,7 @@
             pltpu.VMEM((3 * size, n * depth), BF16),
             pltpu.VMEM((7, n, depth), F32),
         ),
-        cost=pl.CostEstimate(flops=200_000_000, bytes_accessed=8_000_000, transcendentals=0),
+        cost=pl.CostEstimate(flops=1000, bytes_accessed=1000, transcendentals=0),
     )
 
     panels = ((pairs, size, width * depth), BF16)
@@ -728,7 +729,7 @@
         ),
         (
             ids, cap, vent, cond, cond_low, cond_high, rec0, zm, own_inner, projected, face_y,
-            faces, *held,
+            *held,
         ),
         scratch=(
             pltpu.VMEM((3 * size, n * depth), BF16),
@@ -736,7 +737,7 @@
             pltpu.SemaphoreType.DMA((2 * pairs,)),
         ),
         smem=1,
-        free=range(12, 12 + len(held)),
+        free=range(11, 11 + len(held)),
     )
     others = xor_step(wanted, "row", 1)
     rec1, low1, high1 = exchange(sent, pay1)
@@ -757,8 +758,7 @@
         functools.partial(k_partials, grid, pairs, True),
         (field, everyone((places + 1) // 2)),
         (
-            ids, coef, vent, x0, rec, low, high, vents, zm, far, y_faces,
-            mine, others, rhs,
+            ids, coef, vent, x0, rec, low, high, vents, zm, y_faces, mine, others, far, rhs,
         ),
         smem=1,
     )
@@ -770,7 +770,7 @@
             ((places * places,), jnp.int32),
         ),
         (
-            ids, coef, vents, names, zm, mine, others, own, inverse, far, face_y, y_faces,
+            ids, coef, vents, names, zm, mine, others, far, own, inverse, face_y, y_faces,
             solves, pay3,
         ),
         scratch=(pltpu.VMEM((3 * size, width * depth), BF16),),
@@ -792,8 +792,7 @@
         functools.partial(k_partials, grid, pairs, False),
         (field, everyone((places + 1) // 2)),
         (
-            ids, coef, vent, p0, rec, low, high, vents, zm, far, y_faces,
-            mine, others,
+            ids, coef, vent, p0, rec, low, high, vents, zm, y_faces, mine, others, far,
         ),
         smem=1,
     )

time: 122 us -> 112 us (0.918)
  waiting for transfers between devices: 16.6 us -> 24.1 us
  blocking collectives: 27.1 us -> 20.7 us
  starting transfers between devices: 47 us -> 41.1 us
  local copies, waits for them, and re-layouts: 5.97 us -> 1.9 us
    ppermute x10, waiting for transfers between devices: 10.9 us -> 19.7 us  [cyclic(): lax.ppermute(value, axis, [(i, (i + step) % count) for i in range(count)])]
    ppermute x10, starting transfers between devices: 18.7 us -> 11.8 us  [cyclic(): lax.ppermute(value, axis, [(i, (i + step) % count) for i in range(count)])]
    unnamed x26 -> x14, local copies, waits for them, and re-layouts: 5.97 us -> 1.9 us
    all_to_all x1, blocking collectives: 13.4 us -> 10.3 us  [body(): total = lax.all_to_all(pay7, ('row', 'col'), 0, 0)]
    all_to_all x1, blocking collectives: 13.6 us -> 10.5 us  [body(): sums = lax.all_to_all(pay5, ('row', 'col'), 0, 0)]
    all_to_all x5, waiting for transfers between devices: 2.01 us -> 0.01 us  [exchange(): rec = lax.all_to_all(payload, 'row', 0, 0)]
  transfers between devices with their start and end apart: 21 -> 21, of which waited for: 7 -> 10; matrix products, arithmetic and copies ran while one was open for 0% -> 0% of each run, Pallas kernels for 7% -> 8%
where the time goes in v4:
time: 112 us
  starting transfers between devices  41.1 us (37%)
  waiting for transfers between devices  24.1 us (22%)
  Pallas kernels  22.9 us (20%)
  blocking collectives  20.7 us (18%)
  local copies, waits for them, and re-layouts  1.9 us (2%)
    pallas_call x12, Pallas kernels, call(): pl.pallas_call(kernel, out_shape=tuple((jax.ShapeDtypeStruct(s, t) for s,...  22.9 us
    ppermute x10, waiting for transfers between devices, cyclic(): lax.ppermute(value, axis, [(i, (i + step) % count) for i in range(count)])  19.7 us
    all_to_all x5, starting transfers between devices, exchange(): rec = lax.all_to_all(payload, 'row', 0, 0)  19.2 us
    ppermute x10, starting transfers between devices, cyclic(): lax.ppermute(value, axis, [(i, (i + step) % count) for i in range(count)])  11.8 us
    all_to_all x1, blocking collectives, body(): sums = lax.all_to_all(pay5, ('row', 'col'), 0, 0)  10.5 us
    all_to_all x1, blocking collectives, body(): total = lax.all_to_all(pay7, ('row', 'col'), 0, 0)  10.3 us
    ppermute x4, starting transfers between devices, xor_step(): return lax.ppermute(value, axis, [(i, i ^ k) for i in range(count)])  4.67 us
    all_to_all x1, waiting for transfers between devices, body(): sums = lax.all_to_all(pay3, ('row', 'col'), 0, 0)  4.43 us
  transfers between devices with their start and end apart: 21, of which 10 were waited for; matrix products, arithmetic and copies ran while one was open for 0% of the time, Pallas kernels for 8%

profile of v4, /device:TPU:0, one launch (start us, length us, event | category | flops | bytes accessed | tf_op | source)
XLA Modules:
  0.0 111.6 jit_solution(15156105479652336319)
XLA Ops:
  3.3 4.0 %collective-permute-start.4 = (bf16[64,2048]{1,0:T(8,128)(2,1)S(1)}, bf16[64,2048]{1,0:T(8,128)(2,1)S(1)}, u32[]{:S(2)}, u32[]{:S(2)}) collective-permute-start(bf16[64,2048]{1,0:T(8,128)(2,1)S(1)} %get-tuple-element.49), channel_id=1, source_target_pairs={{0,24},{4,28},{8,16},{12,20},{16,8},{20,12},{24,0},{28,4},{1,25},{... | collective-permute-start | bytes 786440 | tf_op jit(solution)/shard_map/ppermute | solution.py:661
  9.9 4.1 %all-to-all-start = ((f32[8,32,128]{2,1,0:T(8,128)}), f32[8,32,128]{2,1,0:T(8,128)S(1)}, u32[]{:S(2)}, u32[]{:S(2)}) async-start(f32[8,32,128]{2,1,0:T(8,128)} %get-tuple-element.44), calls=%async_computation | async-start | bytes 262144 | tf_op jit(solution)/shard_map/all_to_all | solution.py:666
  14.1 3.6 %collective-permute-start.1 = (f32[72,128]{1,0:T(8,128)S(1)}, f32[72,128]{1,0:T(8,128)S(1)}, u32[]{:S(2)}, u32[]{:S(2)}) collective-permute-start(f32[72,128]{1,0:T(8,128)S(1)} %get-tuple-element.43.cond_ref.cond), channel_id=1, source_target_pairs={{0,3},{1,0},{2,1},{3,2},{4,7},{5,4},{6,5},{7,6},{8,11},{9,8},{10,9... | collective-permute-start | bytes 110600 | tf_op jit(solution)/shard_map/ppermute | solution.py:657
  17.8 2.8 %shard_map.96 = (f32[64,64]{1,0:T(8,128)S(1)}, f32[64,128]{1,0:T(8,128)S(1)}, f32[64,128]{1,0:T(8,128)S(1)}) custom-call(bf16[64,8192]{1,0:T(8,128)(2,1)S(1)} %get-tuple-element.45.zm, f32[64,128]{1,0:T(8,128)S(1)} %bitcast.10, f32[72,128]{1,0:T(8,128)S(1)} %get-tuple-element.43.cond_ref.cond, f32[64,128]{1,0:T(8,128)S(1)} %get-tuple-element.41.cap_ref.cap), custom_call_target="tpu_custom_call" | custom-call | flops 1000 | bytes 1000 | tf_op jit(solution)/shard_map/pallas_call | solution.py:624
  20.6 2.9 %collective-permute-done.cond_low = f32[72,128]{1,0:T(8,128)S(1)} collective-permute-done((f32[72,128]{1,0:T(8,128)S(1)}, f32[72,128]{1,0:T(8,128)S(1)}, u32[]{:S(2)}, u32[]{:S(2)}) %collective-permute-start) | collective-permute-done | bytes 36896 | tf_op jit(solution)/shard_map/ppermute | solution.py:657
  23.5 4.0 %shard_map.97 = (f32[7,64,128]{2,1,0:T(8,128)S(1)}, f32[64,64]{1,0:T(8,128)S(1)}, f32[64,64]{1,0:T(8,128)S(1)}, f32[160,128]{1,0:T(8,128)S(1)}, f32[8,56,128]{2,...) custom-call(s32[4]{0:T(128)S(1)} %pad_add_fusion.ids, ...), custom_call_target="tpu_custom_call" | custom-call | tf_op jit(solution)/shard_map/pallas_call | solution.py:624
  27.6 4.3 %all-to-all-start.1 = ((f32[8,56,128]{2,1,0:T(8,128)}), f32[8,56,128]{2,1,0:T(8,128)S(1)}, u32[]{:S(2)}, u32[]{:S(2)}) async-start(f32[8,56,128]{2,1,0:T(8,128)} %get-tuple-element.59), calls=%async_computation.1 | async-start | bytes 458752 | tf_op jit(solution)/shard_map/all_to_all | solution.py:666
  33.9 2.1 %collective-permute-start.6 = (bf16[64,1024]{1,0:T(8,128)(2,1)S(1)}, bf16[64,1024]{1,0:T(8,128)(2,1)S(1)}, u32[]{:S(2)}, u32[]{:S(2)}) collective-permute-start(bf16[64,1024]{1,0:T(8,128)(2,1)S(1)} %get-tuple-element.55), channel_id=1, source_target_pairs={{0,28},{4,8},{8,4},{12,16},{16,12},{20,24},{24,20},{28,0},{1,29},{... | collective-permute-start | bytes 393224 | tf_op jit(solution)/shard_map/ppermute | solution.py:684
  36.7 2.5 %collective-permute-done.7.low = f32[160,128]{1,0:T(8,128)S(1)} collective-permute-done((f32[160,128]{1,0:T(8,128)S(1)}, f32[160,128]{1,0:T(8,128)S(1)}, u32[]{:S(2)}, u32[]{:S(2)}) %collective-permute-start.7) | collective-permute-done | bytes 81952 | tf_op jit(solution)/shard_map/ppermute | solution.py:657
  39.2 1.9 %shard_map.98 = (f32[64,128]{1,0:T(8,128)S(1)}, f32[8,24,128]{2,1,0:T(8,128)}, f32[6,32,128]{2,1,0:T(8,128)S(1)}, f32[2,64,128]{2,1,0:T(8,128)S(1)}) custom-call(s32[4]{0:T(128)S(1)} %pad_add_fusion.ids, f32[7,64,128]{2,1,0:T(8,128)S(1)} %get-tuple-element.50.coef, f32[16,128]{1,0:T(8,128)S(1)} %get-tuple-element.42.vent, ...), custom_call_target="tpu_custom_call" | custom-call | tf_op jit(solution)/shard_map/pallas_call | solution.py:624
  41.1 4.1 %all-to-all-start.2 = ((f32[8,24,128]{2,1,0:T(8,128)}), f32[8,24,128]{2,1,0:T(8,128)S(1)}, u32[]{:S(2)}, u32[]{:S(2)}) async-start(f32[8,24,128]{2,1,0:T(8,128)} %get-tuple-element.63), calls=%async_computation.2 | async-start | bytes 196608 | tf_op jit(solution)/shard_map/all_to_all | solution.py:666
  49.1 2.7 %collective-permute-done.9.low = f32[64,128]{1,0:T(8,128)S(1)} collective-permute-done((f32[64,128]{1,0:T(8,128)S(1)}, f32[64,128]{1,0:T(8,128)S(1)}, u32[]{:S(2)}, u32[]{:S(2)}) %collective-permute-start.9) | collective-permute-done | bytes 32800 | tf_op jit(solution)/shard_map/ppermute | solution.py:657
  51.8 2.1 %shard_map.99 = (f32[64,128]{1,0:T(8,128)S(1)}, f32[32,4,128]{2,1,0:T(4,128)}) custom-call(s32[4]{0:T(128)S(1)} %pad_add_fusion.ids, f32[7,64,128]{2,1,0:T(8,128)S(1)} %get-tuple-element.50.coef, f32[16,128]{1,0:T(8,128)S(1)} %get-tuple-element.42.vent, f32[64,128]{1,0:T(8,128)S(1)} %get-tuple-element.62.field.x0, f32[8,24,128]{2,1,0:T(8,128)S(1)} %all-to-all-done.2.rec, ...), custom_call_target="tpu_custom_call" | custom-call | tf_op jit(solution)/shard_map/pallas_call | solution.py:624
  53.9 3.3 %all-to-all-start.3 = ((f32[32,4,128]{2,1,0:T(4,128)}), f32[32,4,128]{2,1,0:T(4,128)S(1)}, u32[]{:S(2)}, u32[]{:S(2)}) async-start(f32[32,4,128]{2,1,0:T(4,128)} %get-tuple-element.64._), calls=%async_computation.3 | async-start | bytes 131072 | tf_op jit(solution)/shard_map/all_to_all | solution.py:782
  57.2 3.1 %shard_map.100 = (f32[8,64,64]{2,1,0:T(8,128)}, f32[7,64,64]{2,1,0:T(8,128)S(1)}, s32[49]{0:T(128)S(1)}) custom-call(s32[4]{0:T(128)S(1)} %pad_add_fusion.ids, f32[7,64,128]{2,1,0:T(8,128)S(1)} %get-tuple-element.50.coef, f32[2,16,128]{2,1,0:T(8,128)S(1)} %get-tuple-element.51.vents, f32[6,128]{1,0:T(8,128)S(1)} %get-tuple-element.52.names, ...), custom_call_target="tpu_custom_call" | custom-call | flops 100000000 | bytes 4000000 | tf_op jit(solution)/shard_map/pallas_call | solution.py:624
  60.3 4.4 %all-to-all-done.3.rec = f32[32,4,128]{2,1,0:T(4,128)S(1)} async-done(((f32[32,4,128]{2,1,0:T(4,128)}), f32[32,4,128]{2,1,0:T(4,128)S(1)}, u32[]{:S(2)}, u32[]{:S(2)}) %all-to-all-start.3) | async-done | bytes 65568 | tf_op jit(solution)/shard_map/all_to_all | solution.py:782
  66.3 3.4 %all-to-all-start.4 = ((f32[8,24,128]{2,1,0:T(8,128)}), f32[8,24,128]{2,1,0:T(8,128)S(1)}, u32[]{:S(2)}, u32[]{:S(2)}) async-start(f32[8,24,128]{2,1,0:T(8,128)} %get-tuple-element.69), calls=%async_computation.4 | async-start | bytes 196608 | tf_op jit(solution)/shard_map/all_to_all | solution.py:666
  71.8 1.9 %collective-permute-done.12.high = f32[64,128]{1,0:T(8,128)S(1)} collective-permute-done((f32[64,128]{1,0:T(8,128)S(1)}, f32[64,128]{1,0:T(8,128)S(1)}, u32[]{:S(2)}, u32[]{:S(2)}) %collective-permute-start.12) | collective-permute-done | bytes 32800 | tf_op jit(solution)/shard_map/ppermute | solution.py:657
  73.7 2.6 %collective-permute-done.11.low = f32[64,128]{1,0:T(8,128)S(1)} collective-permute-done((f32[64,128]{1,0:T(8,128)S(1)}, f32[64,128]{1,0:T(8,128)S(1)}, u32[]{:S(2)}, u32[]{:S(2)}) %collective-permute-start.11) | collective-permute-done | bytes 32800 | tf_op jit(solution)/shard_map/ppermute | solution.py:657
  77.8 10.5 %all_to_all.40.rec = f32[32,4,128]{2,1,0:T(4,128)S(1)} all-to-all(f32[32,4,128]{2,1,0:T(4,128)S(1)} %get-tuple-element.70), channel_id=1, replica_groups=mesh['row'=8,'col'=4] {'row','col'}, dimensions={0} | all-to-all | bytes 131072 | tf_op jit(solution)/shard_map/all_to_all | solution.py:799
  89.9 3.4 %all-to-all-start.6 = ((f32[8,24,128]{2,1,0:T(8,128)}), f32[8,24,128]{2,1,0:T(8,128)S(1)}, u32[]{:S(2)}, u32[]{:S(2)}) async-start(f32[8,24,128]{2,1,0:T(8,128)} %get-tuple-element.73), calls=%async_computation.6 | async-start | bytes 196608 | tf_op jit(solution)/shard_map/all_to_all | solution.py:666
  95.3 1.9 %collective-permute-done.14.high = f32[64,128]{1,0:T(8,128)S(1)} collective-permute-done((f32[64,128]{1,0:T(8,128)S(1)}, f32[64,128]{1,0:T(8,128)S(1)}, u32[]{:S(2)}, u32[]{:S(2)}) %collective-permute-start.14) | collective-permute-done | bytes 32800 | tf_op jit(solution)/shard_map/ppermute | solution.py:657
  97.2 2.6 %collective-permute-done.13.low = f32[64,128]{1,0:T(8,128)S(1)} collective-permute-done((f32[64,128]{1,0:T(8,128)S(1)}, f32[64,128]{1,0:T(8,128)S(1)}, u32[]{:S(2)}, u32[]{:S(2)}) %collective-permute-start.13) | collective-permute-done | bytes 32800 | tf_op jit(solution)/shard_map/ppermute | solution.py:657
  100.6 10.3 %all_to_all.41.rec = f32[32,2,128]{2,1,0:T(2,128)S(1)} all-to-all(f32[32,2,128]{2,1,0:T(2,128)S(1)} %get-tuple-element.74), channel_id=1, replica_groups=mesh['row'=8,'col'=4] {'row','col'}, dimensions={0} | all-to-all | bytes 65536 | tf_op jit(solution)/shard_map/all_to_all | solution.py:814
  (47 shorter events, 22.6 us)
Async XLA Ops:
  1.9 6.1 %copy-start.2 = (s32[4,16,128]{2,1,0:T(8,128)S(1)}, s32[4,16,128]{2,1,0:T(8,128)}, u32[]{:S(2)}) copy-start(s32[4,16,128]{2,1,0:T(8,128)} %param.8) | copy-start | bytes 98308
  1.9 6.1 %copy-start.3 = (f32[16,128]{1,0:T(8,128)S(1)}, f32[16,128]{1,0:T(8,128)}, u32[]{:S(2)}) copy-start(f32[16,128]{1,0:T(8,128)} %vent.1) | copy-start | bytes 24580
  3.3 20.1 %collective-permute-start.4 = (bf16[64,2048]{1,0:T(8,128)(2,1)S(1)}, bf16[64,2048]{1,0:T(8,128)(2,1)S(1)}, u32[]{:S(2)}, u32[]{:S(2)}) collective-permute-start(bf16[64,2048]{1,0:T(8,128)(2,1)S(1)} %get-tuple-element.49), channel_id=1, source_target_pairs={{0,24},{4,28},{8,16},{12,20},{16,8},{20,12},{24,0},{28,4},{1,25},{... | collective-permute-start | bytes 786440 | tf_op jit(solution)/shard_map/ppermute | solution.py:661
  7.3 16.2 %collective-permute-start.3 = (bf16[64,2048]{1,0:T(8,128)(2,1)S(1)}, bf16[64,2048]{1,0:T(8,128)(2,1)S(1)}, u32[]{:S(2)}, u32[]{:S(2)}) collective-permute-start(bf16[64,2048]{1,0:T(8,128)(2,1)S(1)} %get-tuple-element.49), channel_id=1, source_target_pairs={{0,16},{4,20},{8,24},{12,28},{16,0},{20,4},{24,8},{28,12},{1,17},{... | collective-permute-start | bytes 786440 | tf_op jit(solution)/shard_map/ppermute | solution.py:661
  7.8 15.7 %collective-permute-start.2 = (bf16[64,2048]{1,0:T(8,128)(2,1)S(1)}, bf16[64,2048]{1,0:T(8,128)(2,1)S(1)}, u32[]{:S(2)}, u32[]{:S(2)}) collective-permute-start(bf16[64,2048]{1,0:T(8,128)(2,1)S(1)} %get-tuple-element.49), channel_id=1, source_target_pairs={{0,8},{4,12},{8,0},{12,4},{16,24},{20,28},{24,16},{28,20},{1,9},{5... | collective-permute-start | bytes 786440 | tf_op jit(solution)/shard_map/ppermute | solution.py:661
  9.9 7.8 %copy-start.1 = (f32[4,16,128]{2,1,0:T(8,128)S(1)}, f32[4,16,128]{2,1,0:T(8,128)}, u32[]{:S(2)}) copy-start(f32[4,16,128]{2,1,0:T(8,128)} %param.7) | copy-start | bytes 98308
  9.9 13.5 %all-to-all-start = ((f32[8,32,128]{2,1,0:T(8,128)}), f32[8,32,128]{2,1,0:T(8,128)S(1)}, u32[]{:S(2)}, u32[]{:S(2)}) async-start(f32[8,32,128]{2,1,0:T(8,128)} %get-tuple-element.44), calls=%async_computation | async-start | bytes 262144 | tf_op jit(solution)/shard_map/all_to_all | solution.py:666
  14.1 6.5 %collective-permute-start.1 = (f32[72,128]{1,0:T(8,128)S(1)}, f32[72,128]{1,0:T(8,128)S(1)}, u32[]{:S(2)}, u32[]{:S(2)}) collective-permute-start(f32[72,128]{1,0:T(8,128)S(1)} %get-tuple-element.43.cond_ref.cond), channel_id=1, source_target_pairs={{0,3},{1,0},{2,1},{3,2},{4,7},{5,4},{6,5},{7,6},{8,11},{9,8},{10,9... | collective-permute-start | bytes 110600 | tf_op jit(solution)/shard_map/ppermute | solution.py:657
  17.7 5.8 %collective-permute-start = (f32[72,128]{1,0:T(8,128)S(1)}, f32[72,128]{1,0:T(8,128)S(1)}, u32[]{:S(2)}, u32[]{:S(2)}) collective-permute-start(f32[72,128]{1,0:T(8,128)S(1)} %get-tuple-element.43.cond_ref.cond), channel_id=1, source_target_pairs={{0,1},{1,2},{2,3},{3,0},{4,5},{5,6},{6,7},{7,4},{8,9},{9,10},{10,1... | collective-permute-start | bytes 110600 | tf_op jit(solution)/shard_map/ppermute | solution.py:657
  27.5 24.3 %collective-permute-start.5 = (bf16[64,4608]{1,0:T(8,128)(2,1)}, bf16[64,4608]{1,0:T(8,128)(2,1)S(1)}, u32[]{:S(2)}, u32[]{:S(2)}) collective-permute-start(bf16[64,4608]{1,0:T(8,128)(2,1)} %get-tuple-element.54), channel_id=1, source_target_pairs={{0,4},{4,0},{8,12},{12,8},{16,20},{20,16},{24,28},{28,24},{1,5},{5... | collective-permute-start | bytes 1769480 | tf_op jit(solution)/shard_map/ppermute | solution.py:661
  27.6 11.7 %all-to-all-start.1 = ((f32[8,56,128]{2,1,0:T(8,128)}), f32[8,56,128]{2,1,0:T(8,128)S(1)}, u32[]{:S(2)}, u32[]{:S(2)}) async-start(f32[8,56,128]{2,1,0:T(8,128)} %get-tuple-element.59), calls=%async_computation.1 | async-start | bytes 458752 | tf_op jit(solution)/shard_map/all_to_all | solution.py:666
  31.9 4.9 %collective-permute-start.8 = (f32[160,128]{1,0:T(8,128)S(1)}, f32[160,128]{1,0:T(8,128)S(1)}, u32[]{:S(2)}, u32[]{:S(2)}) collective-permute-start(f32[160,128]{1,0:T(8,128)S(1)} %get-tuple-element.58.field), channel_id=1, source_target_pairs={{0,3},{1,0},{2,1},{3,2},{4,7},{5,4},{6,5},{7,6},{8,11},{9,8},{10,9... | collective-permute-start | bytes 245768 | tf_op jit(solution)/shard_map/ppermute | solution.py:657
  32.8 6.4 %collective-permute-start.7 = (f32[160,128]{1,0:T(8,128)S(1)}, f32[160,128]{1,0:T(8,128)S(1)}, u32[]{:S(2)}, u32[]{:S(2)}) collective-permute-start(f32[160,128]{1,0:T(8,128)S(1)} %get-tuple-element.58.field), channel_id=1, source_target_pairs={{0,1},{1,2},{2,3},{3,0},{4,5},{5,6},{6,7},{7,4},{8,9},{9,10},{10,1... | collective-permute-start | bytes 245768 | tf_op jit(solution)/shard_map/ppermute | solution.py:657
  33.9 13.3 %collective-permute-start.6 = (bf16[64,1024]{1,0:T(8,128)(2,1)S(1)}, bf16[64,1024]{1,0:T(8,128)(2,1)S(1)}, u32[]{:S(2)}, u32[]{:S(2)}) collective-permute-start(bf16[64,1024]{1,0:T(8,128)(2,1)S(1)} %get-tuple-element.55), channel_id=1, source_target_pairs={{0,28},{4,8},{8,4},{12,16},{16,12},{20,24},{24,20},{28,0},{1,29},{... | collective-permute-start | bytes 393224 | tf_op jit(solution)/shard_map/ppermute | solution.py:684
  41.1 10.7 %all-to-all-start.2 = ((f32[8,24,128]{2,1,0:T(8,128)}), f32[8,24,128]{2,1,0:T(8,128)S(1)}, u32[]{:S(2)}, u32[]{:S(2)}) async-start(f32[8,24,128]{2,1,0:T(8,128)} %get-tuple-element.63), calls=%async_computation.2 | async-start | bytes 196608 | tf_op jit(solution)/shard_map/all_to_all | solution.py:666
  45.2 3.9 %collective-permute-start.10 = (f32[64,128]{1,0:T(8,128)S(1)}, f32[64,128]{1,0:T(8,128)S(1)}, u32[]{:S(2)}, u32[]{:S(2)}) collective-permute-start(f32[64,128]{1,0:T(8,128)S(1)} %get-tuple-element.62.field.x0), channel_id=1, source_target_pairs={{0,3},{1,0},{2,1},{3,2},{4,7},{5,4},{6,5},{7,6},{8,11},{9,8},{10,9... | collective-permute-start | bytes 98312 | tf_op jit(solution)/shard_map/ppermute | solution.py:657
  46.1 5.7 %collective-permute-start.9 = (f32[64,128]{1,0:T(8,128)S(1)}, f32[64,128]{1,0:T(8,128)S(1)}, u32[]{:S(2)}, u32[]{:S(2)}) collective-permute-start(f32[64,128]{1,0:T(8,128)S(1)} %get-tuple-element.62.field.x0), channel_id=1, source_target_pairs={{0,1},{1,2},{2,3},{3,0},{4,5},{5,6},{6,7},{7,4},{8,9},{9,10},{10,1... | collective-permute-start | bytes 98312 | tf_op jit(solution)/shard_map/ppermute | solution.py:657
  53.9 10.8 %all-to-all-start.3 = ((f32[32,4,128]{2,1,0:T(4,128)}), f32[32,4,128]{2,1,0:T(4,128)S(1)}, u32[]{:S(2)}, u32[]{:S(2)}) async-start(f32[32,4,128]{2,1,0:T(4,128)} %get-tuple-element.64._), calls=%async_computation.3 | async-start | bytes 131072 | tf_op jit(solution)/shard_map/all_to_all | solution.py:782
  66.3 10.0 %all-to-all-start.4 = ((f32[8,24,128]{2,1,0:T(8,128)}), f32[8,24,128]{2,1,0:T(8,128)S(1)}, u32[]{:S(2)}, u32[]{:S(2)}) async-start(f32[8,24,128]{2,1,0:T(8,128)} %get-tuple-element.69), calls=%async_computation.4 | async-start | bytes 196608 | tf_op jit(solution)/shard_map/all_to_all | solution.py:666
  69.7 4.0 %collective-permute-start.12 = (f32[64,128]{1,0:T(8,128)S(1)}, f32[64,128]{1,0:T(8,128)S(1)}, u32[]{:S(2)}, u32[]{:S(2)}) collective-permute-start(f32[64,128]{1,0:T(8,128)S(1)} %get-tuple-element.68.field.p0), channel_id=1, source_target_pairs={{0,3},{1,0},{2,1},{3,2},{4,7},{5,4},{6,5},{7,6},{8,11},{9,8},{10,9... | collective-permute-start | bytes 98312 | tf_op jit(solution)/shard_map/ppermute | solution.py:657
  70.6 5.7 %collective-permute-start.11 = (f32[64,128]{1,0:T(8,128)S(1)}, f32[64,128]{1,0:T(8,128)S(1)}, u32[]{:S(2)}, u32[]{:S(2)}) collective-permute-start(f32[64,128]{1,0:T(8,128)S(1)} %get-tuple-element.68.field.p0), channel_id=1, source_target_pairs={{0,1},{1,2},{2,3},{3,0},{4,5},{5,6},{6,7},{7,4},{8,9},{9,10},{10,1... | collective-permute-start | bytes 98312 | tf_op jit(solution)/shard_map/ppermute | solution.py:657
  89.9 10.0 %all-to-all-start.6 = ((f32[8,24,128]{2,1,0:T(8,128)}), f32[8,24,128]{2,1,0:T(8,128)S(1)}, u32[]{:S(2)}, u32[]{:S(2)}) async-start(f32[8,24,128]{2,1,0:T(8,128)} %get-tuple-element.73), calls=%async_computation.6 | async-start | bytes 196608 | tf_op jit(solution)/shard_map/all_to_all | solution.py:666
  93.2 4.0 %collective-permute-start.14 = (f32[64,128]{1,0:T(8,128)S(1)}, f32[64,128]{1,0:T(8,128)S(1)}, u32[]{:S(2)}, u32[]{:S(2)}) collective-permute-start(f32[64,128]{1,0:T(8,128)S(1)} %get-tuple-element.72.field.d), channel_id=1, source_target_pairs={{0,3},{1,0},{2,1},{3,2},{4,7},{5,4},{6,5},{7,6},{8,11},{9,8},{10,9... | collective-permute-start | bytes 98312 | tf_op jit(solution)/shard_map/ppermute | solution.py:657
  94.1 5.7 %collective-permute-start.13 = (f32[64,128]{1,0:T(8,128)S(1)}, f32[64,128]{1,0:T(8,128)S(1)}, u32[]{:S(2)}, u32[]{:S(2)}) collective-permute-start(f32[64,128]{1,0:T(8,128)S(1)} %get-tuple-element.72.field.d), channel_id=1, source_target_pairs={{0,1},{1,2},{2,3},{3,0},{4,5},{5,6},{6,7},{7,4},{8,9},{9,10},{10,1... | collective-permute-start | bytes 98312 | tf_op jit(solution)/shard_map/ppermute | solution.py:657
  (4 other events, 3.2 us)

commit v5 on v4

--- a/solution.py
+++ b/solution.py
@@ -234,9 +234,10 @@
     return uz, lz, ux, lx, uy, ly
 
 
-def k_order(grid, basis, zm, panel, faces, wide):
+def k_order(grid, basis, zm, panel, face, wide):
     n, d, w, layers = grid.rows, grid.depth, grid.width, grid.layers
     size = basis.shape[0]
+    odd = lax.bitwise_and(lax.axis_index("row"), 1) == 1
 
     def unpack(a, _):
         wide[pl.ds(a * n, n), :] = basis[a].astype(F32)
@@ -249,10 +250,9 @@
         layer, x = divmod(row, w)
         if layer == layers - 1:
             panel[:, x * d : (x + 1) * d] = packed
-        if x == 0:
-            faces[:, layer * d : (layer + 1) * d] = packed
-        if x == w - 1:
-            faces[:, (layers + layer) * d : (layers + layer + 1) * d] = packed
+    for z in range(layers):
+        x = jnp.where(odd, w - 1, 0)
+        face[:, z * d : (z + 1) * d] = wide[pl.ds(z * w + x, size, stride=n), :].astype(BF16)
 
 
 def k_basis(grid, zm, rhs, cond_ref, cap_ref, own, projected, face_y, zr, w3, coef):
@@ -318,6 +318,16 @@
 def await_picks(sources, targets, sems):
     for i, (_, target) in enumerate(targets):
         pltpu.make_async_copy(sources[0], target, sems.at[i]).wait()
+
+
+def fold(inverse):
+    half = inverse.shape[0] // 2
+    return jnp.concatenate([inverse[0:half, :], inverse[half:, :]], axis=1)
+
+
+def unfold(folded):
+    size = folded.shape[1] // 2
+    return jnp.concatenate([folded[:, :size], folded[:, size:]], axis=0)
 
 
 def k_setup(
@@ -387,12 +397,8 @@
     y0 = solve_own(inverse, jnp.sum(projected[...], axis=1, keepdims=True))
     expand(grid, zm, y0, v0)
     field = v0[...]
-    half = zm.shape[0] // 2
-    folded = jnp.concatenate([inverse[0:half, :], inverse[half:, :]], axis=1)
-    sent[0:n, :] = field
-    sent[n : n + half, :] = folded
-    sent[n + half :, :] = face_y[...]
-    to_all(grid, pay, vent[...] * field[-w:], field, folded)
+    sent[...] = field
+    to_all(grid, pay, vent[...] * field[-w:], field, fold(inverse))
     await_picks(held, targets, sems)
 
 
@@ -403,25 +409,25 @@
 
 
 def k_coarse(
-    grid, pairs, ids, coef, vent, zm, inverse, field, rec, low, high, out, pay, solves, y_faces, scratch
+    grid, pairs, ids, coef, vent, zm, inverse, field, rec, low, high, face_y, _, __,
+    out, wide, pay, solves, scratch,
 ):
     n, w = grid.rows, grid.width
     beside = operate(grid, coef, vent[...], None, incoming(grid, pairs, ids, rec, low, high))
     expand(grid, zm, solve_own(inverse, project(grid, zm, beside)), scratch)
     result = field[0:n, :] - scratch[...]
     out[...] = result
+    size, half = zm.shape[0], solves.shape[1]
+    wide[0:n, :] = result
+    wide[n : n + size, :] = face_y[...]
+    wide[n + size : n + size + half, :] = fold(inverse)
     to_all(grid, pay, vent[...] * result[-w:], result)
-    half = solves.shape[1]
     first = w + 2 * grid.layers
     row_at = ids[pairs]
     solves[0] = rec[jnp.minimum(row_at + 1, rec.shape[0] - 1), first : first + half, :]
     solves[1] = rec[jnp.maximum(row_at - 1, 0), first : first + half, :]
-    solves[2] = high[n : n + half, :]
-    solves[3] = low[n : n + half, :]
     for k in range(pairs):
-        solves[4 + k] = rec[ids[k], first : first + half, :]
-    y_faces[0] = high[n + half :, :]
-    y_faces[1] = low[n + half :, :]
+        solves[2 + k] = rec[ids[k], first : first + half, :]
 
 
 def chosen(grid, pairs, ids, mine, others, k, at):
@@ -432,17 +438,14 @@
 
 
 def x_faces(grid, pairs, ids, others, far):
-    half = grid.layers * grid.depth
     near = others[:, pairs * grid.width * grid.depth :].astype(F32)
+    across = far[...].astype(F32)
     upward = lax.bitwise_and(ids[pairs], 1) == 0
-    return (
-        jnp.where(upward, near, far[:, :half].astype(F32)),
-        jnp.where(upward, far[:, half:].astype(F32), near),
-    )
+    return jnp.where(upward, near, across), jnp.where(upward, across, near)
 
 
 def k_partials(
-    grid, pairs, base, ids, coef, vent, field, rec, low, high, vents, zm, y_faces, mine, others,
+    grid, pairs, base, ids, coef, vent, field, rec, low, high, vents, zm, low2, high2, mine, others,
     far, *rest,
 ):
     n, d, w, layers = grid.rows, grid.depth, grid.width, grid.layers
@@ -473,8 +476,8 @@
     ]
     toward = pltpu.roll(y_weights(grid, ly, uy), n, 1)
     lane = lax.broadcasted_iota(jnp.int32, (1, d), 1)
-    sums.append(-(y_faces[0] * jnp.where(lane < n, toward, 0.0)))
-    sums.append(-(y_faces[1] * jnp.where(lane < n, 0.0, toward)))
+    sums.append(-(high2[n : n + size, :] * jnp.where(lane < n, toward, 0.0)))
+    sums.append(-(low2[n : n + size, :] * jnp.where(lane < n, 0.0, toward)))
     top = v[-w:]
     for k in range(pairs):
         weight = vents[k] * top
@@ -501,7 +504,7 @@
         pay[slot] = block
 
 
-def k_combine(grid, table, rec, weights, zm, base, vent, out, pay, scratch):
+def k_combine(grid, table, rec, weights, zm, base, vent, out, wide, pay, scratch):
     size = zm.shape[0]
     count = weights.shape[0]
     total = None
@@ -510,14 +513,14 @@
         for i in range(count):
             at = table[j * count + i]
             line, side = divmod(opposite(i), 2)
-            term = rec[jnp.maximum(at, 0), line : line + 1, :]
-            term = jnp.where(at >= 0, term, 0.0)
+            term = rec[at, line : line + 1, :]
             sides[side] = term if sides[side] is None else sides[side] + term
         term = weights[j] * (sides[0][:, 0:size] + sides[1][:, size : 2 * size])
         total = term if total is None else total + term
     expand(grid, zm, jnp.sum(total, axis=1, keepdims=True), scratch)
     result = base[...] - scratch[...]
     out[...] = result
+    wide[0 : grid.rows, :] = result
     to_all(grid, pay, vent[...] * result[-grid.width :], result)
 
 
@@ -549,8 +552,8 @@
 
 
 def k_blocks(
-    grid, pairs, cols, scale, ids, coef, vents, names, zm, mine, others, far, own, inverse,
-    face_y, y_faces, solves, _, out, weights, table, w3,
+    grid, pairs, cols, scale, ids, coef, vents, names, zm, mine, others, x_far, own, inverse,
+    face_y, low2, high2, solves, _, out, weights, table, w3,
 ):
     n, d, w, layers = grid.rows, grid.depth, grid.width, grid.layers
     rows, size = out.shape[0], out.shape[1]
@@ -570,10 +573,8 @@
             if j > 0:
                 met = jnp.sum(jnp.where(lane == k, names[j - 1 : j, :], 0.0)).astype(jnp.int32)
             places.append((met, c))
-        there = (r >= 0) & (r < rows) & (c >= 0) & (c < cols)
         for i, (pr, pc) in enumerate(places):
-            good = there & (pr >= 0) & (pr < rows) & (pc >= 0) & (pc < cols)
-            table[j * count + i] = jnp.where(good, pr * cols + pc, -1)
+            table[j * count + i] = lax.rem(pr + 2 * rows, rows) * cols + lax.rem(pc + 2 * cols, cols)
 
     def dot(a, b):
         return lax.dot_general(
@@ -588,16 +589,16 @@
     def basis_rows(at):
         return [zm[:, i * d : (i + 1) * d] for i in at]
 
-    next_first, prev_last = [f.astype(BF16) for f in x_faces(grid, pairs, ids, others, far)]
+    next_first, prev_last = [f.astype(BF16) for f in x_faces(grid, pairs, ids, others, x_far)]
     found = [
         weighted_gram(w3, basis_rows(last), [-ux[i : i + 1] for i in last], next_first),
         weighted_gram(w3, basis_rows(first), [-lx[i : i + 1] for i in first], prev_last),
     ]
     toward = -pltpu.roll(y_weights(grid, ly, uy), n, 1)
     swapped = pltpu.roll(face_y[...], n, 1)
-    for k, there in ((0, lane < n), (1, lane >= n)):
+    for theirs, there in ((high2, lane < n), (low2, lane >= n)):
         weight = jnp.where(there, toward, 0.0)
-        found.append(weighted_gram(w3, [swapped], [weight], y_faces[k].astype(BF16)))
+        found.append(weighted_gram(w3, [swapped], [weight], theirs[n : n + size, :].astype(BF16)))
     top = basis_rows(range(n - w, n))
     for k in range(pairs):
         panel = chosen(grid, pairs, ids, mine, others, k, slice(0, w * d)).astype(BF16)
@@ -612,9 +613,11 @@
         out[ids[k]] = out[ids[k]] + found[4 + k] * scale
 
     weights[0] = inverse[...]
-    for j, block in enumerate(found):
-        theirs = jnp.concatenate([solves[j, :, 0:size], solves[j, :, size:]], axis=0)
-        weights[j + 1] = -dot(inverse[...], dot(block, theirs))
+    start, stop = n + size, n + size + size // 2
+    folded = [solves[0], solves[1], high2[start:stop, :], low2[start:stop, :]]
+    folded += [solves[2 + k] for k in range(pairs)]
+    for j, (block, theirs) in enumerate(zip(found, folded)):
+        weights[j + 1] = -dot(inverse[...], dot(block, unfold(theirs)))
 
 
 def call(kernel, outs, operands, scratch=(), smem=0, free=(), smem_outs=(), cost=None):
@@ -651,6 +654,7 @@
     field = ((n, depth), F32)
     pay = ((row_count, width + 2 * layers, depth), F32)
     small = ((size, size), F32)
+    wide = ((max(n + size + size // 2, row_count * (width + 2 * layers) + 8), depth), F32)
 
     def cyclic(value, axis, step):
         count = lax.axis_size(axis)
@@ -669,20 +673,20 @@
     def rows_of(count):
         return ((row_count, width + 2 * layers + count, depth), F32)
 
-    zm, panel, faces = call(
+    zm, panel, face = call(
         functools.partial(k_order, grid),
         (
             ((size, n * depth), BF16),
             ((size, width * depth), BF16),
-            ((size, 2 * layers * depth), BF16),
+            ((size, layers * depth), BF16),
         ),
         (basis,),
         scratch=(pltpu.VMEM((size * n, depth), F32),),
         cost=pl.CostEstimate(flops=1000, bytes_accessed=1000, transcendentals=0),
     )
     held = [xor_step(panel, "row", k) for k in range(2, row_count, 2)]
-    far = lax.ppermute(
-        faces,
+    x_far = lax.ppermute(
+        face,
         "row",
         [(i, (i + 1 if i % 2 else i - 1) % row_count) for i in range(row_count)],
     )
@@ -720,7 +724,7 @@
             ((7, n, depth), F32),
             small,
             small,
-            ((n + size // 2 + size, depth), F32),
+            field,
             rows_of(size // 2),
             panels,
             ((size, (pairs * width + layers) * depth), BF16),
@@ -742,14 +746,15 @@
     others = xor_step(wanted, "row", 1)
     rec1, low1, high1 = exchange(sent, pay1)
     places = 5 + pairs
-    x0, pay2, solves, y_faces = call(
+    x0, wide2, pay2, solves = call(
         functools.partial(k_coarse, grid, pairs),
-        (field, pay, ((4 + pairs, size // 2, depth), F32), ((2, size, depth), F32)),
-        (ids, coef, vent, zm, inverse, sent, rec1, low1, high1),
+        (field, wide, pay, ((2 + pairs, size // 2, depth), F32)),
+        (ids, coef, vent, zm, inverse, sent, rec1, low1, high1, face_y, others, x_far),
         scratch=(pltpu.VMEM((n, depth), F32),),
         smem=1,
-    )
-    rec, low, high = exchange(x0, pay2)
+        free=(10, 11),
+    )
+    rec, low2, high2 = exchange(wide2, pay2)
 
     def everyone(lines):
         return ((row_count * col_count, lines, depth), F32)
@@ -758,7 +763,7 @@
         functools.partial(k_partials, grid, pairs, True),
         (field, everyone((places + 1) // 2)),
         (
-            ids, coef, vent, x0, rec, low, high, vents, zm, y_faces, mine, others, far, rhs,
+            ids, coef, vent, x0, rec, low2, high2, vents, zm, low2, high2, mine, others, x_far, rhs,
         ),
         smem=1,
     )
@@ -770,41 +775,41 @@
             ((places * places,), jnp.int32),
         ),
         (
-            ids, coef, vents, names, zm, mine, others, far, own, inverse, face_y, y_faces,
-            solves, pay3,
+            ids, coef, vents, names, zm, mine, others, x_far, own, inverse, face_y, low2,
+            high2, solves, pay3,
         ),
         scratch=(pltpu.VMEM((3 * size, width * depth), BF16),),
         smem=1,
-        free=(13,),
+        free=(14,),
         smem_outs=(2,),
         cost=pl.CostEstimate(flops=100_000_000, bytes_accessed=4_000_000, transcendentals=0),
     )
     sums = lax.all_to_all(pay3, ("row", "col"), 0, 0)
-    p0, pay4 = call(
+    p0, wide4, pay4 = call(
         functools.partial(k_combine, grid),
-        (field, pay),
+        (field, wide, pay),
         (table, sums, weights, zm, r0, vent),
         scratch=(pltpu.VMEM((n, depth), F32),),
         smem=1,
     )
-    rec, low, high = exchange(p0, pay4)
+    rec, low, high = exchange(wide4, pay4)
     i0, pay5 = call(
         functools.partial(k_partials, grid, pairs, False),
         (field, everyone((places + 1) // 2)),
         (
-            ids, coef, vent, p0, rec, low, high, vents, zm, y_faces, mine, others, far,
+            ids, coef, vent, p0, rec, low, high, vents, zm, low2, high2, mine, others, x_far,
         ),
         smem=1,
     )
     sums = lax.all_to_all(pay5, ("row", "col"), 0, 0)
-    d0, pay6 = call(
+    d0, wide6, pay6 = call(
         functools.partial(k_combine, grid),
-        (field, pay),
+        (field, wide, pay),
         (table, sums, weights, zm, i0, vent),
         scratch=(pltpu.VMEM((n, depth), F32),),
         smem=1,
     )
-    rec, low, high = exchange(d0, pay6)
+    rec, low, high = exchange(wide6, pay6)
     image, pay7 = call(
         functools.partial(k_dots, grid, pairs),
         (field, everyone(2)),

time: 112 us -> 109 us (0.973)
  blocking collectives: 20.7 us -> 43 us
  waiting for transfers between devices: 24.1 us -> 12.1 us
  starting transfers between devices: 41.1 us -> 30.2 us
  Pallas kernels: 22.9 us -> 20.8 us
    all_to_all x0 -> x3, blocking collectives: none -> 22.7 us  [exchange(): rec = lax.all_to_all(payload, 'row', 0, 0)]
    ppermute x10, waiting for transfers between devices: 19.7 us -> 4.74 us  [cyclic(): lax.ppermute(value, axis, [(i, (i + step) % count) for i in range(count)])]
    all_to_all x5 -> x2, starting transfers between devices: 19.2 us -> 8.44 us  [exchange(): rec = lax.all_to_all(payload, 'row', 0, 0)]
    ppermute x1, waiting for transfers between devices: 0.01 us -> 2.81 us  [body(): lax.ppermute(face, 'row', [(i, (i + 1 if i % 2 else i - 1) % row_count) f...]
    pallas_call x12, Pallas kernels: 22.9 us -> 20.8 us  [call(): pl.pallas_call(kernel, out_shape=tuple((jax.ShapeDtypeStruct(s, t) for s,...]
  transfers between devices with their start and end apart: 21 -> 18, of which waited for: 10 -> 4; matrix products, arithmetic and copies ran while one was open for 0% -> 0% of each run, Pallas kernels for 8% -> 6%
where the time goes in v5:
time: 109 us
  blocking collectives  43 us (39%)
  starting transfers between devices  30.2 us (28%)
  Pallas kernels  20.8 us (19%)
  waiting for transfers between devices  12.1 us (11%)
  local copies, waits for them, and re-layouts  1.9 us (2%)
    all_to_all x3, blocking collectives, exchange(): rec = lax.all_to_all(payload, 'row', 0, 0)  22.7 us
    pallas_call x12, Pallas kernels, call(): pl.pallas_call(kernel, out_shape=tuple((jax.ShapeDtypeStruct(s, t) for s,...  20.8 us
    ppermute x10, starting transfers between devices, cyclic(): lax.ppermute(value, axis, [(i, (i + step) % count) for i in range(count)])  11.8 us
    all_to_all x1, blocking collectives, body(): sums = lax.all_to_all(pay5, ('row', 'col'), 0, 0)  10.2 us
    all_to_all x1, blocking collectives, body(): total = lax.all_to_all(pay7, ('row', 'col'), 0, 0)  10.1 us
    all_to_all x2, starting transfers between devices, exchange(): rec = lax.all_to_all(payload, 'row', 0, 0)  8.44 us
    ppermute x10, waiting for transfers between devices, cyclic(): lax.ppermute(value, axis, [(i, (i + step) % count) for i in range(count)])  4.74 us
    ppermute x4, starting transfers between devices, xor_step(): return lax.ppermute(value, axis, [(i, i ^ k) for i in range(count)])  4.67 us
  transfers between devices with their start and end apart: 18, of which 4 were waited for; matrix products, arithmetic and copies ran while one was open for 0% of the time, Pallas kernels for 6%

profile of v5, /device:TPU:0, one launch (start us, length us, event | category | flops | bytes accessed | tf_op | source)
XLA Modules:
  0.0 108.8 jit_solution(9154129186554146432)
XLA Ops:
  1.9 1.5 %shard_map.95 = (bf16[64,8192]{1,0:T(8,128)(2,1)S(1)}, bf16[64,2048]{1,0:T(8,128)(2,1)S(1)}, bf16[64,512]{1,0:T(8,128)(2,1)S(1)}) custom-call(bf16[64,64,128]{2,1,0:T(8,128)(2,1)S(1)} %bitcast.9), custom_call_target="tpu_custom_call" | custom-call | flops 1000 | bytes 1000 | tf_op jit(solution)/shard_map/pallas_call | solution.py:627
  3.4 4.0 %collective-permute-start.4 = (bf16[64,2048]{1,0:T(8,128)(2,1)S(1)}, bf16[64,2048]{1,0:T(8,128)(2,1)S(1)}, u32[]{:S(2)}, u32[]{:S(2)}) collective-permute-start(bf16[64,2048]{1,0:T(8,128)(2,1)S(1)} %get-tuple-element.51), channel_id=1, source_target_pairs={{0,24},{4,28},{8,16},{12,20},{16,8},{20,12},{24,0},{28,4},{1,25},{... | collective-permute-start | bytes 786440 | tf_op jit(solution)/shard_map/ppermute | solution.py:665
  8.7 1.3 %shard_map.94 = (f32[72,128]{1,0:T(8,128)S(1)}, f32[64,128]{1,0:T(8,128)S(1)}, f32[16,128]{1,0:T(8,128)S(1)}, f32[8,32,128]{2,1,0:T(8,128)}) custom-call(s32[64,128]{1,0:T(8,128)S(1)} %bitcast.12, f32[8]{0:T(128)S(1)} %copy-done.5, f32[8]{0:T(128)S(1)} %copy-done.6, f32[16,128]{1,0:T(8,128)S(1)} %copy-done.3, s32[2]{0:T(128)S(1)} %bitcast.13), custom_call_target="tpu_custom_call" | custom-call | tf_op jit(solution)/shard_map/pallas_call | solution.py:627
  10.0 4.1 %all-to-all-start = ((f32[8,32,128]{2,1,0:T(8,128)}), f32[8,32,128]{2,1,0:T(8,128)S(1)}, u32[]{:S(2)}, u32[]{:S(2)}) async-start(f32[8,32,128]{2,1,0:T(8,128)} %get-tuple-element.46), calls=%async_computation | async-start | bytes 262144 | tf_op jit(solution)/shard_map/all_to_all | solution.py:670
  14.1 3.6 %collective-permute-start.1 = (f32[72,128]{1,0:T(8,128)S(1)}, f32[72,128]{1,0:T(8,128)S(1)}, u32[]{:S(2)}, u32[]{:S(2)}) collective-permute-start(f32[72,128]{1,0:T(8,128)S(1)} %get-tuple-element.45.cond_ref.cond), channel_id=1, source_target_pairs={{0,3},{1,0},{2,1},{3,2},{4,7},{5,4},{6,5},{7,6},{8,11},{9,8},{10,9... | collective-permute-start | bytes 110600 | tf_op jit(solution)/shard_map/ppermute | solution.py:661
  17.8 2.8 %shard_map.96 = (f32[64,64]{1,0:T(8,128)S(1)}, f32[64,128]{1,0:T(8,128)S(1)}, f32[64,128]{1,0:T(8,128)S(1)}) custom-call(bf16[64,8192]{1,0:T(8,128)(2,1)S(1)} %get-tuple-element.47.zm, f32[64,128]{1,0:T(8,128)S(1)} %bitcast.10, f32[72,128]{1,0:T(8,128)S(1)} %get-tuple-element.45.cond_ref.cond, f32[64,128]{1,0:T(8,128)S(1)} %get-tuple-element.43.cap_ref.cap), custom_call_target="tpu_custom_call" | custom-call | flops 1000 | bytes 1000 | tf_op jit(solution)/shard_map/pallas_call | solution.py:627
  20.6 2.9 %collective-permute-done.cond_low = f32[72,128]{1,0:T(8,128)S(1)} collective-permute-done((f32[72,128]{1,0:T(8,128)S(1)}, f32[72,128]{1,0:T(8,128)S(1)}, u32[]{:S(2)}, u32[]{:S(2)}) %collective-permute-start) | collective-permute-done | bytes 36896 | tf_op jit(solution)/shard_map/ppermute | solution.py:661
  23.5 4.0 %shard_map.97 = (f32[7,64,128]{2,1,0:T(8,128)S(1)}, f32[64,64]{1,0:T(8,128)S(1)}, f32[64,64]{1,0:T(8,128)S(1)}, f32[64,128]{1,0:T(8,128)S(1)}, f32[8,56,128]{2,1...) custom-call(s32[4]{0:T(128)S(1)} %pad_add_fusion.ids, ...), custom_call_target="tpu_custom_call" | custom-call | tf_op jit(solution)/shard_map/pallas_call | solution.py:627
  27.6 4.3 %all-to-all-start.1 = ((f32[8,56,128]{2,1,0:T(8,128)}), f32[8,56,128]{2,1,0:T(8,128)S(1)}, u32[]{:S(2)}, u32[]{:S(2)}) async-start(f32[8,56,128]{2,1,0:T(8,128)} %get-tuple-element.61), calls=%async_computation.1 | async-start | bytes 458752 | tf_op jit(solution)/shard_map/all_to_all | solution.py:670
  31.9 2.7 %collective-permute-start.6 = (bf16[64,512]{1,0:T(8,128)(2,1)S(1)}, bf16[64,512]{1,0:T(8,128)(2,1)S(1)}, u32[]{:S(2)}, u32[]{:S(2)}) collective-permute-start(bf16[64,512]{1,0:T(8,128)(2,1)S(1)} %get-tuple-element.57), channel_id=1, source_target_pairs={{0,28},{4,8},{8,4},{12,16},{16,12},{20,24},{24,20},{28,0},{1,29},{... | collective-permute-start | bytes 196616 | tf_op jit(solution)/shard_map/ppermute | solution.py:688
  36.6 2.8 %collective-permute-done.6.__.far.x_far = bf16[64,512]{1,0:T(8,128)(2,1)S(1)} collective-permute-done((bf16[64,512]{1,0:T(8,128)(2,1)S(1)}, bf16[64,512]{1,0:T(8,128)(2,1)S(1)}, u32[]{:S(2)}, u32[]{:S(2)}) %collective-permute-start.6) | collective-permute-done | bytes 65568 | tf_op jit(solution)/shard_map/ppermute | solution.py:688
  39.4 1.8 %collective-permute-done.7.low = f32[64,128]{1,0:T(8,128)S(1)} collective-permute-done((f32[64,128]{1,0:T(8,128)S(1)}, f32[64,128]{1,0:T(8,128)S(1)}, u32[]{:S(2)}, u32[]{:S(2)}) %collective-permute-start.7) | collective-permute-done | bytes 32800 | tf_op jit(solution)/shard_map/ppermute | solution.py:661
  42.6 2.0 %collective-permute-start.9 = (f32[200,128]{1,0:T(8,128)S(1)}, f32[200,128]{1,0:T(8,128)S(1)}, u32[]{:S(2)}, u32[]{:S(2)}) collective-permute-start(f32[200,128]{1,0:T(8,128)S(1)} %get-tuple-element.62), channel_id=1, source_target_pairs={{0,1},{1,2},{2,3},{3,0},{4,5},{5,6},{6,7},{7,4},{8,9},{9,10},{10,1... | collective-permute-start | bytes 307208 | tf_op jit(solution)/shard_map/ppermute | solution.py:661
  44.6 7.6 %all_to_all.40.rec = f32[8,24,128]{2,1,0:T(8,128)S(1)} all-to-all(f32[8,24,128]{2,1,0:T(8,128)S(1)} %get-tuple-element.65), channel_id=1, replica_groups=mesh['row'=8,'col'=4] {'row'}, dimensions={0} | all-to-all | bytes 196608 | tf_op jit(solution)/shard_map/all_to_all | solution.py:670
  52.2 2.1 %shard_map.99 = (f32[64,128]{1,0:T(8,128)S(1)}, f32[32,4,128]{2,1,0:T(4,128)}) custom-call(s32[4]{0:T(128)S(1)} %pad_add_fusion.ids, f32[7,64,128]{2,1,0:T(8,128)S(1)} %get-tuple-element.52.coef, f32[16,128]{1,0:T(8,128)S(1)} %get-tuple-element.44.vent, f32[64,128]{1,0:T(8,128)S(1)} %get-tuple-element.64.field.x0, f32[8,24,128]{2,1,0:T(8,128)S(1)} %all_to_all.40.rec, ...), custom_call_target="tpu_custom_call" | custom-call | tf_op jit(solution)/shard_map/pallas_call | solution.py:627
  54.3 2.5 %all-to-all-start.3 = ((f32[32,4,128]{2,1,0:T(4,128)}), f32[32,4,128]{2,1,0:T(4,128)S(1)}, u32[]{:S(2)}, u32[]{:S(2)}) async-start(f32[32,4,128]{2,1,0:T(4,128)} %get-tuple-element.66._), calls=%async_computation.3 | async-start | bytes 131072 | tf_op jit(solution)/shard_map/all_to_all | solution.py:787
  56.8 2.9 %shard_map.100 = (f32[8,64,64]{2,1,0:T(8,128)}, f32[7,64,64]{2,1,0:T(8,128)S(1)}, s32[49]{0:T(128)S(1)}) custom-call(s32[4]{0:T(128)S(1)} %pad_add_fusion.ids, f32[7,64,128]{2,1,0:T(8,128)S(1)} %get-tuple-element.52.coef, f32[2,16,128]{2,1,0:T(8,128)S(1)} %get-tuple-element.53.vents, f32[6,128]{1,0:T(8,128)S(1)} %get-tuple-element.54.names, ...), custom_call_target="tpu_custom_call" | custom-call | flops 100000000 | bytes 4000000 | tf_op jit(solution)/shard_map/pallas_call | solution.py:627
  59.7 4.6 %all-to-all-done.3.rec = f32[32,4,128]{2,1,0:T(4,128)S(1)} async-done(((f32[32,4,128]{2,1,0:T(4,128)}), f32[32,4,128]{2,1,0:T(4,128)S(1)}, u32[]{:S(2)}, u32[]{:S(2)}) %all-to-all-start.3) | async-done | bytes 65568 | tf_op jit(solution)/shard_map/all_to_all | solution.py:787
  66.1 1.3 %collective-permute-start.11 = (f32[200,128]{1,0:T(8,128)S(1)}, f32[200,128]{1,0:T(8,128)S(1)}, u32[]{:S(2)}, u32[]{:S(2)}) collective-permute-start(f32[200,128]{1,0:T(8,128)S(1)} %get-tuple-element.72), channel_id=1, source_target_pairs={{0,1},{1,2},{2,3},{3,0},{4,5},{5,6},{6,7},{7,4},{8,9},{9,10},{10,1... | collective-permute-start | bytes 307208 | tf_op jit(solution)/shard_map/ppermute | solution.py:661
  67.3 7.6 %all_to_all.41.rec = f32[8,24,128]{2,1,0:T(8,128)S(1)} all-to-all(f32[8,24,128]{2,1,0:T(8,128)S(1)} %get-tuple-element.71), channel_id=1, replica_groups=mesh['row'=8,'col'=4] {'row'}, dimensions={0} | all-to-all | bytes 196608 | tf_op jit(solution)/shard_map/all_to_all | solution.py:670
  74.9 1.5 %shard_map.102 = (f32[64,128]{1,0:T(8,128)S(1)}, f32[32,4,128]{2,1,0:T(4,128)S(1)}) custom-call(s32[4]{0:T(128)S(1)} %pad_add_fusion.ids, f32[7,64,128]{2,1,0:T(8,128)S(1)} %get-tuple-element.52.coef, f32[16,128]{1,0:T(8,128)S(1)} %get-tuple-element.44.vent, f32[64,128]{1,0:T(8,128)S(1)} %get-tuple-element.70.field.p0, f32[8,24,128]{2,1,0:T(8,128)S(1)} %all_to_all.41.rec, ...), custom_call_target="tpu_custom_call" | custom-call | tf_op jit(solution)/shard_map/pallas_call | solution.py:627
  76.4 10.2 %all_to_all.42.rec = f32[32,4,128]{2,1,0:T(4,128)S(1)} all-to-all(f32[32,4,128]{2,1,0:T(4,128)S(1)} %get-tuple-element.73), channel_id=1, replica_groups=mesh['row'=8,'col'=4] {'row','col'}, dimensions={0} | all-to-all | bytes 131072 | tf_op jit(solution)/shard_map/all_to_all | solution.py:804
  89.6 7.6 %all_to_all.43.rec = f32[8,24,128]{2,1,0:T(8,128)S(1)} all-to-all(f32[8,24,128]{2,1,0:T(8,128)S(1)} %get-tuple-element.76), channel_id=1, replica_groups=mesh['row'=8,'col'=4] {'row'}, dimensions={0} | all-to-all | bytes 196608 | tf_op jit(solution)/shard_map/all_to_all | solution.py:670
  98.0 10.1 %all_to_all.44.rec = f32[32,2,128]{2,1,0:T(2,128)S(1)} all-to-all(f32[32,2,128]{2,1,0:T(2,128)S(1)} %get-tuple-element.78), channel_id=1, replica_groups=mesh['row'=8,'col'=4] {'row','col'}, dimensions={0} | all-to-all | bytes 65536 | tf_op jit(solution)/shard_map/all_to_all | solution.py:819
  (44 shorter events, 12.4 us)
Async XLA Ops:
  0.6 1.2 %copy-start = (bf16[64,4,16,128]{3,2,1,0:T(8,128)(2,1)S(1)}, bf16[64,4,16,128]{3,2,1,0:T(8,128)(2,1)}, u32[]{:S(2)}) copy-start(bf16[64,4,16,128]{3,2,1,0:T(8,128)(2,1)} %param.13) | copy-start | bytes 3145732
  1.9 6.1 %copy-start.2 = (s32[4,16,128]{2,1,0:T(8,128)S(1)}, s32[4,16,128]{2,1,0:T(8,128)}, u32[]{:S(2)}) copy-start(s32[4,16,128]{2,1,0:T(8,128)} %param.8) | copy-start | bytes 98308
  1.9 6.1 %copy-start.3 = (f32[16,128]{1,0:T(8,128)S(1)}, f32[16,128]{1,0:T(8,128)}, u32[]{:S(2)}) copy-start(f32[16,128]{1,0:T(8,128)} %vent.1) | copy-start | bytes 24580
  3.4 20.1 %collective-permute-start.4 = (bf16[64,2048]{1,0:T(8,128)(2,1)S(1)}, bf16[64,2048]{1,0:T(8,128)(2,1)S(1)}, u32[]{:S(2)}, u32[]{:S(2)}) collective-permute-start(bf16[64,2048]{1,0:T(8,128)(2,1)S(1)} %get-tuple-element.51), channel_id=1, source_target_pairs={{0,24},{4,28},{8,16},{12,20},{16,8},{20,12},{24,0},{28,4},{1,25},{... | collective-permute-start | bytes 786440 | tf_op jit(solution)/shard_map/ppermute | solution.py:665
  7.3 16.2 %collective-permute-start.3 = (bf16[64,2048]{1,0:T(8,128)(2,1)S(1)}, bf16[64,2048]{1,0:T(8,128)(2,1)S(1)}, u32[]{:S(2)}, u32[]{:S(2)}) collective-permute-start(bf16[64,2048]{1,0:T(8,128)(2,1)S(1)} %get-tuple-element.51), channel_id=1, source_target_pairs={{0,16},{4,20},{8,24},{12,28},{16,0},{20,4},{24,8},{28,12},{1,17},{... | collective-permute-start | bytes 786440 | tf_op jit(solution)/shard_map/ppermute | solution.py:665
  7.8 15.7 %collective-permute-start.2 = (bf16[64,2048]{1,0:T(8,128)(2,1)S(1)}, bf16[64,2048]{1,0:T(8,128)(2,1)S(1)}, u32[]{:S(2)}, u32[]{:S(2)}) collective-permute-start(bf16[64,2048]{1,0:T(8,128)(2,1)S(1)} %get-tuple-element.51), channel_id=1, source_target_pairs={{0,8},{4,12},{8,0},{12,4},{16,24},{20,28},{24,16},{28,20},{1,9},{5... | collective-permute-start | bytes 786440 | tf_op jit(solution)/shard_map/ppermute | solution.py:665
  8.0 0.7 copy-start.5
  8.0 0.7 copy-start.6
  10.0 7.8 %copy-start.1 = (f32[4,16,128]{2,1,0:T(8,128)S(1)}, f32[4,16,128]{2,1,0:T(8,128)}, u32[]{:S(2)}) copy-start(f32[4,16,128]{2,1,0:T(8,128)} %param.7) | copy-start | bytes 98308
  10.0 13.5 %all-to-all-start = ((f32[8,32,128]{2,1,0:T(8,128)}), f32[8,32,128]{2,1,0:T(8,128)S(1)}, u32[]{:S(2)}, u32[]{:S(2)}) async-start(f32[8,32,128]{2,1,0:T(8,128)} %get-tuple-element.46), calls=%async_computation | async-start | bytes 262144 | tf_op jit(solution)/shard_map/all_to_all | solution.py:670
  14.1 6.5 %collective-permute-start.1 = (f32[72,128]{1,0:T(8,128)S(1)}, f32[72,128]{1,0:T(8,128)S(1)}, u32[]{:S(2)}, u32[]{:S(2)}) collective-permute-start(f32[72,128]{1,0:T(8,128)S(1)} %get-tuple-element.45.cond_ref.cond), channel_id=1, source_target_pairs={{0,3},{1,0},{2,1},{3,2},{4,7},{5,4},{6,5},{7,6},{8,11},{9,8},{10,9... | collective-permute-start | bytes 110600 | tf_op jit(solution)/shard_map/ppermute | solution.py:661
  17.7 5.8 %collective-permute-start = (f32[72,128]{1,0:T(8,128)S(1)}, f32[72,128]{1,0:T(8,128)S(1)}, u32[]{:S(2)}, u32[]{:S(2)}) collective-permute-start(f32[72,128]{1,0:T(8,128)S(1)} %get-tuple-element.45.cond_ref.cond), channel_id=1, source_target_pairs={{0,1},{1,2},{2,3},{3,0},{4,5},{5,6},{6,7},{7,4},{8,9},{9,10},{10,1... | collective-permute-start | bytes 110600 | tf_op jit(solution)/shard_map/ppermute | solution.py:661
  27.5 13.7 %collective-permute-start.5 = (bf16[64,4608]{1,0:T(8,128)(2,1)}, bf16[64,4608]{1,0:T(8,128)(2,1)S(1)}, u32[]{:S(2)}, u32[]{:S(2)}) collective-permute-start(bf16[64,4608]{1,0:T(8,128)(2,1)} %get-tuple-element.56), channel_id=1, source_target_pairs={{0,4},{4,0},{8,12},{12,8},{16,20},{20,16},{24,28},{28,24},{1,5},{5... | collective-permute-start | bytes 1769480 | tf_op jit(solution)/shard_map/ppermute | solution.py:665
  27.6 13.7 %all-to-all-start.1 = ((f32[8,56,128]{2,1,0:T(8,128)}), f32[8,56,128]{2,1,0:T(8,128)S(1)}, u32[]{:S(2)}, u32[]{:S(2)}) async-start(f32[8,56,128]{2,1,0:T(8,128)} %get-tuple-element.61), calls=%async_computation.1 | async-start | bytes 458752 | tf_op jit(solution)/shard_map/all_to_all | solution.py:670
  31.9 7.5 %collective-permute-start.6 = (bf16[64,512]{1,0:T(8,128)(2,1)S(1)}, bf16[64,512]{1,0:T(8,128)(2,1)S(1)}, u32[]{:S(2)}, u32[]{:S(2)}) collective-permute-start(bf16[64,512]{1,0:T(8,128)(2,1)S(1)} %get-tuple-element.57), channel_id=1, source_target_pairs={{0,28},{4,8},{8,4},{12,16},{16,12},{20,24},{24,20},{28,0},{1,29},{... | collective-permute-start | bytes 196616 | tf_op jit(solution)/shard_map/ppermute | solution.py:688
  34.6 4.8 %collective-permute-start.8 = (f32[64,128]{1,0:T(8,128)S(1)}, f32[64,128]{1,0:T(8,128)S(1)}, u32[]{:S(2)}, u32[]{:S(2)}) collective-permute-start(f32[64,128]{1,0:T(8,128)S(1)} %get-tuple-element.60.field), channel_id=1, source_target_pairs={{0,3},{1,0},{2,1},{3,2},{4,7},{5,4},{6,5},{7,6},{8,11},{9,8},{10,9... | collective-permute-start | bytes 98312 | tf_op jit(solution)/shard_map/ppermute | solution.py:661
  35.5 5.7 %collective-permute-start.7 = (f32[64,128]{1,0:T(8,128)S(1)}, f32[64,128]{1,0:T(8,128)S(1)}, u32[]{:S(2)}, u32[]{:S(2)}) collective-permute-start(f32[64,128]{1,0:T(8,128)S(1)} %get-tuple-element.60.field), channel_id=1, source_target_pairs={{0,1},{1,2},{2,3},{3,0},{4,5},{5,6},{6,7},{7,4},{8,9},{9,10},{10,1... | collective-permute-start | bytes 98312 | tf_op jit(solution)/shard_map/ppermute | solution.py:661
  42.5 9.6 %collective-permute-start.10 = (f32[200,128]{1,0:T(8,128)S(1)}, f32[200,128]{1,0:T(8,128)S(1)}, u32[]{:S(2)}, u32[]{:S(2)}) collective-permute-start(f32[200,128]{1,0:T(8,128)S(1)} %get-tuple-element.62), channel_id=1, source_target_pairs={{0,3},{1,0},{2,1},{3,2},{4,7},{5,4},{6,5},{7,6},{8,11},{9,8},{10,9... | collective-permute-start | bytes 307208 | tf_op jit(solution)/shard_map/ppermute | solution.py:661
  42.6 9.6 %collective-permute-start.9 = (f32[200,128]{1,0:T(8,128)S(1)}, f32[200,128]{1,0:T(8,128)S(1)}, u32[]{:S(2)}, u32[]{:S(2)}) collective-permute-start(f32[200,128]{1,0:T(8,128)S(1)} %get-tuple-element.62), channel_id=1, source_target_pairs={{0,1},{1,2},{2,3},{3,0},{4,5},{5,6},{6,7},{7,4},{8,9},{9,10},{10,1... | collective-permute-start | bytes 307208 | tf_op jit(solution)/shard_map/ppermute | solution.py:661
  54.3 10.0 %all-to-all-start.3 = ((f32[32,4,128]{2,1,0:T(4,128)}), f32[32,4,128]{2,1,0:T(4,128)S(1)}, u32[]{:S(2)}, u32[]{:S(2)}) async-start(f32[32,4,128]{2,1,0:T(4,128)} %get-tuple-element.66._), calls=%async_computation.3 | async-start | bytes 131072 | tf_op jit(solution)/shard_map/all_to_all | solution.py:787
  65.3 9.6 %collective-permute-start.12 = (f32[200,128]{1,0:T(8,128)S(1)}, f32[200,128]{1,0:T(8,128)S(1)}, u32[]{:S(2)}, u32[]{:S(2)}) collective-permute-start(f32[200,128]{1,0:T(8,128)S(1)} %get-tuple-element.72), channel_id=1, source_target_pairs={{0,3},{1,0},{2,1},{3,2},{4,7},{5,4},{6,5},{7,6},{8,11},{9,8},{10,9... | collective-permute-start | bytes 307208 | tf_op jit(solution)/shard_map/ppermute | solution.py:661
  66.1 8.9 %collective-permute-start.11 = (f32[200,128]{1,0:T(8,128)S(1)}, f32[200,128]{1,0:T(8,128)S(1)}, u32[]{:S(2)}, u32[]{:S(2)}) collective-permute-start(f32[200,128]{1,0:T(8,128)S(1)} %get-tuple-element.72), channel_id=1, source_target_pairs={{0,1},{1,2},{2,3},{3,0},{4,5},{5,6},{6,7},{7,4},{8,9},{9,10},{10,1... | collective-permute-start | bytes 307208 | tf_op jit(solution)/shard_map/ppermute | solution.py:661
  87.6 9.6 %collective-permute-start.14 = (f32[200,128]{1,0:T(8,128)S(1)}, f32[200,128]{1,0:T(8,128)S(1)}, u32[]{:S(2)}, u32[]{:S(2)}) collective-permute-start(f32[200,128]{1,0:T(8,128)S(1)} %get-tuple-element.77), channel_id=1, source_target_pairs={{0,3},{1,0},{2,1},{3,2},{4,7},{5,4},{6,5},{7,6},{8,11},{9,8},{10,9... | collective-permute-start | bytes 307208 | tf_op jit(solution)/shard_map/ppermute | solution.py:661
  88.4 8.8 %collective-permute-start.13 = (f32[200,128]{1,0:T(8,128)S(1)}, f32[200,128]{1,0:T(8,128)S(1)}, u32[]{:S(2)}, u32[]{:S(2)}) collective-permute-start(f32[200,128]{1,0:T(8,128)S(1)} %get-tuple-element.77), channel_id=1, source_target_pairs={{0,1},{1,2},{2,3},{3,0},{4,5},{5,6},{6,7},{7,4},{8,9},{9,10},{10,1... | collective-permute-start | bytes 307208 | tf_op jit(solution)/shard_map/ppermute | solution.py:661
  (1 other events, 0.7 us)

commit v6 on v5

--- a/solution.py
+++ b/solution.py
@@ -195,34 +195,18 @@
 
 
 def k_first(
-    grid, material, conductivity, capacity, vent, partners, cond_out, cap_out, vent_out, pay,
-    classes, cond_table, cap_table, pair_table, sems,
+    grid, conductivity, capacity, partners, material, vent, cond_out, cap_out, vent_out, pay
 ):
-    copies = [
-        pltpu.make_async_copy(src, dst, sems.at[i])
-        for i, (src, dst) in enumerate(
-            (
-                (material, classes),
-                (conductivity, cond_table),
-                (capacity, cap_table),
-                (vent, vent_out),
-                (partners, pair_table),
-            )
-        )
-    ]
-    for copy in copies:
-        copy.start()
-    for copy in copies:
-        copy.wait()
-    cond = lookup(classes[...], cond_table)
+    cond = lookup(material[...], conductivity)
     lane = lax.broadcasted_iota(jnp.int32, (8, grid.depth), 1)
     names = jnp.zeros((8, grid.depth), F32)
-    for k in range(pair_table.shape[0]):
-        names = jnp.where(lane == k, pair_table[k].astype(F32), names)
+    for k in range(partners.shape[0]):
+        names = jnp.where(lane == k, partners[k].astype(F32), names)
     cond_out[0 : grid.rows, :] = cond
     cond_out[grid.rows :, :] = names
-    cap_out[...] = lookup(classes[...], cap_table)
-    to_all(grid, pay, vent_out[...], cond, names)
+    cap_out[...] = lookup(material[...], capacity)
+    vent_out[...] = vent[...]
+    to_all(grid, pay, vent[...], cond, names)
 
 
 def conductances(grid, cond, low_x, high_x, low_y, high_y):
@@ -234,25 +218,22 @@
     return uz, lz, ux, lx, uy, ly
 
 
-def k_order(grid, basis, zm, panel, face, wide):
+def k_order(grid, basis, zm, panel, face):
     n, d, w, layers = grid.rows, grid.depth, grid.width, grid.layers
     size = basis.shape[0]
     odd = lax.bitwise_and(lax.axis_index("row"), 1) == 1
 
-    def unpack(a, _):
-        wide[pl.ds(a * n, n), :] = basis[a].astype(F32)
-        return 0
-
-    lax.fori_loop(0, size, unpack, 0, unroll=4)
-    for row in range(n):
-        packed = wide[pl.ds(row, size, stride=n), :].astype(BF16)
-        zm[:, row * d : (row + 1) * d] = packed
-        layer, x = divmod(row, w)
-        if layer == layers - 1:
-            panel[:, x * d : (x + 1) * d] = packed
+    for row in range(0, n, w):
+        for a in range(0, size, w):
+            turned = jnp.swapaxes(basis[a : a + w, row : row + w, :], 0, 1)
+            for i in range(w):
+                zm[a : a + w, (row + i) * d : (row + i + 1) * d] = turned[i]
+    panel[...] = zm[:, (n - w) * d :]
     for z in range(layers):
-        x = jnp.where(odd, w - 1, 0)
-        face[:, z * d : (z + 1) * d] = wide[pl.ds(z * w + x, size, stride=n), :].astype(BF16)
+        start = z * w * d
+        first = zm[:, start : start + d].astype(F32)
+        last = zm[:, start + (w - 1) * d : start + w * d].astype(F32)
+        face[:, z * d : (z + 1) * d] = jnp.where(odd, last, first).astype(BF16)
 
 
 def k_basis(grid, zm, rhs, cond_ref, cap_ref, own, projected, face_y, zr, w3, coef):
@@ -487,12 +468,13 @@
             term = part * weight[x : x + 1]
             total = term if total is None else total + term
         sums.append(-total)
-    ones = jnp.ones((8, d), F32)
+    eye = lax.broadcasted_iota(jnp.int32, (size, size), 0) == lax.broadcasted_iota(
+        jnp.int32, (size, size), 1
+    )
     rows = [
-        lax.dot_general(
-            ones, q, (((1,), (1,)), ((), ())),
-            precision=lax.Precision.HIGHEST, preferred_element_type=F32,
-        )[0:1]
+        jnp.sum(
+            jnp.where(eye, jnp.sum(q, axis=1, keepdims=True), 0.0), axis=0, keepdims=True
+        )
         for q in sums
     ]
     if len(rows) % 2:
@@ -681,7 +663,6 @@
             ((size, layers * depth), BF16),
         ),
         (basis,),
-        scratch=(pltpu.VMEM((size * n, depth), F32),),
         cost=pl.CostEstimate(flops=1000, bytes_accessed=1000, transcendentals=0),
     )
     held = [xor_step(panel, "row", k) for k in range(2, row_count, 2)]
@@ -693,15 +674,8 @@
     cond, cap, vent, pay0 = call(
         functools.partial(k_first, grid),
         (((n + 8, depth), F32), field, ((width, depth), F32), rows_of(8)),
-        (classes, conductivity, capacity, vent_open, partners.reshape(-1)),
-        scratch=(
-            pltpu.VMEM((n, depth), jnp.int32),
-            pltpu.SMEM(conductivity.shape, F32),
-            pltpu.SMEM(capacity.shape, F32),
-            pltpu.SMEM((pairs,), jnp.int32),
-            pltpu.SemaphoreType.DMA((5,)),
-        ),
-        free=(0, 1, 2, 3, 4),
+        (conductivity, capacity, partners.reshape(-1), classes, vent_open),
+        smem=3,
     )
     rec0, cond_low, cond_high = exchange(cond, pay0)
 

time: 109 us -> 108 us (level)
  Pallas kernels: 20.8 us -> 19.1 us
    pallas_call x12, Pallas kernels: 20.8 us -> 19.1 us  [call(): pl.pallas_call(kernel, out_shape=tuple((jax.ShapeDtypeStruct(s, t) for s,...]
where the time goes in v6:
time: 108 us; the launch traced here: 107 us
  blocking collectives  43 us (40%)
  starting transfers between devices  30.3 us (28%)
  Pallas kernels  19.1 us (18%)
  waiting for transfers between devices  12.1 us (11%)
  local copies, waits for them, and re-layouts  1.9 us (2%)
    all_to_all x3, blocking collectives, exchange(): rec = lax.all_to_all(payload, 'row', 0, 0)  22.7 us
    pallas_call x12, Pallas kernels, call(): pl.pallas_call(kernel, out_shape=tuple((jax.ShapeDtypeStruct(s, t) for s,...  19.1 us
    ppermute x10, starting transfers between devices, cyclic(): lax.ppermute(value, axis, [(i, (i + step) % count) for i in range(count)])  11.8 us
    all_to_all x1, blocking collectives, body(): sums = lax.all_to_all(pay5, ('row', 'col'), 0, 0)  10.2 us
    all_to_all x1, blocking collectives, body(): total = lax.all_to_all(pay7, ('row', 'col'), 0, 0)  10.1 us
    all_to_all x2, starting transfers between devices, exchange(): rec = lax.all_to_all(payload, 'row', 0, 0)  8.55 us
    ppermute x10, waiting for transfers between devices, cyclic(): lax.ppermute(value, axis, [(i, (i + step) % count) for i in range(count)])  4.75 us
    ppermute x4, starting transfers between devices, xor_step(): return lax.ppermute(value, axis, [(i, i ^ k) for i in range(count)])  4.67 us
  transfers between devices with their start and end apart: 18, of which 4 were waited for; matrix products, arithmetic and copies ran while one was open for 0% of the time, Pallas kernels for 6%

profile of v6, /device:TPU:0, one launch (start us, length us, event | category | flops | bytes accessed | tf_op | source)
XLA Modules:
  0.0 107.2 jit_solution(9012092260976279644)
XLA Ops:
  2.2 4.0 %collective-permute-start.4 = (bf16[64,2048]{1,0:T(8,128)(2,1)S(1)}, bf16[64,2048]{1,0:T(8,128)(2,1)S(1)}, u32[]{:S(2)}, u32[]{:S(2)}) collective-permute-start(bf16[64,2048]{1,0:T(8,128)(2,1)S(1)} %get-tuple-element.51), channel_id=1, source_target_pairs={{0,24},{4,28},{8,16},{12,20},{16,8},{20,12},{24,0},{28,4},{1,25},{... | collective-permute-start | bytes 786440 | tf_op jit(solution)/shard_map/ppermute | solution.py:647
  7.5 1.2 %shard_map.94 = (f32[72,128]{1,0:T(8,128)S(1)}, f32[64,128]{1,0:T(8,128)S(1)}, f32[16,128]{1,0:T(8,128)S(1)}, f32[8,32,128]{2,1,0:T(8,128)}) custom-call(f32[8]{0:T(128)S(1)} %copy-done.5, f32[8]{0:T(128)S(1)} %copy-done.6, s32[2]{0:T(128)S(1)} %bitcast.13, s32[64,128]{1,0:T(8,128)S(1)} %bitcast.12, f32[16,128]{1,0:T(8,128)S(1)} %copy-done.3), custom_call_target="tpu_custom_call" | custom-call | tf_op jit(solution)/shard_map/pallas_call | solution.py:609
  8.8 4.3 %all-to-all-start = ((f32[8,32,128]{2,1,0:T(8,128)}), f32[8,32,128]{2,1,0:T(8,128)S(1)}, u32[]{:S(2)}, u32[]{:S(2)}) async-start(f32[8,32,128]{2,1,0:T(8,128)} %get-tuple-element.46), calls=%async_computation | async-start | bytes 262144 | tf_op jit(solution)/shard_map/all_to_all | solution.py:652
  13.0 3.6 %collective-permute-start.1 = (f32[72,128]{1,0:T(8,128)S(1)}, f32[72,128]{1,0:T(8,128)S(1)}, u32[]{:S(2)}, u32[]{:S(2)}) collective-permute-start(f32[72,128]{1,0:T(8,128)S(1)} %get-tuple-element.45.cond_ref.cond), channel_id=1, source_target_pairs={{0,3},{1,0},{2,1},{3,2},{4,7},{5,4},{6,5},{7,6},{8,11},{9,8},{10,9... | collective-permute-start | bytes 110600 | tf_op jit(solution)/shard_map/ppermute | solution.py:643
  16.7 2.8 %shard_map.96 = (f32[64,64]{1,0:T(8,128)S(1)}, f32[64,128]{1,0:T(8,128)S(1)}, f32[64,128]{1,0:T(8,128)S(1)}) custom-call(bf16[64,8192]{1,0:T(8,128)(2,1)S(1)} %get-tuple-element.47.zm, f32[64,128]{1,0:T(8,128)S(1)} %bitcast.10, f32[72,128]{1,0:T(8,128)S(1)} %get-tuple-element.45.cond_ref.cond, f32[64,128]{1,0:T(8,128)S(1)} %get-tuple-element.43.cap_ref.cap), custom_call_target="tpu_custom_call" | custom-call | flops 1000 | bytes 1000 | tf_op jit(solution)/shard_map/pallas_call | solution.py:609
  19.5 2.9 %collective-permute-done.cond_low = f32[72,128]{1,0:T(8,128)S(1)} collective-permute-done((f32[72,128]{1,0:T(8,128)S(1)}, f32[72,128]{1,0:T(8,128)S(1)}, u32[]{:S(2)}, u32[]{:S(2)}) %collective-permute-start) | collective-permute-done | bytes 36896 | tf_op jit(solution)/shard_map/ppermute | solution.py:643
  22.4 4.0 %shard_map.97 = (f32[7,64,128]{2,1,0:T(8,128)S(1)}, f32[64,64]{1,0:T(8,128)S(1)}, f32[64,64]{1,0:T(8,128)S(1)}, f32[64,128]{1,0:T(8,128)S(1)}, f32[8,56,128]{2,1...) custom-call(s32[4]{0:T(128)S(1)} %pad_add_fusion.ids, ...), custom_call_target="tpu_custom_call" | custom-call | tf_op jit(solution)/shard_map/pallas_call | solution.py:609
  26.5 4.3 %all-to-all-start.1 = ((f32[8,56,128]{2,1,0:T(8,128)}), f32[8,56,128]{2,1,0:T(8,128)S(1)}, u32[]{:S(2)}, u32[]{:S(2)}) async-start(f32[8,56,128]{2,1,0:T(8,128)} %get-tuple-element.61), calls=%async_computation.1 | async-start | bytes 458752 | tf_op jit(solution)/shard_map/all_to_all | solution.py:652
  30.8 2.7 %collective-permute-start.6 = (bf16[64,512]{1,0:T(8,128)(2,1)S(1)}, bf16[64,512]{1,0:T(8,128)(2,1)S(1)}, u32[]{:S(2)}, u32[]{:S(2)}) collective-permute-start(bf16[64,512]{1,0:T(8,128)(2,1)S(1)} %get-tuple-element.57), channel_id=1, source_target_pairs={{0,28},{4,8},{8,4},{12,16},{16,12},{20,24},{24,20},{28,0},{1,29},{... | collective-permute-start | bytes 196616 | tf_op jit(solution)/shard_map/ppermute | solution.py:669
  35.5 2.8 %collective-permute-done.6.__.far.x_far = bf16[64,512]{1,0:T(8,128)(2,1)S(1)} collective-permute-done((bf16[64,512]{1,0:T(8,128)(2,1)S(1)}, bf16[64,512]{1,0:T(8,128)(2,1)S(1)}, u32[]{:S(2)}, u32[]{:S(2)}) %collective-permute-start.6) | collective-permute-done | bytes 65568 | tf_op jit(solution)/shard_map/ppermute | solution.py:669
  38.3 1.8 %collective-permute-done.7.low = f32[64,128]{1,0:T(8,128)S(1)} collective-permute-done((f32[64,128]{1,0:T(8,128)S(1)}, f32[64,128]{1,0:T(8,128)S(1)}, u32[]{:S(2)}, u32[]{:S(2)}) %collective-permute-start.7) | collective-permute-done | bytes 32800 | tf_op jit(solution)/shard_map/ppermute | solution.py:643
  40.1 1.3 %shard_map.98 = (f32[64,128]{1,0:T(8,128)S(1)}, f32[200,128]{1,0:T(8,128)S(1)}, f32[8,24,128]{2,1,0:T(8,128)S(1)}, f32[4,32,128]{2,1,0:T(8,128)S(1)}) custom-call(s32[4]{0:T(128)S(1)} %pad_add_fusion.ids, f32[7,64,128]{2,1,0:T(8,128)S(1)} %get-tuple-element.52.coef, f32[16,128]{1,0:T(8,128)S(1)} %get-tuple-element.44.vent, ...), custom_call_target="tpu_custom_call" | custom-call | tf_op jit(solution)/shard_map/pallas_call | solution.py:609
  41.5 2.0 %collective-permute-start.9 = (f32[200,128]{1,0:T(8,128)S(1)}, f32[200,128]{1,0:T(8,128)S(1)}, u32[]{:S(2)}, u32[]{:S(2)}) collective-permute-start(f32[200,128]{1,0:T(8,128)S(1)} %get-tuple-element.62), channel_id=1, source_target_pairs={{0,1},{1,2},{2,3},{3,0},{4,5},{5,6},{6,7},{7,4},{8,9},{9,10},{10,1... | collective-permute-start | bytes 307208 | tf_op jit(solution)/shard_map/ppermute | solution.py:643
  43.5 7.6 %all_to_all.40.rec = f32[8,24,128]{2,1,0:T(8,128)S(1)} all-to-all(f32[8,24,128]{2,1,0:T(8,128)S(1)} %get-tuple-element.65), channel_id=1, replica_groups=mesh['row'=8,'col'=4] {'row'}, dimensions={0} | all-to-all | bytes 196608 | tf_op jit(solution)/shard_map/all_to_all | solution.py:652
  51.1 1.8 %shard_map.99 = (f32[64,128]{1,0:T(8,128)S(1)}, f32[32,4,128]{2,1,0:T(4,128)}) custom-call(s32[4]{0:T(128)S(1)} %pad_add_fusion.ids, f32[7,64,128]{2,1,0:T(8,128)S(1)} %get-tuple-element.52.coef, f32[16,128]{1,0:T(8,128)S(1)} %get-tuple-element.44.vent, f32[64,128]{1,0:T(8,128)S(1)} %get-tuple-element.64.field.x0, f32[8,24,128]{2,1,0:T(8,128)S(1)} %all_to_all.40.rec, ...), custom_call_target="tpu_custom_call" | custom-call | tf_op jit(solution)/shard_map/pallas_call | solution.py:609
  52.9 2.5 %all-to-all-start.3 = ((f32[32,4,128]{2,1,0:T(4,128)}), f32[32,4,128]{2,1,0:T(4,128)S(1)}, u32[]{:S(2)}, u32[]{:S(2)}) async-start(f32[32,4,128]{2,1,0:T(4,128)} %get-tuple-element.66._), calls=%async_computation.3 | async-start | bytes 131072 | tf_op jit(solution)/shard_map/all_to_all | solution.py:761
  55.4 2.9 %shard_map.100 = (f32[8,64,64]{2,1,0:T(8,128)}, f32[7,64,64]{2,1,0:T(8,128)S(1)}, s32[49]{0:T(128)S(1)}) custom-call(s32[4]{0:T(128)S(1)} %pad_add_fusion.ids, f32[7,64,128]{2,1,0:T(8,128)S(1)} %get-tuple-element.52.coef, f32[2,16,128]{2,1,0:T(8,128)S(1)} %get-tuple-element.53.vents, f32[6,128]{1,0:T(8,128)S(1)} %get-tuple-element.54.names, ...), custom_call_target="tpu_custom_call" | custom-call | flops 100000000 | bytes 4000000 | tf_op jit(solution)/shard_map/pallas_call | solution.py:609
  58.4 4.6 %all-to-all-done.3.rec = f32[32,4,128]{2,1,0:T(4,128)S(1)} async-done(((f32[32,4,128]{2,1,0:T(4,128)}), f32[32,4,128]{2,1,0:T(4,128)S(1)}, u32[]{:S(2)}, u32[]{:S(2)}) %all-to-all-start.3) | async-done | bytes 65568 | tf_op jit(solution)/shard_map/all_to_all | solution.py:761
  64.7 1.3 %collective-permute-start.11 = (f32[200,128]{1,0:T(8,128)S(1)}, f32[200,128]{1,0:T(8,128)S(1)}, u32[]{:S(2)}, u32[]{:S(2)}) collective-permute-start(f32[200,128]{1,0:T(8,128)S(1)} %get-tuple-element.72), channel_id=1, source_target_pairs={{0,1},{1,2},{2,3},{3,0},{4,5},{5,6},{6,7},{7,4},{8,9},{9,10},{10,1... | collective-permute-start | bytes 307208 | tf_op jit(solution)/shard_map/ppermute | solution.py:643
  66.0 7.6 %all_to_all.41.rec = f32[8,24,128]{2,1,0:T(8,128)S(1)} all-to-all(f32[8,24,128]{2,1,0:T(8,128)S(1)} %get-tuple-element.71), channel_id=1, replica_groups=mesh['row'=8,'col'=4] {'row'}, dimensions={0} | all-to-all | bytes 196608 | tf_op jit(solution)/shard_map/all_to_all | solution.py:652
  73.5 1.2 %shard_map.102 = (f32[64,128]{1,0:T(8,128)S(1)}, f32[32,4,128]{2,1,0:T(4,128)S(1)}) custom-call(s32[4]{0:T(128)S(1)} %pad_add_fusion.ids, f32[7,64,128]{2,1,0:T(8,128)S(1)} %get-tuple-element.52.coef, f32[16,128]{1,0:T(8,128)S(1)} %get-tuple-element.44.vent, f32[64,128]{1,0:T(8,128)S(1)} %get-tuple-element.70.field.p0, f32[8,24,128]{2,1,0:T(8,128)S(1)} %all_to_all.41.rec, ...), custom_call_target="tpu_custom_call" | custom-call | tf_op jit(solution)/shard_map/pallas_call | solution.py:609
  74.8 10.2 %all_to_all.42.rec = f32[32,4,128]{2,1,0:T(4,128)S(1)} all-to-all(f32[32,4,128]{2,1,0:T(4,128)S(1)} %get-tuple-element.73), channel_id=1, replica_groups=mesh['row'=8,'col'=4] {'row','col'}, dimensions={0} | all-to-all | bytes 131072 | tf_op jit(solution)/shard_map/all_to_all | solution.py:778
  88.0 7.6 %all_to_all.43.rec = f32[8,24,128]{2,1,0:T(8,128)S(1)} all-to-all(f32[8,24,128]{2,1,0:T(8,128)S(1)} %get-tuple-element.76), channel_id=1, replica_groups=mesh['row'=8,'col'=4] {'row'}, dimensions={0} | all-to-all | bytes 196608 | tf_op jit(solution)/shard_map/all_to_all | solution.py:652
  96.3 10.1 %all_to_all.44.rec = f32[32,2,128]{2,1,0:T(2,128)S(1)} all-to-all(f32[32,2,128]{2,1,0:T(2,128)S(1)} %get-tuple-element.78), channel_id=1, replica_groups=mesh['row'=8,'col'=4] {'row','col'}, dimensions={0} | all-to-all | bytes 65536 | tf_op jit(solution)/shard_map/all_to_all | solution.py:793
  (44 shorter events, 11.5 us)
Async XLA Ops:
  0.6 1.2 %copy-start = (bf16[64,4,16,128]{3,2,1,0:T(8,128)(2,1)S(1)}, bf16[64,4,16,128]{3,2,1,0:T(8,128)(2,1)}, u32[]{:S(2)}) copy-start(bf16[64,4,16,128]{3,2,1,0:T(8,128)(2,1)} %param.13) | copy-start | bytes 3145732
  1.9 5.0 %copy-start.2 = (s32[4,16,128]{2,1,0:T(8,128)S(1)}, s32[4,16,128]{2,1,0:T(8,128)}, u32[]{:S(2)}) copy-start(s32[4,16,128]{2,1,0:T(8,128)} %param.8) | copy-start | bytes 98308
  1.9 5.0 %copy-start.3 = (f32[16,128]{1,0:T(8,128)S(1)}, f32[16,128]{1,0:T(8,128)}, u32[]{:S(2)}) copy-start(f32[16,128]{1,0:T(8,128)} %vent.1) | copy-start | bytes 24580
  2.2 20.1 %collective-permute-start.4 = (bf16[64,2048]{1,0:T(8,128)(2,1)S(1)}, bf16[64,2048]{1,0:T(8,128)(2,1)S(1)}, u32[]{:S(2)}, u32[]{:S(2)}) collective-permute-start(bf16[64,2048]{1,0:T(8,128)(2,1)S(1)} %get-tuple-element.51), channel_id=1, source_target_pairs={{0,24},{4,28},{8,16},{12,20},{16,8},{20,12},{24,0},{28,4},{1,25},{... | collective-permute-start | bytes 786440 | tf_op jit(solution)/shard_map/ppermute | solution.py:647
  6.2 16.2 %collective-permute-start.3 = (bf16[64,2048]{1,0:T(8,128)(2,1)S(1)}, bf16[64,2048]{1,0:T(8,128)(2,1)S(1)}, u32[]{:S(2)}, u32[]{:S(2)}) collective-permute-start(bf16[64,2048]{1,0:T(8,128)(2,1)S(1)} %get-tuple-element.51), channel_id=1, source_target_pairs={{0,16},{4,20},{8,24},{12,28},{16,0},{20,4},{24,8},{28,12},{1,17},{... | collective-permute-start | bytes 786440 | tf_op jit(solution)/shard_map/ppermute | solution.py:647
  6.7 15.7 %collective-permute-start.2 = (bf16[64,2048]{1,0:T(8,128)(2,1)S(1)}, bf16[64,2048]{1,0:T(8,128)(2,1)S(1)}, u32[]{:S(2)}, u32[]{:S(2)}) collective-permute-start(bf16[64,2048]{1,0:T(8,128)(2,1)S(1)} %get-tuple-element.51), channel_id=1, source_target_pairs={{0,8},{4,12},{8,0},{12,4},{16,24},{20,28},{24,16},{28,20},{1,9},{5... | collective-permute-start | bytes 786440 | tf_op jit(solution)/shard_map/ppermute | solution.py:647
  6.8 0.7 copy-start.5
  6.8 0.7 copy-start.6
  8.8 7.9 %copy-start.1 = (f32[4,16,128]{2,1,0:T(8,128)S(1)}, f32[4,16,128]{2,1,0:T(8,128)}, u32[]{:S(2)}) copy-start(f32[4,16,128]{2,1,0:T(8,128)} %param.7) | copy-start | bytes 98308
  8.8 13.6 %all-to-all-start = ((f32[8,32,128]{2,1,0:T(8,128)}), f32[8,32,128]{2,1,0:T(8,128)S(1)}, u32[]{:S(2)}, u32[]{:S(2)}) async-start(f32[8,32,128]{2,1,0:T(8,128)} %get-tuple-element.46), calls=%async_computation | async-start | bytes 262144 | tf_op jit(solution)/shard_map/all_to_all | solution.py:652
  13.0 6.5 %collective-permute-start.1 = (f32[72,128]{1,0:T(8,128)S(1)}, f32[72,128]{1,0:T(8,128)S(1)}, u32[]{:S(2)}, u32[]{:S(2)}) collective-permute-start(f32[72,128]{1,0:T(8,128)S(1)} %get-tuple-element.45.cond_ref.cond), channel_id=1, source_target_pairs={{0,3},{1,0},{2,1},{3,2},{4,7},{5,4},{6,5},{7,6},{8,11},{9,8},{10,9... | collective-permute-start | bytes 110600 | tf_op jit(solution)/shard_map/ppermute | solution.py:643
  16.6 5.8 %collective-permute-start = (f32[72,128]{1,0:T(8,128)S(1)}, f32[72,128]{1,0:T(8,128)S(1)}, u32[]{:S(2)}, u32[]{:S(2)}) collective-permute-start(f32[72,128]{1,0:T(8,128)S(1)} %get-tuple-element.45.cond_ref.cond), channel_id=1, source_target_pairs={{0,1},{1,2},{2,3},{3,0},{4,5},{5,6},{6,7},{7,4},{8,9},{9,10},{10,1... | collective-permute-start | bytes 110600 | tf_op jit(solution)/shard_map/ppermute | solution.py:643
  26.4 13.7 %collective-permute-start.5 = (bf16[64,4608]{1,0:T(8,128)(2,1)}, bf16[64,4608]{1,0:T(8,128)(2,1)S(1)}, u32[]{:S(2)}, u32[]{:S(2)}) collective-permute-start(bf16[64,4608]{1,0:T(8,128)(2,1)} %get-tuple-element.56), channel_id=1, source_target_pairs={{0,4},{4,0},{8,12},{12,8},{16,20},{20,16},{24,28},{28,24},{1,5},{5... | collective-permute-start | bytes 1769480 | tf_op jit(solution)/shard_map/ppermute | solution.py:647
  26.5 13.7 %all-to-all-start.1 = ((f32[8,56,128]{2,1,0:T(8,128)}), f32[8,56,128]{2,1,0:T(8,128)S(1)}, u32[]{:S(2)}, u32[]{:S(2)}) async-start(f32[8,56,128]{2,1,0:T(8,128)} %get-tuple-element.61), calls=%async_computation.1 | async-start | bytes 458752 | tf_op jit(solution)/shard_map/all_to_all | solution.py:652
  30.8 7.5 %collective-permute-start.6 = (bf16[64,512]{1,0:T(8,128)(2,1)S(1)}, bf16[64,512]{1,0:T(8,128)(2,1)S(1)}, u32[]{:S(2)}, u32[]{:S(2)}) collective-permute-start(bf16[64,512]{1,0:T(8,128)(2,1)S(1)} %get-tuple-element.57), channel_id=1, source_target_pairs={{0,28},{4,8},{8,4},{12,16},{16,12},{20,24},{24,20},{28,0},{1,29},{... | collective-permute-start | bytes 196616 | tf_op jit(solution)/shard_map/ppermute | solution.py:669
  33.5 4.8 %collective-permute-start.8 = (f32[64,128]{1,0:T(8,128)S(1)}, f32[64,128]{1,0:T(8,128)S(1)}, u32[]{:S(2)}, u32[]{:S(2)}) collective-permute-start(f32[64,128]{1,0:T(8,128)S(1)} %get-tuple-element.60.field), channel_id=1, source_target_pairs={{0,3},{1,0},{2,1},{3,2},{4,7},{5,4},{6,5},{7,6},{8,11},{9,8},{10,9... | collective-permute-start | bytes 98312 | tf_op jit(solution)/shard_map/ppermute | solution.py:643
  34.4 5.7 %collective-permute-start.7 = (f32[64,128]{1,0:T(8,128)S(1)}, f32[64,128]{1,0:T(8,128)S(1)}, u32[]{:S(2)}, u32[]{:S(2)}) collective-permute-start(f32[64,128]{1,0:T(8,128)S(1)} %get-tuple-element.60.field), channel_id=1, source_target_pairs={{0,1},{1,2},{2,3},{3,0},{4,5},{5,6},{6,7},{7,4},{8,9},{9,10},{10,1... | collective-permute-start | bytes 98312 | tf_op jit(solution)/shard_map/ppermute | solution.py:643
  41.4 9.6 %collective-permute-start.10 = (f32[200,128]{1,0:T(8,128)S(1)}, f32[200,128]{1,0:T(8,128)S(1)}, u32[]{:S(2)}, u32[]{:S(2)}) collective-permute-start(f32[200,128]{1,0:T(8,128)S(1)} %get-tuple-element.62), channel_id=1, source_target_pairs={{0,3},{1,0},{2,1},{3,2},{4,7},{5,4},{6,5},{7,6},{8,11},{9,8},{10,9... | collective-permute-start | bytes 307208 | tf_op jit(solution)/shard_map/ppermute | solution.py:643
  41.5 9.6 %collective-permute-start.9 = (f32[200,128]{1,0:T(8,128)S(1)}, f32[200,128]{1,0:T(8,128)S(1)}, u32[]{:S(2)}, u32[]{:S(2)}) collective-permute-start(f32[200,128]{1,0:T(8,128)S(1)} %get-tuple-element.62), channel_id=1, source_target_pairs={{0,1},{1,2},{2,3},{3,0},{4,5},{5,6},{6,7},{7,4},{8,9},{9,10},{10,1... | collective-permute-start | bytes 307208 | tf_op jit(solution)/shard_map/ppermute | solution.py:643
  52.9 10.0 %all-to-all-start.3 = ((f32[32,4,128]{2,1,0:T(4,128)}), f32[32,4,128]{2,1,0:T(4,128)S(1)}, u32[]{:S(2)}, u32[]{:S(2)}) async-start(f32[32,4,128]{2,1,0:T(4,128)} %get-tuple-element.66._), calls=%async_computation.3 | async-start | bytes 131072 | tf_op jit(solution)/shard_map/all_to_all | solution.py:761
  63.9 9.6 %collective-permute-start.12 = (f32[200,128]{1,0:T(8,128)S(1)}, f32[200,128]{1,0:T(8,128)S(1)}, u32[]{:S(2)}, u32[]{:S(2)}) collective-permute-start(f32[200,128]{1,0:T(8,128)S(1)} %get-tuple-element.72), channel_id=1, source_target_pairs={{0,3},{1,0},{2,1},{3,2},{4,7},{5,4},{6,5},{7,6},{8,11},{9,8},{10,9... | collective-permute-start | bytes 307208 | tf_op jit(solution)/shard_map/ppermute | solution.py:643
  64.7 8.9 %collective-permute-start.11 = (f32[200,128]{1,0:T(8,128)S(1)}, f32[200,128]{1,0:T(8,128)S(1)}, u32[]{:S(2)}, u32[]{:S(2)}) collective-permute-start(f32[200,128]{1,0:T(8,128)S(1)} %get-tuple-element.72), channel_id=1, source_target_pairs={{0,1},{1,2},{2,3},{3,0},{4,5},{5,6},{6,7},{7,4},{8,9},{9,10},{10,1... | collective-permute-start | bytes 307208 | tf_op jit(solution)/shard_map/ppermute | solution.py:643
  85.9 9.6 %collective-permute-start.14 = (f32[200,128]{1,0:T(8,128)S(1)}, f32[200,128]{1,0:T(8,128)S(1)}, u32[]{:S(2)}, u32[]{:S(2)}) collective-permute-start(f32[200,128]{1,0:T(8,128)S(1)} %get-tuple-element.77), channel_id=1, source_target_pairs={{0,3},{1,0},{2,1},{3,2},{4,7},{5,4},{6,5},{7,6},{8,11},{9,8},{10,9... | collective-permute-start | bytes 307208 | tf_op jit(solution)/shard_map/ppermute | solution.py:643
  86.8 8.8 %collective-permute-start.13 = (f32[200,128]{1,0:T(8,128)S(1)}, f32[200,128]{1,0:T(8,128)S(1)}, u32[]{:S(2)}, u32[]{:S(2)}) collective-permute-start(f32[200,128]{1,0:T(8,128)S(1)} %get-tuple-element.77), channel_id=1, source_target_pairs={{0,1},{1,2},{2,3},{3,0},{4,5},{5,6},{6,7},{7,4},{8,9},{9,10},{10,1... | collective-permute-start | bytes 307208 | tf_op jit(solution)/shard_map/ppermute | solution.py:643
  (1 other events, 0.7 us)

commit v7 on v6

--- a/solution.py
+++ b/solution.py
@@ -21,7 +21,7 @@
 
 def lookup(material, table):
     result = jnp.zeros(material.shape, F32)
-    for class_id in range(table.shape[0]):
+    for class_id in range(len(table)):
         result = jnp.where(material == class_id, table[class_id], result)
     return result
 
@@ -195,13 +195,16 @@
 
 
 def k_first(
-    grid, conductivity, capacity, partners, material, vent, cond_out, cap_out, vent_out, pay
+    grid, pairs, tables, material, vent, cond_out, cap_out, vent_out, pay
 ):
+    classes = (tables.shape[0] - pairs) // 2
+    conductivity = [tables[i] for i in range(classes)]
+    capacity = [tables[classes + i] for i in range(classes)]
     cond = lookup(material[...], conductivity)
     lane = lax.broadcasted_iota(jnp.int32, (8, grid.depth), 1)
     names = jnp.zeros((8, grid.depth), F32)
-    for k in range(partners.shape[0]):
-        names = jnp.where(lane == k, partners[k].astype(F32), names)
+    for k in range(pairs):
+        names = jnp.where(lane == k, tables[2 * classes + k], names)
     cond_out[0 : grid.rows, :] = cond
     cond_out[grid.rows :, :] = names
     cap_out[...] = lookup(material[...], capacity)
@@ -655,6 +658,7 @@
     def rows_of(count):
         return ((row_count, width + 2 * layers + count, depth), F32)
 
+    tables = jnp.concatenate([conductivity, capacity, partners.reshape(-1).astype(F32)])
     zm, panel, face = call(
         functools.partial(k_order, grid),
         (
@@ -672,10 +676,10 @@
         [(i, (i + 1 if i % 2 else i - 1) % row_count) for i in range(row_count)],
     )
     cond, cap, vent, pay0 = call(
-        functools.partial(k_first, grid),
+        functools.partial(k_first, grid, pairs),
         (((n + 8, depth), F32), field, ((width, depth), F32), rows_of(8)),
-        (conductivity, capacity, partners.reshape(-1), classes, vent_open),
-        smem=3,
+        (tables, classes, vent_open),
+        smem=1,
     )
     rec0, cond_low, cond_high = exchange(cond, pay0)
 

time: 108 us -> 107 us (level)
  no operation moved by 1% of the time
where the time goes in v7:
time: 107 us
  blocking collectives  43 us (40%)
  starting transfers between devices  30.3 us (28%)
  Pallas kernels  19.1 us (18%)
  waiting for transfers between devices  12.1 us (11%)
  local copies, waits for them, and re-layouts  1.25 us (1%)
    all_to_all x3, blocking collectives, exchange(): rec = lax.all_to_all(payload, 'row', 0, 0)  22.7 us
    pallas_call x12, Pallas kernels, call(): pl.pallas_call(kernel, out_shape=tuple((jax.ShapeDtypeStruct(s, t) for s,...  19.1 us
    ppermute x10, starting transfers between devices, cyclic(): lax.ppermute(value, axis, [(i, (i + step) % count) for i in range(count)])  11.8 us
    all_to_all x1, blocking collectives, body(): sums = lax.all_to_all(pay5, ('row', 'col'), 0, 0)  10.2 us
    all_to_all x1, blocking collectives, body(): total = lax.all_to_all(pay7, ('row', 'col'), 0, 0)  10.1 us
    all_to_all x2, starting transfers between devices, exchange(): rec = lax.all_to_all(payload, 'row', 0, 0)  8.56 us
    ppermute x10, waiting for transfers between devices, cyclic(): lax.ppermute(value, axis, [(i, (i + step) % count) for i in range(count)])  4.75 us
    ppermute x4, starting transfers between devices, xor_step(): return lax.ppermute(value, axis, [(i, i ^ k) for i in range(count)])  4.67 us
  transfers between devices with their start and end apart: 18, of which 4 were waited for; matrix products, arithmetic and copies ran while one was open for 0% of the time, Pallas kernels for 6%

profile of v7, /device:TPU:0, one launch (start us, length us, event | category | flops | bytes accessed | tf_op | source)
XLA Modules:
  0.0 106.6 jit_solution(7682756100372391454)
XLA Ops:
  2.3 4.0 %collective-permute-start.4 = (bf16[64,2048]{1,0:T(8,128)(2,1)S(1)}, bf16[64,2048]{1,0:T(8,128)(2,1)S(1)}, u32[]{:S(2)}, u32[]{:S(2)}) collective-permute-start(bf16[64,2048]{1,0:T(8,128)(2,1)S(1)} %get-tuple-element.51), channel_id=1, source_target_pairs={{0,24},{4,28},{8,16},{12,20},{16,8},{20,12},{24,0},{28,4},{1,25},{... | collective-permute-start | bytes 786440 | tf_op jit(solution)/shard_map/ppermute | solution.py:650
  7.0 1.2 %shard_map.94 = (f32[72,128]{1,0:T(8,128)S(1)}, f32[64,128]{1,0:T(8,128)S(1)}, f32[16,128]{1,0:T(8,128)S(1)}, f32[8,32,128]{2,1,0:T(8,128)}) custom-call(f32[18]{0:T(128)S(1)} %pad_maximum_fusion.tables, s32[64,128]{1,0:T(8,128)S(1)} %bitcast.13, f32[16,128]{1,0:T(8,128)S(1)} %copy-done.3), custom_call_target="tpu_custom_call" | custom-call | tf_op jit(solution)/shard_map/pallas_call | solution.py:612
  8.2 4.3 %all-to-all-start = ((f32[8,32,128]{2,1,0:T(8,128)}), f32[8,32,128]{2,1,0:T(8,128)S(1)}, u32[]{:S(2)}, u32[]{:S(2)}) async-start(f32[8,32,128]{2,1,0:T(8,128)} %get-tuple-element.46), calls=%async_computation | async-start | bytes 262144 | tf_op jit(solution)/shard_map/all_to_all | solution.py:655
  12.5 3.6 %collective-permute-start.1 = (f32[72,128]{1,0:T(8,128)S(1)}, f32[72,128]{1,0:T(8,128)S(1)}, u32[]{:S(2)}, u32[]{:S(2)}) collective-permute-start(f32[72,128]{1,0:T(8,128)S(1)} %get-tuple-element.45.cond_ref.cond), channel_id=1, source_target_pairs={{0,3},{1,0},{2,1},{3,2},{4,7},{5,4},{6,5},{7,6},{8,11},{9,8},{10,9... | collective-permute-start | bytes 110600 | tf_op jit(solution)/shard_map/ppermute | solution.py:646
  16.1 2.8 %shard_map.96 = (f32[64,64]{1,0:T(8,128)S(1)}, f32[64,128]{1,0:T(8,128)S(1)}, f32[64,128]{1,0:T(8,128)S(1)}) custom-call(bf16[64,8192]{1,0:T(8,128)(2,1)S(1)} %get-tuple-element.47.zm, f32[64,128]{1,0:T(8,128)S(1)} %bitcast.11, f32[72,128]{1,0:T(8,128)S(1)} %get-tuple-element.45.cond_ref.cond, f32[64,128]{1,0:T(8,128)S(1)} %get-tuple-element.43.cap_ref.cap), custom_call_target="tpu_custom_call" | custom-call | flops 1000 | bytes 1000 | tf_op jit(solution)/shard_map/pallas_call | solution.py:612
  18.9 2.9 %collective-permute-done.cond_low = f32[72,128]{1,0:T(8,128)S(1)} collective-permute-done((f32[72,128]{1,0:T(8,128)S(1)}, f32[72,128]{1,0:T(8,128)S(1)}, u32[]{:S(2)}, u32[]{:S(2)}) %collective-permute-start) | collective-permute-done | bytes 36896 | tf_op jit(solution)/shard_map/ppermute | solution.py:646
  21.8 4.0 %shard_map.97 = (f32[7,64,128]{2,1,0:T(8,128)S(1)}, f32[64,64]{1,0:T(8,128)S(1)}, f32[64,64]{1,0:T(8,128)S(1)}, f32[64,128]{1,0:T(8,128)S(1)}, f32[8,56,128]{2,1...) custom-call(s32[4]{0:T(128)S(1)} %pad_add_fusion.ids, ...), custom_call_target="tpu_custom_call" | custom-call | tf_op jit(solution)/shard_map/pallas_call | solution.py:612
  25.9 4.3 %all-to-all-start.1 = ((f32[8,56,128]{2,1,0:T(8,128)}), f32[8,56,128]{2,1,0:T(8,128)S(1)}, u32[]{:S(2)}, u32[]{:S(2)}) async-start(f32[8,56,128]{2,1,0:T(8,128)} %get-tuple-element.61), calls=%async_computation.1 | async-start | bytes 458752 | tf_op jit(solution)/shard_map/all_to_all | solution.py:655
  30.2 2.7 %collective-permute-start.6 = (bf16[64,512]{1,0:T(8,128)(2,1)S(1)}, bf16[64,512]{1,0:T(8,128)(2,1)S(1)}, u32[]{:S(2)}, u32[]{:S(2)}) collective-permute-start(bf16[64,512]{1,0:T(8,128)(2,1)S(1)} %get-tuple-element.57), channel_id=1, source_target_pairs={{0,28},{4,8},{8,4},{12,16},{16,12},{20,24},{24,20},{28,0},{1,29},{... | collective-permute-start | bytes 196616 | tf_op jit(solution)/shard_map/ppermute | solution.py:673
  34.9 2.8 %collective-permute-done.6.__.far.x_far = bf16[64,512]{1,0:T(8,128)(2,1)S(1)} collective-permute-done((bf16[64,512]{1,0:T(8,128)(2,1)S(1)}, bf16[64,512]{1,0:T(8,128)(2,1)S(1)}, u32[]{:S(2)}, u32[]{:S(2)}) %collective-permute-start.6) | collective-permute-done | bytes 65568 | tf_op jit(solution)/shard_map/ppermute | solution.py:673
  37.7 1.8 %collective-permute-done.7.low = f32[64,128]{1,0:T(8,128)S(1)} collective-permute-done((f32[64,128]{1,0:T(8,128)S(1)}, f32[64,128]{1,0:T(8,128)S(1)}, u32[]{:S(2)}, u32[]{:S(2)}) %collective-permute-start.7) | collective-permute-done | bytes 32800 | tf_op jit(solution)/shard_map/ppermute | solution.py:646
  39.6 1.3 %shard_map.98 = (f32[64,128]{1,0:T(8,128)S(1)}, f32[200,128]{1,0:T(8,128)S(1)}, f32[8,24,128]{2,1,0:T(8,128)S(1)}, f32[4,32,128]{2,1,0:T(8,128)S(1)}) custom-call(s32[4]{0:T(128)S(1)} %pad_add_fusion.ids, f32[7,64,128]{2,1,0:T(8,128)S(1)} %get-tuple-element.52.coef, f32[16,128]{1,0:T(8,128)S(1)} %get-tuple-element.44.vent, ...), custom_call_target="tpu_custom_call" | custom-call | tf_op jit(solution)/shard_map/pallas_call | solution.py:612
  40.9 2.0 %collective-permute-start.9 = (f32[200,128]{1,0:T(8,128)S(1)}, f32[200,128]{1,0:T(8,128)S(1)}, u32[]{:S(2)}, u32[]{:S(2)}) collective-permute-start(f32[200,128]{1,0:T(8,128)S(1)} %get-tuple-element.62), channel_id=1, source_target_pairs={{0,1},{1,2},{2,3},{3,0},{4,5},{5,6},{6,7},{7,4},{8,9},{9,10},{10,1... | collective-permute-start | bytes 307208 | tf_op jit(solution)/shard_map/ppermute | solution.py:646
  42.9 7.6 %all_to_all.40.rec = f32[8,24,128]{2,1,0:T(8,128)S(1)} all-to-all(f32[8,24,128]{2,1,0:T(8,128)S(1)} %get-tuple-element.65), channel_id=1, replica_groups=mesh['row'=8,'col'=4] {'row'}, dimensions={0} | all-to-all | bytes 196608 | tf_op jit(solution)/shard_map/all_to_all | solution.py:655
  50.5 1.8 %shard_map.99 = (f32[64,128]{1,0:T(8,128)S(1)}, f32[32,4,128]{2,1,0:T(4,128)}) custom-call(s32[4]{0:T(128)S(1)} %pad_add_fusion.ids, f32[7,64,128]{2,1,0:T(8,128)S(1)} %get-tuple-element.52.coef, f32[16,128]{1,0:T(8,128)S(1)} %get-tuple-element.44.vent, f32[64,128]{1,0:T(8,128)S(1)} %get-tuple-element.64.field.x0, f32[8,24,128]{2,1,0:T(8,128)S(1)} %all_to_all.40.rec, ...), custom_call_target="tpu_custom_call" | custom-call | tf_op jit(solution)/shard_map/pallas_call | solution.py:612
  52.3 2.5 %all-to-all-start.3 = ((f32[32,4,128]{2,1,0:T(4,128)}), f32[32,4,128]{2,1,0:T(4,128)S(1)}, u32[]{:S(2)}, u32[]{:S(2)}) async-start(f32[32,4,128]{2,1,0:T(4,128)} %get-tuple-element.66._), calls=%async_computation.3 | async-start | bytes 131072 | tf_op jit(solution)/shard_map/all_to_all | solution.py:765
  54.9 2.9 %shard_map.100 = (f32[8,64,64]{2,1,0:T(8,128)}, f32[7,64,64]{2,1,0:T(8,128)S(1)}, s32[49]{0:T(128)S(1)}) custom-call(s32[4]{0:T(128)S(1)} %pad_add_fusion.ids, f32[7,64,128]{2,1,0:T(8,128)S(1)} %get-tuple-element.52.coef, f32[2,16,128]{2,1,0:T(8,128)S(1)} %get-tuple-element.53.vents, f32[6,128]{1,0:T(8,128)S(1)} %get-tuple-element.54.names, ...), custom_call_target="tpu_custom_call" | custom-call | flops 100000000 | bytes 4000000 | tf_op jit(solution)/shard_map/pallas_call | solution.py:612
  57.8 4.6 %all-to-all-done.3.rec = f32[32,4,128]{2,1,0:T(4,128)S(1)} async-done(((f32[32,4,128]{2,1,0:T(4,128)}), f32[32,4,128]{2,1,0:T(4,128)S(1)}, u32[]{:S(2)}, u32[]{:S(2)}) %all-to-all-start.3) | async-done | bytes 65568 | tf_op jit(solution)/shard_map/all_to_all | solution.py:765
  64.1 1.3 %collective-permute-start.11 = (f32[200,128]{1,0:T(8,128)S(1)}, f32[200,128]{1,0:T(8,128)S(1)}, u32[]{:S(2)}, u32[]{:S(2)}) collective-permute-start(f32[200,128]{1,0:T(8,128)S(1)} %get-tuple-element.72), channel_id=1, source_target_pairs={{0,1},{1,2},{2,3},{3,0},{4,5},{5,6},{6,7},{7,4},{8,9},{9,10},{10,1... | collective-permute-start | bytes 307208 | tf_op jit(solution)/shard_map/ppermute | solution.py:646
  65.4 7.6 %all_to_all.41.rec = f32[8,24,128]{2,1,0:T(8,128)S(1)} all-to-all(f32[8,24,128]{2,1,0:T(8,128)S(1)} %get-tuple-element.71), channel_id=1, replica_groups=mesh['row'=8,'col'=4] {'row'}, dimensions={0} | all-to-all | bytes 196608 | tf_op jit(solution)/shard_map/all_to_all | solution.py:655
  73.0 1.2 %shard_map.102 = (f32[64,128]{1,0:T(8,128)S(1)}, f32[32,4,128]{2,1,0:T(4,128)S(1)}) custom-call(s32[4]{0:T(128)S(1)} %pad_add_fusion.ids, f32[7,64,128]{2,1,0:T(8,128)S(1)} %get-tuple-element.52.coef, f32[16,128]{1,0:T(8,128)S(1)} %get-tuple-element.44.vent, f32[64,128]{1,0:T(8,128)S(1)} %get-tuple-element.70.field.p0, f32[8,24,128]{2,1,0:T(8,128)S(1)} %all_to_all.41.rec, ...), custom_call_target="tpu_custom_call" | custom-call | tf_op jit(solution)/shard_map/pallas_call | solution.py:612
  74.2 10.2 %all_to_all.42.rec = f32[32,4,128]{2,1,0:T(4,128)S(1)} all-to-all(f32[32,4,128]{2,1,0:T(4,128)S(1)} %get-tuple-element.73), channel_id=1, replica_groups=mesh['row'=8,'col'=4] {'row','col'}, dimensions={0} | all-to-all | bytes 131072 | tf_op jit(solution)/shard_map/all_to_all | solution.py:782
  87.5 7.6 %all_to_all.43.rec = f32[8,24,128]{2,1,0:T(8,128)S(1)} all-to-all(f32[8,24,128]{2,1,0:T(8,128)S(1)} %get-tuple-element.76), channel_id=1, replica_groups=mesh['row'=8,'col'=4] {'row'}, dimensions={0} | all-to-all | bytes 196608 | tf_op jit(solution)/shard_map/all_to_all | solution.py:655
  95.8 10.1 %all_to_all.44.rec = f32[32,2,128]{2,1,0:T(2,128)S(1)} all-to-all(f32[32,2,128]{2,1,0:T(2,128)S(1)} %get-tuple-element.78), channel_id=1, replica_groups=mesh['row'=8,'col'=4] {'row','col'}, dimensions={0} | all-to-all | bytes 65536 | tf_op jit(solution)/shard_map/all_to_all | solution.py:797
  (46 shorter events, 10.9 us)
Async XLA Ops:
  1.9 5.1 %copy-start.2 = (s32[4,16,128]{2,1,0:T(8,128)S(1)}, s32[4,16,128]{2,1,0:T(8,128)}, u32[]{:S(2)}) copy-start(s32[4,16,128]{2,1,0:T(8,128)} %param.8) | copy-start | bytes 98308
  1.9 5.1 %copy-start.3 = (f32[16,128]{1,0:T(8,128)S(1)}, f32[16,128]{1,0:T(8,128)}, u32[]{:S(2)}) copy-start(f32[16,128]{1,0:T(8,128)} %vent.1) | copy-start | bytes 24580
  2.2 4.6 %copy-start.6 = (s32[1,1,2]{2,1,0:T(1,128)S(1)}, s32[1,1,2]{2,1,0:T(1,128)}, u32[]{:S(2)}) copy-start(s32[1,1,2]{2,1,0:T(1,128)} %param.12) | copy-start | bytes 28
  2.2 4.6 %copy-start.4 = (f32[8]{0:T(128)S(1)}, f32[8]{0:T(128)}, u32[]{:S(2)}) copy-start(f32[8]{0:T(128)} %param.9) | copy-start | bytes 100
  2.3 4.6 %copy-start.5 = (f32[8]{0:T(128)S(1)}, f32[8]{0:T(128)}, u32[]{:S(2)}) copy-start(f32[8]{0:T(128)} %param.10) | copy-start | bytes 100
  2.3 19.5 %collective-permute-start.4 = (bf16[64,2048]{1,0:T(8,128)(2,1)S(1)}, bf16[64,2048]{1,0:T(8,128)(2,1)S(1)}, u32[]{:S(2)}, u32[]{:S(2)}) collective-permute-start(bf16[64,2048]{1,0:T(8,128)(2,1)S(1)} %get-tuple-element.51), channel_id=1, source_target_pairs={{0,24},{4,28},{8,16},{12,20},{16,8},{20,12},{24,0},{28,4},{1,25},{... | collective-permute-start | bytes 786440 | tf_op jit(solution)/shard_map/ppermute | solution.py:650
  6.2 15.6 %collective-permute-start.3 = (bf16[64,2048]{1,0:T(8,128)(2,1)S(1)}, bf16[64,2048]{1,0:T(8,128)(2,1)S(1)}, u32[]{:S(2)}, u32[]{:S(2)}) collective-permute-start(bf16[64,2048]{1,0:T(8,128)(2,1)S(1)} %get-tuple-element.51), channel_id=1, source_target_pairs={{0,16},{4,20},{8,24},{12,28},{16,0},{20,4},{24,8},{28,12},{1,17},{... | collective-permute-start | bytes 786440 | tf_op jit(solution)/shard_map/ppermute | solution.py:650
  6.7 15.1 %collective-permute-start.2 = (bf16[64,2048]{1,0:T(8,128)(2,1)S(1)}, bf16[64,2048]{1,0:T(8,128)(2,1)S(1)}, u32[]{:S(2)}, u32[]{:S(2)}) collective-permute-start(bf16[64,2048]{1,0:T(8,128)(2,1)S(1)} %get-tuple-element.51), channel_id=1, source_target_pairs={{0,8},{4,12},{8,0},{12,4},{16,24},{20,28},{24,16},{28,20},{1,9},{5... | collective-permute-start | bytes 786440 | tf_op jit(solution)/shard_map/ppermute | solution.py:650
  8.2 7.9 %copy-start.1 = (f32[4,16,128]{2,1,0:T(8,128)S(1)}, f32[4,16,128]{2,1,0:T(8,128)}, u32[]{:S(2)}) copy-start(f32[4,16,128]{2,1,0:T(8,128)} %param.7) | copy-start | bytes 98308
  8.2 13.6 %all-to-all-start = ((f32[8,32,128]{2,1,0:T(8,128)}), f32[8,32,128]{2,1,0:T(8,128)S(1)}, u32[]{:S(2)}, u32[]{:S(2)}) async-start(f32[8,32,128]{2,1,0:T(8,128)} %get-tuple-element.46), calls=%async_computation | async-start | bytes 262144 | tf_op jit(solution)/shard_map/all_to_all | solution.py:655
  12.5 6.5 %collective-permute-start.1 = (f32[72,128]{1,0:T(8,128)S(1)}, f32[72,128]{1,0:T(8,128)S(1)}, u32[]{:S(2)}, u32[]{:S(2)}) collective-permute-start(f32[72,128]{1,0:T(8,128)S(1)} %get-tuple-element.45.cond_ref.cond), channel_id=1, source_target_pairs={{0,3},{1,0},{2,1},{3,2},{4,7},{5,4},{6,5},{7,6},{8,11},{9,8},{10,9... | collective-permute-start | bytes 110600 | tf_op jit(solution)/shard_map/ppermute | solution.py:646
  16.1 5.8 %collective-permute-start = (f32[72,128]{1,0:T(8,128)S(1)}, f32[72,128]{1,0:T(8,128)S(1)}, u32[]{:S(2)}, u32[]{:S(2)}) collective-permute-start(f32[72,128]{1,0:T(8,128)S(1)} %get-tuple-element.45.cond_ref.cond), channel_id=1, source_target_pairs={{0,1},{1,2},{2,3},{3,0},{4,5},{5,6},{6,7},{7,4},{8,9},{9,10},{10,1... | collective-permute-start | bytes 110600 | tf_op jit(solution)/shard_map/ppermute | solution.py:646
  25.8 13.7 %collective-permute-start.5 = (bf16[64,4608]{1,0:T(8,128)(2,1)}, bf16[64,4608]{1,0:T(8,128)(2,1)S(1)}, u32[]{:S(2)}, u32[]{:S(2)}) collective-permute-start(bf16[64,4608]{1,0:T(8,128)(2,1)} %get-tuple-element.56), channel_id=1, source_target_pairs={{0,4},{4,0},{8,12},{12,8},{16,20},{20,16},{24,28},{28,24},{1,5},{5... | collective-permute-start | bytes 1769480 | tf_op jit(solution)/shard_map/ppermute | solution.py:650
  25.9 13.7 %all-to-all-start.1 = ((f32[8,56,128]{2,1,0:T(8,128)}), f32[8,56,128]{2,1,0:T(8,128)S(1)}, u32[]{:S(2)}, u32[]{:S(2)}) async-start(f32[8,56,128]{2,1,0:T(8,128)} %get-tuple-element.61), calls=%async_computation.1 | async-start | bytes 458752 | tf_op jit(solution)/shard_map/all_to_all | solution.py:655
  30.2 7.5 %collective-permute-start.6 = (bf16[64,512]{1,0:T(8,128)(2,1)S(1)}, bf16[64,512]{1,0:T(8,128)(2,1)S(1)}, u32[]{:S(2)}, u32[]{:S(2)}) collective-permute-start(bf16[64,512]{1,0:T(8,128)(2,1)S(1)} %get-tuple-element.57), channel_id=1, source_target_pairs={{0,28},{4,8},{8,4},{12,16},{16,12},{20,24},{24,20},{28,0},{1,29},{... | collective-permute-start | bytes 196616 | tf_op jit(solution)/shard_map/ppermute | solution.py:673
  32.9 4.8 %collective-permute-start.8 = (f32[64,128]{1,0:T(8,128)S(1)}, f32[64,128]{1,0:T(8,128)S(1)}, u32[]{:S(2)}, u32[]{:S(2)}) collective-permute-start(f32[64,128]{1,0:T(8,128)S(1)} %get-tuple-element.60.field), channel_id=1, source_target_pairs={{0,3},{1,0},{2,1},{3,2},{4,7},{5,4},{6,5},{7,6},{8,11},{9,8},{10,9... | collective-permute-start | bytes 98312 | tf_op jit(solution)/shard_map/ppermute | solution.py:646
  33.8 5.7 %collective-permute-start.7 = (f32[64,128]{1,0:T(8,128)S(1)}, f32[64,128]{1,0:T(8,128)S(1)}, u32[]{:S(2)}, u32[]{:S(2)}) collective-permute-start(f32[64,128]{1,0:T(8,128)S(1)} %get-tuple-element.60.field), channel_id=1, source_target_pairs={{0,1},{1,2},{2,3},{3,0},{4,5},{5,6},{6,7},{7,4},{8,9},{9,10},{10,1... | collective-permute-start | bytes 98312 | tf_op jit(solution)/shard_map/ppermute | solution.py:646
  40.8 9.6 %collective-permute-start.10 = (f32[200,128]{1,0:T(8,128)S(1)}, f32[200,128]{1,0:T(8,128)S(1)}, u32[]{:S(2)}, u32[]{:S(2)}) collective-permute-start(f32[200,128]{1,0:T(8,128)S(1)} %get-tuple-element.62), channel_id=1, source_target_pairs={{0,3},{1,0},{2,1},{3,2},{4,7},{5,4},{6,5},{7,6},{8,11},{9,8},{10,9... | collective-permute-start | bytes 307208 | tf_op jit(solution)/shard_map/ppermute | solution.py:646
  40.9 9.6 %collective-permute-start.9 = (f32[200,128]{1,0:T(8,128)S(1)}, f32[200,128]{1,0:T(8,128)S(1)}, u32[]{:S(2)}, u32[]{:S(2)}) collective-permute-start(f32[200,128]{1,0:T(8,128)S(1)} %get-tuple-element.62), channel_id=1, source_target_pairs={{0,1},{1,2},{2,3},{3,0},{4,5},{5,6},{6,7},{7,4},{8,9},{9,10},{10,1... | collective-permute-start | bytes 307208 | tf_op jit(solution)/shard_map/ppermute | solution.py:646
  52.3 10.0 %all-to-all-start.3 = ((f32[32,4,128]{2,1,0:T(4,128)}), f32[32,4,128]{2,1,0:T(4,128)S(1)}, u32[]{:S(2)}, u32[]{:S(2)}) async-start(f32[32,4,128]{2,1,0:T(4,128)} %get-tuple-element.66._), calls=%async_computation.3 | async-start | bytes 131072 | tf_op jit(solution)/shard_map/all_to_all | solution.py:765
  63.3 9.6 %collective-permute-start.12 = (f32[200,128]{1,0:T(8,128)S(1)}, f32[200,128]{1,0:T(8,128)S(1)}, u32[]{:S(2)}, u32[]{:S(2)}) collective-permute-start(f32[200,128]{1,0:T(8,128)S(1)} %get-tuple-element.72), channel_id=1, source_target_pairs={{0,3},{1,0},{2,1},{3,2},{4,7},{5,4},{6,5},{7,6},{8,11},{9,8},{10,9... | collective-permute-start | bytes 307208 | tf_op jit(solution)/shard_map/ppermute | solution.py:646
  64.1 8.9 %collective-permute-start.11 = (f32[200,128]{1,0:T(8,128)S(1)}, f32[200,128]{1,0:T(8,128)S(1)}, u32[]{:S(2)}, u32[]{:S(2)}) collective-permute-start(f32[200,128]{1,0:T(8,128)S(1)} %get-tuple-element.72), channel_id=1, source_target_pairs={{0,1},{1,2},{2,3},{3,0},{4,5},{5,6},{6,7},{7,4},{8,9},{9,10},{10,1... | collective-permute-start | bytes 307208 | tf_op jit(solution)/shard_map/ppermute | solution.py:646
  85.4 9.6 %collective-permute-start.14 = (f32[200,128]{1,0:T(8,128)S(1)}, f32[200,128]{1,0:T(8,128)S(1)}, u32[]{:S(2)}, u32[]{:S(2)}) collective-permute-start(f32[200,128]{1,0:T(8,128)S(1)} %get-tuple-element.77), channel_id=1, source_target_pairs={{0,3},{1,0},{2,1},{3,2},{4,7},{5,4},{6,5},{7,6},{8,11},{9,8},{10,9... | collective-permute-start | bytes 307208 | tf_op jit(solution)/shard_map/ppermute | solution.py:646
  86.3 8.8 %collective-permute-start.13 = (f32[200,128]{1,0:T(8,128)S(1)}, f32[200,128]{1,0:T(8,128)S(1)}, u32[]{:S(2)}, u32[]{:S(2)}) collective-permute-start(f32[200,128]{1,0:T(8,128)S(1)} %get-tuple-element.77), channel_id=1, source_target_pairs={{0,1},{1,2},{2,3},{3,0},{4,5},{5,6},{6,7},{7,4},{8,9},{9,10},{10,1... | collective-permute-start | bytes 307208 | tf_op jit(solution)/shard_map/ppermute | solution.py:646
  (1 other events, 1.2 us)

commit v8 on v7

--- a/solution.py
+++ b/solution.py
@@ -381,7 +381,7 @@
     y0 = solve_own(inverse, jnp.sum(projected[...], axis=1, keepdims=True))
     expand(grid, zm, y0, v0)
     field = v0[...]
-    sent[...] = field
+    sent[0:n, :] = field
     to_all(grid, pay, vent[...] * field[-w:], field, fold(inverse))
     await_picks(held, targets, sems)
 
@@ -393,7 +393,7 @@
 
 
 def k_coarse(
-    grid, pairs, ids, coef, vent, zm, inverse, field, rec, low, high, face_y, _, __,
+    grid, pairs, ids, coef, vent, zm, inverse, field, rec, low, high, face_y, _,
     out, wide, pay, solves, scratch,
 ):
     n, w = grid.rows, grid.width
@@ -429,8 +429,8 @@
 
 
 def k_partials(
-    grid, pairs, base, ids, coef, vent, field, rec, low, high, vents, zm, low2, high2, mine, others,
-    far, *rest,
+    grid, pairs, base, ids, coef, vent, field, far, rec, low, high, vents, zm, low2, high2, mine,
+    others, *rest,
 ):
     n, d, w, layers = grid.rows, grid.depth, grid.width, grid.layers
     size = zm.shape[0]
@@ -702,7 +702,7 @@
             ((7, n, depth), F32),
             small,
             small,
-            field,
+            ((136, depth), F32),
             rows_of(size // 2),
             panels,
             ((size, (pairs * width + layers) * depth), BF16),
@@ -727,11 +727,12 @@
     x0, wide2, pay2, solves = call(
         functools.partial(k_coarse, grid, pairs),
         (field, wide, pay, ((2 + pairs, size // 2, depth), F32)),
-        (ids, coef, vent, zm, inverse, sent, rec1, low1, high1, face_y, others, x_far),
+        (ids, coef, vent, zm, inverse, sent, rec1, low1, high1, face_y, others),
         scratch=(pltpu.VMEM((n, depth), F32),),
         smem=1,
-        free=(10, 11),
-    )
+        free=(10,),
+    )
+    pay2, x_far = lax.optimization_barrier((pay2, x_far))
     rec, low2, high2 = exchange(wide2, pay2)
 
     def everyone(lines):
@@ -741,7 +742,7 @@
         functools.partial(k_partials, grid, pairs, True),
         (field, everyone((places + 1) // 2)),
         (
-            ids, coef, vent, x0, rec, low2, high2, vents, zm, low2, high2, mine, others, x_far, rhs,
+            ids, coef, vent, x0, x_far, rec, low2, high2, vents, zm, low2, high2, mine, others, rhs,
         ),
         smem=1,
     )
@@ -775,7 +776,7 @@
         functools.partial(k_partials, grid, pairs, False),
         (field, everyone((places + 1) // 2)),
         (
-            ids, coef, vent, p0, rec, low, high, vents, zm, low2, high2, mine, others, x_far,
+            ids, coef, vent, p0, x_far, rec, low, high, vents, zm, low2, high2, mine, others,
         ),
         smem=1,
     )

time: 107 us -> 107 us (level)
  blocking collectives: 43 us -> 44.7 us
  waiting for transfers between devices: 12.1 us -> 10.4 us
    ppermute x1, waiting for transfers between devices: 2.81 us -> 0.01 us  [body(): lax.ppermute(face, 'row', [(i, (i + 1 if i % 2 else i - 1) % row_count) f...]
    all_to_all x3, blocking collectives: 22.7 us -> 24.3 us  [exchange(): rec = lax.all_to_all(payload, 'row', 0, 0)]
    ppermute x10, waiting for transfers between devices: 4.75 us -> 5.83 us  [cyclic(): lax.ppermute(value, axis, [(i, (i + step) % count) for i in range(count)])]
  transfers between devices with their start and end apart: 18 -> 18, of which waited for: 4 -> 4; matrix products, arithmetic and copies ran while one was open for 0% -> 0% of each run, Pallas kernels for 6% -> 8%
where the time goes in v8:
time: 107 us; the launch traced here: 106 us
  blocking collectives  44.7 us (42%)
  starting transfers between devices  30.1 us (28%)
  Pallas kernels  19.1 us (18%)
  waiting for transfers between devices  10.4 us (10%)
  local copies, waits for them, and re-layouts  1.25 us (1%)
    all_to_all x3, blocking collectives, exchange(): rec = lax.all_to_all(payload, 'row', 0, 0)  24.3 us
    pallas_call x12, Pallas kernels, call(): pl.pallas_call(kernel, out_shape=tuple((jax.ShapeDtypeStruct(s, t) for s,...  19.1 us
    ppermute x10, starting transfers between devices, cyclic(): lax.ppermute(value, axis, [(i, (i + step) % count) for i in range(count)])  11.9 us
    all_to_all x1, blocking collectives, body(): sums = lax.all_to_all(pay5, ('row', 'col'), 0, 0)  10.3 us
    all_to_all x1, blocking collectives, body(): total = lax.all_to_all(pay7, ('row', 'col'), 0, 0)  10.1 us
    all_to_all x2, starting transfers between devices, exchange(): rec = lax.all_to_all(payload, 'row', 0, 0)  8.55 us
    ppermute x10, waiting for transfers between devices, cyclic(): lax.ppermute(value, axis, [(i, (i + step) % count) for i in range(count)])  5.83 us
    ppermute x4, starting transfers between devices, xor_step(): return lax.ppermute(value, axis, [(i, i ^ k) for i in range(count)])  4.67 us
  transfers between devices with their start and end apart: 18, of which 4 were waited for; matrix products, arithmetic and copies ran while one was open for 0% of the time, Pallas kernels for 8%

profile of v8, /device:TPU:0, one launch (start us, length us, event | category | flops | bytes accessed | tf_op | source)
XLA Modules:
  0.0 106.4 jit_solution(16343918697117094525)
XLA Ops:
  0.6 1.2 %copy-done = bf16[64,4,16,128]{3,2,1,0:T(8,128)(2,1)S(1)} copy-done((bf16[64,4,16,128]{3,2,1,0:T(8,128)(2,1)S(1)}, bf16[64,4,16,128]{3,2,1,0:T(8,128)(2,1)}, u32[]{:S(2)}) %copy-start) | copy-done | bytes 1048600
  2.3 4.0 %collective-permute-start.4 = (bf16[64,2048]{1,0:T(8,128)(2,1)S(1)}, bf16[64,2048]{1,0:T(8,128)(2,1)S(1)}, u32[]{:S(2)}, u32[]{:S(2)}) collective-permute-start(bf16[64,2048]{1,0:T(8,128)(2,1)S(1)} %get-tuple-element.53), channel_id=1, source_target_pairs={{0,24},{4,28},{8,16},{12,20},{16,8},{20,12},{24,0},{28,4},{1,25},{... | collective-permute-start | bytes 786440 | tf_op jit(solution)/shard_map/ppermute | solution.py:650
  7.0 1.2 %shard_map.94 = (f32[72,128]{1,0:T(8,128)S(1)}, f32[64,128]{1,0:T(8,128)S(1)}, f32[16,128]{1,0:T(8,128)S(1)}, f32[8,32,128]{2,1,0:T(8,128)}) custom-call(f32[18]{0:T(128)S(1)} %pad_maximum_fusion.tables, s32[64,128]{1,0:T(8,128)S(1)} %bitcast.13, f32[16,128]{1,0:T(8,128)S(1)} %copy-done.3), custom_call_target="tpu_custom_call" | custom-call | tf_op jit(solution)/shard_map/pallas_call | solution.py:612
  8.2 4.3 %all-to-all-start = ((f32[8,32,128]{2,1,0:T(8,128)}), f32[8,32,128]{2,1,0:T(8,128)S(1)}, u32[]{:S(2)}, u32[]{:S(2)}) async-start(f32[8,32,128]{2,1,0:T(8,128)} %get-tuple-element.48), calls=%async_computation | async-start | bytes 262144 | tf_op jit(solution)/shard_map/all_to_all | solution.py:655
  12.5 3.6 %collective-permute-start.1 = (f32[72,128]{1,0:T(8,128)S(1)}, f32[72,128]{1,0:T(8,128)S(1)}, u32[]{:S(2)}, u32[]{:S(2)}) collective-permute-start(f32[72,128]{1,0:T(8,128)S(1)} %get-tuple-element.47.cond_ref.cond), channel_id=1, source_target_pairs={{0,3},{1,0},{2,1},{3,2},{4,7},{5,4},{6,5},{7,6},{8,11},{9,8},{10,9... | collective-permute-start | bytes 110600 | tf_op jit(solution)/shard_map/ppermute | solution.py:646
  16.1 2.8 %shard_map.96 = (f32[64,64]{1,0:T(8,128)S(1)}, f32[64,128]{1,0:T(8,128)S(1)}, f32[64,128]{1,0:T(8,128)S(1)}) custom-call(bf16[64,8192]{1,0:T(8,128)(2,1)S(1)} %get-tuple-element.49.zm, f32[64,128]{1,0:T(8,128)S(1)} %bitcast.11, f32[72,128]{1,0:T(8,128)S(1)} %get-tuple-element.47.cond_ref.cond, f32[64,128]{1,0:T(8,128)S(1)} %get-tuple-element.45.cap_ref.cap), custom_call_target="tpu_custom_call" | custom-call | flops 1000 | bytes 1000 | tf_op jit(solution)/shard_map/pallas_call | solution.py:612
  18.9 2.9 %collective-permute-done.cond_low = f32[72,128]{1,0:T(8,128)S(1)} collective-permute-done((f32[72,128]{1,0:T(8,128)S(1)}, f32[72,128]{1,0:T(8,128)S(1)}, u32[]{:S(2)}, u32[]{:S(2)}) %collective-permute-start) | collective-permute-done | bytes 36896 | tf_op jit(solution)/shard_map/ppermute | solution.py:646
  21.8 4.0 %shard_map.97 = (f32[7,64,128]{2,1,0:T(8,128)S(1)}, f32[64,64]{1,0:T(8,128)S(1)}, f32[64,64]{1,0:T(8,128)S(1)}, f32[136,128]{1,0:T(8,128)S(1)}, f32[8,56,128]{2,...) custom-call(s32[4]{0:T(128)S(1)} %pad_add_fusion.ids, ...), custom_call_target="tpu_custom_call" | custom-call | tf_op jit(solution)/shard_map/pallas_call | solution.py:612
  25.9 4.3 %all-to-all-start.1 = ((f32[8,56,128]{2,1,0:T(8,128)}), f32[8,56,128]{2,1,0:T(8,128)S(1)}, u32[]{:S(2)}, u32[]{:S(2)}) async-start(f32[8,56,128]{2,1,0:T(8,128)} %get-tuple-element.61), calls=%async_computation.1 | async-start | bytes 458752 | tf_op jit(solution)/shard_map/all_to_all | solution.py:655
  32.2 2.1 %collective-permute-start.8 = (bf16[64,512]{1,0:T(8,128)(2,1)S(1)}, bf16[64,512]{1,0:T(8,128)(2,1)S(1)}, u32[]{:S(2)}, u32[]{:S(2)}) collective-permute-start(bf16[64,512]{1,0:T(8,128)(2,1)S(1)} %get-tuple-element.63), channel_id=1, source_target_pairs={{0,28},{4,8},{8,4},{12,16},{16,12},{20,24},{24,20},{28,0},{1,29},{... | collective-permute-start | bytes 196616 | tf_op jit(solution)/shard_map/ppermute | solution.py:673
  34.8 2.5 %collective-permute-done.6.low = f32[136,128]{1,0:T(8,128)S(1)} collective-permute-done((f32[136,128]{1,0:T(8,128)S(1)}, f32[136,128]{1,0:T(8,128)S(1)}, u32[]{:S(2)}, u32[]{:S(2)}) %collective-permute-start.6) | collective-permute-done | bytes 69664 | tf_op jit(solution)/shard_map/ppermute | solution.py:646
  37.3 1.3 %shard_map.98 = (f32[64,128]{1,0:T(8,128)S(1)}, f32[200,128]{1,0:T(8,128)S(1)}, f32[8,24,128]{2,1,0:T(8,128)S(1)}, f32[4,32,128]{2,1,0:T(8,128)S(1)}) custom-call(s32[4]{0:T(128)S(1)} %pad_add_fusion.ids, f32[7,64,128]{2,1,0:T(8,128)S(1)} %get-tuple-element.54.coef, f32[16,128]{1,0:T(8,128)S(1)} %get-tuple-element.46.vent, ...), custom_call_target="tpu_custom_call" | custom-call | tf_op jit(solution)/shard_map/pallas_call | solution.py:612
  39.3 1.3 %collective-permute-start.9 = (f32[200,128]{1,0:T(8,128)S(1)}, f32[200,128]{1,0:T(8,128)S(1)}, u32[]{:S(2)}, u32[]{:S(2)}) collective-permute-start(f32[200,128]{1,0:T(8,128)S(1)} %get-tuple-element.66), channel_id=1, source_target_pairs={{0,1},{1,2},{2,3},{3,0},{4,5},{5,6},{6,7},{7,4},{8,9},{9,10},{10,1... | collective-permute-start | bytes 307208 | tf_op jit(solution)/shard_map/ppermute | solution.py:646
  40.7 9.2 %all_to_all.40.rec = f32[8,24,128]{2,1,0:T(8,128)S(1)} all-to-all(f32[8,24,128]{2,1,0:T(8,128)S(1)} %get-tuple-element.69), channel_id=1, replica_groups=mesh['row'=8,'col'=4] {'row'}, dimensions={0} | all-to-all | bytes 196608 | tf_op jit(solution)/shard_map/all_to_all | solution.py:655
  49.8 1.8 %shard_map.99 = (f32[64,128]{1,0:T(8,128)S(1)}, f32[32,4,128]{2,1,0:T(4,128)}) custom-call(s32[4]{0:T(128)S(1)} %pad_add_fusion.ids, f32[7,64,128]{2,1,0:T(8,128)S(1)} %get-tuple-element.54.coef, f32[16,128]{1,0:T(8,128)S(1)} %get-tuple-element.46.vent, f32[64,128]{1,0:T(8,128)S(1)} %get-tuple-element.68.field.x0, ...), custom_call_target="tpu_custom_call" | custom-call | tf_op jit(solution)/shard_map/pallas_call | solution.py:612
  51.7 2.9 %all-to-all-start.3 = ((f32[32,4,128]{2,1,0:T(4,128)}), f32[32,4,128]{2,1,0:T(4,128)S(1)}, u32[]{:S(2)}, u32[]{:S(2)}) async-start(f32[32,4,128]{2,1,0:T(4,128)} %get-tuple-element.70._), calls=%async_computation.3 | async-start | bytes 131072 | tf_op jit(solution)/shard_map/all_to_all | solution.py:766
  54.6 2.9 %shard_map.100 = (f32[8,64,64]{2,1,0:T(8,128)}, f32[7,64,64]{2,1,0:T(8,128)S(1)}, s32[49]{0:T(128)S(1)}) custom-call(s32[4]{0:T(128)S(1)} %pad_add_fusion.ids, f32[7,64,128]{2,1,0:T(8,128)S(1)} %get-tuple-element.54.coef, f32[2,16,128]{2,1,0:T(8,128)S(1)} %get-tuple-element.55.vents, f32[6,128]{1,0:T(8,128)S(1)} %get-tuple-element.56.names, ...), custom_call_target="tpu_custom_call" | custom-call | flops 100000000 | bytes 4000000 | tf_op jit(solution)/shard_map/pallas_call | solution.py:612
  57.5 4.6 %all-to-all-done.3.rec = f32[32,4,128]{2,1,0:T(4,128)S(1)} async-done(((f32[32,4,128]{2,1,0:T(4,128)}), f32[32,4,128]{2,1,0:T(4,128)S(1)}, u32[]{:S(2)}, u32[]{:S(2)}) %all-to-all-start.3) | async-done | bytes 65568 | tf_op jit(solution)/shard_map/all_to_all | solution.py:766
  63.9 1.2 %collective-permute-start.11 = (f32[200,128]{1,0:T(8,128)S(1)}, f32[200,128]{1,0:T(8,128)S(1)}, u32[]{:S(2)}, u32[]{:S(2)}) collective-permute-start(f32[200,128]{1,0:T(8,128)S(1)} %get-tuple-element.76), channel_id=1, source_target_pairs={{0,1},{1,2},{2,3},{3,0},{4,5},{5,6},{6,7},{7,4},{8,9},{9,10},{10,1... | collective-permute-start | bytes 307208 | tf_op jit(solution)/shard_map/ppermute | solution.py:646
  65.1 7.6 %all_to_all.41.rec = f32[8,24,128]{2,1,0:T(8,128)S(1)} all-to-all(f32[8,24,128]{2,1,0:T(8,128)S(1)} %get-tuple-element.75), channel_id=1, replica_groups=mesh['row'=8,'col'=4] {'row'}, dimensions={0} | all-to-all | bytes 196608 | tf_op jit(solution)/shard_map/all_to_all | solution.py:655
  72.7 1.2 %shard_map.102 = (f32[64,128]{1,0:T(8,128)S(1)}, f32[32,4,128]{2,1,0:T(4,128)S(1)}) custom-call(s32[4]{0:T(128)S(1)} %pad_add_fusion.ids, f32[7,64,128]{2,1,0:T(8,128)S(1)} %get-tuple-element.54.coef, f32[16,128]{1,0:T(8,128)S(1)} %get-tuple-element.46.vent, f32[64,128]{1,0:T(8,128)S(1)} %get-tuple-element.74.field.p0, ...), custom_call_target="tpu_custom_call" | custom-call | tf_op jit(solution)/shard_map/pallas_call | solution.py:612
  73.9 10.3 %all_to_all.42.rec = f32[32,4,128]{2,1,0:T(4,128)S(1)} all-to-all(f32[32,4,128]{2,1,0:T(4,128)S(1)} %get-tuple-element.77), channel_id=1, replica_groups=mesh['row'=8,'col'=4] {'row','col'}, dimensions={0} | all-to-all | bytes 131072 | tf_op jit(solution)/shard_map/all_to_all | solution.py:783
  87.2 7.6 %all_to_all.43.rec = f32[8,24,128]{2,1,0:T(8,128)S(1)} all-to-all(f32[8,24,128]{2,1,0:T(8,128)S(1)} %get-tuple-element.80), channel_id=1, replica_groups=mesh['row'=8,'col'=4] {'row'}, dimensions={0} | all-to-all | bytes 196608 | tf_op jit(solution)/shard_map/all_to_all | solution.py:655
  95.6 10.1 %all_to_all.44.rec = f32[32,2,128]{2,1,0:T(2,128)S(1)} all-to-all(f32[32,2,128]{2,1,0:T(2,128)S(1)} %get-tuple-element.82), channel_id=1, replica_groups=mesh['row'=8,'col'=4] {'row','col'}, dimensions={0} | all-to-all | bytes 65536 | tf_op jit(solution)/shard_map/all_to_all | solution.py:798
  (46 shorter events, 11.0 us)
Async XLA Ops:
  1.9 5.1 %copy-start.2 = (s32[4,16,128]{2,1,0:T(8,128)S(1)}, s32[4,16,128]{2,1,0:T(8,128)}, u32[]{:S(2)}) copy-start(s32[4,16,128]{2,1,0:T(8,128)} %param.8) | copy-start | bytes 98308
  1.9 5.1 %copy-start.3 = (f32[16,128]{1,0:T(8,128)S(1)}, f32[16,128]{1,0:T(8,128)}, u32[]{:S(2)}) copy-start(f32[16,128]{1,0:T(8,128)} %vent.1) | copy-start | bytes 24580
  2.2 4.6 %copy-start.6 = (s32[1,1,2]{2,1,0:T(1,128)S(1)}, s32[1,1,2]{2,1,0:T(1,128)}, u32[]{:S(2)}) copy-start(s32[1,1,2]{2,1,0:T(1,128)} %param.12) | copy-start | bytes 28
  2.2 4.6 %copy-start.4 = (f32[8]{0:T(128)S(1)}, f32[8]{0:T(128)}, u32[]{:S(2)}) copy-start(f32[8]{0:T(128)} %param.9) | copy-start | bytes 100
  2.3 4.6 %copy-start.5 = (f32[8]{0:T(128)S(1)}, f32[8]{0:T(128)}, u32[]{:S(2)}) copy-start(f32[8]{0:T(128)} %param.10) | copy-start | bytes 100
  2.3 19.5 %collective-permute-start.4 = (bf16[64,2048]{1,0:T(8,128)(2,1)S(1)}, bf16[64,2048]{1,0:T(8,128)(2,1)S(1)}, u32[]{:S(2)}, u32[]{:S(2)}) collective-permute-start(bf16[64,2048]{1,0:T(8,128)(2,1)S(1)} %get-tuple-element.53), channel_id=1, source_target_pairs={{0,24},{4,28},{8,16},{12,20},{16,8},{20,12},{24,0},{28,4},{1,25},{... | collective-permute-start | bytes 786440 | tf_op jit(solution)/shard_map/ppermute | solution.py:650
  6.2 15.6 %collective-permute-start.3 = (bf16[64,2048]{1,0:T(8,128)(2,1)S(1)}, bf16[64,2048]{1,0:T(8,128)(2,1)S(1)}, u32[]{:S(2)}, u32[]{:S(2)}) collective-permute-start(bf16[64,2048]{1,0:T(8,128)(2,1)S(1)} %get-tuple-element.53), channel_id=1, source_target_pairs={{0,16},{4,20},{8,24},{12,28},{16,0},{20,4},{24,8},{28,12},{1,17},{... | collective-permute-start | bytes 786440 | tf_op jit(solution)/shard_map/ppermute | solution.py:650
  6.7 15.1 %collective-permute-start.2 = (bf16[64,2048]{1,0:T(8,128)(2,1)S(1)}, bf16[64,2048]{1,0:T(8,128)(2,1)S(1)}, u32[]{:S(2)}, u32[]{:S(2)}) collective-permute-start(bf16[64,2048]{1,0:T(8,128)(2,1)S(1)} %get-tuple-element.53), channel_id=1, source_target_pairs={{0,8},{4,12},{8,0},{12,4},{16,24},{20,28},{24,16},{28,20},{1,9},{5... | collective-permute-start | bytes 786440 | tf_op jit(solution)/shard_map/ppermute | solution.py:650
  8.2 7.9 %copy-start.1 = (f32[4,16,128]{2,1,0:T(8,128)S(1)}, f32[4,16,128]{2,1,0:T(8,128)}, u32[]{:S(2)}) copy-start(f32[4,16,128]{2,1,0:T(8,128)} %param.7) | copy-start | bytes 98308
  8.2 13.6 %all-to-all-start = ((f32[8,32,128]{2,1,0:T(8,128)}), f32[8,32,128]{2,1,0:T(8,128)S(1)}, u32[]{:S(2)}, u32[]{:S(2)}) async-start(f32[8,32,128]{2,1,0:T(8,128)} %get-tuple-element.48), calls=%async_computation | async-start | bytes 262144 | tf_op jit(solution)/shard_map/all_to_all | solution.py:655
  12.5 6.5 %collective-permute-start.1 = (f32[72,128]{1,0:T(8,128)S(1)}, f32[72,128]{1,0:T(8,128)S(1)}, u32[]{:S(2)}, u32[]{:S(2)}) collective-permute-start(f32[72,128]{1,0:T(8,128)S(1)} %get-tuple-element.47.cond_ref.cond), channel_id=1, source_target_pairs={{0,3},{1,0},{2,1},{3,2},{4,7},{5,4},{6,5},{7,6},{8,11},{9,8},{10,9... | collective-permute-start | bytes 110600 | tf_op jit(solution)/shard_map/ppermute | solution.py:646
  16.1 5.8 %collective-permute-start = (f32[72,128]{1,0:T(8,128)S(1)}, f32[72,128]{1,0:T(8,128)S(1)}, u32[]{:S(2)}, u32[]{:S(2)}) collective-permute-start(f32[72,128]{1,0:T(8,128)S(1)} %get-tuple-element.47.cond_ref.cond), channel_id=1, source_target_pairs={{0,1},{1,2},{2,3},{3,0},{4,5},{5,6},{6,7},{7,4},{8,9},{9,10},{10,1... | collective-permute-start | bytes 110600 | tf_op jit(solution)/shard_map/ppermute | solution.py:646
  25.8 11.5 %collective-permute-start.5 = (bf16[64,4608]{1,0:T(8,128)(2,1)}, bf16[64,4608]{1,0:T(8,128)(2,1)S(1)}, u32[]{:S(2)}, u32[]{:S(2)}) collective-permute-start(bf16[64,4608]{1,0:T(8,128)(2,1)} %get-tuple-element.58), channel_id=1, source_target_pairs={{0,4},{4,0},{8,12},{12,8},{16,20},{20,16},{24,28},{28,24},{1,5},{5... | collective-permute-start | bytes 1769480 | tf_op jit(solution)/shard_map/ppermute | solution.py:650
  25.9 11.4 %all-to-all-start.1 = ((f32[8,56,128]{2,1,0:T(8,128)}), f32[8,56,128]{2,1,0:T(8,128)S(1)}, u32[]{:S(2)}, u32[]{:S(2)}) async-start(f32[8,56,128]{2,1,0:T(8,128)} %get-tuple-element.61), calls=%async_computation.1 | async-start | bytes 458752 | tf_op jit(solution)/shard_map/all_to_all | solution.py:655
  30.2 4.6 %collective-permute-start.7 = (f32[136,128]{1,0:T(8,128)S(1)}, f32[136,128]{1,0:T(8,128)S(1)}, u32[]{:S(2)}, u32[]{:S(2)}) collective-permute-start(f32[136,128]{1,0:T(8,128)S(1)} %get-tuple-element.60.field), channel_id=1, source_target_pairs={{0,3},{1,0},{2,1},{3,2},{4,7},{5,4},{6,5},{7,6},{8,11},{9,8},{10,9... | collective-permute-start | bytes 208904 | tf_op jit(solution)/shard_map/ppermute | solution.py:646
  31.2 6.1 %collective-permute-start.6 = (f32[136,128]{1,0:T(8,128)S(1)}, f32[136,128]{1,0:T(8,128)S(1)}, u32[]{:S(2)}, u32[]{:S(2)}) collective-permute-start(f32[136,128]{1,0:T(8,128)S(1)} %get-tuple-element.60.field), channel_id=1, source_target_pairs={{0,1},{1,2},{2,3},{3,0},{4,5},{5,6},{6,7},{7,4},{8,9},{9,10},{10,1... | collective-permute-start | bytes 208904 | tf_op jit(solution)/shard_map/ppermute | solution.py:646
  32.2 8.4 %collective-permute-start.8 = (bf16[64,512]{1,0:T(8,128)(2,1)S(1)}, bf16[64,512]{1,0:T(8,128)(2,1)S(1)}, u32[]{:S(2)}, u32[]{:S(2)}) collective-permute-start(bf16[64,512]{1,0:T(8,128)(2,1)S(1)} %get-tuple-element.63), channel_id=1, source_target_pairs={{0,28},{4,8},{8,4},{12,16},{16,12},{20,24},{24,20},{28,0},{1,29},{... | collective-permute-start | bytes 196616 | tf_op jit(solution)/shard_map/ppermute | solution.py:673
  38.6 11.3 %collective-permute-start.10 = (f32[200,128]{1,0:T(8,128)S(1)}, f32[200,128]{1,0:T(8,128)S(1)}, u32[]{:S(2)}, u32[]{:S(2)}) collective-permute-start(f32[200,128]{1,0:T(8,128)S(1)} %get-tuple-element.66), channel_id=1, source_target_pairs={{0,3},{1,0},{2,1},{3,2},{4,7},{5,4},{6,5},{7,6},{8,11},{9,8},{10,9... | collective-permute-start | bytes 307208 | tf_op jit(solution)/shard_map/ppermute | solution.py:646
  39.3 10.5 %collective-permute-start.9 = (f32[200,128]{1,0:T(8,128)S(1)}, f32[200,128]{1,0:T(8,128)S(1)}, u32[]{:S(2)}, u32[]{:S(2)}) collective-permute-start(f32[200,128]{1,0:T(8,128)S(1)} %get-tuple-element.66), channel_id=1, source_target_pairs={{0,1},{1,2},{2,3},{3,0},{4,5},{5,6},{6,7},{7,4},{8,9},{9,10},{10,1... | collective-permute-start | bytes 307208 | tf_op jit(solution)/shard_map/ppermute | solution.py:646
  51.7 10.4 %all-to-all-start.3 = ((f32[32,4,128]{2,1,0:T(4,128)}), f32[32,4,128]{2,1,0:T(4,128)S(1)}, u32[]{:S(2)}, u32[]{:S(2)}) async-start(f32[32,4,128]{2,1,0:T(4,128)} %get-tuple-element.70._), calls=%async_computation.3 | async-start | bytes 131072 | tf_op jit(solution)/shard_map/all_to_all | solution.py:766
  63.0 9.6 %collective-permute-start.12 = (f32[200,128]{1,0:T(8,128)S(1)}, f32[200,128]{1,0:T(8,128)S(1)}, u32[]{:S(2)}, u32[]{:S(2)}) collective-permute-start(f32[200,128]{1,0:T(8,128)S(1)} %get-tuple-element.76), channel_id=1, source_target_pairs={{0,3},{1,0},{2,1},{3,2},{4,7},{5,4},{6,5},{7,6},{8,11},{9,8},{10,9... | collective-permute-start | bytes 307208 | tf_op jit(solution)/shard_map/ppermute | solution.py:646
  63.9 8.8 %collective-permute-start.11 = (f32[200,128]{1,0:T(8,128)S(1)}, f32[200,128]{1,0:T(8,128)S(1)}, u32[]{:S(2)}, u32[]{:S(2)}) collective-permute-start(f32[200,128]{1,0:T(8,128)S(1)} %get-tuple-element.76), channel_id=1, source_target_pairs={{0,1},{1,2},{2,3},{3,0},{4,5},{5,6},{6,7},{7,4},{8,9},{9,10},{10,1... | collective-permute-start | bytes 307208 | tf_op jit(solution)/shard_map/ppermute | solution.py:646
  85.2 9.6 %collective-permute-start.14 = (f32[200,128]{1,0:T(8,128)S(1)}, f32[200,128]{1,0:T(8,128)S(1)}, u32[]{:S(2)}, u32[]{:S(2)}) collective-permute-start(f32[200,128]{1,0:T(8,128)S(1)} %get-tuple-element.81), channel_id=1, source_target_pairs={{0,3},{1,0},{2,1},{3,2},{4,7},{5,4},{6,5},{7,6},{8,11},{9,8},{10,9... | collective-permute-start | bytes 307208 | tf_op jit(solution)/shard_map/ppermute | solution.py:646
  86.0 8.8 %collective-permute-start.13 = (f32[200,128]{1,0:T(8,128)S(1)}, f32[200,128]{1,0:T(8,128)S(1)}, u32[]{:S(2)}, u32[]{:S(2)}) collective-permute-start(f32[200,128]{1,0:T(8,128)S(1)} %get-tuple-element.81), channel_id=1, source_target_pairs={{0,1},{1,2},{2,3},{3,0},{4,5},{5,6},{6,7},{7,4},{8,9},{9,10},{10,1... | collective-permute-start | bytes 307208 | tf_op jit(solution)/shard_map/ppermute | solution.py:646
  (1 other events, 1.2 us)

commit v9 on v8

--- a/solution.py
+++ b/solution.py
@@ -221,7 +221,7 @@
     return uz, lz, ux, lx, uy, ly
 
 
-def k_order(grid, basis, zm, panel, face):
+def k_order(grid, basis, zm, panel, face_a, face_b):
     n, d, w, layers = grid.rows, grid.depth, grid.width, grid.layers
     size = basis.shape[0]
     odd = lax.bitwise_and(lax.axis_index("row"), 1) == 1
@@ -236,7 +236,9 @@
         start = z * w * d
         first = zm[:, start : start + d].astype(F32)
         last = zm[:, start + (w - 1) * d : start + w * d].astype(F32)
-        face[:, z * d : (z + 1) * d] = jnp.where(odd, last, first).astype(BF16)
+        half = layers // 2
+        face, at = (face_a, z) if z < half else (face_b, z - half)
+        face[:, at * d : (at + 1) * d] = jnp.where(odd, last, first).astype(BF16)
 
 
 def k_basis(grid, zm, rhs, cond_ref, cap_ref, own, projected, face_y, zr, w3, coef):
@@ -423,20 +425,20 @@
 
 def x_faces(grid, pairs, ids, others, far):
     near = others[:, pairs * grid.width * grid.depth :].astype(F32)
-    across = far[...].astype(F32)
+    across = jnp.concatenate([part[...].astype(F32) for part in far], axis=1)
     upward = lax.bitwise_and(ids[pairs], 1) == 0
     return jnp.where(upward, near, across), jnp.where(upward, across, near)
 
 
 def k_partials(
-    grid, pairs, base, ids, coef, vent, field, far, rec, low, high, vents, zm, low2, high2, mine,
+    grid, pairs, base, ids, coef, vent, field, far_a, far_b, rec, low, high, vents, zm, low2, high2, mine,
     others, *rest,
 ):
     n, d, w, layers = grid.rows, grid.depth, grid.width, grid.layers
     size = zm.shape[0]
     base_ref = rest[0] if base else None
     out, pay = rest[-2:]
-    next_first, prev_last = x_faces(grid, pairs, ids, others, far)
+    next_first, prev_last = x_faces(grid, pairs, ids, others, (far_a, far_b))
     v = operate(grid, coef, vent[...], field[...], incoming(grid, pairs, ids, rec, low, high))
     if base:
         v = base_ref[...] - v
@@ -537,7 +539,7 @@
 
 
 def k_blocks(
-    grid, pairs, cols, scale, ids, coef, vents, names, zm, mine, others, x_far, own, inverse,
+    grid, pairs, cols, scale, ids, coef, vents, names, zm, mine, others, x_far_a, x_far_b, own, inverse,
     face_y, low2, high2, solves, _, out, weights, table, w3,
 ):
     n, d, w, layers = grid.rows, grid.depth, grid.width, grid.layers
@@ -574,7 +576,7 @@
     def basis_rows(at):
         return [zm[:, i * d : (i + 1) * d] for i in at]
 
-    next_first, prev_last = [f.astype(BF16) for f in x_faces(grid, pairs, ids, others, x_far)]
+    next_first, prev_last = [f.astype(BF16) for f in x_faces(grid, pairs, ids, others, (x_far_a, x_far_b))]
     found = [
         weighted_gram(w3, basis_rows(last), [-ux[i : i + 1] for i in last], next_first),
         weighted_gram(w3, basis_rows(first), [-lx[i : i + 1] for i in first], prev_last),
@@ -659,22 +661,20 @@
         return ((row_count, width + 2 * layers + count, depth), F32)
 
     tables = jnp.concatenate([conductivity, capacity, partners.reshape(-1).astype(F32)])
-    zm, panel, face = call(
+    zm, panel, *face = call(
         functools.partial(k_order, grid),
         (
             ((size, n * depth), BF16),
             ((size, width * depth), BF16),
-            ((size, layers * depth), BF16),
+            ((size, layers // 2 * depth), BF16),
+            ((size, (layers - layers // 2) * depth), BF16),
         ),
         (basis,),
         cost=pl.CostEstimate(flops=1000, bytes_accessed=1000, transcendentals=0),
     )
     held = [xor_step(panel, "row", k) for k in range(2, row_count, 2)]
-    x_far = lax.ppermute(
-        face,
-        "row",
-        [(i, (i + 1 if i % 2 else i - 1) % row_count) for i in range(row_count)],
-    )
+    across = [(i, (i + 1 if i % 2 else i - 1) % row_count) for i in range(row_count)]
+    x_far_a, x_far_b = [lax.ppermute(part, "row", across) for part in face]
     cond, cap, vent, pay0 = call(
         functools.partial(k_first, grid, pairs),
         (((n + 8, depth), F32), field, ((width, depth), F32), rows_of(8)),
@@ -702,7 +702,7 @@
             ((7, n, depth), F32),
             small,
             small,
-            ((136, depth), F32),
+            ((n + 8, depth), F32),
             rows_of(size // 2),
             panels,
             ((size, (pairs * width + layers) * depth), BF16),
@@ -732,7 +732,7 @@
         smem=1,
         free=(10,),
     )
-    pay2, x_far = lax.optimization_barrier((pay2, x_far))
+    pay2, x_far_a, x_far_b = lax.optimization_barrier((pay2, x_far_a, x_far_b))
     rec, low2, high2 = exchange(wide2, pay2)
 
     def everyone(lines):
@@ -742,7 +742,7 @@
         functools.partial(k_partials, grid, pairs, True),
         (field, everyone((places + 1) // 2)),
         (
-            ids, coef, vent, x0, x_far, rec, low2, high2, vents, zm, low2, high2, mine, others, rhs,
+            ids, coef, vent, x0, x_far_a, x_far_b, rec, low2, high2, vents, zm, low2, high2, mine, others, rhs,
         ),
         smem=1,
     )
@@ -754,12 +754,12 @@
             ((places * places,), jnp.int32),
         ),
         (
-            ids, coef, vents, names, zm, mine, others, x_far, own, inverse, face_y, low2,
+            ids, coef, vents, names, zm, mine, others, x_far_a, x_far_b, own, inverse, face_y, low2,
             high2, solves, pay3,
         ),
         scratch=(pltpu.VMEM((3 * size, width * depth), BF16),),
         smem=1,
-        free=(14,),
+        free=(15,),
         smem_outs=(2,),
         cost=pl.CostEstimate(flops=100_000_000, bytes_accessed=4_000_000, transcendentals=0),
     )
@@ -776,7 +776,7 @@
         functools.partial(k_partials, grid, pairs, False),
         (field, everyone((places + 1) // 2)),
         (
-            ids, coef, vent, p0, x_far, rec, low, high, vents, zm, low2, high2, mine, others,
+            ids, coef, vent, p0, x_far_a, x_far_b, rec, low, high, vents, zm, low2, high2, mine, others,
         ),
         smem=1,
     )

time: 107 us -> 106 us (level)
    ppermute x1 -> x2, starting transfers between devices: 2.12 us -> 2.64 us  [body(): x_far_a, x_far_b = [lax.ppermute(part, 'row', across) for part in face]]
  transfers between devices with their start and end apart: 18 -> 19, of which waited for: 4 -> 4; matrix products, arithmetic and copies ran while one was open for 0% -> 0% of each run, Pallas kernels for 8% -> 8%
where the time goes in v9:
time: 106 us
  blocking collectives  44.5 us (42%)
  starting transfers between devices  30.3 us (29%)
  Pallas kernels  19.1 us (18%)
  waiting for transfers between devices  9.73 us (9%)
  local copies, waits for them, and re-layouts  1.25 us (1%)
    all_to_all x3, blocking collectives, exchange(): rec = lax.all_to_all(payload, 'row', 0, 0)  24.1 us
    pallas_call x12, Pallas kernels, call(): pl.pallas_call(kernel, out_shape=tuple((jax.ShapeDtypeStruct(s, t) for s,...  19.1 us
    ppermute x10, starting transfers between devices, cyclic(): lax.ppermute(value, axis, [(i, (i + step) % count) for i in range(count)])  11.9 us
    all_to_all x1, blocking collectives, body(): sums = lax.all_to_all(pay5, ('row', 'col'), 0, 0)  10.3 us
    all_to_all x1, blocking collectives, body(): total = lax.all_to_all(pay7, ('row', 'col'), 0, 0)  10.1 us
    all_to_all x2, starting transfers between devices, exchange(): rec = lax.all_to_all(payload, 'row', 0, 0)  8.55 us
    ppermute x10, waiting for transfers between devices, cyclic(): lax.ppermute(value, axis, [(i, (i + step) % count) for i in range(count)])  4.95 us
    ppermute x4, starting transfers between devices, xor_step(): return lax.ppermute(value, axis, [(i, i ^ k) for i in range(count)])  4.67 us
  transfers between devices with their start and end apart: 19, of which 4 were waited for; matrix products, arithmetic and copies ran while one was open for 0% of the time, Pallas kernels for 8%

profile of v9, /device:TPU:0, one launch (start us, length us, event | category | flops | bytes accessed | tf_op | source)
XLA Modules:
  0.0 105.7 jit_solution(6530720625470440433)
XLA Ops:
  0.6 1.2 %copy-done = bf16[64,4,16,128]{3,2,1,0:T(8,128)(2,1)S(1)} copy-done((bf16[64,4,16,128]{3,2,1,0:T(8,128)(2,1)S(1)}, bf16[64,4,16,128]{3,2,1,0:T(8,128)(2,1)}, u32[]{:S(2)}) %copy-start) | copy-done | bytes 1048600
  2.3 4.0 %collective-permute-start.4 = (bf16[64,2048]{1,0:T(8,128)(2,1)S(1)}, bf16[64,2048]{1,0:T(8,128)(2,1)S(1)}, u32[]{:S(2)}, u32[]{:S(2)}) collective-permute-start(bf16[64,2048]{1,0:T(8,128)(2,1)S(1)} %get-tuple-element.55), channel_id=1, source_target_pairs={{0,24},{4,28},{8,16},{12,20},{16,8},{20,12},{24,0},{28,4},{1,25},{... | collective-permute-start | bytes 786440 | tf_op jit(solution)/shard_map/ppermute | solution.py:652
  7.0 1.2 %shard_map.94 = (f32[72,128]{1,0:T(8,128)S(1)}, f32[64,128]{1,0:T(8,128)S(1)}, f32[16,128]{1,0:T(8,128)S(1)}, f32[8,32,128]{2,1,0:T(8,128)}) custom-call(f32[18]{0:T(128)S(1)} %pad_maximum_fusion.tables, s32[64,128]{1,0:T(8,128)S(1)} %bitcast.13, f32[16,128]{1,0:T(8,128)S(1)} %copy-done.3), custom_call_target="tpu_custom_call" | custom-call | tf_op jit(solution)/shard_map/pallas_call | solution.py:614
  8.2 4.3 %all-to-all-start = ((f32[8,32,128]{2,1,0:T(8,128)}), f32[8,32,128]{2,1,0:T(8,128)S(1)}, u32[]{:S(2)}, u32[]{:S(2)}) async-start(f32[8,32,128]{2,1,0:T(8,128)} %get-tuple-element.50), calls=%async_computation | async-start | bytes 262144 | tf_op jit(solution)/shard_map/all_to_all | solution.py:657
  12.5 3.6 %collective-permute-start.1 = (f32[72,128]{1,0:T(8,128)S(1)}, f32[72,128]{1,0:T(8,128)S(1)}, u32[]{:S(2)}, u32[]{:S(2)}) collective-permute-start(f32[72,128]{1,0:T(8,128)S(1)} %get-tuple-element.49.cond_ref.cond), channel_id=1, source_target_pairs={{0,3},{1,0},{2,1},{3,2},{4,7},{5,4},{6,5},{7,6},{8,11},{9,8},{10,9... | collective-permute-start | bytes 110600 | tf_op jit(solution)/shard_map/ppermute | solution.py:648
  16.1 2.8 %shard_map.96 = (f32[64,64]{1,0:T(8,128)S(1)}, f32[64,128]{1,0:T(8,128)S(1)}, f32[64,128]{1,0:T(8,128)S(1)}) custom-call(bf16[64,8192]{1,0:T(8,128)(2,1)S(1)} %get-tuple-element.51.zm, f32[64,128]{1,0:T(8,128)S(1)} %bitcast.11, f32[72,128]{1,0:T(8,128)S(1)} %get-tuple-element.49.cond_ref.cond, f32[64,128]{1,0:T(8,128)S(1)} %get-tuple-element.47.cap_ref.cap), custom_call_target="tpu_custom_call" | custom-call | flops 1000 | bytes 1000 | tf_op jit(solution)/shard_map/pallas_call | solution.py:614
  18.9 2.9 %collective-permute-done.cond_low = f32[72,128]{1,0:T(8,128)S(1)} collective-permute-done((f32[72,128]{1,0:T(8,128)S(1)}, f32[72,128]{1,0:T(8,128)S(1)}, u32[]{:S(2)}, u32[]{:S(2)}) %collective-permute-start) | collective-permute-done | bytes 36896 | tf_op jit(solution)/shard_map/ppermute | solution.py:648
  21.8 4.0 %shard_map.97 = (f32[7,64,128]{2,1,0:T(8,128)S(1)}, f32[64,64]{1,0:T(8,128)S(1)}, f32[64,64]{1,0:T(8,128)S(1)}, f32[72,128]{1,0:T(8,128)S(1)}, f32[8,56,128]{2,1...) custom-call(s32[4]{0:T(128)S(1)} %pad_add_fusion.ids, ...), custom_call_target="tpu_custom_call" | custom-call | tf_op jit(solution)/shard_map/pallas_call | solution.py:614
  25.9 4.3 %all-to-all-start.1 = ((f32[8,56,128]{2,1,0:T(8,128)}), f32[8,56,128]{2,1,0:T(8,128)S(1)}, u32[]{:S(2)}, u32[]{:S(2)}) async-start(f32[8,56,128]{2,1,0:T(8,128)} %get-tuple-element.63), calls=%async_computation.1 | async-start | bytes 458752 | tf_op jit(solution)/shard_map/all_to_all | solution.py:657
  32.3 2.1 %collective-permute-start.8 = (bf16[64,256]{1,0:T(8,128)(2,1)S(1)}, bf16[64,256]{1,0:T(8,128)(2,1)S(1)}, u32[]{:S(2)}, u32[]{:S(2)}) collective-permute-start(bf16[64,256]{1,0:T(8,128)(2,1)S(1)} %get-tuple-element.65), channel_id=1, source_target_pairs={{0,28},{4,8},{8,4},{12,16},{16,12},{20,24},{24,20},{28,0},{1,29},{... | collective-permute-start | bytes 98312 | tf_op jit(solution)/shard_map/ppermute | solution.py:677
  34.9 2.1 %collective-permute-done.6.low = f32[72,128]{1,0:T(8,128)S(1)} collective-permute-done((f32[72,128]{1,0:T(8,128)S(1)}, f32[72,128]{1,0:T(8,128)S(1)}, u32[]{:S(2)}, u32[]{:S(2)}) %collective-permute-start.6) | collective-permute-done | bytes 36896 | tf_op jit(solution)/shard_map/ppermute | solution.py:648
  37.2 1.3 %shard_map.98 = (f32[64,128]{1,0:T(8,128)S(1)}, f32[200,128]{1,0:T(8,128)S(1)}, f32[8,24,128]{2,1,0:T(8,128)S(1)}, f32[4,32,128]{2,1,0:T(8,128)S(1)}) custom-call(s32[4]{0:T(128)S(1)} %pad_add_fusion.ids, f32[7,64,128]{2,1,0:T(8,128)S(1)} %get-tuple-element.56.coef, f32[16,128]{1,0:T(8,128)S(1)} %get-tuple-element.48.vent, ...), custom_call_target="tpu_custom_call" | custom-call | tf_op jit(solution)/shard_map/pallas_call | solution.py:614
  39.1 1.4 %collective-permute-start.10 = (f32[200,128]{1,0:T(8,128)S(1)}, f32[200,128]{1,0:T(8,128)S(1)}, u32[]{:S(2)}, u32[]{:S(2)}) collective-permute-start(f32[200,128]{1,0:T(8,128)S(1)} %get-tuple-element.70), channel_id=1, source_target_pairs={{0,1},{1,2},{2,3},{3,0},{4,5},{5,6},{6,7},{7,4},{8,9},{9,10},{10,1... | collective-permute-start | bytes 307208 | tf_op jit(solution)/shard_map/ppermute | solution.py:648
  40.5 9.0 %all_to_all.40.rec = f32[8,24,128]{2,1,0:T(8,128)S(1)} all-to-all(f32[8,24,128]{2,1,0:T(8,128)S(1)} %get-tuple-element.73), channel_id=1, replica_groups=mesh['row'=8,'col'=4] {'row'}, dimensions={0} | all-to-all | bytes 196608 | tf_op jit(solution)/shard_map/all_to_all | solution.py:657
  49.5 1.8 %shard_map.99 = (f32[64,128]{1,0:T(8,128)S(1)}, f32[32,4,128]{2,1,0:T(4,128)}) custom-call(s32[4]{0:T(128)S(1)} %pad_add_fusion.ids, f32[7,64,128]{2,1,0:T(8,128)S(1)} %get-tuple-element.56.coef, f32[16,128]{1,0:T(8,128)S(1)} %get-tuple-element.48.vent, f32[64,128]{1,0:T(8,128)S(1)} %get-tuple-element.72.field.x0, ...), custom_call_target="tpu_custom_call" | custom-call | tf_op jit(solution)/shard_map/pallas_call | solution.py:614
  51.3 2.6 %all-to-all-start.3 = ((f32[32,4,128]{2,1,0:T(4,128)}), f32[32,4,128]{2,1,0:T(4,128)S(1)}, u32[]{:S(2)}, u32[]{:S(2)}) async-start(f32[32,4,128]{2,1,0:T(4,128)} %get-tuple-element.74._), calls=%async_computation.3 | async-start | bytes 131072 | tf_op jit(solution)/shard_map/all_to_all | solution.py:766
  53.9 2.9 %shard_map.100 = (f32[8,64,64]{2,1,0:T(8,128)}, f32[7,64,64]{2,1,0:T(8,128)S(1)}, s32[49]{0:T(128)S(1)}) custom-call(s32[4]{0:T(128)S(1)} %pad_add_fusion.ids, f32[7,64,128]{2,1,0:T(8,128)S(1)} %get-tuple-element.56.coef, f32[2,16,128]{2,1,0:T(8,128)S(1)} %get-tuple-element.57.vents, f32[6,128]{1,0:T(8,128)S(1)} %get-tuple-element.58.names, ...), custom_call_target="tpu_custom_call" | custom-call | flops 100000000 | bytes 4000000 | tf_op jit(solution)/shard_map/pallas_call | solution.py:614
  56.8 4.6 %all-to-all-done.3.rec = f32[32,4,128]{2,1,0:T(4,128)S(1)} async-done(((f32[32,4,128]{2,1,0:T(4,128)}), f32[32,4,128]{2,1,0:T(4,128)S(1)}, u32[]{:S(2)}, u32[]{:S(2)}) %all-to-all-start.3) | async-done | bytes 65568 | tf_op jit(solution)/shard_map/all_to_all | solution.py:766
  63.2 1.2 %collective-permute-start.12 = (f32[200,128]{1,0:T(8,128)S(1)}, f32[200,128]{1,0:T(8,128)S(1)}, u32[]{:S(2)}, u32[]{:S(2)}) collective-permute-start(f32[200,128]{1,0:T(8,128)S(1)} %get-tuple-element.80), channel_id=1, source_target_pairs={{0,1},{1,2},{2,3},{3,0},{4,5},{5,6},{6,7},{7,4},{8,9},{9,10},{10,1... | collective-permute-start | bytes 307208 | tf_op jit(solution)/shard_map/ppermute | solution.py:648
  64.5 7.6 %all_to_all.41.rec = f32[8,24,128]{2,1,0:T(8,128)S(1)} all-to-all(f32[8,24,128]{2,1,0:T(8,128)S(1)} %get-tuple-element.79), channel_id=1, replica_groups=mesh['row'=8,'col'=4] {'row'}, dimensions={0} | all-to-all | bytes 196608 | tf_op jit(solution)/shard_map/all_to_all | solution.py:657
  72.0 1.2 %shard_map.102 = (f32[64,128]{1,0:T(8,128)S(1)}, f32[32,4,128]{2,1,0:T(4,128)S(1)}) custom-call(s32[4]{0:T(128)S(1)} %pad_add_fusion.ids, f32[7,64,128]{2,1,0:T(8,128)S(1)} %get-tuple-element.56.coef, f32[16,128]{1,0:T(8,128)S(1)} %get-tuple-element.48.vent, f32[64,128]{1,0:T(8,128)S(1)} %get-tuple-element.78.field.p0, ...), custom_call_target="tpu_custom_call" | custom-call | tf_op jit(solution)/shard_map/pallas_call | solution.py:614
  73.2 10.3 %all_to_all.42.rec = f32[32,4,128]{2,1,0:T(4,128)S(1)} all-to-all(f32[32,4,128]{2,1,0:T(4,128)S(1)} %get-tuple-element.81), channel_id=1, replica_groups=mesh['row'=8,'col'=4] {'row','col'}, dimensions={0} | all-to-all | bytes 131072 | tf_op jit(solution)/shard_map/all_to_all | solution.py:783
  86.5 7.6 %all_to_all.43.rec = f32[8,24,128]{2,1,0:T(8,128)S(1)} all-to-all(f32[8,24,128]{2,1,0:T(8,128)S(1)} %get-tuple-element.84), channel_id=1, replica_groups=mesh['row'=8,'col'=4] {'row'}, dimensions={0} | all-to-all | bytes 196608 | tf_op jit(solution)/shard_map/all_to_all | solution.py:657
  94.9 10.1 %all_to_all.44.rec = f32[32,2,128]{2,1,0:T(2,128)S(1)} all-to-all(f32[32,2,128]{2,1,0:T(2,128)S(1)} %get-tuple-element.86), channel_id=1, replica_groups=mesh['row'=8,'col'=4] {'row','col'}, dimensions={0} | all-to-all | bytes 65536 | tf_op jit(solution)/shard_map/all_to_all | solution.py:798
  (48 shorter events, 11.1 us)
Async XLA Ops:
  1.9 5.1 %copy-start.2 = (s32[4,16,128]{2,1,0:T(8,128)S(1)}, s32[4,16,128]{2,1,0:T(8,128)}, u32[]{:S(2)}) copy-start(s32[4,16,128]{2,1,0:T(8,128)} %param.8) | copy-start | bytes 98308
  1.9 5.1 %copy-start.3 = (f32[16,128]{1,0:T(8,128)S(1)}, f32[16,128]{1,0:T(8,128)}, u32[]{:S(2)}) copy-start(f32[16,128]{1,0:T(8,128)} %vent.1) | copy-start | bytes 24580
  2.2 4.6 %copy-start.6 = (s32[1,1,2]{2,1,0:T(1,128)S(1)}, s32[1,1,2]{2,1,0:T(1,128)}, u32[]{:S(2)}) copy-start(s32[1,1,2]{2,1,0:T(1,128)} %param.12) | copy-start | bytes 28
  2.2 4.6 %copy-start.4 = (f32[8]{0:T(128)S(1)}, f32[8]{0:T(128)}, u32[]{:S(2)}) copy-start(f32[8]{0:T(128)} %param.9) | copy-start | bytes 100
  2.3 19.5 %collective-permute-start.4 = (bf16[64,2048]{1,0:T(8,128)(2,1)S(1)}, bf16[64,2048]{1,0:T(8,128)(2,1)S(1)}, u32[]{:S(2)}, u32[]{:S(2)}) collective-permute-start(bf16[64,2048]{1,0:T(8,128)(2,1)S(1)} %get-tuple-element.55), channel_id=1, source_target_pairs={{0,24},{4,28},{8,16},{12,20},{16,8},{20,12},{24,0},{28,4},{1,25},{... | collective-permute-start | bytes 786440 | tf_op jit(solution)/shard_map/ppermute | solution.py:652
  6.2 15.6 %collective-permute-start.3 = (bf16[64,2048]{1,0:T(8,128)(2,1)S(1)}, bf16[64,2048]{1,0:T(8,128)(2,1)S(1)}, u32[]{:S(2)}, u32[]{:S(2)}) collective-permute-start(bf16[64,2048]{1,0:T(8,128)(2,1)S(1)} %get-tuple-element.55), channel_id=1, source_target_pairs={{0,16},{4,20},{8,24},{12,28},{16,0},{20,4},{24,8},{28,12},{1,17},{... | collective-permute-start | bytes 786440 | tf_op jit(solution)/shard_map/ppermute | solution.py:652
  6.7 15.1 %collective-permute-start.2 = (bf16[64,2048]{1,0:T(8,128)(2,1)S(1)}, bf16[64,2048]{1,0:T(8,128)(2,1)S(1)}, u32[]{:S(2)}, u32[]{:S(2)}) collective-permute-start(bf16[64,2048]{1,0:T(8,128)(2,1)S(1)} %get-tuple-element.55), channel_id=1, source_target_pairs={{0,8},{4,12},{8,0},{12,4},{16,24},{20,28},{24,16},{28,20},{1,9},{5... | collective-permute-start | bytes 786440 | tf_op jit(solution)/shard_map/ppermute | solution.py:652
  8.2 7.9 %copy-start.1 = (f32[4,16,128]{2,1,0:T(8,128)S(1)}, f32[4,16,128]{2,1,0:T(8,128)}, u32[]{:S(2)}) copy-start(f32[4,16,128]{2,1,0:T(8,128)} %param.7) | copy-start | bytes 98308
  8.2 13.6 %all-to-all-start = ((f32[8,32,128]{2,1,0:T(8,128)}), f32[8,32,128]{2,1,0:T(8,128)S(1)}, u32[]{:S(2)}, u32[]{:S(2)}) async-start(f32[8,32,128]{2,1,0:T(8,128)} %get-tuple-element.50), calls=%async_computation | async-start | bytes 262144 | tf_op jit(solution)/shard_map/all_to_all | solution.py:657
  12.5 6.5 %collective-permute-start.1 = (f32[72,128]{1,0:T(8,128)S(1)}, f32[72,128]{1,0:T(8,128)S(1)}, u32[]{:S(2)}, u32[]{:S(2)}) collective-permute-start(f32[72,128]{1,0:T(8,128)S(1)} %get-tuple-element.49.cond_ref.cond), channel_id=1, source_target_pairs={{0,3},{1,0},{2,1},{3,2},{4,7},{5,4},{6,5},{7,6},{8,11},{9,8},{10,9... | collective-permute-start | bytes 110600 | tf_op jit(solution)/shard_map/ppermute | solution.py:648
  16.1 5.8 %collective-permute-start = (f32[72,128]{1,0:T(8,128)S(1)}, f32[72,128]{1,0:T(8,128)S(1)}, u32[]{:S(2)}, u32[]{:S(2)}) collective-permute-start(f32[72,128]{1,0:T(8,128)S(1)} %get-tuple-element.49.cond_ref.cond), channel_id=1, source_target_pairs={{0,1},{1,2},{2,3},{3,0},{4,5},{5,6},{6,7},{7,4},{8,9},{9,10},{10,1... | collective-permute-start | bytes 110600 | tf_op jit(solution)/shard_map/ppermute | solution.py:648
  25.9 11.3 %collective-permute-start.5 = (bf16[64,4608]{1,0:T(8,128)(2,1)}, bf16[64,4608]{1,0:T(8,128)(2,1)S(1)}, u32[]{:S(2)}, u32[]{:S(2)}) collective-permute-start(bf16[64,4608]{1,0:T(8,128)(2,1)} %get-tuple-element.60), channel_id=1, source_target_pairs={{0,4},{4,0},{8,12},{12,8},{16,20},{20,16},{24,28},{28,24},{1,5},{5... | collective-permute-start | bytes 1769480 | tf_op jit(solution)/shard_map/ppermute | solution.py:652
  25.9 11.2 %all-to-all-start.1 = ((f32[8,56,128]{2,1,0:T(8,128)}), f32[8,56,128]{2,1,0:T(8,128)S(1)}, u32[]{:S(2)}, u32[]{:S(2)}) async-start(f32[8,56,128]{2,1,0:T(8,128)} %get-tuple-element.63), calls=%async_computation.1 | async-start | bytes 458752 | tf_op jit(solution)/shard_map/all_to_all | solution.py:657
  30.2 4.7 %collective-permute-start.7 = (f32[72,128]{1,0:T(8,128)S(1)}, f32[72,128]{1,0:T(8,128)S(1)}, u32[]{:S(2)}, u32[]{:S(2)}) collective-permute-start(f32[72,128]{1,0:T(8,128)S(1)} %get-tuple-element.62.field), channel_id=1, source_target_pairs={{0,3},{1,0},{2,1},{3,2},{4,7},{5,4},{6,5},{7,6},{8,11},{9,8},{10,9... | collective-permute-start | bytes 110600 | tf_op jit(solution)/shard_map/ppermute | solution.py:648
  31.2 5.8 %collective-permute-start.6 = (f32[72,128]{1,0:T(8,128)S(1)}, f32[72,128]{1,0:T(8,128)S(1)}, u32[]{:S(2)}, u32[]{:S(2)}) collective-permute-start(f32[72,128]{1,0:T(8,128)S(1)} %get-tuple-element.62.field), channel_id=1, source_target_pairs={{0,1},{1,2},{2,3},{3,0},{4,5},{5,6},{6,7},{7,4},{8,9},{9,10},{10,1... | collective-permute-start | bytes 110600 | tf_op jit(solution)/shard_map/ppermute | solution.py:648
  32.3 8.3 %collective-permute-start.8 = (bf16[64,256]{1,0:T(8,128)(2,1)S(1)}, bf16[64,256]{1,0:T(8,128)(2,1)S(1)}, u32[]{:S(2)}, u32[]{:S(2)}) collective-permute-start(bf16[64,256]{1,0:T(8,128)(2,1)S(1)} %get-tuple-element.65), channel_id=1, source_target_pairs={{0,28},{4,8},{8,4},{12,16},{16,12},{20,24},{24,20},{28,0},{1,29},{... | collective-permute-start | bytes 98312 | tf_op jit(solution)/shard_map/ppermute | solution.py:677
  34.4 6.1 %collective-permute-start.9 = (bf16[64,256]{1,0:T(8,128)(2,1)S(1)}, bf16[64,256]{1,0:T(8,128)(2,1)S(1)}, u32[]{:S(2)}, u32[]{:S(2)}) collective-permute-start(bf16[64,256]{1,0:T(8,128)(2,1)S(1)} %get-tuple-element.66), channel_id=1, source_target_pairs={{0,28},{4,8},{8,4},{12,16},{16,12},{20,24},{24,20},{28,0},{1,29},{... | collective-permute-start | bytes 98312 | tf_op jit(solution)/shard_map/ppermute | solution.py:677
  38.4 11.1 %collective-permute-start.11 = (f32[200,128]{1,0:T(8,128)S(1)}, f32[200,128]{1,0:T(8,128)S(1)}, u32[]{:S(2)}, u32[]{:S(2)}) collective-permute-start(f32[200,128]{1,0:T(8,128)S(1)} %get-tuple-element.70), channel_id=1, source_target_pairs={{0,3},{1,0},{2,1},{3,2},{4,7},{5,4},{6,5},{7,6},{8,11},{9,8},{10,9... | collective-permute-start | bytes 307208 | tf_op jit(solution)/shard_map/ppermute | solution.py:648
  39.1 10.4 %collective-permute-start.10 = (f32[200,128]{1,0:T(8,128)S(1)}, f32[200,128]{1,0:T(8,128)S(1)}, u32[]{:S(2)}, u32[]{:S(2)}) collective-permute-start(f32[200,128]{1,0:T(8,128)S(1)} %get-tuple-element.70), channel_id=1, source_target_pairs={{0,1},{1,2},{2,3},{3,0},{4,5},{5,6},{6,7},{7,4},{8,9},{9,10},{10,1... | collective-permute-start | bytes 307208 | tf_op jit(solution)/shard_map/ppermute | solution.py:648
  51.3 10.1 %all-to-all-start.3 = ((f32[32,4,128]{2,1,0:T(4,128)}), f32[32,4,128]{2,1,0:T(4,128)S(1)}, u32[]{:S(2)}, u32[]{:S(2)}) async-start(f32[32,4,128]{2,1,0:T(4,128)} %get-tuple-element.74._), calls=%async_computation.3 | async-start | bytes 131072 | tf_op jit(solution)/shard_map/all_to_all | solution.py:766
  62.4 9.6 %collective-permute-start.13 = (f32[200,128]{1,0:T(8,128)S(1)}, f32[200,128]{1,0:T(8,128)S(1)}, u32[]{:S(2)}, u32[]{:S(2)}) collective-permute-start(f32[200,128]{1,0:T(8,128)S(1)} %get-tuple-element.80), channel_id=1, source_target_pairs={{0,3},{1,0},{2,1},{3,2},{4,7},{5,4},{6,5},{7,6},{8,11},{9,8},{10,9... | collective-permute-start | bytes 307208 | tf_op jit(solution)/shard_map/ppermute | solution.py:648
  63.2 8.8 %collective-permute-start.12 = (f32[200,128]{1,0:T(8,128)S(1)}, f32[200,128]{1,0:T(8,128)S(1)}, u32[]{:S(2)}, u32[]{:S(2)}) collective-permute-start(f32[200,128]{1,0:T(8,128)S(1)} %get-tuple-element.80), channel_id=1, source_target_pairs={{0,1},{1,2},{2,3},{3,0},{4,5},{5,6},{6,7},{7,4},{8,9},{9,10},{10,1... | collective-permute-start | bytes 307208 | tf_op jit(solution)/shard_map/ppermute | solution.py:648
  84.5 9.6 %collective-permute-start.15 = (f32[200,128]{1,0:T(8,128)S(1)}, f32[200,128]{1,0:T(8,128)S(1)}, u32[]{:S(2)}, u32[]{:S(2)}) collective-permute-start(f32[200,128]{1,0:T(8,128)S(1)} %get-tuple-element.85), channel_id=1, source_target_pairs={{0,3},{1,0},{2,1},{3,2},{4,7},{5,4},{6,5},{7,6},{8,11},{9,8},{10,9... | collective-permute-start | bytes 307208 | tf_op jit(solution)/shard_map/ppermute | solution.py:648
  85.3 8.8 %collective-permute-start.14 = (f32[200,128]{1,0:T(8,128)S(1)}, f32[200,128]{1,0:T(8,128)S(1)}, u32[]{:S(2)}, u32[]{:S(2)}) collective-permute-start(f32[200,128]{1,0:T(8,128)S(1)} %get-tuple-element.85), channel_id=1, source_target_pairs={{0,1},{1,2},{2,3},{3,0},{4,5},{5,6},{6,7},{7,4},{8,9},{9,10},{10,1... | collective-permute-start | bytes 307208 | tf_op jit(solution)/shard_map/ppermute | solution.py:648
  (2 other events, 5.9 us)

commit v10 on v9

--- a/solution.py
+++ b/solution.py
@@ -209,7 +209,7 @@
     cond_out[grid.rows :, :] = names
     cap_out[...] = lookup(material[...], capacity)
     vent_out[...] = vent[...]
-    to_all(grid, pay, vent[...], cond, names)
+    to_all(grid, pay, vent[...], cond, names[0:1])
 
 
 def conductances(grid, cond, low_x, high_x, low_y, high_y):
@@ -677,7 +677,7 @@
     x_far_a, x_far_b = [lax.ppermute(part, "row", across) for part in face]
     cond, cap, vent, pay0 = call(
         functools.partial(k_first, grid, pairs),
-        (((n + 8, depth), F32), field, ((width, depth), F32), rows_of(8)),
+        (((n + 8, depth), F32), field, ((width, depth), F32), rows_of(1)),
         (tables, classes, vent_open),
         smem=1,
     )

time: 106 us -> 108 us (1.019)
    all_to_all x2, waiting for transfers between devices: 0.2 us -> 2.64 us  [exchange(): rec = lax.all_to_all(payload, 'row', 0, 0)]
    ppermute x10, starting transfers between devices: 11.9 us -> 14.1 us  [cyclic(): lax.ppermute(value, axis, [(i, (i + step) % count) for i in range(count)])]
    ppermute x10, waiting for transfers between devices: 4.95 us -> 3.13 us  [cyclic(): lax.ppermute(value, axis, [(i, (i + step) % count) for i in range(count)])]
    all_to_all x2, starting transfers between devices: 8.55 us -> 7.27 us  [exchange(): rec = lax.all_to_all(payload, 'row', 0, 0)]
  transfers between devices with their start and end apart: 19 -> 19, of which waited for: 4 -> 3; matrix products, arithmetic and copies ran while one was open for 0% -> 0% of each run, Pallas kernels for 8% -> 8%
where the time goes in v10:
time: 108 us; the launch traced here: 107 us
  blocking collectives  44.5 us (41%)
  starting transfers between devices  31.2 us (29%)
  Pallas kernels  19.1 us (18%)
  waiting for transfers between devices  10.3 us (10%)
  local copies, waits for them, and re-layouts  1.25 us (1%)
    all_to_all x3, blocking collectives, exchange(): rec = lax.all_to_all(payload, 'row', 0, 0)  24.2 us
    pallas_call x12, Pallas kernels, call(): pl.pallas_call(kernel, out_shape=tuple((jax.ShapeDtypeStruct(s, t) for s,...  19.1 us
    ppermute x10, starting transfers between devices, cyclic(): lax.ppermute(value, axis, [(i, (i + step) % count) for i in range(count)])  14.1 us
    all_to_all x1, blocking collectives, body(): sums = lax.all_to_all(pay5, ('row', 'col'), 0, 0)  10.2 us
    all_to_all x1, blocking collectives, body(): total = lax.all_to_all(pay7, ('row', 'col'), 0, 0)  10.1 us
    all_to_all x2, starting transfers between devices, exchange(): rec = lax.all_to_all(payload, 'row', 0, 0)  7.27 us
    ppermute x4, starting transfers between devices, xor_step(): return lax.ppermute(value, axis, [(i, i ^ k) for i in range(count)])  4.67 us
    all_to_all x1, waiting for transfers between devices, body(): sums = lax.all_to_all(pay3, ('row', 'col'), 0, 0)  4.56 us
  transfers between devices with their start and end apart: 19, of which 3 were waited for; matrix products, arithmetic and copies ran while one was open for 0% of the time, Pallas kernels for 8%

profile of v10, /device:TPU:0, one launch (start us, length us, event | category | flops | bytes accessed | tf_op | source)
XLA Modules:
  0.0 107.4 jit_solution(1714151886400040623)
XLA Ops:
  0.6 1.2 %copy-done = bf16[64,4,16,128]{3,2,1,0:T(8,128)(2,1)S(1)} copy-done((bf16[64,4,16,128]{3,2,1,0:T(8,128)(2,1)S(1)}, bf16[64,4,16,128]{3,2,1,0:T(8,128)(2,1)}, u32[]{:S(2)}) %copy-start) | copy-done | bytes 1048600
  2.3 4.0 %collective-permute-start.4 = (bf16[64,2048]{1,0:T(8,128)(2,1)S(1)}, bf16[64,2048]{1,0:T(8,128)(2,1)S(1)}, u32[]{:S(2)}, u32[]{:S(2)}) collective-permute-start(bf16[64,2048]{1,0:T(8,128)(2,1)S(1)} %get-tuple-element.55), channel_id=1, source_target_pairs={{0,24},{4,28},{8,16},{12,20},{16,8},{20,12},{24,0},{28,4},{1,25},{... | collective-permute-start | bytes 786440 | tf_op jit(solution)/shard_map/ppermute | solution.py:652
  7.0 1.2 %shard_map.94 = (f32[72,128]{1,0:T(8,128)S(1)}, f32[64,128]{1,0:T(8,128)S(1)}, f32[16,128]{1,0:T(8,128)S(1)}, f32[8,25,128]{2,1,0:T(8,128)}) custom-call(f32[18]{0:T(128)S(1)} %pad_maximum_fusion.tables, s32[64,128]{1,0:T(8,128)S(1)} %bitcast.13, f32[16,128]{1,0:T(8,128)S(1)} %copy-done.3), custom_call_target="tpu_custom_call" | custom-call | tf_op jit(solution)/shard_map/pallas_call | solution.py:614
  8.2 4.0 %collective-permute-start.1 = (f32[72,128]{1,0:T(8,128)S(1)}, f32[72,128]{1,0:T(8,128)S(1)}, u32[]{:S(2)}, u32[]{:S(2)}) collective-permute-start(f32[72,128]{1,0:T(8,128)S(1)} %get-tuple-element.49.cond_ref.cond), channel_id=1, source_target_pairs={{0,3},{1,0},{2,1},{3,2},{4,7},{5,4},{6,5},{7,6},{8,11},{9,8},{10,9... | collective-permute-start | bytes 110600 | tf_op jit(solution)/shard_map/ppermute | solution.py:648
  12.2 3.9 %all-to-all-start = ((f32[8,25,128]{2,1,0:T(8,128)}), f32[8,25,128]{2,1,0:T(8,128)S(1)}, u32[]{:S(2)}, u32[]{:S(2)}) async-start(f32[8,25,128]{2,1,0:T(8,128)} %get-tuple-element.50), calls=%async_computation | async-start | bytes 262144 | tf_op jit(solution)/shard_map/all_to_all | solution.py:657
  16.1 2.8 %shard_map.96 = (f32[64,64]{1,0:T(8,128)S(1)}, f32[64,128]{1,0:T(8,128)S(1)}, f32[64,128]{1,0:T(8,128)S(1)}) custom-call(bf16[64,8192]{1,0:T(8,128)(2,1)S(1)} %get-tuple-element.51.zm, f32[64,128]{1,0:T(8,128)S(1)} %bitcast.11, f32[72,128]{1,0:T(8,128)S(1)} %get-tuple-element.49.cond_ref.cond, f32[64,128]{1,0:T(8,128)S(1)} %get-tuple-element.47.cap_ref.cap), custom_call_target="tpu_custom_call" | custom-call | flops 1000 | bytes 1000 | tf_op jit(solution)/shard_map/pallas_call | solution.py:614
  19.0 2.6 %all-to-all-done.rec = f32[8,25,128]{2,1,0:T(8,128)S(1)} async-done(((f32[8,25,128]{2,1,0:T(8,128)}), f32[8,25,128]{2,1,0:T(8,128)S(1)}, u32[]{:S(2)}, u32[]{:S(2)}) %all-to-all-start) | async-done | bytes 102432 | tf_op jit(solution)/shard_map/all_to_all | solution.py:657
  21.6 4.0 %shard_map.97 = (f32[7,64,128]{2,1,0:T(8,128)S(1)}, f32[64,64]{1,0:T(8,128)S(1)}, f32[64,64]{1,0:T(8,128)S(1)}, f32[72,128]{1,0:T(8,128)S(1)}, f32[8,56,128]{2,1...) custom-call(s32[4]{0:T(128)S(1)} %pad_add_fusion.ids, ...), custom_call_target="tpu_custom_call" | custom-call | tf_op jit(solution)/shard_map/pallas_call | solution.py:614
  25.7 3.4 %all-to-all-start.1 = ((f32[8,56,128]{2,1,0:T(8,128)}), f32[8,56,128]{2,1,0:T(8,128)S(1)}, u32[]{:S(2)}, u32[]{:S(2)}) async-start(f32[8,56,128]{2,1,0:T(8,128)} %get-tuple-element.63), calls=%async_computation.1 | async-start | bytes 458752 | tf_op jit(solution)/shard_map/all_to_all | solution.py:657
  29.1 3.9 %collective-permute-start.7 = (f32[72,128]{1,0:T(8,128)S(1)}, f32[72,128]{1,0:T(8,128)S(1)}, u32[]{:S(2)}, u32[]{:S(2)}) collective-permute-start(f32[72,128]{1,0:T(8,128)S(1)} %get-tuple-element.62.field), channel_id=1, source_target_pairs={{0,3},{1,0},{2,1},{3,2},{4,7},{5,4},{6,5},{7,6},{8,11},{9,8},{10,9... | collective-permute-start | bytes 110600 | tf_op jit(solution)/shard_map/ppermute | solution.py:648
  33.0 2.3 %collective-permute-start.8 = (bf16[64,256]{1,0:T(8,128)(2,1)S(1)}, bf16[64,256]{1,0:T(8,128)(2,1)S(1)}, u32[]{:S(2)}, u32[]{:S(2)}) collective-permute-start(bf16[64,256]{1,0:T(8,128)(2,1)S(1)} %get-tuple-element.65), channel_id=1, source_target_pairs={{0,28},{4,8},{8,4},{12,16},{16,12},{20,24},{24,20},{28,0},{1,29},{... | collective-permute-start | bytes 98312 | tf_op jit(solution)/shard_map/ppermute | solution.py:677
  35.6 3.1 %collective-permute-done.6.low = f32[72,128]{1,0:T(8,128)S(1)} collective-permute-done((f32[72,128]{1,0:T(8,128)S(1)}, f32[72,128]{1,0:T(8,128)S(1)}, u32[]{:S(2)}, u32[]{:S(2)}) %collective-permute-start.6) | collective-permute-done | bytes 36896 | tf_op jit(solution)/shard_map/ppermute | solution.py:648
  38.8 1.3 %shard_map.98 = (f32[64,128]{1,0:T(8,128)S(1)}, f32[200,128]{1,0:T(8,128)S(1)}, f32[8,24,128]{2,1,0:T(8,128)S(1)}, f32[4,32,128]{2,1,0:T(8,128)S(1)}) custom-call(s32[4]{0:T(128)S(1)} %pad_add_fusion.ids, f32[7,64,128]{2,1,0:T(8,128)S(1)} %get-tuple-element.56.coef, f32[16,128]{1,0:T(8,128)S(1)} %get-tuple-element.48.vent, ...), custom_call_target="tpu_custom_call" | custom-call | tf_op jit(solution)/shard_map/pallas_call | solution.py:614
  40.8 1.3 %collective-permute-start.10 = (f32[200,128]{1,0:T(8,128)S(1)}, f32[200,128]{1,0:T(8,128)S(1)}, u32[]{:S(2)}, u32[]{:S(2)}) collective-permute-start(f32[200,128]{1,0:T(8,128)S(1)} %get-tuple-element.70), channel_id=1, source_target_pairs={{0,1},{1,2},{2,3},{3,0},{4,5},{5,6},{6,7},{7,4},{8,9},{9,10},{10,1... | collective-permute-start | bytes 307208 | tf_op jit(solution)/shard_map/ppermute | solution.py:648
  42.1 9.1 %all_to_all.40.rec = f32[8,24,128]{2,1,0:T(8,128)S(1)} all-to-all(f32[8,24,128]{2,1,0:T(8,128)S(1)} %get-tuple-element.73), channel_id=1, replica_groups=mesh['row'=8,'col'=4] {'row'}, dimensions={0} | all-to-all | bytes 196608 | tf_op jit(solution)/shard_map/all_to_all | solution.py:657
  51.2 1.8 %shard_map.99 = (f32[64,128]{1,0:T(8,128)S(1)}, f32[32,4,128]{2,1,0:T(4,128)}) custom-call(s32[4]{0:T(128)S(1)} %pad_add_fusion.ids, f32[7,64,128]{2,1,0:T(8,128)S(1)} %get-tuple-element.56.coef, f32[16,128]{1,0:T(8,128)S(1)} %get-tuple-element.48.vent, f32[64,128]{1,0:T(8,128)S(1)} %get-tuple-element.72.field.x0, ...), custom_call_target="tpu_custom_call" | custom-call | tf_op jit(solution)/shard_map/pallas_call | solution.py:614
  53.0 2.6 %all-to-all-start.3 = ((f32[32,4,128]{2,1,0:T(4,128)}), f32[32,4,128]{2,1,0:T(4,128)S(1)}, u32[]{:S(2)}, u32[]{:S(2)}) async-start(f32[32,4,128]{2,1,0:T(4,128)} %get-tuple-element.74._), calls=%async_computation.3 | async-start | bytes 131072 | tf_op jit(solution)/shard_map/all_to_all | solution.py:766
  55.6 2.9 %shard_map.100 = (f32[8,64,64]{2,1,0:T(8,128)}, f32[7,64,64]{2,1,0:T(8,128)S(1)}, s32[49]{0:T(128)S(1)}) custom-call(s32[4]{0:T(128)S(1)} %pad_add_fusion.ids, f32[7,64,128]{2,1,0:T(8,128)S(1)} %get-tuple-element.56.coef, f32[2,16,128]{2,1,0:T(8,128)S(1)} %get-tuple-element.57.vents, f32[6,128]{1,0:T(8,128)S(1)} %get-tuple-element.58.names, ...), custom_call_target="tpu_custom_call" | custom-call | flops 100000000 | bytes 4000000 | tf_op jit(solution)/shard_map/pallas_call | solution.py:614
  58.5 4.6 %all-to-all-done.3.rec = f32[32,4,128]{2,1,0:T(4,128)S(1)} async-done(((f32[32,4,128]{2,1,0:T(4,128)}), f32[32,4,128]{2,1,0:T(4,128)S(1)}, u32[]{:S(2)}, u32[]{:S(2)}) %all-to-all-start.3) | async-done | bytes 65568 | tf_op jit(solution)/shard_map/all_to_all | solution.py:766
  64.8 1.3 %collective-permute-start.12 = (f32[200,128]{1,0:T(8,128)S(1)}, f32[200,128]{1,0:T(8,128)S(1)}, u32[]{:S(2)}, u32[]{:S(2)}) collective-permute-start(f32[200,128]{1,0:T(8,128)S(1)} %get-tuple-element.80), channel_id=1, source_target_pairs={{0,1},{1,2},{2,3},{3,0},{4,5},{5,6},{6,7},{7,4},{8,9},{9,10},{10,1... | collective-permute-start | bytes 307208 | tf_op jit(solution)/shard_map/ppermute | solution.py:648
  66.1 7.6 %all_to_all.41.rec = f32[8,24,128]{2,1,0:T(8,128)S(1)} all-to-all(f32[8,24,128]{2,1,0:T(8,128)S(1)} %get-tuple-element.79), channel_id=1, replica_groups=mesh['row'=8,'col'=4] {'row'}, dimensions={0} | all-to-all | bytes 196608 | tf_op jit(solution)/shard_map/all_to_all | solution.py:657
  74.9 10.2 %all_to_all.42.rec = f32[32,4,128]{2,1,0:T(4,128)S(1)} all-to-all(f32[32,4,128]{2,1,0:T(4,128)S(1)} %get-tuple-element.81), channel_id=1, replica_groups=mesh['row'=8,'col'=4] {'row','col'}, dimensions={0} | all-to-all | bytes 131072 | tf_op jit(solution)/shard_map/all_to_all | solution.py:783
  88.2 7.6 %all_to_all.43.rec = f32[8,24,128]{2,1,0:T(8,128)S(1)} all-to-all(f32[8,24,128]{2,1,0:T(8,128)S(1)} %get-tuple-element.84), channel_id=1, replica_groups=mesh['row'=8,'col'=4] {'row'}, dimensions={0} | all-to-all | bytes 196608 | tf_op jit(solution)/shard_map/all_to_all | solution.py:657
  96.5 10.1 %all_to_all.44.rec = f32[32,2,128]{2,1,0:T(2,128)S(1)} all-to-all(f32[32,2,128]{2,1,0:T(2,128)S(1)} %get-tuple-element.86), channel_id=1, replica_groups=mesh['row'=8,'col'=4] {'row','col'}, dimensions={0} | all-to-all | bytes 65536 | tf_op jit(solution)/shard_map/all_to_all | solution.py:798
  (48 shorter events, 10.0 us)
Async XLA Ops:
  1.9 5.1 %copy-start.2 = (s32[4,16,128]{2,1,0:T(8,128)S(1)}, s32[4,16,128]{2,1,0:T(8,128)}, u32[]{:S(2)}) copy-start(s32[4,16,128]{2,1,0:T(8,128)} %param.8) | copy-start | bytes 98308
  1.9 5.1 %copy-start.3 = (f32[16,128]{1,0:T(8,128)S(1)}, f32[16,128]{1,0:T(8,128)}, u32[]{:S(2)}) copy-start(f32[16,128]{1,0:T(8,128)} %vent.1) | copy-start | bytes 24580
  2.2 4.6 %copy-start.6 = (s32[1,1,2]{2,1,0:T(1,128)S(1)}, s32[1,1,2]{2,1,0:T(1,128)}, u32[]{:S(2)}) copy-start(s32[1,1,2]{2,1,0:T(1,128)} %param.12) | copy-start | bytes 28
  2.2 4.6 %copy-start.4 = (f32[8]{0:T(128)S(1)}, f32[8]{0:T(128)}, u32[]{:S(2)}) copy-start(f32[8]{0:T(128)} %param.9) | copy-start | bytes 100
  2.3 4.6 %copy-start.5 = (f32[8]{0:T(128)S(1)}, f32[8]{0:T(128)}, u32[]{:S(2)}) copy-start(f32[8]{0:T(128)} %param.10) | copy-start | bytes 100
  2.3 19.3 %collective-permute-start.4 = (bf16[64,2048]{1,0:T(8,128)(2,1)S(1)}, bf16[64,2048]{1,0:T(8,128)(2,1)S(1)}, u32[]{:S(2)}, u32[]{:S(2)}) collective-permute-start(bf16[64,2048]{1,0:T(8,128)(2,1)S(1)} %get-tuple-element.55), channel_id=1, source_target_pairs={{0,24},{4,28},{8,16},{12,20},{16,8},{20,12},{24,0},{28,4},{1,25},{... | collective-permute-start | bytes 786440 | tf_op jit(solution)/shard_map/ppermute | solution.py:652
  6.2 15.4 %collective-permute-start.3 = (bf16[64,2048]{1,0:T(8,128)(2,1)S(1)}, bf16[64,2048]{1,0:T(8,128)(2,1)S(1)}, u32[]{:S(2)}, u32[]{:S(2)}) collective-permute-start(bf16[64,2048]{1,0:T(8,128)(2,1)S(1)} %get-tuple-element.55), channel_id=1, source_target_pairs={{0,16},{4,20},{8,24},{12,28},{16,0},{20,4},{24,8},{28,12},{1,17},{... | collective-permute-start | bytes 786440 | tf_op jit(solution)/shard_map/ppermute | solution.py:652
  6.7 14.9 %collective-permute-start.2 = (bf16[64,2048]{1,0:T(8,128)(2,1)S(1)}, bf16[64,2048]{1,0:T(8,128)(2,1)S(1)}, u32[]{:S(2)}, u32[]{:S(2)}) collective-permute-start(bf16[64,2048]{1,0:T(8,128)(2,1)S(1)} %get-tuple-element.55), channel_id=1, source_target_pairs={{0,8},{4,12},{8,0},{12,4},{16,24},{20,28},{24,16},{28,20},{1,9},{5... | collective-permute-start | bytes 786440 | tf_op jit(solution)/shard_map/ppermute | solution.py:652
  8.2 10.7 %collective-permute-start.1 = (f32[72,128]{1,0:T(8,128)S(1)}, f32[72,128]{1,0:T(8,128)S(1)}, u32[]{:S(2)}, u32[]{:S(2)}) collective-permute-start(f32[72,128]{1,0:T(8,128)S(1)} %get-tuple-element.49.cond_ref.cond), channel_id=1, source_target_pairs={{0,3},{1,0},{2,1},{3,2},{4,7},{5,4},{6,5},{7,6},{8,11},{9,8},{10,9... | collective-permute-start | bytes 110600 | tf_op jit(solution)/shard_map/ppermute | solution.py:648
  12.2 6.7 %collective-permute-start = (f32[72,128]{1,0:T(8,128)S(1)}, f32[72,128]{1,0:T(8,128)S(1)}, u32[]{:S(2)}, u32[]{:S(2)}) collective-permute-start(f32[72,128]{1,0:T(8,128)S(1)} %get-tuple-element.49.cond_ref.cond), channel_id=1, source_target_pairs={{0,1},{1,2},{2,3},{3,0},{4,5},{5,6},{6,7},{7,4},{8,9},{9,10},{10,1... | collective-permute-start | bytes 110600 | tf_op jit(solution)/shard_map/ppermute | solution.py:648
  12.2 9.4 %all-to-all-start = ((f32[8,25,128]{2,1,0:T(8,128)}), f32[8,25,128]{2,1,0:T(8,128)S(1)}, u32[]{:S(2)}, u32[]{:S(2)}) async-start(f32[8,25,128]{2,1,0:T(8,128)} %get-tuple-element.50), calls=%async_computation | async-start | bytes 262144 | tf_op jit(solution)/shard_map/all_to_all | solution.py:657
  25.6 13.1 %collective-permute-start.5 = (bf16[64,4608]{1,0:T(8,128)(2,1)}, bf16[64,4608]{1,0:T(8,128)(2,1)S(1)}, u32[]{:S(2)}, u32[]{:S(2)}) collective-permute-start(bf16[64,4608]{1,0:T(8,128)(2,1)} %get-tuple-element.60), channel_id=1, source_target_pairs={{0,4},{4,0},{8,12},{12,8},{16,20},{20,16},{24,28},{28,24},{1,5},{5... | collective-permute-start | bytes 1769480 | tf_op jit(solution)/shard_map/ppermute | solution.py:652
  25.7 13.1 %all-to-all-start.1 = ((f32[8,56,128]{2,1,0:T(8,128)}), f32[8,56,128]{2,1,0:T(8,128)S(1)}, u32[]{:S(2)}, u32[]{:S(2)}) async-start(f32[8,56,128]{2,1,0:T(8,128)} %get-tuple-element.63), calls=%async_computation.1 | async-start | bytes 458752 | tf_op jit(solution)/shard_map/all_to_all | solution.py:657
  29.1 6.5 %collective-permute-start.7 = (f32[72,128]{1,0:T(8,128)S(1)}, f32[72,128]{1,0:T(8,128)S(1)}, u32[]{:S(2)}, u32[]{:S(2)}) collective-permute-start(f32[72,128]{1,0:T(8,128)S(1)} %get-tuple-element.62.field), channel_id=1, source_target_pairs={{0,3},{1,0},{2,1},{3,2},{4,7},{5,4},{6,5},{7,6},{8,11},{9,8},{10,9... | collective-permute-start | bytes 110600 | tf_op jit(solution)/shard_map/ppermute | solution.py:648
  33.0 5.8 %collective-permute-start.6 = (f32[72,128]{1,0:T(8,128)S(1)}, f32[72,128]{1,0:T(8,128)S(1)}, u32[]{:S(2)}, u32[]{:S(2)}) collective-permute-start(f32[72,128]{1,0:T(8,128)S(1)} %get-tuple-element.62.field), channel_id=1, source_target_pairs={{0,1},{1,2},{2,3},{3,0},{4,5},{5,6},{6,7},{7,4},{8,9},{9,10},{10,1... | collective-permute-start | bytes 110600 | tf_op jit(solution)/shard_map/ppermute | solution.py:648
  33.0 9.1 %collective-permute-start.8 = (bf16[64,256]{1,0:T(8,128)(2,1)S(1)}, bf16[64,256]{1,0:T(8,128)(2,1)S(1)}, u32[]{:S(2)}, u32[]{:S(2)}) collective-permute-start(bf16[64,256]{1,0:T(8,128)(2,1)S(1)} %get-tuple-element.65), channel_id=1, source_target_pairs={{0,28},{4,8},{8,4},{12,16},{16,12},{20,24},{24,20},{28,0},{1,29},{... | collective-permute-start | bytes 98312 | tf_op jit(solution)/shard_map/ppermute | solution.py:677
  35.3 6.8 %collective-permute-start.9 = (bf16[64,256]{1,0:T(8,128)(2,1)S(1)}, bf16[64,256]{1,0:T(8,128)(2,1)S(1)}, u32[]{:S(2)}, u32[]{:S(2)}) collective-permute-start(bf16[64,256]{1,0:T(8,128)(2,1)S(1)} %get-tuple-element.66), channel_id=1, source_target_pairs={{0,28},{4,8},{8,4},{12,16},{16,12},{20,24},{24,20},{28,0},{1,29},{... | collective-permute-start | bytes 98312 | tf_op jit(solution)/shard_map/ppermute | solution.py:677
  40.0 11.1 %collective-permute-start.11 = (f32[200,128]{1,0:T(8,128)S(1)}, f32[200,128]{1,0:T(8,128)S(1)}, u32[]{:S(2)}, u32[]{:S(2)}) collective-permute-start(f32[200,128]{1,0:T(8,128)S(1)} %get-tuple-element.70), channel_id=1, source_target_pairs={{0,3},{1,0},{2,1},{3,2},{4,7},{5,4},{6,5},{7,6},{8,11},{9,8},{10,9... | collective-permute-start | bytes 307208 | tf_op jit(solution)/shard_map/ppermute | solution.py:648
  40.8 10.4 %collective-permute-start.10 = (f32[200,128]{1,0:T(8,128)S(1)}, f32[200,128]{1,0:T(8,128)S(1)}, u32[]{:S(2)}, u32[]{:S(2)}) collective-permute-start(f32[200,128]{1,0:T(8,128)S(1)} %get-tuple-element.70), channel_id=1, source_target_pairs={{0,1},{1,2},{2,3},{3,0},{4,5},{5,6},{6,7},{7,4},{8,9},{9,10},{10,1... | collective-permute-start | bytes 307208 | tf_op jit(solution)/shard_map/ppermute | solution.py:648
  53.0 10.1 %all-to-all-start.3 = ((f32[32,4,128]{2,1,0:T(4,128)}), f32[32,4,128]{2,1,0:T(4,128)S(1)}, u32[]{:S(2)}, u32[]{:S(2)}) async-start(f32[32,4,128]{2,1,0:T(4,128)} %get-tuple-element.74._), calls=%async_computation.3 | async-start | bytes 131072 | tf_op jit(solution)/shard_map/all_to_all | solution.py:766
  64.0 9.6 %collective-permute-start.13 = (f32[200,128]{1,0:T(8,128)S(1)}, f32[200,128]{1,0:T(8,128)S(1)}, u32[]{:S(2)}, u32[]{:S(2)}) collective-permute-start(f32[200,128]{1,0:T(8,128)S(1)} %get-tuple-element.80), channel_id=1, source_target_pairs={{0,3},{1,0},{2,1},{3,2},{4,7},{5,4},{6,5},{7,6},{8,11},{9,8},{10,9... | collective-permute-start | bytes 307208 | tf_op jit(solution)/shard_map/ppermute | solution.py:648
  64.8 8.9 %collective-permute-start.12 = (f32[200,128]{1,0:T(8,128)S(1)}, f32[200,128]{1,0:T(8,128)S(1)}, u32[]{:S(2)}, u32[]{:S(2)}) collective-permute-start(f32[200,128]{1,0:T(8,128)S(1)} %get-tuple-element.80), channel_id=1, source_target_pairs={{0,1},{1,2},{2,3},{3,0},{4,5},{5,6},{6,7},{7,4},{8,9},{9,10},{10,1... | collective-permute-start | bytes 307208 | tf_op jit(solution)/shard_map/ppermute | solution.py:648
  86.1 9.6 %collective-permute-start.15 = (f32[200,128]{1,0:T(8,128)S(1)}, f32[200,128]{1,0:T(8,128)S(1)}, u32[]{:S(2)}, u32[]{:S(2)}) collective-permute-start(f32[200,128]{1,0:T(8,128)S(1)} %get-tuple-element.85), channel_id=1, source_target_pairs={{0,3},{1,0},{2,1},{3,2},{4,7},{5,4},{6,5},{7,6},{8,11},{9,8},{10,9... | collective-permute-start | bytes 307208 | tf_op jit(solution)/shard_map/ppermute | solution.py:648
  87.0 8.8 %collective-permute-start.14 = (f32[200,128]{1,0:T(8,128)S(1)}, f32[200,128]{1,0:T(8,128)S(1)}, u32[]{:S(2)}, u32[]{:S(2)}) collective-permute-start(f32[200,128]{1,0:T(8,128)S(1)} %get-tuple-element.85), channel_id=1, source_target_pairs={{0,1},{1,2},{2,3},{3,0},{4,5},{5,6},{6,7},{7,4},{8,9},{9,10},{10,1... | collective-permute-start | bytes 307208 | tf_op jit(solution)/shard_map/ppermute | solution.py:648
  (2 other events, 5.2 us)
